TPU v7x, 32 devices: a whole 2x2x4 slice. The times are simulated.
32 devices in a mesh: groups: 2 (over y), owners: 4 (over z), split: 4 (over x, core).
Axes of the slice: x: 2, y: 2, z: 4, core: 2. Of those that a mesh axis runs over, the one named last changes fastest.
Arguments:
- embeddings: bfloat16 [16384, 4096], P(('groups', 'owners', 'split')), parts along dimension 0, may hold values from -6 to 6
- basis: bfloat16 [4096, 256], replicated, may hold values from -0.09375 to 0.09375
- owner_ids: int32 [16384, 1], P(('groups', 'owners', 'split')), parts along dimension 0, may hold values from 0 to 3; in each aligned block of 512 rows (0 to 511, 512 to 1023, ...) at most 256 rows name the same one
- sub_cluster: int32 [16384], P(('groups', 'owners', 'split')), parts along dimension 0, may hold values from 0 to 7, as said below
Outputs:
- nearest: float32 [16384], P(('groups', 'owners', 'split')), parts along dimension 0
There are 2 independent parts, one for each index of `groups`. A program takes and returns all parts, laid end to end along the dimension named above; an argument that names none is the same for every part. Nothing has to cross between parts.
Inputs may be any that keep to these rules, and one draw needn't show every extreme that they name: `owner_ids`: among the rows of one device no value is named by more than 256 rows, a bound that some block reaches. `sub_cluster`: some clusters hold a single document.
All inputs are finite; a program needn't handle non-finite values.
Results may differ from a plain program's by a relative error of at most 0.0014.
Values may be sent and summed in bfloat16 or wider, within the bound.
No kernel may reach another device: no remote copies, remote signals or barrier semaphores. Data moves between devices by JAX's collectives and lax.ppermute only.
A program may use at most 64 MiB of HBM per device.

v0:
```python
import jax
import jax.numpy as jnp
from jax import lax
from jax.sharding import PartitionSpec as P

CPO = 8


def unitize(source, basis):
    projected = jnp.dot(source, basis, preferred_element_type=jnp.float32)
    return (
        projected * lax.rsqrt(jnp.sum(projected * projected, axis=1, keepdims=True) + 1e-06)
    ).astype(jnp.bfloat16)


def cosines(query_rows, key_rows):
    return lax.dot_general(
        query_rows, key_rows, (((1,), (1,)), ((), ())), preferred_element_type=jnp.float32
    )


def per_device(embeddings, basis, owner_ids, sub_cluster):
    row_count = embeddings.shape[0]
    owner_count = lax.axis_size("owners")
    capacity = 2 * row_count // owner_count
    owner_flat = owner_ids[:, 0]
    cluster = owner_flat * CPO + sub_cluster
    matches = (owner_flat[:, None] == jnp.arange(owner_count, dtype=jnp.int32)[None, :]).astype(
        jnp.int32
    )
    places = jnp.sum(jnp.cumsum(matches, axis=0) * matches, axis=1) - 1
    target = owner_flat * capacity + places
    labels = (
        jnp.full((owner_count * capacity,), -1, jnp.int32)
        .at[target]
        .set(cluster)
        .reshape(owner_count, capacity)
    )
    unit_rows = unitize(embeddings, basis)
    packed = (
        jnp.zeros((owner_count * capacity, basis.shape[1]), jnp.bfloat16).at[target].set(unit_rows)
    )
    packed = packed.reshape(owner_count, capacity, basis.shape[1])
    arrived, tag_rows = (
        lax.all_to_all(packed, "owners", split_axis=0, concat_axis=0, tiled=True),
        lax.all_to_all(labels, "owners", split_axis=0, concat_axis=0, tiled=True),
    )
    local_units = arrived.reshape(owner_count * capacity, basis.shape[1])
    tag_flat = tag_rows.reshape(-1)
    slot_count = local_units.shape[0]
    own_index = lax.axis_index("split") * slot_count + jnp.arange(slot_count, dtype=jnp.int32)
    initial = jnp.full((slot_count,), -1.0, jnp.float32)
    key_rows = lax.all_gather(local_units, "split", axis=0, tiled=True)
    key_tags = lax.all_gather(tag_flat, "split", axis=0, tiled=True)
    scores = cosines(local_units, key_rows)
    other_index = jnp.arange(key_rows.shape[0], dtype=jnp.int32)
    same_cluster = (
        (tag_flat[:, None] == key_tags[None, :])
        & (key_tags[None, :] >= 0)
        & (own_index[:, None] != other_index[None, :])
    )
    scored = jnp.maximum(
        initial, jnp.max(jnp.where(same_cluster, scores, jnp.float32(-2.0)), axis=1)
    )
    returned = lax.all_to_all(
        scored.reshape(owner_count, capacity), "owners", split_axis=0, concat_axis=0, tiled=True
    )
    return returned.reshape(-1)[target]


def solution(mesh):
    placed = (
        P(("groups", "owners", "split"), None),
        P(),
        P(("groups", "owners", "split"), None),
        P(("groups", "owners", "split")),
    )
    return jax.shard_map(
        per_device,
        mesh=mesh,
        in_specs=placed,
        out_specs=P(("groups", "owners", "split")),
        check_vma=False,
    )
```

profile of v0, /device:TPU:0, one launch (start us, length us, event | category | flops | bytes accessed | tf_op | source)
XLA Modules:
  0.0 88.5 jit_solution(8313643271268236927)
XLA Ops:
  6.5 0.8 fusion.5
  7.4 1.2 %reduce-window.6 = s32[4,4,128]{2,1,0:T(4,128)S(1)} reduce-window(s32[4,4,128]{2,1,0:T(4,128)S(1)} %fusion.5, s32[]{:T(128)} %constant.14.clone.1), window={size=1x1x128 pad=0_0x0_0x127_0}, to_apply=%region_0.0 | reduce-window | flops 260096 | bytes 16388 | tf_op jit(solution)/shard_map/reduce-window
  8.6 0.2 slice_reduce_fusion
  8.8 0.2 reduce-window.9
  9.0 0.1 add_bitcast_fusion
  9.1 0.7 fusion.4
  9.8 0.7 compare_select_fusion
  10.5 0.0 copy-start.1
  10.5 0.0 copy-start.2
  10.5 3.5 %multiply_reduce_fusion = (f32[512]{0:T(512)S(1)}, f32[512,256]{0,1:T(8,128)S(1)}) fusion(bf16[512,4096]{1,0:T(8,128)(2,1)} %param.4, bf16[4096,256]{1,0:T(8,128)(2,1)S(1)} %copy-done), kind=kOutput, calls=%fused_computation.7 | convolution fusion | flops 1074003456 | bytes 6817792 | tf_op jit(solution)/shard_map/dot_general | solution.py:10
  14.1 0.1 copy.6
  14.2 2.5 %scatter_custom_fusion.1 = bf16[1024,256]{1,0:T(8,128)(2,1)S(1)} fusion(s32[512]{0:T(512)S(1)} %bitcast.38, bf16[512,256]{1,0:T(8,128)(2,1)S(1)} %copy.6, bf16[]{:T(256)} %constant.5.clone.1), kind=kCustom, calls=%fused_computation.8 | custom fusion | bytes 524290 | tf_op jit(solution)/shard_map/scatter | solution.py:41
  16.7 20.7 %all_to_all.20 = bf16[4,256,256]{2,1,0:T(8,128)(2,1)} all-to-all(bf16[4,256,256]{2,1,0:T(8,128)(2,1)S(1)} %bitcast.32), channel_id=1, replica_groups=mesh['groups'=2,'owners'=4,'split'=4] {'owners'}, dimensions={0} | all-to-all | bytes 1048576 | tf_op jit(solution)/shard_map/all_to_all | solution.py:45
  37.4 0.0 all-gather.2.cloned.1.call-update
  37.5 3.0 %scatter_custom_fusion = s32[1024]{0:T(1024)} fusion(s32[512]{0:T(512)S(1)} %bitcast.39, s32[512]{0:T(512)S(1)} %multiply_add_fusion, s32[]{:T(128)} %constant.12.clone.1), kind=kCustom, calls=%fused_computation.25 | custom fusion | bytes 4100 | tf_op jit(solution)/shard_map/scatter | solution.py:36
  40.5 3.2 %all-to-all-start = ((s32[4,1,256]{2,1,0:T(1,128)}), s32[4,1,256]{2,1,0:T(1,128)S(1)}, u32[]{:S(2)}, u32[]{:S(2)}) async-start(s32[4,1,256]{2,1,0:T(1,128)} %bitcast.5), calls=%async_computation | async-start | bytes 8192 | tf_op jit(solution)/shard_map/all_to_all | solution.py:46
  43.7 5.5 %all-to-all-done = s32[4,1,256]{2,1,0:T(1,128)S(1)} async-done(((s32[4,1,256]{2,1,0:T(1,128)}), s32[4,1,256]{2,1,0:T(1,128)S(1)}, u32[]{:S(2)}, u32[]{:S(2)}) %all-to-all-start) | async-done | bytes 4128 | tf_op jit(solution)/shard_map/all_to_all | solution.py:46
  49.3 5.2 %all_gather.6 = s32[4096]{0:T(1024)S(1)} all-gather(s32[1024]{0:T(1024)S(1)} %bitcast.36), channel_id=1, replica_groups=mesh['groups'=2,'owners'=4,'split'=4] {'split'}, dimensions={0}, use_global_device_ids=true | all-gather | bytes 20480 | tf_op jit(solution)/shard_map/all_gather | solution.py:54
  54.5 4.9 %all-gather.2.cloned.1.call-done = bf16[4096,256]{1,0:T(8,128)(2,1)} async-done(((bf16[1024,256]{1,0:T(8,128)(2,1)}), bf16[4096,256]{1,0:T(8,128)(2,1)}) %all-gather.2.cloned.1.call-update) | async-done | bytes 2097168 | tf_op jit(solution)/shard_map/all_gather | solution.py:53
  59.4 8.1 %select_reduce_fusion = f32[1024]{0:T(1024)S(1)} fusion(bf16[1024,256]{1,0:T(8,128)(2,1)} %bitcast.31, bf16[4096,256]{1,0:T(8,128)(2,1)} %all-gather.2.cloned.1.call-done, s32[1024]{0:T(1024)S(1)} %iota_add_fusion, s32[4096]{0:T(1024)S(1)} %all_gather.6, s32[1024]{0:T(1024)S(1)} %bitcast.37, pred[4096]{0:T(1024)(128)(4,1)S(1)} %broadcast_compare_fusion), kind=kOutput, calls=%fused_computation.3 | convolution fusion | flops 2172648448 | bytes 2654208 | tf_op jit(solution)/shard_map/dot_general | solution.py:17
  67.4 0.6 broadcast_maximum_fusion
  68.0 4.6 %all-to-all-start.2 = ((f32[4,1,256]{2,1,0:T(1,128)}), f32[4,1,256]{2,1,0:T(1,128)S(1)}, u32[]{:S(2)}, u32[]{:S(2)}) async-start(f32[4,1,256]{2,1,0:T(1,128)} %bitcast.9), calls=%async_computation.2 | async-start | bytes 8192 | tf_op jit(solution)/shard_map/all_to_all | solution.py:65
  72.7 5.6 %all-to-all-done.2 = f32[4,1,256]{2,1,0:T(1,128)S(1)} async-done(((f32[4,1,256]{2,1,0:T(1,128)}), f32[4,1,256]{2,1,0:T(1,128)S(1)}, u32[]{:S(2)}, u32[]{:S(2)}) %all-to-all-start.2) | async-done | bytes 4128 | tf_op jit(solution)/shard_map/all_to_all | solution.py:65
  78.2 3.4 %gather_fusion = f32[512]{0:T(512)} fusion(f32[1024]{0:T(1024)S(1)} %bitcast.29, s32[1024]{0:T(1024)S(1)} %pad_clamp_fusion), kind=kCustom, calls=%fused_computation | custom fusion | bytes 6144 | tf_op jit(solution)/shard_map/gather | solution.py:68
  (12 shorter events, 0.1 us)
Async XLA Ops:
  6.5 3.9 %copy-start = (bf16[4096,256]{1,0:T(8,128)(2,1)S(1)}, bf16[4096,256]{1,0:T(8,128)(2,1)}, u32[]{:S(2)}) copy-start(bf16[4096,256]{1,0:T(8,128)(2,1)} %param.5) | copy-start | bytes 6291460
  6.5 52.8 %all-gather.2.cloned.1.call-start = ((), (), s32[]{:S(2)}) async-start(), calls=%async_computation.3 | async-start | bytes 2621440 | tf_op jit(solution)/shard_map/all_gather | solution.py:53
  10.5 27.0 %copy-start.1 = (s32[512,1]{0,1:T(1,128)S(1)}, s32[512,1]{0,1:T(1,128)}, u32[]{:S(2)}) copy-start(s32[512,1]{0,1:T(1,128)} %param.6) | copy-start | bytes 6148
  10.5 27.0 %copy-start.2 = (s32[512]{0:T(512)S(1)}, s32[512]{0:T(512)}, u32[]{:S(2)}) copy-start(s32[512]{0:T(512)} %param.7) | copy-start | bytes 6148
  40.5 8.8 %all-to-all-start = ((s32[4,1,256]{2,1,0:T(1,128)}), s32[4,1,256]{2,1,0:T(1,128)S(1)}, u32[]{:S(2)}, u32[]{:S(2)}) async-start(s32[4,1,256]{2,1,0:T(1,128)} %bitcast.5), calls=%async_computation | async-start | bytes 8192 | tf_op jit(solution)/shard_map/all_to_all | solution.py:46
  68.0 10.2 %all-to-all-start.2 = ((f32[4,1,256]{2,1,0:T(1,128)}), f32[4,1,256]{2,1,0:T(1,128)S(1)}, u32[]{:S(2)}, u32[]{:S(2)}) async-start(f32[4,1,256]{2,1,0:T(1,128)} %bitcast.9), calls=%async_computation.2 | async-start | bytes 8192 | tf_op jit(solution)/shard_map/all_to_all | solution.py:65
Sparse Core Ops, SparseCore 0:
  37.6 21.7 all-gather.1
where the time goes:
time: 88.9 us; the launch traced here: 88.5 us
  blocking collectives  25.9 us (29%)
  waiting for transfers between devices  16 us (18%)
  between operations  13.5 us (15%)
  matrix products  11.6 us (13%)
  local copies, waits for them, and re-layouts  9.27 us (10%)
  starting transfers between devices  7.84 us (9%)
  other arithmetic  4.37 us (5%)
    all_to_all x1, blocking collectives, per_device(): lax.all_to_all(packed, 'owners', split_axis=0, concat_axis=0, tiled=True)  20.7 us
    dot_general x1, matrix products, cosines(): lax.dot_general(query_rows, key_rows, (((1,), (1,)), ((), ())), preferred...  8.05 us
    all_to_all x1, waiting for transfers between devices, per_device(): lax.all_to_all(scored.reshape(owner_count, capacity), 'owners', split_axi...  5.57 us
    all_to_all x1, waiting for transfers between devices, per_device(): lax.all_to_all(labels, 'owners', split_axis=0, concat_axis=0, tiled=True)  5.53 us
    all_gather x1, blocking collectives, per_device(): key_tags = lax.all_gather(tag_flat, 'split', axis=0, tiled=True)  5.21 us
    all_gather x1, waiting for transfers between devices, per_device(): key_rows = lax.all_gather(local_units, 'split', axis=0, tiled=True)  4.9 us
    all_to_all x1, starting transfers between devices, per_device(): lax.all_to_all(scored.reshape(owner_count, capacity), 'owners', split_axi...  4.6 us
    dot_general x1, matrix products, unitize(): projected = jnp.dot(source, basis, preferred_element_type=jnp.float32)  3.5 us
  transfers between devices with their start and end apart: 3, of which 3 were waited for; matrix products, arithmetic and copies ran while one was open for 3% of the time, Pallas kernels for 0%

commit v1 on v0

v1 whole, which is shorter than its diff:
```python
import functools

import jax
import jax.numpy as jnp
from jax import lax
from jax.experimental import pallas as pl
from jax.experimental.pallas import tpu as pltpu
from jax.sharding import PartitionSpec as P

CPO = 8
LANES = 128
TAG_ROWS = 16
ABSENT = -2.0
VMEM_LIMIT = 48 * 1024 * 1024


def project_kernel(source_ref, basis_ref, owner_ref, sub_ref, packed_ref, total_ref):
    step = pl.program_id(0)
    row_count = total_ref.shape[0]
    part = jnp.dot(source_ref[...], basis_ref[...], preferred_element_type=jnp.float32)

    @pl.when(step == 0)
    def _():
        total_ref[...] = part

    @pl.when(step > 0)
    def _():
        total_ref[...] += part

    @pl.when(step == pl.num_programs(0) - 1)
    def _():
        projected = total_ref[...]
        norms = jnp.sum(projected * projected, axis=1, keepdims=True)
        packed_ref[:row_count, :] = (projected * lax.rsqrt(norms + 1e-06)).astype(jnp.bfloat16)
        tags = (owner_ref[...] * CPO + sub_ref[...] + 1).astype(jnp.float32)
        width = packed_ref.shape[1]
        tags = jnp.concatenate(
            [tags, jnp.zeros((TAG_ROWS - tags.shape[0], LANES), jnp.float32)], axis=0
        )
        tags = jnp.concatenate(
            [tags, jnp.zeros((TAG_ROWS, width - LANES), jnp.float32)], axis=1
        )
        packed_ref[row_count:, :] = tags.astype(jnp.bfloat16)


def project(embeddings, basis, owner_ids, sub_cluster):
    row_count, depth = embeddings.shape
    width = basis.shape[1]
    step_depth = 512
    tag_shape = (row_count // LANES, LANES)
    return pl.pallas_call(
        project_kernel,
        grid=(depth // step_depth,),
        in_specs=[
            pl.BlockSpec((row_count, step_depth), lambda k: (0, k)),
            pl.BlockSpec((step_depth, width), lambda k: (k, 0)),
            pl.BlockSpec(tag_shape, lambda k: (0, 0)),
            pl.BlockSpec(tag_shape, lambda k: (0, 0)),
        ],
        out_specs=pl.BlockSpec((row_count + TAG_ROWS, width), lambda k: (0, 0)),
        out_shape=jax.ShapeDtypeStruct((row_count + TAG_ROWS, width), jnp.bfloat16),
        scratch_shapes=[pltpu.VMEM((row_count, width), jnp.float32)],
        compiler_params=pltpu.CompilerParams(vmem_limit_bytes=VMEM_LIMIT),
        cost_estimate=pl.CostEstimate(
            flops=2 * row_count * depth * width,
            bytes_accessed=2 * depth * (row_count + width),
            transcendentals=0,
        ),
    )(embeddings, basis, owner_ids.reshape(tag_shape), sub_cluster.reshape(tag_shape))


def score_kernel(row_blocks, own_first, want_rows, *refs):
    key_ref, row_refs = refs[0], refs[1 : 1 + row_blocks]
    col_out = refs[1 + row_blocks]
    row_out = refs[2 + row_blocks] if want_rows else None
    row_count = key_ref.shape[0] - TAG_ROWS
    tiles = row_count // LANES
    keys = key_ref[:row_count, :]
    key_tags = key_ref[row_count:, :LANES].astype(jnp.float32)
    best = [jnp.full((8, LANES), ABSENT, jnp.float32) for _ in range(tiles)]
    for block, row_ref in enumerate(row_refs):
        row_tags = row_ref[row_count:, :LANES].astype(jnp.float32)
        for tile in range(tiles):
            scores = lax.dot_general(
                row_ref[tile * LANES : (tile + 1) * LANES, :],
                keys,
                (((1,), (1,)), ((), ())),
                preferred_element_type=jnp.float32,
            )
            tags = jnp.broadcast_to(row_tags[tile : tile + 1, :], (LANES, LANES)).T
            across = None
            for at in range(tiles):
                same = tags == jnp.broadcast_to(key_tags[at : at + 1, :], (LANES, LANES))
                if own_first and block == 0 and at == tile:
                    same = same & (
                        lax.broadcasted_iota(jnp.int32, (LANES, LANES), 0)
                        != lax.broadcasted_iota(jnp.int32, (LANES, LANES), 1)
                    )
                kept = jnp.where(same, scores[:, at * LANES : (at + 1) * LANES], ABSENT)
                best[at] = jnp.maximum(
                    best[at], jnp.max(kept.reshape(LANES // 8, 8, LANES), axis=0)
                )
                if want_rows:
                    across = kept if across is None else jnp.maximum(across, kept)
            if want_rows:
                at = block * tiles + tile
                row_out[at : at + 1, :] = jnp.max(across.T, axis=0, keepdims=True)
    for at in range(tiles):
        col_out[at : at + 1, :] = jnp.max(best[at], axis=0, keepdims=True)


def score(keys, rows, own_first, want_rows):
    row_count, width = keys.shape[0] - TAG_ROWS, keys.shape[1]
    tiles = row_count // LANES
    out_shape = [jax.ShapeDtypeStruct((tiles, LANES), jnp.float32)]
    if want_rows:
        out_shape.append(jax.ShapeDtypeStruct((tiles * len(rows), LANES), jnp.float32))
    whole = pl.BlockSpec(memory_space=pltpu.VMEM)
    return pl.pallas_call(
        functools.partial(score_kernel, len(rows), own_first, want_rows),
        in_specs=[whole] * (1 + len(rows)),
        out_specs=[whole] * len(out_shape),
        out_shape=out_shape,
        compiler_params=pltpu.CompilerParams(vmem_limit_bytes=VMEM_LIMIT),
        cost_estimate=pl.CostEstimate(
            flops=2 * row_count * row_count * width * len(rows),
            bytes_accessed=2 * row_count * width * (1 + len(rows)),
            transcendentals=0,
        ),
    )(keys, *rows)


def owner_steps(count):
    steps = [[(i, (i + k) % count) for i in range(count)] for k in range(1, (count + 1) // 2)]
    if count % 2 == 0 and count > 1:
        half = count // 2
        steps.append([(i, i + half) if i % 2 == 0 else (i + half, i) for i in range(half)])
    return steps


def per_device(embeddings, basis, owner_ids, sub_cluster):
    row_count = embeddings.shape[0]
    tiles = row_count // LANES
    split_count, owner_count = lax.axis_size("split"), lax.axis_size("owners")
    steps = owner_steps(owner_count)

    def swap(block, offset):
        return lax.ppermute(block, "split", [(s, s ^ offset) for s in range(split_count)])

    own = project(embeddings, basis, owner_ids, sub_cluster)
    arrived = [lax.ppermute(own, "owners", step) for step in steps]
    rows = [own, swap(own, 1)]
    for offset in range(2, split_count, 2):
        beside = swap(own, offset)
        rows += [beside, swap(beside, 1)]
    best = score(own, rows, True, False)[0]
    across = None
    for block, step in zip(arrived, steps):
        col_best, row_best = score(block, rows, False, True)
        across = row_best if across is None else jnp.maximum(across, row_best)
        back = lax.ppermute(col_best, "owners", [(b, a) for a, b in step])
        if len(step) < owner_count:
            sent = functools.reduce(
                jnp.logical_or, [lax.axis_index("owners") == a for a, _ in step]
            )
            back = jnp.where(sent, back, ABSENT)
        best = jnp.maximum(best, back)
    parts = across.reshape(split_count, tiles, LANES)
    best = jnp.maximum(best, parts[0])
    for offset in range(1, split_count):
        best = jnp.maximum(best, swap(parts[offset], offset))
    return jnp.maximum(best, -1.0).reshape(row_count)


def solution(mesh):
    placed = (
        P(("groups", "owners", "split"), None),
        P(),
        P(("groups", "owners", "split"), None),
        P(("groups", "owners", "split")),
    )
    return jax.shard_map(
        per_device,
        mesh=mesh,
        in_specs=placed,
        out_specs=P(("groups", "owners", "split")),
        check_vma=False,
    )
```

time: 88.9 us -> 41.5 us (0.47)
  blocking collectives: 25.9 us -> 0 us
  between operations: 13.5 us -> 0.1 us
  matrix products: 11.6 us -> 0 us
  Pallas kernels: 0 us -> 10.9 us
  local copies, waits for them, and re-layouts: 9.27 us -> 2.96 us
  starting transfers between devices: 7.84 us -> 13.4 us
  other arithmetic: 4.37 us -> 0.59 us
  waiting for transfers between devices: 16 us -> 13.3 us
    all_to_all x1 -> x0, blocking collectives: 20.7 us -> none  [per_device(): lax.all_to_all(packed, 'owners', split_axis=0, concat_axis=0, tiled=True)]
    ppermute x0 -> x10, starting transfers between devices: none -> 13.4 us  [the longest x2 6.32 us: per_device(): arrived = [lax.ppermute(own, 'owners', step) for step in steps]]
    ppermute x0 -> x10, waiting for transfers between devices: none -> 13.3 us  [the longest x2 8.56 us: per_device(): arrived = [lax.ppermute(own, 'owners', step) for step in steps]]
    dot_general x2 -> x0, matrix products: 11.6 us -> none  [the longest x1 8.05 us: cosines(): lax.dot_general(query_rows, key_rows, (((1,), (1,)), ((), ())), preferred...]
    all_to_all x2 -> x0, waiting for transfers between devices: 11.1 us -> none  [the longest x1 5.57 us: per_device(): lax.all_to_all(scored.reshape(owner_count, capacity), 'owners', split_axi...]
    pallas_call x0 -> x4, Pallas kernels: none -> 10.9 us  [the longest x1 6.19 us: project(): pl.pallas_call(project_kernel, grid=(depth // step_depth,), in_specs=[pl....]
    all_to_all x2 -> x0, starting transfers between devices: 7.84 us -> none  [the longest x1 4.6 us: per_device(): lax.all_to_all(scored.reshape(owner_count, capacity), 'owners', split_axi...]
    scatter x2 -> x0, local copies, waits for them, and re-layouts: 5.49 us -> none  [the longest x1 3 us: per_device(): labels = jnp.full((owner_count * capacity,), -1, jnp.int32).at[target].se...]
  transfers between devices with their start and end apart: 3 -> 10, of which waited for: 3 -> 4; matrix products, arithmetic and copies ran while one was open for 3% -> 0% of each run, Pallas kernels for 0% -> 8%
where the time goes in v1:
time: 41.5 us; the launch traced here: 41.2 us
  starting transfers between devices  13.4 us (32%)
  waiting for transfers between devices  13.3 us (32%)
  Pallas kernels  10.9 us (26%)
  local copies, waits for them, and re-layouts  2.96 us (7%)
  other arithmetic  0.59 us (1%)
    ppermute x2, waiting for transfers between devices, per_device(): arrived = [lax.ppermute(own, 'owners', step) for step in steps]  8.56 us
    ppermute x2, starting transfers between devices, per_device(): arrived = [lax.ppermute(own, 'owners', step) for step in steps]  6.32 us
    pallas_call x1, Pallas kernels, project(): pl.pallas_call(project_kernel, grid=(depth // step_depth,), in_specs=[pl....  6.19 us
    ppermute x6, starting transfers between devices, swap(): lax.ppermute(block, 'split', [(s, s ^ offset) for s in range(split_count)])  4.95 us
    pallas_call x3, Pallas kernels, score(): pl.pallas_call(functools.partial(score_kernel, len(rows), own_first, want...  4.71 us
    unnamed x6, local copies, waits for them, and re-layouts  2.95 us
    ppermute x2, waiting for transfers between devices, per_device(): back = lax.ppermute(col_best, 'owners', [(b, a) for a, b in step])  2.72 us
    ppermute x2, starting transfers between devices, per_device(): back = lax.ppermute(col_best, 'owners', [(b, a) for a, b in step])  2.08 us
  transfers between devices with their start and end apart: 10, of which 4 were waited for; matrix products, arithmetic and copies ran while one was open for 0% of the time, Pallas kernels for 8%

profile of v1, /device:TPU:0, one launch (start us, length us, event | category | flops | bytes accessed | tf_op | source)
XLA Modules:
  0.0 41.2 jit_solution(15735147506467047069)
XLA Ops:
  0.0 1.6 %copy-done = bf16[4096,256]{1,0:T(8,128)(2,1)S(1)} copy-done((bf16[4096,256]{1,0:T(8,128)(2,1)S(1)}, bf16[4096,256]{1,0:T(8,128)(2,1)}, u32[]{:S(2)}) %copy-start) | copy-done | bytes 2097176
  1.6 0.7 %copy-done.1 = s32[512,1]{0,1:T(1,128)S(1)} copy-done((s32[512,1]{0,1:T(1,128)S(1)}, s32[512,1]{0,1:T(1,128)}, u32[]{:S(2)}) %copy-start.1) | copy-done | bytes 2072
  2.3 0.7 %copy-done.2 = s32[512]{0:T(512)S(1)} copy-done((s32[512]{0:T(512)S(1)}, s32[512]{0:T(512)}, u32[]{:S(2)}) %copy-start.2) | copy-done | bytes 2072
  3.0 6.2 %shard_map.46.refs_0_.refs_1_ = bf16[528,256]{1,0:T(8,128)(2,1)S(1)} custom-call(bf16[512,4096]{1,0:T(8,128)(2,1)} %source_ref.1, bf16[4096,256]{1,0:T(8,128)(2,1)S(1)} %copy-done, s32[4,128]{1,0:T(4,128)S(1)} %bitcast.4, s32[4,128]{1,0:T(4,128)S(1)} %bitcast.5), custom_call_target="tpu_custom_call" | custom-call | flops 1073741824 | bytes 6291456 | tf_op jit(solution)/shard_map/pallas_call | solution.py:51
  9.2 3.0 %collective-permute-start.1 = (bf16[528,256]{1,0:T(8,128)(2,1)S(1)}, bf16[528,256]{1,0:T(8,128)(2,1)S(1)}, u32[]{:S(2)}, u32[]{:S(2)}) collective-permute-start(bf16[528,256]{1,0:T(8,128)(2,1)S(1)} %shard_map.46.refs_0_.refs_1_), channel_id=1, source_target_pairs={{0,2},{1,3},{2,0},{3,1},{4,6},{5,7},{6,4},{7,5},{8,10},{9,11},{10,... | collective-permute-start | bytes 811016 | tf_op jit(solution)/shard_map/ppermute | solution.py:148
  12.2 0.0 collective-permute-start
  12.2 4.5 %collective-permute-start.5 = (bf16[528,256]{1,0:T(8,128)(2,1)S(1)}, bf16[528,256]{1,0:T(8,128)(2,1)S(1)}, u32[]{:S(2)}, u32[]{:S(2)}) collective-permute-start(bf16[528,256]{1,0:T(8,128)(2,1)S(1)} %shard_map.46.refs_0_.refs_1_), channel_id=1, source_target_pairs={{0,8},{12,4},{1,9},{13,5},{2,10},{14,6},{3,11},{15,7},{16,24},{28,... | collective-permute-start | bytes 811016 | tf_op jit(solution)/shard_map/ppermute | solution.py:151
  16.7 2.0 %collective-permute-done.1.refs_3_ = bf16[528,256]{1,0:T(8,128)(2,1)S(1)} collective-permute-done((bf16[528,256]{1,0:T(8,128)(2,1)S(1)}, bf16[528,256]{1,0:T(8,128)(2,1)S(1)}, u32[]{:S(2)}, u32[]{:S(2)}) %collective-permute-start.1) | collective-permute-done | bytes 270368 | tf_op jit(solution)/shard_map/ppermute | solution.py:148
  18.6 1.8 %collective-permute-start.3 = (bf16[528,256]{1,0:T(8,128)(2,1)S(1)}, bf16[528,256]{1,0:T(8,128)(2,1)S(1)}, u32[]{:S(2)}, u32[]{:S(2)}) collective-permute-start(bf16[528,256]{1,0:T(8,128)(2,1)S(1)} %shard_map.46.refs_0_.refs_1_), channel_id=1, source_target_pairs={{0,4},{4,8},{8,12},{12,0},{1,5},{5,9},{9,13},{13,1},{2,6},{6,10},{... | collective-permute-start | bytes 811016 | tf_op jit(solution)/shard_map/ppermute | solution.py:151
  20.5 2.9 %collective-permute-done.5.refs_0_ = bf16[528,256]{1,0:T(8,128)(2,1)S(1)} collective-permute-done((bf16[528,256]{1,0:T(8,128)(2,1)S(1)}, bf16[528,256]{1,0:T(8,128)(2,1)S(1)}, u32[]{:S(2)}, u32[]{:S(2)}) %collective-permute-start.5) | collective-permute-done | bytes 270368 | tf_op jit(solution)/shard_map/ppermute | solution.py:151
  23.4 1.6 %shard_map.49 = (f32[4,128]{1,0:T(4,128)S(1)}, f32[16,128]{1,0:T(8,128)S(1)}) custom-call(bf16[528,256]{1,0:T(8,128)(2,1)S(1)} %collective-permute-done.5.refs_0_, bf16[528,256]{1,0:T(8,128)(2,1)S(1)} %shard_map.46.refs_0_.refs_1_, bf16[528,256]{1,0:T(8,128)(2,1)S(1)} %collective-permute-done.refs_2_, bf16[528,256]{1,0:T(8,128)(2,1)S(1)} %collective-permute-done.1.refs_3_, ...), custom_call_target="tpu_custom_call" | custom-call | flops 536870912 | bytes 1310720 | tf_op jit(solution)/shard_map/pallas_call | solution.py:119
  25.0 5.6 %collective-permute-done.3.refs_0_ = bf16[528,256]{1,0:T(8,128)(2,1)S(1)} collective-permute-done((bf16[528,256]{1,0:T(8,128)(2,1)S(1)}, bf16[528,256]{1,0:T(8,128)(2,1)S(1)}, u32[]{:S(2)}, u32[]{:S(2)}) %collective-permute-start.3) | collective-permute-done | bytes 270368 | tf_op jit(solution)/shard_map/ppermute | solution.py:151
  30.6 1.6 %shard_map.48 = (f32[4,128]{1,0:T(4,128)S(1)}, f32[16,128]{1,0:T(8,128)S(1)}) custom-call(bf16[528,256]{1,0:T(8,128)(2,1)S(1)} %collective-permute-done.3.refs_0_, bf16[528,256]{1,0:T(8,128)(2,1)S(1)} %shard_map.46.refs_0_.refs_1_, bf16[528,256]{1,0:T(8,128)(2,1)S(1)} %collective-permute-done.refs_2_, bf16[528,256]{1,0:T(8,128)(2,1)S(1)} %collective-permute-done.1.refs_3_, ...), custom_call_target="tpu_custom_call" | custom-call | flops 536870912 | bytes 1310720 | tf_op jit(solution)/shard_map/pallas_call | solution.py:119
  32.3 0.1 collective-permute-start.7
  32.4 0.6 %collective-permute-start.8 = (f32[4,128]{1,0:T(4,128)S(1)}, f32[4,128]{1,0:T(4,128)S(1)}, u32[]{:S(2)}, u32[]{:S(2)}) collective-permute-start(f32[4,128]{1,0:T(4,128)S(1)} %get-tuple-element.15), channel_id=1, source_target_pairs={{0,2},{1,3},{2,0},{3,1},{4,6},{5,7},{6,4},{7,5},{8,10},{9,11},{10,... | collective-permute-start | bytes 6152 | tf_op jit(solution)/shard_map/ppermute | solution.py:148
  32.9 1.3 %collective-permute-start.9 = (f32[4,128]{1,0:T(4,128)S(1)}, f32[4,128]{1,0:T(4,128)S(1)}, u32[]{:S(2)}, u32[]{:S(2)}) collective-permute-start(f32[4,128]{1,0:T(4,128)S(1)} %get-tuple-element.14), channel_id=1, source_target_pairs={{0,3},{1,2},{2,1},{3,0},{4,7},{5,6},{6,5},{7,4},{8,11},{9,10},{10,... | collective-permute-start | bytes 6152 | tf_op jit(solution)/shard_map/ppermute | solution.py:148
  34.2 1.3 %collective-permute-start.6 = (f32[4,128]{1,0:T(4,128)S(1)}, f32[4,128]{1,0:T(4,128)S(1)}, u32[]{:S(2)}, u32[]{:S(2)}) collective-permute-start(f32[4,128]{1,0:T(4,128)S(1)} %get-tuple-element.10), channel_id=1, source_target_pairs={{8,0},{4,12},{9,1},{5,13},{10,2},{6,14},{11,3},{7,15},{24,16},{20,... | collective-permute-start | bytes 6152 | tf_op jit(solution)/shard_map/ppermute | solution.py:161
  35.5 0.8 %collective-permute-start.4 = (f32[4,128]{1,0:T(4,128)S(1)}, f32[4,128]{1,0:T(4,128)S(1)}, u32[]{:S(2)}, u32[]{:S(2)}) collective-permute-start(f32[4,128]{1,0:T(4,128)S(1)} %get-tuple-element.9), channel_id=1, source_target_pairs={{4,0},{8,4},{12,8},{0,12},{5,1},{9,5},{13,9},{1,13},{6,2},{10,6},{... | collective-permute-start | bytes 6152 | tf_op jit(solution)/shard_map/ppermute | solution.py:161
  36.3 1.5 %shard_map.47 = f32[4,128]{1,0:T(4,128)S(1)} custom-call(bf16[528,256]{1,0:T(8,128)(2,1)S(1)} %shard_map.46.refs_0_.refs_1_, bf16[528,256]{1,0:T(8,128)(2,1)S(1)} %shard_map.46.refs_0_.refs_1_, bf16[528,256]{1,0:T(8,128)(2,1)S(1)} %collective-permute-done.refs_2_, bf16[528,256]{1,0:T(8,128)(2,1)S(1)} %collective-permute-done.1.refs_3_, ...), custom_call_target="tpu_custom_call" | custom-call | flops 536870912 | bytes 1310720 | tf_op jit(solution)/shard_map/pallas_call | solution.py:119
  37.8 0.0 collective-permute-done.8
  37.9 0.0 collective-permute-done.9
  37.9 2.7 %collective-permute-done.6 = f32[4,128]{1,0:T(4,128)S(1)} collective-permute-done((f32[4,128]{1,0:T(4,128)S(1)}, f32[4,128]{1,0:T(4,128)S(1)}, u32[]{:S(2)}, u32[]{:S(2)}) %collective-permute-start.6) | collective-permute-done | bytes 2080 | tf_op jit(solution)/shard_map/ppermute | solution.py:161
  40.6 0.0 collective-permute-done.4
  40.6 0.6 %fusion.4 = f32[512]{0:T(512)} fusion(f32[4,128]{1,0:T(4,128)S(1)} %collective-permute-done.9, f32[4,128]{1,0:T(4,128)S(1)} %collective-permute-done.8, f32[4,128]{1,0:T(4,128)S(1)} %collective-permute-done.7, f32[16,128]{1,0:T(8,128)S(1)} %max.29, f32[4,128]{1,0:T(4,128)S(1)} %collective-permute-done.6, f32[4,128]{1,0:T(4,128)S(1)} %shard_map.47, ...), kind=kLoop, calls=%fused_computation.5 | loop fusion | flops 4096 | bytes 16385 | tf_op jit(solution)/shard_map/reshape | solution.py:172
  (9 shorter events, 0.0 us)
Async XLA Ops:
  0.0 1.6 %copy-start = (bf16[4096,256]{1,0:T(8,128)(2,1)S(1)}, bf16[4096,256]{1,0:T(8,128)(2,1)}, u32[]{:S(2)}) copy-start(bf16[4096,256]{1,0:T(8,128)(2,1)} %basis_ref.1) | copy-start | bytes 6291460
  1.6 0.7 %copy-start.1 = (s32[512,1]{0,1:T(1,128)S(1)}, s32[512,1]{0,1:T(1,128)}, u32[]{:S(2)}) copy-start(s32[512,1]{0,1:T(1,128)} %param.6) | copy-start | bytes 6148
  2.3 0.7 %copy-start.2 = (s32[512]{0:T(512)S(1)}, s32[512]{0:T(512)}, u32[]{:S(2)}) copy-start(s32[512]{0:T(512)} %param.7) | copy-start | bytes 6148
  9.2 9.5 %collective-permute-start.1 = (bf16[528,256]{1,0:T(8,128)(2,1)S(1)}, bf16[528,256]{1,0:T(8,128)(2,1)S(1)}, u32[]{:S(2)}, u32[]{:S(2)}) collective-permute-start(bf16[528,256]{1,0:T(8,128)(2,1)S(1)} %shard_map.46.refs_0_.refs_1_), channel_id=1, source_target_pairs={{0,2},{1,3},{2,0},{3,1},{4,6},{5,7},{6,4},{7,5},{8,10},{9,11},{10,... | collective-permute-start | bytes 811016 | tf_op jit(solution)/shard_map/ppermute | solution.py:148
  12.2 8.3 %collective-permute-start = (bf16[528,256]{1,0:T(8,128)(2,1)S(1)}, bf16[528,256]{1,0:T(8,128)(2,1)S(1)}, u32[]{:S(2)}, u32[]{:S(2)}) collective-permute-start(bf16[528,256]{1,0:T(8,128)(2,1)S(1)} %shard_map.46.refs_0_.refs_1_), channel_id=1, source_target_pairs={{0,1},{1,0},{2,3},{3,2},{4,5},{5,4},{6,7},{7,6},{8,9},{9,8},{10,11... | collective-permute-start | bytes 811016 | tf_op jit(solution)/shard_map/ppermute | solution.py:148
  12.2 11.3 %collective-permute-start.5 = (bf16[528,256]{1,0:T(8,128)(2,1)S(1)}, bf16[528,256]{1,0:T(8,128)(2,1)S(1)}, u32[]{:S(2)}, u32[]{:S(2)}) collective-permute-start(bf16[528,256]{1,0:T(8,128)(2,1)S(1)} %shard_map.46.refs_0_.refs_1_), channel_id=1, source_target_pairs={{0,8},{12,4},{1,9},{13,5},{2,10},{14,6},{3,11},{15,7},{16,24},{28,... | collective-permute-start | bytes 811016 | tf_op jit(solution)/shard_map/ppermute | solution.py:151
  18.6 4.8 %collective-permute-start.2 = (bf16[528,256]{1,0:T(8,128)(2,1)S(1)}, bf16[528,256]{1,0:T(8,128)(2,1)S(1)}, u32[]{:S(2)}, u32[]{:S(2)}) collective-permute-start(bf16[528,256]{1,0:T(8,128)(2,1)S(1)} %collective-permute-done.1.refs_3_), channel_id=1, source_target_pairs={{0,1},{1,0},{2,3},{3,2},{4,5},{5,4},{6,7},{7,6},{8,9},{9,8},{10,11... | collective-permute-start | bytes 811016 | tf_op jit(solution)/shard_map/ppermute | solution.py:148
  18.6 12.0 %collective-permute-start.3 = (bf16[528,256]{1,0:T(8,128)(2,1)S(1)}, bf16[528,256]{1,0:T(8,128)(2,1)S(1)}, u32[]{:S(2)}, u32[]{:S(2)}) collective-permute-start(bf16[528,256]{1,0:T(8,128)(2,1)S(1)} %shard_map.46.refs_0_.refs_1_), channel_id=1, source_target_pairs={{0,4},{4,8},{8,12},{12,0},{1,5},{5,9},{9,13},{13,1},{2,6},{6,10},{... | collective-permute-start | bytes 811016 | tf_op jit(solution)/shard_map/ppermute | solution.py:151
  32.3 5.6 %collective-permute-start.7 = (f32[4,128]{1,0:T(4,128)S(1)}, f32[4,128]{1,0:T(4,128)S(1)}, u32[]{:S(2)}, u32[]{:S(2)}) collective-permute-start(f32[4,128]{1,0:T(4,128)S(1)} %get-tuple-element.13), channel_id=1, source_target_pairs={{0,1},{1,0},{2,3},{3,2},{4,5},{5,4},{6,7},{7,6},{8,9},{9,8},{10,11... | collective-permute-start | bytes 6152 | tf_op jit(solution)/shard_map/ppermute | solution.py:148
  32.4 5.5 %collective-permute-start.8 = (f32[4,128]{1,0:T(4,128)S(1)}, f32[4,128]{1,0:T(4,128)S(1)}, u32[]{:S(2)}, u32[]{:S(2)}) collective-permute-start(f32[4,128]{1,0:T(4,128)S(1)} %get-tuple-element.15), channel_id=1, source_target_pairs={{0,2},{1,3},{2,0},{3,1},{4,6},{5,7},{6,4},{7,5},{8,10},{9,11},{10,... | collective-permute-start | bytes 6152 | tf_op jit(solution)/shard_map/ppermute | solution.py:148
  32.9 4.9 %collective-permute-start.9 = (f32[4,128]{1,0:T(4,128)S(1)}, f32[4,128]{1,0:T(4,128)S(1)}, u32[]{:S(2)}, u32[]{:S(2)}) collective-permute-start(f32[4,128]{1,0:T(4,128)S(1)} %get-tuple-element.14), channel_id=1, source_target_pairs={{0,3},{1,2},{2,1},{3,0},{4,7},{5,6},{6,5},{7,4},{8,11},{9,10},{10,... | collective-permute-start | bytes 6152 | tf_op jit(solution)/shard_map/ppermute | solution.py:148
  34.2 6.4 %collective-permute-start.6 = (f32[4,128]{1,0:T(4,128)S(1)}, f32[4,128]{1,0:T(4,128)S(1)}, u32[]{:S(2)}, u32[]{:S(2)}) collective-permute-start(f32[4,128]{1,0:T(4,128)S(1)} %get-tuple-element.10), channel_id=1, source_target_pairs={{8,0},{4,12},{9,1},{5,13},{10,2},{6,14},{11,3},{7,15},{24,16},{20,... | collective-permute-start | bytes 6152 | tf_op jit(solution)/shard_map/ppermute | solution.py:161
  35.5 5.1 %collective-permute-start.4 = (f32[4,128]{1,0:T(4,128)S(1)}, f32[4,128]{1,0:T(4,128)S(1)}, u32[]{:S(2)}, u32[]{:S(2)}) collective-permute-start(f32[4,128]{1,0:T(4,128)S(1)} %get-tuple-element.9), channel_id=1, source_target_pairs={{4,0},{8,4},{12,8},{0,12},{5,1},{9,5},{13,9},{1,13},{6,2},{10,6},{... | collective-permute-start | bytes 6152 | tf_op jit(solution)/shard_map/ppermute | solution.py:161

commit v2 on v1

v2 whole, which is shorter than its diff:
```python
import functools

import jax
import jax.numpy as jnp
from jax import lax
from jax.experimental import pallas as pl
from jax.experimental.pallas import tpu as pltpu
from jax.sharding import PartitionSpec as P

CPO = 8
LANES = 128
TAG_ROWS = 16
ABSENT = -2.0
STEPS = 8
PIECES = 1
VMEM_LIMIT = 48 * 1024 * 1024


def project_kernel(source_hbm, basis_hbm, owner_hbm, sub_hbm, *refs):
    packed_refs, (source, basis, owner, sub, sems, tag_sems) = refs[:-6], refs[-6:]
    row_count, depth = source.shape
    width = basis.shape[1]
    chunk = depth // STEPS
    tag_copies = [
        pltpu.make_async_copy(owner_hbm, owner, tag_sems.at[0]),
        pltpu.make_async_copy(sub_hbm, sub, tag_sems.at[1]),
    ]
    copies = []
    for step in range(STEPS):
        span = pl.ds(step * chunk, chunk)
        copies.append(
            (
                pltpu.make_async_copy(
                    basis_hbm.at[span, :], basis.at[span, :], sems.at[0, step]
                ),
                pltpu.make_async_copy(
                    source_hbm.at[:, span], source.at[:, span], sems.at[1, step]
                ),
            )
        )
    for pair in copies:
        for copy in pair:
            copy.start()
    for copy in tag_copies:
        copy.start()
    projected = None
    for step, pair in enumerate(copies):
        for copy in pair:
            copy.wait()
        part = jnp.dot(
            source[:, step * chunk : (step + 1) * chunk],
            basis[step * chunk : (step + 1) * chunk, :],
            preferred_element_type=jnp.float32,
        )
        projected = part if projected is None else projected + part
    for copy in tag_copies:
        copy.wait()
    norms = jnp.sum(projected * projected, axis=1, keepdims=True)
    units = (projected * lax.rsqrt(norms + 1e-06)).astype(jnp.bfloat16)
    tags = (owner[...] * CPO + sub[...] + 1).astype(jnp.float32)
    for packed_ref in packed_refs:
        rows = packed_ref.shape[0] - TAG_ROWS
        at = 0 if rows == row_count else packed_refs[1:].index(packed_ref) * rows
        here = tags[at // LANES : (at + rows) // LANES, :]
        here = jnp.concatenate(
            [here, jnp.zeros((TAG_ROWS - here.shape[0], LANES), jnp.float32)], axis=0
        )
        here = jnp.concatenate([here, jnp.zeros((TAG_ROWS, width - LANES), jnp.float32)], axis=1)
        packed_ref[:rows, :] = units[at : at + rows, :]
        packed_ref[rows:, :] = here.astype(jnp.bfloat16)


def project(embeddings, basis, owner_ids, sub_cluster):
    row_count, depth = embeddings.shape
    width = basis.shape[1]
    tag_shape = (row_count // LANES, LANES)
    sizes = [row_count] + ([row_count // PIECES] * PIECES if PIECES > 1 else [])
    return pl.pallas_call(
        project_kernel,
        in_specs=[pl.BlockSpec(memory_space=pltpu.HBM)] * 4,
        out_specs=[pl.BlockSpec(memory_space=pltpu.VMEM)] * len(sizes),
        out_shape=[
            jax.ShapeDtypeStruct((size + TAG_ROWS, width), jnp.bfloat16) for size in sizes
        ],
        scratch_shapes=[
            pltpu.VMEM((row_count, depth), jnp.bfloat16),
            pltpu.VMEM((depth, width), jnp.bfloat16),
            pltpu.VMEM(tag_shape, jnp.int32),
            pltpu.VMEM(tag_shape, jnp.int32),
            pltpu.SemaphoreType.DMA((2, STEPS)),
            pltpu.SemaphoreType.DMA((2,)),
        ],
        compiler_params=pltpu.CompilerParams(vmem_limit_bytes=VMEM_LIMIT),
        cost_estimate=pl.CostEstimate(
            flops=2 * row_count * depth * width,
            bytes_accessed=2 * depth * (row_count + width),
            transcendentals=0,
        ),
    )(
        *[
            pltpu.with_memory_space_constraint(array, pltpu.HBM)
            for array in (
                embeddings,
                basis,
                owner_ids.reshape(tag_shape),
                sub_cluster.reshape(tag_shape),
            )
        ]
    )


def score_kernel(key_blocks, row_blocks, own_first, want_rows, *refs):
    refs = list(refs)
    key_refs = [refs.pop(0) for _ in range(key_blocks)]
    row_refs = [refs.pop(0) for _ in range(row_blocks)]
    base_ref = None if own_first else refs.pop(0)
    col_refs = [refs.pop(0) for _ in range(key_blocks)]
    key_count, row_count = key_refs[0].shape[0] - TAG_ROWS, row_refs[0].shape[0] - TAG_ROWS
    key_tiles, row_tiles = key_count // LANES, row_count // LANES
    best = [jnp.full((8, LANES), ABSENT, jnp.float32) for _ in range(key_tiles * key_blocks)]
    for block, row_ref in enumerate(row_refs):
        row_tags = row_ref[row_count:, :LANES].astype(jnp.float32)
        across = [None] * row_tiles
        tags = [
            jnp.broadcast_to(row_tags[tile : tile + 1, :], (LANES, LANES)).T
            for tile in range(row_tiles)
        ]
        for key_block, key_ref in enumerate(key_refs):
            key_tags = key_ref[key_count:, :LANES].astype(jnp.float32)
            scores = lax.dot_general(
                row_ref[:row_count, :],
                key_ref[:key_count, :],
                (((1,), (1,)), ((), ())),
                preferred_element_type=jnp.float32,
            )
            for tile in range(row_tiles):
                for at in range(key_tiles):
                    same = tags[tile] == key_tags[at : at + 1, :]
                    if own_first and block == 0 and at == tile:
                        same = same & (
                            lax.broadcasted_iota(jnp.int32, (LANES, LANES), 0)
                            != lax.broadcasted_iota(jnp.int32, (LANES, LANES), 1)
                        )
                    kept = scores[
                        tile * LANES : (tile + 1) * LANES, at * LANES : (at + 1) * LANES
                    ]
                    kept = jnp.where(same, kept, ABSENT)
                    to = key_block * key_tiles + at
                    best[to] = jnp.maximum(
                        best[to], jnp.max(kept.reshape(LANES // 8, 8, LANES), axis=0)
                    )
                    if want_rows:
                        across[tile] = (
                            kept if across[tile] is None else jnp.maximum(across[tile], kept)
                        )
        if want_rows:
            row_out = refs[block // 2]
            for tile in range(row_tiles):
                at = block % 2 * row_tiles + tile
                found = jnp.max(across[tile].T, axis=0, keepdims=True)
                if block == 0:
                    found = jnp.maximum(found, base_ref[tile : tile + 1, :])
                row_out[at : at + 1, :] = found
    for key_block, col_out in enumerate(col_refs):
        for at in range(key_tiles):
            found = jnp.max(best[key_block * key_tiles + at], axis=0, keepdims=True)
            if not own_first and not want_rows:
                found = jnp.maximum(found, base_ref[at : at + 1, :])
            col_out[at : at + 1, :] = found


def score(keys, rows, base, want_rows):
    key_count, row_count = keys[0].shape[0] - TAG_ROWS, rows[0].shape[0] - TAG_ROWS
    out_shape = [jax.ShapeDtypeStruct((key_count // LANES, LANES), jnp.float32)] * len(keys)
    if want_rows:
        out_shape += [
            jax.ShapeDtypeStruct((2 * row_count // LANES, LANES), jnp.float32)
        ] * (len(rows) // 2)
    operands = [*keys, *rows] + ([] if base is None else [base])
    whole = pl.BlockSpec(memory_space=pltpu.VMEM)
    return pl.pallas_call(
        functools.partial(score_kernel, len(keys), len(rows), base is None, want_rows),
        in_specs=[whole] * len(operands),
        out_specs=[whole] * len(out_shape),
        out_shape=out_shape,
        compiler_params=pltpu.CompilerParams(vmem_limit_bytes=VMEM_LIMIT),
        cost_estimate=pl.CostEstimate(flops=0, bytes_accessed=0, transcendentals=0),
    )(*operands)


def owner_steps(count):
    steps = [[(i, (i + k) % count) for i in range(count)] for k in range(1, (count + 1) // 2)]
    if count % 2 == 0 and count > 1:
        half = count // 2
        steps.append([(i, i + half) if i % 2 == 0 else (i + half, i) for i in range(half)])
    return steps


def per_device(embeddings, basis, owner_ids, sub_cluster):
    row_count = embeddings.shape[0]
    tiles = row_count // LANES
    split_count, owner_count = lax.axis_size("split"), lax.axis_size("owners")
    steps = owner_steps(owner_count)

    def swap(block, offset):
        return lax.ppermute(block, "split", [(s, s ^ offset) for s in range(split_count)])

    own, *pieces = project(embeddings, basis, owner_ids, sub_cluster)
    pieces = pieces or [own]
    arrived = [
        [lax.ppermute(piece, "owners", step) for piece in pieces] for step in reversed(steps)
    ]
    rows = [own, swap(own, 1)]
    best = score([own], rows, None, False)[0]
    for offset in range(2, split_count, 2):
        beside = swap(own, offset)
        pair = [beside, swap(own, offset + 1)]
        best = score([own], pair, best, False)[0]
        rows += pair
    keys = [block for blocks in arrived for block in blocks]
    found = score(keys, rows, best, True)
    col_best, row_best = found[: len(keys)], found[len(keys) :]
    local = row_best[0]
    for at in range(1, split_count // 2):
        local = jnp.maximum(local, swap(row_best[at], 2 * at))
    best, beside = local[:tiles], local[tiles:]
    best = jnp.maximum(best, swap(beside, 1))
    for at, step in enumerate(reversed(steps)):
        back = lax.ppermute(col_best[at], "owners", [(b, a) for a, b in step])
        if len(step) < owner_count:
            sent = functools.reduce(
                jnp.logical_or, [lax.axis_index("owners") == a for a, _ in step]
            )
            back = jnp.where(sent, back, ABSENT)
        best = jnp.maximum(best, back)
    return jnp.maximum(best, -1.0).reshape(row_count)


def solution(mesh):
    placed = (
        P(("groups", "owners", "split"), None),
        P(),
        P(("groups", "owners", "split"), None),
        P(("groups", "owners", "split")),
    )
    return jax.shard_map(
        per_device,
        mesh=mesh,
        in_specs=placed,
        out_specs=P(("groups", "owners", "split")),
        check_vma=False,
    )
```

time: 41.5 us -> 36.2 us (0.87)
  waiting for transfers between devices: 13.3 us -> 17.7 us
  Pallas kernels: 10.9 us -> 6.75 us
  local copies, waits for them, and re-layouts: 2.96 us -> 0.01 us
  starting transfers between devices: 13.4 us -> 10.8 us
    ppermute x6 -> x5, waiting for transfers between devices: 1.98 us -> 7.99 us  [swap(): lax.ppermute(block, 'split', [(s, s ^ offset) for s in range(split_count)])]
    pallas_call x4, Pallas kernels: 10.9 us -> 6.75 us  [the longest x1 4.32 us: project(): pl.pallas_call(project_kernel, in_specs=[pl.BlockSpec(memory_space=pltpu....]
    unnamed x6 -> x0, local copies, waits for them, and re-layouts: 2.95 us -> none
    ppermute x4, starting transfers between devices: 8.4 us -> 6.13 us  [the longest x2 4.79 us: per_device(): lax.ppermute(piece, 'owners', step)]
    ppermute x4, waiting for transfers between devices: 11.3 us -> 9.74 us  [the longest x2 5.52 us: per_device(): lax.ppermute(piece, 'owners', step)]
    ppermute x6 -> x5, starting transfers between devices: 4.95 us -> 4.71 us  [swap(): lax.ppermute(block, 'split', [(s, s ^ offset) for s in range(split_count)])]
  transfers between devices with their start and end apart: 10 -> 9, of which waited for: 4 -> 5; matrix products, arithmetic and copies ran while one was open for 0% -> 0% of each run, Pallas kernels for 8% -> 3%
where the time goes in v2:
time: 36.2 us; the launch traced here: 36 us
  waiting for transfers between devices  17.7 us (49%)
  starting transfers between devices  10.8 us (30%)
  Pallas kernels  6.75 us (19%)
  other arithmetic  0.59 us (2%)
    ppermute x5, waiting for transfers between devices, swap(): lax.ppermute(block, 'split', [(s, s ^ offset) for s in range(split_count)])  7.99 us
    ppermute x2, waiting for transfers between devices, per_device(): lax.ppermute(piece, 'owners', step)  5.52 us
    ppermute x2, starting transfers between devices, per_device(): lax.ppermute(piece, 'owners', step)  4.79 us
    ppermute x5, starting transfers between devices, swap(): lax.ppermute(block, 'split', [(s, s ^ offset) for s in range(split_count)])  4.71 us
    pallas_call x1, Pallas kernels, project(): pl.pallas_call(project_kernel, in_specs=[pl.BlockSpec(memory_space=pltpu....  4.32 us
    ppermute x2, waiting for transfers between devices, per_device(): back = lax.ppermute(col_best[at], 'owners', [(b, a) for a, b in step])  4.22 us
    pallas_call x3, Pallas kernels, score(): pl.pallas_call(functools.partial(score_kernel, len(keys), len(rows), base...  2.43 us
    ppermute x2, starting transfers between devices, per_device(): back = lax.ppermute(col_best[at], 'owners', [(b, a) for a, b in step])  1.34 us
  transfers between devices with their start and end apart: 9, of which 5 were waited for; matrix products, arithmetic and copies ran while one was open for 0% of the time, Pallas kernels for 3%

profile of v2, /device:TPU:0, one launch (start us, length us, event | category | flops | bytes accessed | tf_op | source)
XLA Modules:
  0.0 36.0 jit_solution(8352092857706287077)
XLA Ops:
  0.0 4.3 %shard_map.46.refs_0_.refs_1_.refs_2_ = bf16[528,256]{1,0:T(8,128)(2,1)S(1)} custom-call(bf16[512,4096]{1,0:T(8,128)(2,1)} %source_hbm.1, bf16[4096,256]{1,0:T(8,128)(2,1)} %basis_hbm.1, s32[4,128]{1,0:T(4,128)} %bitcast.4, s32[4,128]{1,0:T(4,128)} %bitcast.5), custom_call_target="tpu_custom_call" | custom-call | flops 1073741824 | bytes 6291456 | tf_op jit(solution)/shard_map/pallas_call | solution.py:78
  4.3 0.5 %collective-permute-start.2 = (bf16[528,256]{1,0:T(8,128)(2,1)S(1)}, bf16[528,256]{1,0:T(8,128)(2,1)S(1)}, u32[]{:S(2)}, u32[]{:S(2)}) collective-permute-start(bf16[528,256]{1,0:T(8,128)(2,1)S(1)} %shard_map.46.refs_0_.refs_1_.refs_2_), channel_id=1, source_target_pairs={{0,1},{1,0},{2,3},{3,2},{4,5},{5,4},{6,7},{7,6},{8,9},{9,8},{10,11... | collective-permute-start | bytes 811016 | tf_op jit(solution)/shard_map/ppermute | solution.py:206
  4.8 2.6 %collective-permute-start.3 = (bf16[528,256]{1,0:T(8,128)(2,1)S(1)}, bf16[528,256]{1,0:T(8,128)(2,1)S(1)}, u32[]{:S(2)}, u32[]{:S(2)}) collective-permute-start(bf16[528,256]{1,0:T(8,128)(2,1)S(1)} %shard_map.46.refs_0_.refs_1_.refs_2_), channel_id=1, source_target_pairs={{0,2},{1,3},{2,0},{3,1},{4,6},{5,7},{6,4},{7,5},{8,10},{9,11},{10,... | collective-permute-start | bytes 811016 | tf_op jit(solution)/shard_map/ppermute | solution.py:206
  7.4 0.1 collective-permute-start.4
  7.5 4.7 %collective-permute-start = (bf16[528,256]{1,0:T(8,128)(2,1)S(1)}, bf16[528,256]{1,0:T(8,128)(2,1)S(1)}, u32[]{:S(2)}, u32[]{:S(2)}) collective-permute-start(bf16[528,256]{1,0:T(8,128)(2,1)S(1)} %shard_map.46.refs_0_.refs_1_.refs_2_), channel_id=1, source_target_pairs={{0,8},{12,4},{1,9},{13,5},{2,10},{14,6},{3,11},{15,7},{16,24},{28,... | collective-permute-start | bytes 811016 | tf_op jit(solution)/shard_map/ppermute | solution.py:211
  12.2 0.1 collective-permute-start.1
  12.3 0.0 collective-permute-done.2.refs_2_.refs_3_
  12.3 0.5 %shard_map.47.refs_3_ = f32[4,128]{1,0:T(4,128)S(1)} custom-call(bf16[528,256]{1,0:T(8,128)(2,1)S(1)} %shard_map.46.refs_0_.refs_1_.refs_2_, bf16[528,256]{1,0:T(8,128)(2,1)S(1)} %shard_map.46.refs_0_.refs_1_.refs_2_, bf16[528,256]{1,0:T(8,128)(2,1)S(1)} %collective-permute-done.2.refs_2_.refs_3_), custom_call_target="tpu_custom_call" | custom-call | tf_op jit(solution)/shard_map/pallas_call | solution.py:181
  12.8 2.0 %collective-permute-done.3.refs_1_.refs_4_ = bf16[528,256]{1,0:T(8,128)(2,1)S(1)} collective-permute-done((bf16[528,256]{1,0:T(8,128)(2,1)S(1)}, bf16[528,256]{1,0:T(8,128)(2,1)S(1)}, u32[]{:S(2)}, u32[]{:S(2)}) %collective-permute-start.3) | collective-permute-done | bytes 270368 | tf_op jit(solution)/shard_map/ppermute | solution.py:206
  14.7 5.3 %collective-permute-done.4.refs_2_.refs_5_ = bf16[528,256]{1,0:T(8,128)(2,1)S(1)} collective-permute-done((bf16[528,256]{1,0:T(8,128)(2,1)S(1)}, bf16[528,256]{1,0:T(8,128)(2,1)S(1)}, u32[]{:S(2)}, u32[]{:S(2)}) %collective-permute-start.4) | collective-permute-done | bytes 270368 | tf_op jit(solution)/shard_map/ppermute | solution.py:206
  20.0 0.5 %shard_map.48.refs_6_ = f32[4,128]{1,0:T(4,128)S(1)} custom-call(bf16[528,256]{1,0:T(8,128)(2,1)S(1)} %shard_map.46.refs_0_.refs_1_.refs_2_, bf16[528,256]{1,0:T(8,128)(2,1)S(1)} %collective-permute-done.3.refs_1_.refs_4_, bf16[528,256]{1,0:T(8,128)(2,1)S(1)} %collective-permute-done.4.refs_2_.refs_5_, f32[4,128]{1,0:T(4,128)S(1)} %shard_map.47.refs_3_), custom_call_target="tpu_custom_call" | custom-call | tf_op jit(solution)/shard_map/pallas_call | solution.py:181
  20.5 0.0 collective-permute-done.refs_0_
  20.5 5.5 %collective-permute-done.1.refs_1_ = bf16[528,256]{1,0:T(8,128)(2,1)S(1)} collective-permute-done((bf16[528,256]{1,0:T(8,128)(2,1)S(1)}, bf16[528,256]{1,0:T(8,128)(2,1)S(1)}, u32[]{:S(2)}, u32[]{:S(2)}) %collective-permute-start.1) | collective-permute-done | bytes 270368 | tf_op jit(solution)/shard_map/ppermute | solution.py:211
  26.0 1.5 %shard_map.49 = (f32[4,128]{1,0:T(4,128)S(1)}, f32[4,128]{1,0:T(4,128)S(1)}, f32[8,128]{1,0:T(8,128)S(1)}, f32[8,128]{1,0:T(8,128)S(1)}) custom-call(bf16[528,256]{1,0:T(8,128)(2,1)S(1)} %collective-permute-done.refs_0_, bf16[528,256]{1,0:T(8,128)(2,1)S(1)} %collective-permute-done.1.refs_1_, bf16[528,256]{1,0:T(8,128)(2,1)S(1)} %shard_map.46.refs_0_.refs_1_.refs_2_, ...), custom_call_target="tpu_custom_call" | custom-call | tf_op jit(solution)/shard_map/pallas_call | solution.py:181
  27.5 1.6 %collective-permute-start.5 = (f32[8,128]{1,0:T(8,128)S(1)}, f32[8,128]{1,0:T(8,128)S(1)}, u32[]{:S(2)}, u32[]{:S(2)}) collective-permute-start(f32[8,128]{1,0:T(8,128)S(1)} %get-tuple-element.10), channel_id=1, source_target_pairs={{0,2},{1,3},{2,0},{3,1},{4,6},{5,7},{6,4},{7,5},{8,10},{9,11},{10,... | collective-permute-start | bytes 12296 | tf_op jit(solution)/shard_map/ppermute | solution.py:206
  29.0 1.3 %collective-permute-start.7 = (f32[4,128]{1,0:T(4,128)S(1)}, f32[4,128]{1,0:T(4,128)S(1)}, u32[]{:S(2)}, u32[]{:S(2)}) collective-permute-start(f32[4,128]{1,0:T(4,128)S(1)} %get-tuple-element.11), channel_id=1, source_target_pairs={{8,0},{4,12},{9,1},{5,13},{10,2},{6,14},{11,3},{7,15},{24,16},{20,... | collective-permute-start | bytes 6152 | tf_op jit(solution)/shard_map/ppermute | solution.py:229
  30.3 0.1 collective-permute-start.8
  30.4 0.8 %collective-permute-done.5 = f32[8,128]{1,0:T(8,128)S(1)} collective-permute-done((f32[8,128]{1,0:T(8,128)S(1)}, f32[8,128]{1,0:T(8,128)S(1)}, u32[]{:S(2)}, u32[]{:S(2)}) %collective-permute-start.5) | collective-permute-done | bytes 4128 | tf_op jit(solution)/shard_map/ppermute | solution.py:206
  31.2 0.0 collective-permute-start.6
  31.2 4.2 %collective-permute-done.7 = f32[4,128]{1,0:T(4,128)S(1)} collective-permute-done((f32[4,128]{1,0:T(4,128)S(1)}, f32[4,128]{1,0:T(4,128)S(1)}, u32[]{:S(2)}, u32[]{:S(2)}) %collective-permute-start.7) | collective-permute-done | bytes 2080 | tf_op jit(solution)/shard_map/ppermute | solution.py:229
  35.4 0.0 collective-permute-done.8
  35.4 0.0 collective-permute-done.6
  35.4 0.6 %maximum_bitcast_fusion = f32[512]{0:T(512)} fusion(f32[4,128]{1,0:T(4,128)S(1)} %collective-permute-done.8, f32[4,128]{1,0:T(4,128)S(1)} %collective-permute-done.7, f32[4,128]{1,0:T(4,128)S(1)} %collective-permute-done.6, f32[8,128]{1,0:T(8,128)S(1)} %max.18, pred[]{:T(512)S(6)} %or.3), kind=kLoop, calls=%fused_computation | loop fusion | flops 2560 | bytes 10241 | tf_op jit(solution)/shard_map/reshape | solution.py:236
  (2 shorter events, 0.0 us)
Async XLA Ops:
  4.3 8.0 %collective-permute-start.2 = (bf16[528,256]{1,0:T(8,128)(2,1)S(1)}, bf16[528,256]{1,0:T(8,128)(2,1)S(1)}, u32[]{:S(2)}, u32[]{:S(2)}) collective-permute-start(bf16[528,256]{1,0:T(8,128)(2,1)S(1)} %shard_map.46.refs_0_.refs_1_.refs_2_), channel_id=1, source_target_pairs={{0,1},{1,0},{2,3},{3,2},{4,5},{5,4},{6,7},{7,6},{8,9},{9,8},{10,11... | collective-permute-start | bytes 811016 | tf_op jit(solution)/shard_map/ppermute | solution.py:206
  4.8 9.9 %collective-permute-start.3 = (bf16[528,256]{1,0:T(8,128)(2,1)S(1)}, bf16[528,256]{1,0:T(8,128)(2,1)S(1)}, u32[]{:S(2)}, u32[]{:S(2)}) collective-permute-start(bf16[528,256]{1,0:T(8,128)(2,1)S(1)} %shard_map.46.refs_0_.refs_1_.refs_2_), channel_id=1, source_target_pairs={{0,2},{1,3},{2,0},{3,1},{4,6},{5,7},{6,4},{7,5},{8,10},{9,11},{10,... | collective-permute-start | bytes 811016 | tf_op jit(solution)/shard_map/ppermute | solution.py:206
  7.4 12.6 %collective-permute-start.4 = (bf16[528,256]{1,0:T(8,128)(2,1)S(1)}, bf16[528,256]{1,0:T(8,128)(2,1)S(1)}, u32[]{:S(2)}, u32[]{:S(2)}) collective-permute-start(bf16[528,256]{1,0:T(8,128)(2,1)S(1)} %shard_map.46.refs_0_.refs_1_.refs_2_), channel_id=1, source_target_pairs={{0,3},{1,2},{2,1},{3,0},{4,7},{5,6},{6,5},{7,4},{8,11},{9,10},{10,... | collective-permute-start | bytes 811016 | tf_op jit(solution)/shard_map/ppermute | solution.py:206
  7.5 13.0 %collective-permute-start = (bf16[528,256]{1,0:T(8,128)(2,1)S(1)}, bf16[528,256]{1,0:T(8,128)(2,1)S(1)}, u32[]{:S(2)}, u32[]{:S(2)}) collective-permute-start(bf16[528,256]{1,0:T(8,128)(2,1)S(1)} %shard_map.46.refs_0_.refs_1_.refs_2_), channel_id=1, source_target_pairs={{0,8},{12,4},{1,9},{13,5},{2,10},{14,6},{3,11},{15,7},{16,24},{28,... | collective-permute-start | bytes 811016 | tf_op jit(solution)/shard_map/ppermute | solution.py:211
  12.2 13.8 %collective-permute-start.1 = (bf16[528,256]{1,0:T(8,128)(2,1)S(1)}, bf16[528,256]{1,0:T(8,128)(2,1)S(1)}, u32[]{:S(2)}, u32[]{:S(2)}) collective-permute-start(bf16[528,256]{1,0:T(8,128)(2,1)S(1)} %shard_map.46.refs_0_.refs_1_.refs_2_), channel_id=1, source_target_pairs={{0,4},{4,8},{8,12},{12,0},{1,5},{5,9},{9,13},{13,1},{2,6},{6,10},{... | collective-permute-start | bytes 811016 | tf_op jit(solution)/shard_map/ppermute | solution.py:211
  27.5 3.7 %collective-permute-start.5 = (f32[8,128]{1,0:T(8,128)S(1)}, f32[8,128]{1,0:T(8,128)S(1)}, u32[]{:S(2)}, u32[]{:S(2)}) collective-permute-start(f32[8,128]{1,0:T(8,128)S(1)} %get-tuple-element.10), channel_id=1, source_target_pairs={{0,2},{1,3},{2,0},{3,1},{4,6},{5,7},{6,4},{7,5},{8,10},{9,11},{10,... | collective-permute-start | bytes 12296 | tf_op jit(solution)/shard_map/ppermute | solution.py:206
  29.0 6.4 %collective-permute-start.7 = (f32[4,128]{1,0:T(4,128)S(1)}, f32[4,128]{1,0:T(4,128)S(1)}, u32[]{:S(2)}, u32[]{:S(2)}) collective-permute-start(f32[4,128]{1,0:T(4,128)S(1)} %get-tuple-element.11), channel_id=1, source_target_pairs={{8,0},{4,12},{9,1},{5,13},{10,2},{6,14},{11,3},{7,15},{24,16},{20,... | collective-permute-start | bytes 6152 | tf_op jit(solution)/shard_map/ppermute | solution.py:229
  30.3 5.1 %collective-permute-start.8 = (f32[4,128]{1,0:T(4,128)S(1)}, f32[4,128]{1,0:T(4,128)S(1)}, u32[]{:S(2)}, u32[]{:S(2)}) collective-permute-start(f32[4,128]{1,0:T(4,128)S(1)} %get-tuple-element.12), channel_id=1, source_target_pairs={{4,0},{8,4},{12,8},{0,12},{5,1},{9,5},{13,9},{1,13},{6,2},{10,6},{... | collective-permute-start | bytes 6152 | tf_op jit(solution)/shard_map/ppermute | solution.py:229
  31.2 4.2 %collective-permute-start.6 = (f32[4,128]{1,0:T(4,128)S(1)}, f32[4,128]{1,0:T(4,128)S(1)}, u32[]{:S(2)}, u32[]{:S(2)}) collective-permute-start(f32[4,128]{1,0:T(4,128)S(1)} %slice.7), channel_id=1, source_target_pairs={{0,1},{1,0},{2,3},{3,2},{4,5},{5,4},{6,7},{7,6},{8,9},{9,8},{10,11... | collective-permute-start | bytes 6152 | tf_op jit(solution)/shard_map/ppermute | solution.py:206

commit v3 on v2

--- a/solution.py
+++ b/solution.py
@@ -12,7 +12,8 @@
 TAG_ROWS = 16
 ABSENT = -2.0
 STEPS = 8
-PIECES = 1
+PIECES = 2
+WEIGHT = 32
 VMEM_LIMIT = 48 * 1024 * 1024
 
 
@@ -58,9 +59,9 @@
     norms = jnp.sum(projected * projected, axis=1, keepdims=True)
     units = (projected * lax.rsqrt(norms + 1e-06)).astype(jnp.bfloat16)
     tags = (owner[...] * CPO + sub[...] + 1).astype(jnp.float32)
-    for packed_ref in packed_refs:
+    for place, packed_ref in enumerate(packed_refs):
         rows = packed_ref.shape[0] - TAG_ROWS
-        at = 0 if rows == row_count else packed_refs[1:].index(packed_ref) * rows
+        at = max(place - 1, 0) * rows
         here = tags[at // LANES : (at + rows) // LANES, :]
         here = jnp.concatenate(
             [here, jnp.zeros((TAG_ROWS - here.shape[0], LANES), jnp.float32)], axis=0
@@ -74,7 +75,7 @@
     row_count, depth = embeddings.shape
     width = basis.shape[1]
     tag_shape = (row_count // LANES, LANES)
-    sizes = [row_count] + ([row_count // PIECES] * PIECES if PIECES > 1 else [])
+    sizes = [row_count] + [row_count // PIECES] * PIECES
     return pl.pallas_call(
         project_kernel,
         in_specs=[pl.BlockSpec(memory_space=pltpu.HBM)] * 4,
@@ -109,12 +110,15 @@
     )
 
 
-def score_kernel(key_blocks, row_blocks, own_first, want_rows, *refs):
+def score_kernel(key_blocks, row_blocks, with_base, own_first, pass_on, *refs):
     refs = list(refs)
+    if pass_on:
+        refs.pop()[...] = refs[0][...]
     key_refs = [refs.pop(0) for _ in range(key_blocks)]
     row_refs = [refs.pop(0) for _ in range(row_blocks)]
-    base_ref = None if own_first else refs.pop(0)
+    base_refs = [refs.pop(0) if given else None for given in with_base]
     col_refs = [refs.pop(0) for _ in range(key_blocks)]
+    row_outs = refs
     key_count, row_count = key_refs[0].shape[0] - TAG_ROWS, row_refs[0].shape[0] - TAG_ROWS
     key_tiles, row_tiles = key_count // LANES, row_count // LANES
     best = [jnp.full((8, LANES), ABSENT, jnp.float32) for _ in range(key_tiles * key_blocks)]
@@ -149,89 +153,103 @@
                     best[to] = jnp.maximum(
                         best[to], jnp.max(kept.reshape(LANES // 8, 8, LANES), axis=0)
                     )
-                    if want_rows:
+                    if row_outs:
                         across[tile] = (
                             kept if across[tile] is None else jnp.maximum(across[tile], kept)
                         )
-        if want_rows:
-            row_out = refs[block // 2]
+        if row_outs:
             for tile in range(row_tiles):
-                at = block % 2 * row_tiles + tile
                 found = jnp.max(across[tile].T, axis=0, keepdims=True)
-                if block == 0:
-                    found = jnp.maximum(found, base_ref[tile : tile + 1, :])
-                row_out[at : at + 1, :] = found
+                if base_refs[block] is not None:
+                    found = jnp.maximum(found, base_refs[block][tile : tile + 1, :])
+                row_outs[block][tile : tile + 1, :] = found
     for key_block, col_out in enumerate(col_refs):
         for at in range(key_tiles):
-            found = jnp.max(best[key_block * key_tiles + at], axis=0, keepdims=True)
-            if not own_first and not want_rows:
-                found = jnp.maximum(found, base_ref[at : at + 1, :])
-            col_out[at : at + 1, :] = found
-
-
-def score(keys, rows, base, want_rows):
+            col_out[at : at + 1, :] = jnp.max(best[key_block * key_tiles + at], axis=0, keepdims=True)
+
+
+def score(keys, rows, bases=None, own_first=False, pass_on=False):
     key_count, row_count = keys[0].shape[0] - TAG_ROWS, rows[0].shape[0] - TAG_ROWS
     out_shape = [jax.ShapeDtypeStruct((key_count // LANES, LANES), jnp.float32)] * len(keys)
-    if want_rows:
-        out_shape += [
-            jax.ShapeDtypeStruct((2 * row_count // LANES, LANES), jnp.float32)
-        ] * (len(rows) // 2)
-    operands = [*keys, *rows] + ([] if base is None else [base])
+    if bases is not None:
+        out_shape += [jax.ShapeDtypeStruct((row_count // LANES, LANES), jnp.float32)] * len(rows)
+    if pass_on:
+        out_shape.append(jax.ShapeDtypeStruct(keys[0].shape, keys[0].dtype))
+    given = [base for base in bases or [] if base is not None]
+    operands = [*keys, *rows, *given]
     whole = pl.BlockSpec(memory_space=pltpu.VMEM)
-    return pl.pallas_call(
-        functools.partial(score_kernel, len(keys), len(rows), base is None, want_rows),
+    found = pl.pallas_call(
+        functools.partial(
+            score_kernel,
+            len(keys),
+            len(rows),
+            tuple(base is not None for base in bases or []),
+            own_first,
+            pass_on,
+        ),
         in_specs=[whole] * len(operands),
         out_specs=[whole] * len(out_shape),
         out_shape=out_shape,
         compiler_params=pltpu.CompilerParams(vmem_limit_bytes=VMEM_LIMIT),
-        cost_estimate=pl.CostEstimate(flops=0, bytes_accessed=0, transcendentals=0),
+        cost_estimate=pl.CostEstimate(
+            flops=WEIGHT * len(keys) * len(rows) * key_count * row_count * keys[0].shape[1],
+            bytes_accessed=0,
+            transcendentals=0,
+        ),
     )(*operands)
-
-
-def owner_steps(count):
-    steps = [[(i, (i + k) % count) for i in range(count)] for k in range(1, (count + 1) // 2)]
-    if count % 2 == 0 and count > 1:
-        half = count // 2
-        steps.append([(i, i + half) if i % 2 == 0 else (i + half, i) for i in range(half)])
-    return steps
+    return found[: len(keys)], list(found[len(keys) :])
+
+
+def receivers(step, count):
+    if 2 * step == count:
+        return range(count // 4, count // 4 + count // 2)
+    return range(count)
 
 
 def per_device(embeddings, basis, owner_ids, sub_cluster):
     row_count = embeddings.shape[0]
-    tiles = row_count // LANES
     split_count, owner_count = lax.axis_size("split"), lax.axis_size("owners")
-    steps = owner_steps(owner_count)
+    steps = range(1, owner_count // 2 + 1)
 
     def swap(block, offset):
         return lax.ppermute(block, "split", [(s, s ^ offset) for s in range(split_count)])
 
-    own, *pieces = project(embeddings, basis, owner_ids, sub_cluster)
-    pieces = pieces or [own]
-    arrived = [
-        [lax.ppermute(piece, "owners", step) for piece in pieces] for step in reversed(steps)
-    ]
-    rows = [own, swap(own, 1)]
-    best = score([own], rows, None, False)[0]
-    for offset in range(2, split_count, 2):
-        beside = swap(own, offset)
-        pair = [beside, swap(own, offset + 1)]
-        best = score([own], pair, best, False)[0]
-        rows += pair
-    keys = [block for blocks in arrived for block in blocks]
-    found = score(keys, rows, best, True)
-    col_best, row_best = found[: len(keys)], found[len(keys) :]
-    local = row_best[0]
-    for at in range(1, split_count // 2):
-        local = jnp.maximum(local, swap(row_best[at], 2 * at))
-    best, beside = local[:tiles], local[tiles:]
-    best = jnp.maximum(best, swap(beside, 1))
-    for at, step in enumerate(reversed(steps)):
-        back = lax.ppermute(col_best[at], "owners", [(b, a) for a, b in step])
-        if len(step) < owner_count:
-            sent = functools.reduce(
-                jnp.logical_or, [lax.axis_index("owners") == a for a, _ in step]
-            )
-            back = jnp.where(sent, back, ABSENT)
+    own, *moving = project(embeddings, basis, owner_ids, sub_cluster)
+    arrived = []
+    for step in steps:
+        pairs = [((z - 1) % owner_count, z) for z in receivers(step, owner_count)]
+        moving = [lax.ppermute(piece, "owners", pairs) for piece in moving]
+        arrived.append([(piece, swap(piece, 1)) for piece in moving])
+    arrived[-1][-1] = (moving[-1], None)
+    core = swap(own, 1)
+    rows = [own] + [swap(own, offset) for offset in range(2, split_count, 2)]
+    (best,), _ = score([own], rows, own_first=True)
+    _, bases = score([core], rows, [best] + [None] * (len(rows) - 1))
+    backs = []
+    for step, pieces in zip(steps, arrived):
+        direct, beside = [], []
+        for at, (piece, other) in enumerate(pieces):
+            if backs and at == len(pieces) - 1:
+                bases = [jnp.maximum(bases[0], backs.pop()), *bases[1:]]
+            (found,), bases = score([piece], rows, bases, pass_on=other is None)
+            direct.append(found)
+            if other is None:
+                other = swap(bases.pop(), 1)
+            (found,), bases = score([other], rows, bases)
+            beside.append(found)
+        found = jnp.maximum(jnp.concatenate(direct), swap(jnp.concatenate(beside), 1))
+        targets = receivers(step, owner_count)
+        back = lax.ppermute(
+            found, "owners", [(z, (z - step) % owner_count) for z in targets]
+        )
+        if len(targets) < owner_count:
+            here = lax.axis_index("owners")
+            back = jnp.where((here < targets[0]) | (here > targets[-1]), back, ABSENT)
+        backs.append(back)
+    best = bases[0]
+    for offset, found in zip(range(2, split_count, 2), bases[1:]):
+        best = jnp.maximum(best, swap(found, offset))
+    for back in backs:
         best = jnp.maximum(best, back)
     return jnp.maximum(best, -1.0).reshape(row_count)
 

time: 36.2 us -> 40.3 us (1.11)
  starting transfers between devices: 10.8 us -> 14.3 us
  Pallas kernels: 6.75 us -> 9.52 us
  waiting for transfers between devices: 17.7 us -> 15.4 us
    ppermute x5 -> x9, waiting for transfers between devices: 7.99 us -> 3.56 us  [swap(): lax.ppermute(block, 'split', [(s, s ^ offset) for s in range(split_count)])]
    ppermute x4 -> x6, starting transfers between devices: 6.13 us -> 9.66 us  [the longest x4 8.31 us: per_device(): moving = [lax.ppermute(piece, 'owners', pairs) for piece in moving]]
    pallas_call x3 -> x10, Pallas kernels: 2.43 us -> 5.21 us  [score(): pl.pallas_call(functools.partial(score_kernel, len(keys), len(rows), tupl...]
    ppermute x4 -> x6, waiting for transfers between devices: 9.74 us -> 11.9 us  [the longest x2 6.63 us: per_device(): lax.ppermute(found, 'owners', [(z, (z - step) % owner_count) for z in tar...]
    ppermute x5 -> x9, starting transfers between devices: 4.71 us -> 4.69 us  [swap(): lax.ppermute(block, 'split', [(s, s ^ offset) for s in range(split_count)])]
  transfers between devices with their start and end apart: 9 -> 15, of which waited for: 5 -> 8; matrix products, arithmetic and copies ran while one was open for 0% -> 0% of each run, Pallas kernels for 3% -> 11%
where the time goes in v3:
time: 40.3 us; the launch traced here: 40.1 us
  waiting for transfers between devices  15.4 us (38%)
  starting transfers between devices  14.3 us (35%)
  Pallas kernels  9.52 us (24%)
  other arithmetic  0.62 us (2%)
    ppermute x4, starting transfers between devices, per_device(): moving = [lax.ppermute(piece, 'owners', pairs) for piece in moving]  8.31 us
    ppermute x2, waiting for transfers between devices, per_device(): lax.ppermute(found, 'owners', [(z, (z - step) % owner_count) for z in tar...  6.63 us
    ppermute x4, waiting for transfers between devices, per_device(): moving = [lax.ppermute(piece, 'owners', pairs) for piece in moving]  5.25 us
    pallas_call x10, Pallas kernels, score(): pl.pallas_call(functools.partial(score_kernel, len(keys), len(rows), tupl...  5.21 us
    ppermute x9, starting transfers between devices, swap(): lax.ppermute(block, 'split', [(s, s ^ offset) for s in range(split_count)])  4.69 us
    pallas_call x1, Pallas kernels, project(): pl.pallas_call(project_kernel, in_specs=[pl.BlockSpec(memory_space=pltpu....  4.32 us
    ppermute x9, waiting for transfers between devices, swap(): lax.ppermute(block, 'split', [(s, s ^ offset) for s in range(split_count)])  3.56 us
    ppermute x2, starting transfers between devices, per_device(): lax.ppermute(found, 'owners', [(z, (z - step) % owner_count) for z in tar...  1.35 us
  transfers between devices with their start and end apart: 15, of which 8 were waited for; matrix products, arithmetic and copies ran while one was open for 0% of the time, Pallas kernels for 11%

profile of v3, /device:TPU:0, one launch (start us, length us, event | category | flops | bytes accessed | tf_op | source)
XLA Modules:
  0.0 40.1 jit_solution(3688631063048208554)
XLA Ops:
  0.0 4.3 %shard_map.46 = (bf16[528,256]{1,0:T(8,128)(2,1)S(1)}, bf16[272,256]{1,0:T(8,128)(2,1)S(1)}, bf16[272,256]{1,0:T(8,128)(2,1)S(1)}) custom-call(bf16[512,4096]{1,0:T(8,128)(2,1)} %source_hbm.1, bf16[4096,256]{1,0:T(8,128)(2,1)} %basis_hbm.1, s32[4,128]{1,0:T(4,128)} %bitcast.4, s32[4,128]{1,0:T(4,128)} %bitcast.5), custom_call_target="tpu_custom_call" | custom-call | flops 1073741824 | bytes 6291456 | tf_op jit(solution)/shard_map/pallas_call | solution.py:79
  4.3 3.0 %collective-permute-start.2 = (bf16[528,256]{1,0:T(8,128)(2,1)S(1)}, bf16[528,256]{1,0:T(8,128)(2,1)S(1)}, u32[]{:S(2)}, u32[]{:S(2)}) collective-permute-start(bf16[528,256]{1,0:T(8,128)(2,1)S(1)} %get-tuple-element.36.refs_0_.refs_1_), channel_id=1, source_target_pairs={{0,2},{1,3},{2,0},{3,1},{4,6},{5,7},{6,4},{7,5},{8,10},{9,11},{10,... | collective-permute-start | bytes 811016 | tf_op jit(solution)/shard_map/ppermute | solution.py:215
  7.3 1.6 %collective-permute-start.3 = (bf16[272,256]{1,0:T(8,128)(2,1)S(1)}, bf16[272,256]{1,0:T(8,128)(2,1)S(1)}, u32[]{:S(2)}, u32[]{:S(2)}) collective-permute-start(bf16[272,256]{1,0:T(8,128)(2,1)S(1)} %get-tuple-element.37), channel_id=1, source_target_pairs={{12,0},{0,4},{4,8},{8,12},{13,1},{1,5},{5,9},{9,13},{14,2},{2,6},{... | collective-permute-start | bytes 417800 | tf_op jit(solution)/shard_map/ppermute | solution.py:221
  8.9 1.6 %collective-permute-start = (bf16[272,256]{1,0:T(8,128)(2,1)S(1)}, bf16[272,256]{1,0:T(8,128)(2,1)S(1)}, u32[]{:S(2)}, u32[]{:S(2)}) collective-permute-start(bf16[272,256]{1,0:T(8,128)(2,1)S(1)} %get-tuple-element.35), channel_id=1, source_target_pairs={{12,0},{0,4},{4,8},{8,12},{13,1},{1,5},{5,9},{9,13},{14,2},{2,6},{... | collective-permute-start | bytes 417800 | tf_op jit(solution)/shard_map/ppermute | solution.py:221
  10.5 5.2 %collective-permute-done.3.refs_0_ = bf16[272,256]{1,0:T(8,128)(2,1)S(1)} collective-permute-done((bf16[272,256]{1,0:T(8,128)(2,1)S(1)}, bf16[272,256]{1,0:T(8,128)(2,1)S(1)}, u32[]{:S(2)}, u32[]{:S(2)}) %collective-permute-start.3) | collective-permute-done | bytes 139296 | tf_op jit(solution)/shard_map/ppermute | solution.py:221
  15.7 1.7 %collective-permute-start.4 = (bf16[272,256]{1,0:T(8,128)(2,1)S(1)}, bf16[272,256]{1,0:T(8,128)(2,1)S(1)}, u32[]{:S(2)}, u32[]{:S(2)}) collective-permute-start(bf16[272,256]{1,0:T(8,128)(2,1)S(1)} %collective-permute-done.3.refs_0_), channel_id=1, source_target_pairs={{0,4},{4,8},{1,5},{5,9},{2,6},{6,10},{3,7},{7,11},{16,20},{20,24},... | collective-permute-start | bytes 417800 | tf_op jit(solution)/shard_map/ppermute | solution.py:221
  17.7 3.5 %collective-permute-start.1 = (bf16[272,256]{1,0:T(8,128)(2,1)S(1)}, bf16[272,256]{1,0:T(8,128)(2,1)S(1)}, u32[]{:S(2)}, u32[]{:S(2)}) collective-permute-start(bf16[272,256]{1,0:T(8,128)(2,1)S(1)} %collective-permute-done.refs_0_), channel_id=1, source_target_pairs={{0,4},{4,8},{1,5},{5,9},{2,6},{6,10},{3,7},{7,11},{16,20},{20,24},... | collective-permute-start | bytes 417800 | tf_op jit(solution)/shard_map/ppermute | solution.py:221
  21.2 0.5 %shard_map.47.refs_3_ = f32[4,128]{1,0:T(4,128)S(1)} custom-call(bf16[528,256]{1,0:T(8,128)(2,1)S(1)} %get-tuple-element.36.refs_0_.refs_1_, bf16[528,256]{1,0:T(8,128)(2,1)S(1)} %get-tuple-element.36.refs_0_.refs_1_, bf16[528,256]{1,0:T(8,128)(2,1)S(1)} %collective-permute-done.2.refs_2_), custom_call_target="tpu_custom_call" | custom-call | flops 4294967296 | tf_op jit(solution)/shard_map/pallas_call | solution.py:181
  21.7 1.1 %shard_map.48 = (f32[4,128]{1,0:T(4,128)}, f32[4,128]{1,0:T(4,128)S(1)}, f32[4,128]{1,0:T(4,128)S(1)}) custom-call(bf16[528,256]{1,0:T(8,128)(2,1)S(1)} %collective-permute-done.8.refs_0_, bf16[528,256]{1,0:T(8,128)(2,1)S(1)} %get-tuple-element.36.refs_0_.refs_1_, bf16[528,256]{1,0:T(8,128)(2,1)S(1)} %collective-permute-done.2.refs_2_, ...), custom_call_target="tpu_custom_call" | custom-call | flops 4294967296 | tf_op jit(solution)/shard_map/pallas_call | solution.py:181
  22.8 0.5 %shard_map.49 = (f32[2,128]{1,0:T(2,128)S(1)}, f32[4,128]{1,0:T(4,128)S(1)}, f32[4,128]{1,0:T(4,128)S(1)}) custom-call(bf16[272,256]{1,0:T(8,128)(2,1)S(1)} %collective-permute-done.3.refs_0_, bf16[528,256]{1,0:T(8,128)(2,1)S(1)} %get-tuple-element.36.refs_0_.refs_1_, bf16[528,256]{1,0:T(8,128)(2,1)S(1)} %collective-permute-done.2.refs_2_, ...), custom_call_target="tpu_custom_call" | custom-call | flops 2147483648 | tf_op jit(solution)/shard_map/pallas_call | solution.py:181
  23.3 0.5 %shard_map.50 = (f32[2,128]{1,0:T(2,128)S(1)}, f32[4,128]{1,0:T(4,128)S(1)}, f32[4,128]{1,0:T(4,128)S(1)}) custom-call(bf16[272,256]{1,0:T(8,128)(2,1)S(1)} %collective-permute-done.7.refs_0_, bf16[528,256]{1,0:T(8,128)(2,1)S(1)} %get-tuple-element.36.refs_0_.refs_1_, bf16[528,256]{1,0:T(8,128)(2,1)S(1)} %collective-permute-done.2.refs_2_, ...), custom_call_target="tpu_custom_call" | custom-call | flops 2147483648 | tf_op jit(solution)/shard_map/pallas_call | solution.py:181
  23.7 0.5 %shard_map.51 = (f32[2,128]{1,0:T(2,128)S(1)}, f32[4,128]{1,0:T(4,128)S(1)}, f32[4,128]{1,0:T(4,128)S(1)}) custom-call(bf16[272,256]{1,0:T(8,128)(2,1)S(1)} %collective-permute-done.refs_0_, bf16[528,256]{1,0:T(8,128)(2,1)S(1)} %get-tuple-element.36.refs_0_.refs_1_, bf16[528,256]{1,0:T(8,128)(2,1)S(1)} %collective-permute-done.2.refs_2_, ...), custom_call_target="tpu_custom_call" | custom-call | flops 2147483648 | tf_op jit(solution)/shard_map/pallas_call | solution.py:181
  24.2 0.5 %shard_map.52 = (f32[2,128]{1,0:T(2,128)S(1)}, f32[4,128]{1,0:T(4,128)S(1)}, f32[4,128]{1,0:T(4,128)S(1)}) custom-call(bf16[272,256]{1,0:T(8,128)(2,1)S(1)} %collective-permute-done.6.refs_0_, bf16[528,256]{1,0:T(8,128)(2,1)S(1)} %get-tuple-element.36.refs_0_.refs_1_, bf16[528,256]{1,0:T(8,128)(2,1)S(1)} %collective-permute-done.2.refs_2_, ...), custom_call_target="tpu_custom_call" | custom-call | flops 2147483648 | tf_op jit(solution)/shard_map/pallas_call | solution.py:181
  24.7 0.5 %collective-permute-start.5 = (bf16[272,256]{1,0:T(8,128)(2,1)S(1)}, bf16[272,256]{1,0:T(8,128)(2,1)S(1)}, u32[]{:S(2)}, u32[]{:S(2)}) collective-permute-start(bf16[272,256]{1,0:T(8,128)(2,1)S(1)} %collective-permute-done.4.refs_0_), channel_id=1, source_target_pairs={{0,1},{1,0},{2,3},{3,2},{4,5},{5,4},{6,7},{7,6},{8,9},{9,8},{10,11... | collective-permute-start | bytes 417800 | tf_op jit(solution)/shard_map/ppermute | solution.py:215
  25.2 0.5 %shard_map.53 = (f32[2,128]{1,0:T(2,128)S(1)}, f32[4,128]{1,0:T(4,128)S(1)}, f32[4,128]{1,0:T(4,128)S(1)}) custom-call(bf16[272,256]{1,0:T(8,128)(2,1)S(1)} %collective-permute-done.4.refs_0_, bf16[528,256]{1,0:T(8,128)(2,1)S(1)} %get-tuple-element.36.refs_0_.refs_1_, bf16[528,256]{1,0:T(8,128)(2,1)S(1)} %collective-permute-done.2.refs_2_, ...), custom_call_target="tpu_custom_call" | custom-call | flops 2147483648 | tf_op jit(solution)/shard_map/pallas_call | solution.py:181
  26.7 2.8 %collective-permute-done.10 = f32[4,128]{1,0:T(4,128)S(1)} collective-permute-done((f32[4,128]{1,0:T(4,128)S(1)}, f32[4,128]{1,0:T(4,128)S(1)}, u32[]{:S(2)}, u32[]{:S(2)}) %collective-permute-start.10) | collective-permute-done | bytes 2080 | tf_op jit(solution)/shard_map/ppermute | solution.py:242
  29.5 0.5 %shard_map.55 = (f32[2,128]{1,0:T(2,128)S(1)}, f32[4,128]{1,0:T(4,128)S(1)}, f32[4,128]{1,0:T(4,128)S(1)}, bf16[272,256]{1,0:T(8,128)(2,1)S(1)}) custom-call(bf16[272,256]{1,0:T(8,128)(2,1)S(1)} %collective-permute-done.1.refs_0_, bf16[528,256]{1,0:T(8,128)(2,1)S(1)} %get-tuple-element.36.refs_0_.refs_1_, ...), custom_call_target="tpu_custom_call" | custom-call | flops 2147483648 | tf_op jit(solution)/shard_map/pallas_call | solution.py:181
  30.1 1.3 %collective-permute-done.11.refs_0_ = bf16[272,256]{1,0:T(8,128)(2,1)S(1)} collective-permute-done((bf16[272,256]{1,0:T(8,128)(2,1)S(1)}, bf16[272,256]{1,0:T(8,128)(2,1)S(1)}, u32[]{:S(2)}, u32[]{:S(2)}) %collective-permute-start.11) | collective-permute-done | bytes 139296 | tf_op jit(solution)/shard_map/ppermute | solution.py:215
  32.1 0.5 %collective-permute-start.12 = (f32[4,128]{1,0:T(4,128)S(1)}, f32[4,128]{1,0:T(4,128)S(1)}, u32[]{:S(2)}, u32[]{:S(2)}) collective-permute-start(f32[4,128]{1,0:T(4,128)S(1)} %get-tuple-element.60), channel_id=1, source_target_pairs={{0,2},{1,3},{2,0},{3,1},{4,6},{5,7},{6,4},{7,5},{8,10},{9,11},{10,... | collective-permute-start | bytes 6152 | tf_op jit(solution)/shard_map/ppermute | solution.py:215
  32.6 0.5 %collective-permute-done.13 = f32[4,128]{1,0:T(4,128)S(1)} collective-permute-done((f32[4,128]{1,0:T(4,128)S(1)}, f32[4,128]{1,0:T(4,128)S(1)}, u32[]{:S(2)}, u32[]{:S(2)}) %collective-permute-start.13) | collective-permute-done | bytes 2080 | tf_op jit(solution)/shard_map/ppermute | solution.py:215
  33.1 1.3 %collective-permute-start.14 = (f32[4,128]{1,0:T(4,128)S(1)}, f32[4,128]{1,0:T(4,128)S(1)}, u32[]{:S(2)}, u32[]{:S(2)}) collective-permute-start(f32[4,128]{1,0:T(4,128)S(1)} %maximum_maximum_fusion.1), channel_id=1, source_target_pairs={{4,12},{8,0},{5,13},{9,1},{6,14},{10,2},{7,15},{11,3},{20,28},{24,... | collective-permute-start | bytes 6152 | tf_op jit(solution)/shard_map/ppermute | solution.py:242
  34.4 1.3 %collective-permute-done.12 = f32[4,128]{1,0:T(4,128)S(1)} collective-permute-done((f32[4,128]{1,0:T(4,128)S(1)}, f32[4,128]{1,0:T(4,128)S(1)}, u32[]{:S(2)}, u32[]{:S(2)}) %collective-permute-start.12) | collective-permute-done | bytes 2080 | tf_op jit(solution)/shard_map/ppermute | solution.py:215
  35.7 3.8 %collective-permute-done.14 = f32[4,128]{1,0:T(4,128)S(1)} collective-permute-done((f32[4,128]{1,0:T(4,128)S(1)}, f32[4,128]{1,0:T(4,128)S(1)}, u32[]{:S(2)}, u32[]{:S(2)}) %collective-permute-start.14) | collective-permute-done | bytes 2080 | tf_op jit(solution)/shard_map/ppermute | solution.py:242
  39.5 0.6 %maximum_bitcast_fusion = f32[512]{0:T(512)} fusion(f32[4,128]{1,0:T(4,128)S(1)} %collective-permute-done.14, f32[4,128]{1,0:T(4,128)S(1)} %get-tuple-element.59, f32[4,128]{1,0:T(4,128)S(1)} %collective-permute-done.12, pred[]{:T(512)S(6)} %or.3), kind=kLoop, calls=%fused_computation.4 | loop fusion | flops 2048 | bytes 8193 | tf_op jit(solution)/shard_map/reshape | solution.py:254
  (23 shorter events, 2.1 us)
Async XLA Ops:
  4.3 13.4 %collective-permute-start.2 = (bf16[528,256]{1,0:T(8,128)(2,1)S(1)}, bf16[528,256]{1,0:T(8,128)(2,1)S(1)}, u32[]{:S(2)}, u32[]{:S(2)}) collective-permute-start(bf16[528,256]{1,0:T(8,128)(2,1)S(1)} %get-tuple-element.36.refs_0_.refs_1_), channel_id=1, source_target_pairs={{0,2},{1,3},{2,0},{3,1},{4,6},{5,7},{6,4},{7,5},{8,10},{9,11},{10,... | collective-permute-start | bytes 811016 | tf_op jit(solution)/shard_map/ppermute | solution.py:215
  7.3 8.4 %collective-permute-start.3 = (bf16[272,256]{1,0:T(8,128)(2,1)S(1)}, bf16[272,256]{1,0:T(8,128)(2,1)S(1)}, u32[]{:S(2)}, u32[]{:S(2)}) collective-permute-start(bf16[272,256]{1,0:T(8,128)(2,1)S(1)} %get-tuple-element.37), channel_id=1, source_target_pairs={{12,0},{0,4},{4,8},{8,12},{13,1},{1,5},{5,9},{9,13},{14,2},{2,6},{... | collective-permute-start | bytes 417800 | tf_op jit(solution)/shard_map/ppermute | solution.py:221
  8.9 8.5 %collective-permute-start = (bf16[272,256]{1,0:T(8,128)(2,1)S(1)}, bf16[272,256]{1,0:T(8,128)(2,1)S(1)}, u32[]{:S(2)}, u32[]{:S(2)}) collective-permute-start(bf16[272,256]{1,0:T(8,128)(2,1)S(1)} %get-tuple-element.35), channel_id=1, source_target_pairs={{12,0},{0,4},{4,8},{8,12},{13,1},{1,5},{5,9},{9,13},{14,2},{2,6},{... | collective-permute-start | bytes 417800 | tf_op jit(solution)/shard_map/ppermute | solution.py:221
  10.5 11.2 %collective-permute-start.8 = (bf16[528,256]{1,0:T(8,128)(2,1)S(1)}, bf16[528,256]{1,0:T(8,128)(2,1)S(1)}, u32[]{:S(2)}, u32[]{:S(2)}) collective-permute-start(bf16[528,256]{1,0:T(8,128)(2,1)S(1)} %get-tuple-element.36.refs_0_.refs_1_), channel_id=1, source_target_pairs={{0,1},{1,0},{2,3},{3,2},{4,5},{5,4},{6,7},{7,6},{8,9},{9,8},{10,11... | collective-permute-start | bytes 811016 | tf_op jit(solution)/shard_map/ppermute | solution.py:215
  15.7 7.5 %collective-permute-start.7 = (bf16[272,256]{1,0:T(8,128)(2,1)S(1)}, bf16[272,256]{1,0:T(8,128)(2,1)S(1)}, u32[]{:S(2)}, u32[]{:S(2)}) collective-permute-start(bf16[272,256]{1,0:T(8,128)(2,1)S(1)} %collective-permute-done.3.refs_0_), channel_id=1, source_target_pairs={{0,1},{1,0},{2,3},{3,2},{4,5},{5,4},{6,7},{7,6},{8,9},{9,8},{10,11... | collective-permute-start | bytes 417800 | tf_op jit(solution)/shard_map/ppermute | solution.py:215
  15.7 9.0 %collective-permute-start.4 = (bf16[272,256]{1,0:T(8,128)(2,1)S(1)}, bf16[272,256]{1,0:T(8,128)(2,1)S(1)}, u32[]{:S(2)}, u32[]{:S(2)}) collective-permute-start(bf16[272,256]{1,0:T(8,128)(2,1)S(1)} %collective-permute-done.3.refs_0_), channel_id=1, source_target_pairs={{0,4},{4,8},{1,5},{5,9},{2,6},{6,10},{3,7},{7,11},{16,20},{20,24},... | collective-permute-start | bytes 417800 | tf_op jit(solution)/shard_map/ppermute | solution.py:221
  17.4 6.7 %collective-permute-start.6 = (bf16[272,256]{1,0:T(8,128)(2,1)S(1)}, bf16[272,256]{1,0:T(8,128)(2,1)S(1)}, u32[]{:S(2)}, u32[]{:S(2)}) collective-permute-start(bf16[272,256]{1,0:T(8,128)(2,1)S(1)} %collective-permute-done.refs_0_), channel_id=1, source_target_pairs={{0,1},{1,0},{2,3},{3,2},{4,5},{5,4},{6,7},{7,6},{8,9},{9,8},{10,11... | collective-permute-start | bytes 417800 | tf_op jit(solution)/shard_map/ppermute | solution.py:215
  17.7 11.8 %collective-permute-start.1 = (bf16[272,256]{1,0:T(8,128)(2,1)S(1)}, bf16[272,256]{1,0:T(8,128)(2,1)S(1)}, u32[]{:S(2)}, u32[]{:S(2)}) collective-permute-start(bf16[272,256]{1,0:T(8,128)(2,1)S(1)} %collective-permute-done.refs_0_), channel_id=1, source_target_pairs={{0,4},{4,8},{1,5},{5,9},{2,6},{6,10},{3,7},{7,11},{16,20},{20,24},... | collective-permute-start | bytes 417800 | tf_op jit(solution)/shard_map/ppermute | solution.py:221
  24.7 1.2 %collective-permute-start.9 = (f32[4,128]{1,0:T(4,128)S(1)}, f32[4,128]{1,0:T(4,128)S(1)}, u32[]{:S(2)}, u32[]{:S(2)}) collective-permute-start(f32[4,128]{1,0:T(4,128)S(1)} %pad_maximum_fusion), channel_id=1, source_target_pairs={{0,1},{1,0},{2,3},{3,2},{4,5},{5,4},{6,7},{7,6},{8,9},{9,8},{10,11... | collective-permute-start | bytes 6152 | tf_op jit(solution)/shard_map/ppermute | solution.py:215
  24.7 1.5 %collective-permute-start.5 = (bf16[272,256]{1,0:T(8,128)(2,1)S(1)}, bf16[272,256]{1,0:T(8,128)(2,1)S(1)}, u32[]{:S(2)}, u32[]{:S(2)}) collective-permute-start(bf16[272,256]{1,0:T(8,128)(2,1)S(1)} %collective-permute-done.4.refs_0_), channel_id=1, source_target_pairs={{0,1},{1,0},{2,3},{3,2},{4,5},{5,4},{6,7},{7,6},{8,9},{9,8},{10,11... | collective-permute-start | bytes 417800 | tf_op jit(solution)/shard_map/ppermute | solution.py:215
  25.9 3.6 %collective-permute-start.10 = (f32[4,128]{1,0:T(4,128)S(1)}, f32[4,128]{1,0:T(4,128)S(1)}, u32[]{:S(2)}, u32[]{:S(2)}) collective-permute-start(f32[4,128]{1,0:T(4,128)S(1)} %maximum_maximum_fusion), channel_id=1, source_target_pairs={{0,12},{4,0},{8,4},{12,8},{1,13},{5,1},{9,5},{13,9},{2,14},{6,2},{... | collective-permute-start | bytes 6152 | tf_op jit(solution)/shard_map/ppermute | solution.py:242
  30.0 1.4 %collective-permute-start.11 = (bf16[272,256]{1,0:T(8,128)(2,1)S(1)}, bf16[272,256]{1,0:T(8,128)(2,1)S(1)}, u32[]{:S(2)}, u32[]{:S(2)}) collective-permute-start(bf16[272,256]{1,0:T(8,128)(2,1)S(1)} %get-tuple-element.56), channel_id=1, source_target_pairs={{0,1},{1,0},{2,3},{3,2},{4,5},{5,4},{6,7},{7,6},{8,9},{9,8},{10,11... | collective-permute-start | bytes 417800 | tf_op jit(solution)/shard_map/ppermute | solution.py:215
  31.9 1.2 %collective-permute-start.13 = (f32[4,128]{1,0:T(4,128)S(1)}, f32[4,128]{1,0:T(4,128)S(1)}, u32[]{:S(2)}, u32[]{:S(2)}) collective-permute-start(f32[4,128]{1,0:T(4,128)S(1)} %pad_maximum_fusion.1), channel_id=1, source_target_pairs={{0,1},{1,0},{2,3},{3,2},{4,5},{5,4},{6,7},{7,6},{8,9},{9,8},{10,11... | collective-permute-start | bytes 6152 | tf_op jit(solution)/shard_map/ppermute | solution.py:215
  32.1 3.6 %collective-permute-start.12 = (f32[4,128]{1,0:T(4,128)S(1)}, f32[4,128]{1,0:T(4,128)S(1)}, u32[]{:S(2)}, u32[]{:S(2)}) collective-permute-start(f32[4,128]{1,0:T(4,128)S(1)} %get-tuple-element.60), channel_id=1, source_target_pairs={{0,2},{1,3},{2,0},{3,1},{4,6},{5,7},{6,4},{7,5},{8,10},{9,11},{10,... | collective-permute-start | bytes 6152 | tf_op jit(solution)/shard_map/ppermute | solution.py:215
  33.1 6.4 %collective-permute-start.14 = (f32[4,128]{1,0:T(4,128)S(1)}, f32[4,128]{1,0:T(4,128)S(1)}, u32[]{:S(2)}, u32[]{:S(2)}) collective-permute-start(f32[4,128]{1,0:T(4,128)S(1)} %maximum_maximum_fusion.1), channel_id=1, source_target_pairs={{4,12},{8,0},{5,13},{9,1},{6,14},{10,2},{7,15},{11,3},{20,28},{24,... | collective-permute-start | bytes 6152 | tf_op jit(solution)/shard_map/ppermute | solution.py:242

commit v4 on v2

--- a/solution.py
+++ b/solution.py
@@ -12,7 +12,7 @@
 TAG_ROWS = 16
 ABSENT = -2.0
 STEPS = 8
-PIECES = 1
+WEIGHT = 0
 VMEM_LIMIT = 48 * 1024 * 1024
 
 
@@ -58,9 +58,9 @@
     norms = jnp.sum(projected * projected, axis=1, keepdims=True)
     units = (projected * lax.rsqrt(norms + 1e-06)).astype(jnp.bfloat16)
     tags = (owner[...] * CPO + sub[...] + 1).astype(jnp.float32)
-    for packed_ref in packed_refs:
+    for place, packed_ref in enumerate(packed_refs):
         rows = packed_ref.shape[0] - TAG_ROWS
-        at = 0 if rows == row_count else packed_refs[1:].index(packed_ref) * rows
+        at = max(place - 1, 0) * rows
         here = tags[at // LANES : (at + rows) // LANES, :]
         here = jnp.concatenate(
             [here, jnp.zeros((TAG_ROWS - here.shape[0], LANES), jnp.float32)], axis=0
@@ -74,7 +74,7 @@
     row_count, depth = embeddings.shape
     width = basis.shape[1]
     tag_shape = (row_count // LANES, LANES)
-    sizes = [row_count] + ([row_count // PIECES] * PIECES if PIECES > 1 else [])
+    sizes = [row_count]
     return pl.pallas_call(
         project_kernel,
         in_specs=[pl.BlockSpec(memory_space=pltpu.HBM)] * 4,
@@ -109,12 +109,10 @@
     )
 
 
-def score_kernel(key_blocks, row_blocks, own_first, want_rows, *refs):
-    refs = list(refs)
-    key_refs = [refs.pop(0) for _ in range(key_blocks)]
-    row_refs = [refs.pop(0) for _ in range(row_blocks)]
-    base_ref = None if own_first else refs.pop(0)
-    col_refs = [refs.pop(0) for _ in range(key_blocks)]
+def score_kernel(key_blocks, row_blocks, own_first, unread, *refs):
+    key_refs, refs = refs[unread : unread + key_blocks], refs[unread + key_blocks :]
+    row_refs, refs = refs[:row_blocks], refs[row_blocks:]
+    col_refs, row_outs = refs[:key_blocks], refs[key_blocks:]
     key_count, row_count = key_refs[0].shape[0] - TAG_ROWS, row_refs[0].shape[0] - TAG_ROWS
     key_tiles, row_tiles = key_count // LANES, row_count // LANES
     best = [jnp.full((8, LANES), ABSENT, jnp.float32) for _ in range(key_tiles * key_blocks)]
@@ -149,43 +147,41 @@
                     best[to] = jnp.maximum(
                         best[to], jnp.max(kept.reshape(LANES // 8, 8, LANES), axis=0)
                     )
-                    if want_rows:
+                    if row_outs:
                         across[tile] = (
                             kept if across[tile] is None else jnp.maximum(across[tile], kept)
                         )
-        if want_rows:
-            row_out = refs[block // 2]
+        if row_outs:
             for tile in range(row_tiles):
                 at = block % 2 * row_tiles + tile
-                found = jnp.max(across[tile].T, axis=0, keepdims=True)
-                if block == 0:
-                    found = jnp.maximum(found, base_ref[tile : tile + 1, :])
-                row_out[at : at + 1, :] = found
+                row_outs[block // 2][at : at + 1, :] = jnp.max(
+                    across[tile].T, axis=0, keepdims=True
+                )
     for key_block, col_out in enumerate(col_refs):
         for at in range(key_tiles):
-            found = jnp.max(best[key_block * key_tiles + at], axis=0, keepdims=True)
-            if not own_first and not want_rows:
-                found = jnp.maximum(found, base_ref[at : at + 1, :])
-            col_out[at : at + 1, :] = found
-
-
-def score(keys, rows, base, want_rows):
+            col_out[at : at + 1, :] = jnp.max(best[key_block * key_tiles + at], axis=0, keepdims=True)
+
+
+def score(keys, rows, want_rows=True, own_first=False, after=()):
     key_count, row_count = keys[0].shape[0] - TAG_ROWS, rows[0].shape[0] - TAG_ROWS
     out_shape = [jax.ShapeDtypeStruct((key_count // LANES, LANES), jnp.float32)] * len(keys)
     if want_rows:
-        out_shape += [
-            jax.ShapeDtypeStruct((2 * row_count // LANES, LANES), jnp.float32)
-        ] * (len(rows) // 2)
-    operands = [*keys, *rows] + ([] if base is None else [base])
+        pair = jax.ShapeDtypeStruct((2 * row_count // LANES, LANES), jnp.float32)
+        out_shape += [pair] * (len(rows) // 2)
     whole = pl.BlockSpec(memory_space=pltpu.VMEM)
-    return pl.pallas_call(
-        functools.partial(score_kernel, len(keys), len(rows), base is None, want_rows),
-        in_specs=[whole] * len(operands),
+    found = pl.pallas_call(
+        functools.partial(score_kernel, len(keys), len(rows), own_first, len(after)),
+        in_specs=[pl.BlockSpec(memory_space=pl.ANY)] * len(after) + [whole] * (len(keys) + len(rows)),
         out_specs=[whole] * len(out_shape),
         out_shape=out_shape,
         compiler_params=pltpu.CompilerParams(vmem_limit_bytes=VMEM_LIMIT),
-        cost_estimate=pl.CostEstimate(flops=0, bytes_accessed=0, transcendentals=0),
-    )(*operands)
+        cost_estimate=pl.CostEstimate(
+            flops=WEIGHT * len(keys) * len(rows) * key_count * row_count * keys[0].shape[1],
+            bytes_accessed=0,
+            transcendentals=0,
+        ),
+    )(*after, *keys, *rows)
+    return found[: len(keys)], found[len(keys) :]
 
 
 def owner_steps(count):
@@ -200,40 +196,33 @@
     row_count = embeddings.shape[0]
     tiles = row_count // LANES
     split_count, owner_count = lax.axis_size("split"), lax.axis_size("owners")
-    steps = owner_steps(owner_count)
+    steps = owner_steps(owner_count)[::-1]
 
     def swap(block, offset):
         return lax.ppermute(block, "split", [(s, s ^ offset) for s in range(split_count)])
 
-    own, *pieces = project(embeddings, basis, owner_ids, sub_cluster)
-    pieces = pieces or [own]
-    arrived = [
-        [lax.ppermute(piece, "owners", step) for piece in pieces] for step in reversed(steps)
-    ]
+    (own,) = project(embeddings, basis, owner_ids, sub_cluster)
+    keys = [lax.ppermute(own, "owners", step) for step in steps]
     rows = [own, swap(own, 1)]
-    best = score([own], rows, None, False)[0]
     for offset in range(2, split_count, 2):
         beside = swap(own, offset)
-        pair = [beside, swap(own, offset + 1)]
-        best = score([own], pair, best, False)[0]
-        rows += pair
-    keys = [block for blocks in arrived for block in blocks]
-    found = score(keys, rows, best, True)
-    col_best, row_best = found[: len(keys)], found[len(keys) :]
+        rows += [beside, swap(beside, 1)]
+    col_best, row_best = score(keys, rows)
     local = row_best[0]
     for at in range(1, split_count // 2):
         local = jnp.maximum(local, swap(row_best[at], 2 * at))
     best, beside = local[:tiles], local[tiles:]
     best = jnp.maximum(best, swap(beside, 1))
-    for at, step in enumerate(reversed(steps)):
-        back = lax.ppermute(col_best[at], "owners", [(b, a) for a, b in step])
+    for found, step in zip(col_best, steps):
+        back = lax.ppermute(found, "owners", [(b, a) for a, b in step])
         if len(step) < owner_count:
             sent = functools.reduce(
                 jnp.logical_or, [lax.axis_index("owners") == a for a, _ in step]
             )
             back = jnp.where(sent, back, ABSENT)
         best = jnp.maximum(best, back)
-    return jnp.maximum(best, -1.0).reshape(row_count)
+    (alone,), _ = score([own], rows, want_rows=False, own_first=True, after=keys)
+    return jnp.maximum(jnp.maximum(best, alone), -1.0).reshape(row_count)
 
 
 def solution(mesh):

time: 36.2 us -> 34.1 us (0.942)
  starting transfers between devices: 10.8 us -> 9.53 us
  waiting for transfers between devices: 17.7 us -> 17.2 us
    ppermute x5, waiting for transfers between devices: 7.99 us -> 3.61 us  [swap(): lax.ppermute(block, 'split', [(s, s ^ offset) for s in range(split_count)])]
    ppermute x4, waiting for transfers between devices: 9.74 us -> 13.5 us  [the longest x2 11 us: per_device(): keys = [lax.ppermute(own, 'owners', step) for step in steps]]
    ppermute x5, starting transfers between devices: 4.71 us -> 3.69 us  [swap(): lax.ppermute(block, 'split', [(s, s ^ offset) for s in range(split_count)])]
    pallas_call x3 -> x2, Pallas kernels: 2.43 us -> 2.23 us  [score(): pl.pallas_call(functools.partial(score_kernel, len(keys), len(rows), own_...]
  transfers between devices with their start and end apart: 9 -> 9, of which waited for: 5 -> 5; matrix products, arithmetic and copies ran while one was open for 0% -> 0% of each run, Pallas kernels for 3% -> 2%
where the time goes in v4:
time: 34.1 us; the launch traced here: 33.9 us
  waiting for transfers between devices  17.2 us (50%)
  starting transfers between devices  9.53 us (28%)
  Pallas kernels  6.55 us (19%)
  other arithmetic  0.59 us (2%)
    ppermute x2, waiting for transfers between devices, per_device(): keys = [lax.ppermute(own, 'owners', step) for step in steps]  11 us
    ppermute x2, starting transfers between devices, per_device(): keys = [lax.ppermute(own, 'owners', step) for step in steps]  4.56 us
    pallas_call x1, Pallas kernels, project(): pl.pallas_call(project_kernel, in_specs=[pl.BlockSpec(memory_space=pltpu....  4.32 us
    ppermute x5, starting transfers between devices, swap(): lax.ppermute(block, 'split', [(s, s ^ offset) for s in range(split_count)])  3.69 us
    ppermute x5, waiting for transfers between devices, swap(): lax.ppermute(block, 'split', [(s, s ^ offset) for s in range(split_count)])  3.61 us
    ppermute x2, waiting for transfers between devices, per_device(): back = lax.ppermute(found, 'owners', [(b, a) for a, b in step])  2.51 us
    pallas_call x2, Pallas kernels, score(): pl.pallas_call(functools.partial(score_kernel, len(keys), len(rows), own_...  2.23 us
    ppermute x2, starting transfers between devices, per_device(): back = lax.ppermute(found, 'owners', [(b, a) for a, b in step])  1.28 us
  transfers between devices with their start and end apart: 9, of which 5 were waited for; matrix products, arithmetic and copies ran while one was open for 0% of the time, Pallas kernels for 2%

profile of v4, /device:TPU:0, one launch (start us, length us, event | category | flops | bytes accessed | tf_op | source)
XLA Modules:
  0.0 33.9 jit_solution(7479630495665606410)
XLA Ops:
  0.0 4.3 %shard_map.46.refs_2_.refs_3_ = bf16[528,256]{1,0:T(8,128)(2,1)S(1)} custom-call(bf16[512,4096]{1,0:T(8,128)(2,1)} %source_hbm.1, bf16[4096,256]{1,0:T(8,128)(2,1)} %basis_hbm.1, s32[4,128]{1,0:T(4,128)} %bitcast.4, s32[4,128]{1,0:T(4,128)} %bitcast.5), custom_call_target="tpu_custom_call" | custom-call | flops 1073741824 | bytes 6291456 | tf_op jit(solution)/shard_map/pallas_call | solution.py:78
  4.3 3.0 %collective-permute-start.3 = (bf16[528,256]{1,0:T(8,128)(2,1)S(1)}, bf16[528,256]{1,0:T(8,128)(2,1)S(1)}, u32[]{:S(2)}, u32[]{:S(2)}) collective-permute-start(bf16[528,256]{1,0:T(8,128)(2,1)S(1)} %shard_map.46.refs_2_.refs_3_), channel_id=1, source_target_pairs={{0,2},{1,3},{2,0},{3,1},{4,6},{5,7},{6,4},{7,5},{8,10},{9,11},{10,... | collective-permute-start | bytes 811016 | tf_op jit(solution)/shard_map/ppermute | solution.py:202
  7.3 4.5 %collective-permute-start = (bf16[528,256]{1,0:T(8,128)(2,1)S(1)}, bf16[528,256]{1,0:T(8,128)(2,1)S(1)}, u32[]{:S(2)}, u32[]{:S(2)}) collective-permute-start(bf16[528,256]{1,0:T(8,128)(2,1)S(1)} %shard_map.46.refs_2_.refs_3_), channel_id=1, source_target_pairs={{0,8},{12,4},{1,9},{13,5},{2,10},{14,6},{3,11},{15,7},{16,24},{28,... | collective-permute-start | bytes 811016 | tf_op jit(solution)/shard_map/ppermute | solution.py:205
  11.8 0.1 collective-permute-start.1
  11.9 0.1 collective-permute-start.2
  12.0 1.8 %collective-permute-done.3.refs_4_.refs_5_ = bf16[528,256]{1,0:T(8,128)(2,1)S(1)} collective-permute-done((bf16[528,256]{1,0:T(8,128)(2,1)S(1)}, bf16[528,256]{1,0:T(8,128)(2,1)S(1)}, u32[]{:S(2)}, u32[]{:S(2)}) %collective-permute-start.3) | collective-permute-done | bytes 270368 | tf_op jit(solution)/shard_map/ppermute | solution.py:202
  13.8 0.0 collective-permute-start.4
  13.8 4.9 %collective-permute-done.refs_0_ = bf16[528,256]{1,0:T(8,128)(2,1)S(1)} collective-permute-done((bf16[528,256]{1,0:T(8,128)(2,1)S(1)}, bf16[528,256]{1,0:T(8,128)(2,1)S(1)}, u32[]{:S(2)}, u32[]{:S(2)}) %collective-permute-start) | collective-permute-done | bytes 270368 | tf_op jit(solution)/shard_map/ppermute | solution.py:205
  18.7 6.1 %collective-permute-done.1.refs_1_ = bf16[528,256]{1,0:T(8,128)(2,1)S(1)} collective-permute-done((bf16[528,256]{1,0:T(8,128)(2,1)S(1)}, bf16[528,256]{1,0:T(8,128)(2,1)S(1)}, u32[]{:S(2)}, u32[]{:S(2)}) %collective-permute-start.1) | collective-permute-done | bytes 270368 | tf_op jit(solution)/shard_map/ppermute | solution.py:205
  24.9 0.0 collective-permute-done.2.refs_3_.refs_4_
  24.9 0.0 collective-permute-done.4.refs_5_.refs_6_
  24.9 1.5 %shard_map.47 = (f32[4,128]{1,0:T(4,128)S(1)}, f32[4,128]{1,0:T(4,128)S(1)}, f32[8,128]{1,0:T(8,128)S(1)}, f32[8,128]{1,0:T(8,128)S(1)}) custom-call(bf16[528,256]{1,0:T(8,128)(2,1)S(1)} %collective-permute-done.refs_0_, bf16[528,256]{1,0:T(8,128)(2,1)S(1)} %collective-permute-done.1.refs_1_, bf16[528,256]{1,0:T(8,128)(2,1)S(1)} %shard_map.46.refs_2_.refs_3_, ...), custom_call_target="tpu_custom_call" | custom-call | tf_op jit(solution)/shard_map/pallas_call | solution.py:172
  26.3 0.6 %collective-permute-start.5 = (f32[8,128]{1,0:T(8,128)S(1)}, f32[8,128]{1,0:T(8,128)S(1)}, u32[]{:S(2)}, u32[]{:S(2)}) collective-permute-start(f32[8,128]{1,0:T(8,128)S(1)} %get-tuple-element.10), channel_id=1, source_target_pairs={{0,2},{1,3},{2,0},{3,1},{4,6},{5,7},{6,4},{7,5},{8,10},{9,11},{10,... | collective-permute-start | bytes 12296 | tf_op jit(solution)/shard_map/ppermute | solution.py:202
  26.9 0.0 collective-permute-start.8
  27.0 1.3 %collective-permute-start.7 = (f32[4,128]{1,0:T(4,128)S(1)}, f32[4,128]{1,0:T(4,128)S(1)}, u32[]{:S(2)}, u32[]{:S(2)}) collective-permute-start(f32[4,128]{1,0:T(4,128)S(1)} %get-tuple-element.11), channel_id=1, source_target_pairs={{8,0},{4,12},{9,1},{5,13},{10,2},{6,14},{11,3},{7,15},{24,16},{20,... | collective-permute-start | bytes 6152 | tf_op jit(solution)/shard_map/ppermute | solution.py:217
  28.2 1.8 %collective-permute-done.5 = f32[8,128]{1,0:T(8,128)S(1)} collective-permute-done((f32[8,128]{1,0:T(8,128)S(1)}, f32[8,128]{1,0:T(8,128)S(1)}, u32[]{:S(2)}, u32[]{:S(2)}) %collective-permute-start.5) | collective-permute-done | bytes 4128 | tf_op jit(solution)/shard_map/ppermute | solution.py:202
  30.0 0.0 collective-permute-start.6
  30.0 0.8 %shard_map.48 = f32[4,128]{1,0:T(4,128)S(1)} custom-call(bf16[528,256]{1,0:T(8,128)(2,1)S(1)} %collective-permute-done.refs_0_, bf16[528,256]{1,0:T(8,128)(2,1)S(1)} %collective-permute-done.1.refs_1_, bf16[528,256]{1,0:T(8,128)(2,1)S(1)} %shard_map.46.refs_2_.refs_3_, bf16[528,256]{1,0:T(8,128)(2,1)S(1)} %shard_map.46.refs_2_.refs_3_, ...), custom_call_target="tpu_custom_call" | custom-call | tf_op jit(solution)/shard_map/pallas_call | solution.py:172
  30.8 0.0 collective-permute-done.8
  30.8 2.5 %collective-permute-done.7 = f32[4,128]{1,0:T(4,128)S(1)} collective-permute-done((f32[4,128]{1,0:T(4,128)S(1)}, f32[4,128]{1,0:T(4,128)S(1)}, u32[]{:S(2)}, u32[]{:S(2)}) %collective-permute-start.7) | collective-permute-done | bytes 2080 | tf_op jit(solution)/shard_map/ppermute | solution.py:217
  33.3 0.0 collective-permute-done.6
  33.3 0.6 %maximum_bitcast_fusion = f32[512]{0:T(512)} fusion(f32[4,128]{1,0:T(4,128)S(1)} %shard_map.48, f32[4,128]{1,0:T(4,128)S(1)} %collective-permute-done.8, f32[4,128]{1,0:T(4,128)S(1)} %collective-permute-done.7, f32[4,128]{1,0:T(4,128)S(1)} %collective-permute-done.6, f32[8,128]{1,0:T(8,128)S(1)} %max.21, pred[]{:T(512)S(6)} %or.3), kind=kLoop, calls=%fused_computation | loop fusion | flops 3072 | bytes 12289 | tf_op jit(solution)/shard_map/reshape | solution.py:225
  (2 shorter events, 0.0 us)
Async XLA Ops:
  4.3 9.5 %collective-permute-start.3 = (bf16[528,256]{1,0:T(8,128)(2,1)S(1)}, bf16[528,256]{1,0:T(8,128)(2,1)S(1)}, u32[]{:S(2)}, u32[]{:S(2)}) collective-permute-start(bf16[528,256]{1,0:T(8,128)(2,1)S(1)} %shard_map.46.refs_2_.refs_3_), channel_id=1, source_target_pairs={{0,2},{1,3},{2,0},{3,1},{4,6},{5,7},{6,4},{7,5},{8,10},{9,11},{10,... | collective-permute-start | bytes 811016 | tf_op jit(solution)/shard_map/ppermute | solution.py:202
  7.3 11.4 %collective-permute-start = (bf16[528,256]{1,0:T(8,128)(2,1)S(1)}, bf16[528,256]{1,0:T(8,128)(2,1)S(1)}, u32[]{:S(2)}, u32[]{:S(2)}) collective-permute-start(bf16[528,256]{1,0:T(8,128)(2,1)S(1)} %shard_map.46.refs_2_.refs_3_), channel_id=1, source_target_pairs={{0,8},{12,4},{1,9},{13,5},{2,10},{14,6},{3,11},{15,7},{16,24},{28,... | collective-permute-start | bytes 811016 | tf_op jit(solution)/shard_map/ppermute | solution.py:205
  11.8 13.0 %collective-permute-start.1 = (bf16[528,256]{1,0:T(8,128)(2,1)S(1)}, bf16[528,256]{1,0:T(8,128)(2,1)S(1)}, u32[]{:S(2)}, u32[]{:S(2)}) collective-permute-start(bf16[528,256]{1,0:T(8,128)(2,1)S(1)} %shard_map.46.refs_2_.refs_3_), channel_id=1, source_target_pairs={{0,4},{4,8},{8,12},{12,0},{1,5},{5,9},{9,13},{13,1},{2,6},{6,10},{... | collective-permute-start | bytes 811016 | tf_op jit(solution)/shard_map/ppermute | solution.py:205
  11.9 13.0 %collective-permute-start.2 = (bf16[528,256]{1,0:T(8,128)(2,1)S(1)}, bf16[528,256]{1,0:T(8,128)(2,1)S(1)}, u32[]{:S(2)}, u32[]{:S(2)}) collective-permute-start(bf16[528,256]{1,0:T(8,128)(2,1)S(1)} %shard_map.46.refs_2_.refs_3_), channel_id=1, source_target_pairs={{0,1},{1,0},{2,3},{3,2},{4,5},{5,4},{6,7},{7,6},{8,9},{9,8},{10,11... | collective-permute-start | bytes 811016 | tf_op jit(solution)/shard_map/ppermute | solution.py:202
  13.8 11.1 %collective-permute-start.4 = (bf16[528,256]{1,0:T(8,128)(2,1)S(1)}, bf16[528,256]{1,0:T(8,128)(2,1)S(1)}, u32[]{:S(2)}, u32[]{:S(2)}) collective-permute-start(bf16[528,256]{1,0:T(8,128)(2,1)S(1)} %collective-permute-done.3.refs_4_.refs_5_), channel_id=1, source_target_pairs={{0,1},{1,0},{2,3},{3,2},{4,5},{5,4},{6,7},{7,6},{8,9},{9,8},{10,11... | collective-permute-start | bytes 811016 | tf_op jit(solution)/shard_map/ppermute | solution.py:202
  26.3 3.7 %collective-permute-start.5 = (f32[8,128]{1,0:T(8,128)S(1)}, f32[8,128]{1,0:T(8,128)S(1)}, u32[]{:S(2)}, u32[]{:S(2)}) collective-permute-start(f32[8,128]{1,0:T(8,128)S(1)} %get-tuple-element.10), channel_id=1, source_target_pairs={{0,2},{1,3},{2,0},{3,1},{4,6},{5,7},{6,4},{7,5},{8,10},{9,11},{10,... | collective-permute-start | bytes 12296 | tf_op jit(solution)/shard_map/ppermute | solution.py:202
  26.9 3.9 %collective-permute-start.8 = (f32[4,128]{1,0:T(4,128)S(1)}, f32[4,128]{1,0:T(4,128)S(1)}, u32[]{:S(2)}, u32[]{:S(2)}) collective-permute-start(f32[4,128]{1,0:T(4,128)S(1)} %get-tuple-element.12), channel_id=1, source_target_pairs={{4,0},{8,4},{12,8},{0,12},{5,1},{9,5},{13,9},{1,13},{6,2},{10,6},{... | collective-permute-start | bytes 6152 | tf_op jit(solution)/shard_map/ppermute | solution.py:217
  27.0 6.4 %collective-permute-start.7 = (f32[4,128]{1,0:T(4,128)S(1)}, f32[4,128]{1,0:T(4,128)S(1)}, u32[]{:S(2)}, u32[]{:S(2)}) collective-permute-start(f32[4,128]{1,0:T(4,128)S(1)} %get-tuple-element.11), channel_id=1, source_target_pairs={{8,0},{4,12},{9,1},{5,13},{10,2},{6,14},{11,3},{7,15},{24,16},{20,... | collective-permute-start | bytes 6152 | tf_op jit(solution)/shard_map/ppermute | solution.py:217
  30.0 3.3 %collective-permute-start.6 = (f32[4,128]{1,0:T(4,128)S(1)}, f32[4,128]{1,0:T(4,128)S(1)}, u32[]{:S(2)}, u32[]{:S(2)}) collective-permute-start(f32[4,128]{1,0:T(4,128)S(1)} %slice.7), channel_id=1, source_target_pairs={{0,1},{1,0},{2,3},{3,2},{4,5},{5,4},{6,7},{7,6},{8,9},{9,8},{10,11... | collective-permute-start | bytes 6152 | tf_op jit(solution)/shard_map/ppermute | solution.py:202

commit v5 on v4

v5 whole, which is shorter than its diff:
```python
import functools

import jax
import jax.numpy as jnp
from jax import lax
from jax.experimental import pallas as pl
from jax.experimental.pallas import tpu as pltpu
from jax.sharding import PartitionSpec as P

CPO = 8
LANES = 128
TAG_ROWS = 16
ABSENT = -2.0
EIGHTHS = (2, 2, 2, 1, 1)
PARTS = 2
VMEM_LIMIT = 48 * 1024 * 1024


def project_kernel(source_hbm, basis_hbm, owner_hbm, sub_hbm, *refs):
    packed_refs, (source, basis, owner, sub, sems, tag_sems) = refs[:-6], refs[-6:]
    row_count, depth = source.shape
    width = basis.shape[1]
    ends = [depth * sum(EIGHTHS[: step + 1]) // 8 for step in range(len(EIGHTHS))]
    spans = list(zip([0] + ends, ends))
    tag_copies = [
        pltpu.make_async_copy(owner_hbm, owner, tag_sems.at[0]),
        pltpu.make_async_copy(sub_hbm, sub, tag_sems.at[1]),
    ]
    copies = []
    for step, (start, end) in enumerate(spans):
        span = pl.ds(start, end - start)
        copies.append(
            (
                pltpu.make_async_copy(
                    basis_hbm.at[span, :], basis.at[span, :], sems.at[0, step]
                ),
                pltpu.make_async_copy(
                    source_hbm.at[:, span], source.at[:, span], sems.at[1, step]
                ),
            )
        )
    for pair in copies:
        for copy in pair:
            copy.start()
    for copy in tag_copies:
        copy.start()
    projected = None
    for (start, end), pair in zip(spans, copies):
        for copy in pair:
            copy.wait()
        part = jnp.dot(
            source[:, start:end], basis[start:end, :], preferred_element_type=jnp.float32
        )
        projected = part if projected is None else projected + part
    for copy in tag_copies:
        copy.wait()
    norms = jnp.sum(projected * projected, axis=1, keepdims=True)
    units = (projected * lax.rsqrt(norms + 1e-06)).astype(jnp.bfloat16)
    tags = (owner[...] * CPO + sub[...] + 1).astype(jnp.float32)
    for place, packed_ref in enumerate(packed_refs):
        rows = packed_ref.shape[0] - TAG_ROWS
        at = max(place - 1, 0) * rows
        here = tags[at // LANES : (at + rows) // LANES, :]
        here = jnp.concatenate(
            [here, jnp.zeros((TAG_ROWS - here.shape[0], LANES), jnp.float32)], axis=0
        )
        here = jnp.concatenate([here, jnp.zeros((TAG_ROWS, width - LANES), jnp.float32)], axis=1)
        packed_ref[:rows, :] = units[at : at + rows, :]
        packed_ref[rows:, :] = here.astype(jnp.bfloat16)


def project(embeddings, basis, owner_ids, sub_cluster):
    row_count, depth = embeddings.shape
    width = basis.shape[1]
    tag_shape = (row_count // LANES, LANES)
    sizes = [row_count]
    return pl.pallas_call(
        project_kernel,
        in_specs=[pl.BlockSpec(memory_space=pltpu.HBM)] * 4,
        out_specs=[pl.BlockSpec(memory_space=pltpu.VMEM)] * len(sizes),
        out_shape=[
            jax.ShapeDtypeStruct((size + TAG_ROWS, width), jnp.bfloat16) for size in sizes
        ],
        scratch_shapes=[
            pltpu.VMEM((row_count, depth), jnp.bfloat16),
            pltpu.VMEM((depth, width), jnp.bfloat16),
            pltpu.VMEM(tag_shape, jnp.int32),
            pltpu.VMEM(tag_shape, jnp.int32),
            pltpu.SemaphoreType.DMA((2, len(EIGHTHS))),
            pltpu.SemaphoreType.DMA((2,)),
        ],
        compiler_params=pltpu.CompilerParams(vmem_limit_bytes=VMEM_LIMIT),
        cost_estimate=pl.CostEstimate(
            flops=2 * row_count * depth * width,
            bytes_accessed=2 * depth * (row_count + width),
            transcendentals=0,
        ),
    )(
        *[
            pltpu.with_memory_space_constraint(array, pltpu.HBM)
            for array in (
                embeddings,
                basis,
                owner_ids.reshape(tag_shape),
                sub_cluster.reshape(tag_shape),
            )
        ]
    )


def score_kernel(row_parts, own_first, bases, unread, *refs):
    refs = list(refs[unread:])
    key_ref = refs.pop(0)
    row_refs = [[refs.pop(0) for _ in range(parts)] for parts in row_parts]
    base_refs = [refs.pop(0) for _ in range(bases)]
    col_out, row_outs = refs[0], refs[1:]
    row_count = key_ref.shape[0] - TAG_ROWS
    tiles = row_count // LANES
    key_tags = key_ref[row_count:, :LANES].astype(jnp.float32)
    best = [jnp.full((8, LANES), ABSENT, jnp.float32) for _ in range(tiles)]
    for block, part_refs in enumerate(row_refs):
        tag_ref = part_refs[-1]
        row_tags = tag_ref[tag_ref.shape[0] - TAG_ROWS :, :LANES].astype(jnp.float32)
        place = 0
        for part_ref in part_refs:
            count = row_count // len(part_refs)
            scores = lax.dot_general(
                part_ref[:count, :],
                key_ref[:row_count, :],
                (((1,), (1,)), ((), ())),
                preferred_element_type=jnp.float32,
            )
            for start in range(0, count, LANES):
                tags = jnp.broadcast_to(row_tags[place : place + 1, :], (LANES, LANES)).T
                across = None
                for at in range(tiles):
                    same = tags == key_tags[at : at + 1, :]
                    if own_first and block == 0 and at == place:
                        same = same & (
                            lax.broadcasted_iota(jnp.int32, (LANES, LANES), 0)
                            != lax.broadcasted_iota(jnp.int32, (LANES, LANES), 1)
                        )
                    kept = scores[start : start + LANES, at * LANES : (at + 1) * LANES]
                    kept = jnp.where(same, kept, ABSENT)
                    best[at] = jnp.maximum(
                        best[at], jnp.max(kept.reshape(LANES // 8, 8, LANES), axis=0)
                    )
                    if row_outs:
                        across = kept if across is None else jnp.maximum(across, kept)
                if row_outs:
                    at = block % 2 * tiles + place
                    found = jnp.max(across.T, axis=0, keepdims=True)
                    if base_refs:
                        found = jnp.maximum(found, base_refs[block // 2][at : at + 1, :])
                    row_outs[block // 2][at : at + 1, :] = found
                place += 1
    for at in range(tiles):
        found = jnp.max(best[at], axis=0, keepdims=True)
        if own_first:
            for base_ref in base_refs:
                found = jnp.maximum(found, base_ref[at : at + 1, :])
        col_out[at : at + 1, :] = found
    if own_first:
        col_out[tiles:, :] = base_refs[0][tiles:, :]


def score(key, rows, bases, own_first=False, after=()):
    tiles = (key.shape[0] - TAG_ROWS) // LANES
    parts = [row if isinstance(row, tuple) else (row,) for row in rows]
    blocks = [part for row in parts for part in row]
    pair = jax.ShapeDtypeStruct((2 * tiles, LANES), jnp.float32)
    out_shape = [pair]
    if not own_first:
        out_shape = [jax.ShapeDtypeStruct((tiles, LANES), jnp.float32)] + [pair] * (len(rows) // 2)
    whole = pl.BlockSpec(memory_space=pltpu.VMEM)
    found = pl.pallas_call(
        functools.partial(
            score_kernel, [len(row) for row in parts], own_first, len(bases), len(after)
        ),
        in_specs=[pl.BlockSpec(memory_space=pl.ANY)] * len(after)
        + [whole] * (1 + len(blocks) + len(bases)),
        out_specs=[whole] * len(out_shape),
        out_shape=out_shape,
        compiler_params=pltpu.CompilerParams(vmem_limit_bytes=VMEM_LIMIT),
        cost_estimate=pl.CostEstimate(flops=0, bytes_accessed=0, transcendentals=0),
    )(*after, key, *blocks, *bases)
    return found[0], list(found[1:])


def owner_steps(count):
    steps = [[(i, (i + k) % count) for i in range(count)] for k in range(1, (count + 1) // 2)]
    if count % 2 == 0 and count > 1:
        half = count // 2
        steps.append([(i, i + half) if i % 2 == 0 else (i + half, i) for i in range(half)])
    return steps


def per_device(embeddings, basis, owner_ids, sub_cluster):
    row_count = embeddings.shape[0]
    tiles = row_count // LANES
    split_count, owner_count = lax.axis_size("split"), lax.axis_size("owners")
    steps = owner_steps(owner_count)[::-1]

    def swap(block, offset):
        return lax.ppermute(block, "split", [(s, s ^ offset) for s in range(split_count)])

    (own,) = project(embeddings, basis, owner_ids, sub_cluster)
    rows = [own, swap(own, 1)]
    for offset in range(2, split_count, 2):
        beside = swap(own, offset)
        part = row_count // PARTS
        starts = [part * at for at in range(PARTS)]
        ends = starts[1:] + [row_count + TAG_ROWS]
        rows += [beside, tuple(swap(beside[a:b], 1) for a, b in zip(starts, ends))]
    keys = [lax.ppermute(own, "owners", step) for step in steps]
    row_best, backs = [], []
    for block, step in zip(keys, steps):
        found, row_best = score(block, rows, row_best)
        back = lax.ppermute(found, "owners", [(b, a) for a, b in step])
        if len(step) < owner_count:
            sent = functools.reduce(
                jnp.logical_or, [lax.axis_index("owners") == a for a, _ in step]
            )
            back = jnp.where(sent, back, ABSENT)
        backs.append(back)
    others = [swap(row_best[at], 2 * at) for at in range(1, split_count // 2)]
    local, _ = score(own, rows, [row_best[0], *backs[:-1]], own_first=True, after=keys)
    for other in others:
        local = jnp.maximum(local, other)
    best = jnp.maximum(local[:tiles], swap(local[tiles:], 1))
    return jnp.maximum(jnp.maximum(best, backs[-1]), -1.0).reshape(row_count)


def solution(mesh):
    placed = (
        P(("groups", "owners", "split"), None),
        P(),
        P(("groups", "owners", "split"), None),
        P(("groups", "owners", "split")),
    )
    return jax.shard_map(
        per_device,
        mesh=mesh,
        in_specs=placed,
        out_specs=P(("groups", "owners", "split")),
        check_vma=False,
    )
```

time: 34.1 us -> 32.6 us (0.956)
  waiting for transfers between devices: 17.2 us -> 14.6 us
  starting transfers between devices: 9.53 us -> 10.1 us
  Pallas kernels: 6.55 us -> 7.09 us
    ppermute x2, waiting for transfers between devices: 2.51 us -> 0.5 us  [per_device(): back = lax.ppermute(found, 'owners', [(b, a) for a, b in step])]
    ppermute x2, waiting for transfers between devices: 11 us -> 9.2 us  [per_device(): keys = [lax.ppermute(own, 'owners', step) for step in steps]]
    ppermute x5 -> x6, waiting for transfers between devices: 3.61 us -> 4.86 us  [swap(): lax.ppermute(block, 'split', [(s, s ^ offset) for s in range(split_count)])]
    ppermute x5 -> x6, starting transfers between devices: 3.69 us -> 4.24 us  [swap(): lax.ppermute(block, 'split', [(s, s ^ offset) for s in range(split_count)])]
    pallas_call x2 -> x3, Pallas kernels: 2.23 us -> 2.43 us  [score(): pl.pallas_call(functools.partial(score_kernel, [len(row) for row in parts...]
  transfers between devices with their start and end apart: 9 -> 10, of which waited for: 5 -> 6; matrix products, arithmetic and copies ran while one was open for 0% -> 0% of each run, Pallas kernels for 2% -> 8%
where the time goes in v5:
time: 32.6 us; the launch traced here: 32.4 us
  waiting for transfers between devices  14.6 us (45%)
  starting transfers between devices  10.1 us (31%)
  Pallas kernels  7.09 us (22%)
  other arithmetic  0.59 us (2%)
    ppermute x2, waiting for transfers between devices, per_device(): keys = [lax.ppermute(own, 'owners', step) for step in steps]  9.2 us
    ppermute x6, waiting for transfers between devices, swap(): lax.ppermute(block, 'split', [(s, s ^ offset) for s in range(split_count)])  4.86 us
    pallas_call x1, Pallas kernels, project(): pl.pallas_call(project_kernel, in_specs=[pl.BlockSpec(memory_space=pltpu....  4.66 us
    ppermute x2, starting transfers between devices, per_device(): keys = [lax.ppermute(own, 'owners', step) for step in steps]  4.56 us
    ppermute x6, starting transfers between devices, swap(): lax.ppermute(block, 'split', [(s, s ^ offset) for s in range(split_count)])  4.24 us
    pallas_call x3, Pallas kernels, score(): pl.pallas_call(functools.partial(score_kernel, [len(row) for row in parts...  2.43 us
    ppermute x2, starting transfers between devices, per_device(): back = lax.ppermute(found, 'owners', [(b, a) for a, b in step])  1.29 us
  transfers between devices with their start and end apart: 10, of which 6 were waited for; matrix products, arithmetic and copies ran while one was open for 0% of the time, Pallas kernels for 8%

profile of v5, /device:TPU:0, one launch (start us, length us, event | category | flops | bytes accessed | tf_op | source)
XLA Modules:
  0.0 32.4 jit_solution(5230667754263714522)
XLA Ops:
  0.0 4.7 %shard_map.46.refs_1_.refs_2_.refs_3_ = bf16[528,256]{1,0:T(8,128)(2,1)S(1)} custom-call(bf16[512,4096]{1,0:T(8,128)(2,1)} %source_hbm.1, bf16[4096,256]{1,0:T(8,128)(2,1)} %basis_hbm.1, s32[4,128]{1,0:T(4,128)} %bitcast.4, s32[4,128]{1,0:T(4,128)} %bitcast.5), custom_call_target="tpu_custom_call" | custom-call | flops 1073741824 | bytes 6291456 | tf_op jit(solution)/shard_map/pallas_call | solution.py:77
  4.7 3.0 %collective-permute-start.3 = (bf16[528,256]{1,0:T(8,128)(2,1)S(1)}, bf16[528,256]{1,0:T(8,128)(2,1)S(1)}, u32[]{:S(2)}, u32[]{:S(2)}) collective-permute-start(bf16[528,256]{1,0:T(8,128)(2,1)S(1)} %shard_map.46.refs_1_.refs_2_.refs_3_), channel_id=1, source_target_pairs={{0,2},{1,3},{2,0},{3,1},{4,6},{5,7},{6,4},{7,5},{8,10},{9,11},{10,... | collective-permute-start | bytes 811016 | tf_op jit(solution)/shard_map/ppermute | solution.py:205
  7.7 0.0 collective-permute-start.2
  7.7 4.5 %collective-permute-start = (bf16[528,256]{1,0:T(8,128)(2,1)S(1)}, bf16[528,256]{1,0:T(8,128)(2,1)S(1)}, u32[]{:S(2)}, u32[]{:S(2)}) collective-permute-start(bf16[528,256]{1,0:T(8,128)(2,1)S(1)} %shard_map.46.refs_1_.refs_2_.refs_3_), channel_id=1, source_target_pairs={{0,8},{12,4},{1,9},{13,5},{2,10},{14,6},{3,11},{15,7},{16,24},{28,... | collective-permute-start | bytes 811016 | tf_op jit(solution)/shard_map/ppermute | solution.py:215
  12.2 0.1 collective-permute-start.1
  12.2 1.9 %collective-permute-done.3.refs_3_.refs_5_ = bf16[528,256]{1,0:T(8,128)(2,1)S(1)} collective-permute-done((bf16[528,256]{1,0:T(8,128)(2,1)S(1)}, bf16[528,256]{1,0:T(8,128)(2,1)S(1)}, u32[]{:S(2)}, u32[]{:S(2)}) %collective-permute-start.3) | collective-permute-done | bytes 270368 | tf_op jit(solution)/shard_map/ppermute | solution.py:205
  14.2 0.1 collective-permute-start.5
  14.3 0.6 %collective-permute-start.4 = (bf16[256,256]{1,0:T(8,128)(2,1)S(1)}, bf16[256,256]{1,0:T(8,128)(2,1)S(1)}, u32[]{:S(2)}, u32[]{:S(2)}) collective-permute-start(bf16[256,256]{1,0:T(8,128)(2,1)S(1)} %slice.16), channel_id=1, source_target_pairs={{0,1},{1,0},{2,3},{3,2},{4,5},{5,4},{6,7},{7,6},{8,9},{9,8},{10,11... | collective-permute-start | bytes 393224 | tf_op jit(solution)/shard_map/ppermute | solution.py:205
  14.8 0.0 collective-permute-done.2.refs_2_.refs_4_
  14.8 4.2 %collective-permute-done.refs_0_ = bf16[528,256]{1,0:T(8,128)(2,1)S(1)} collective-permute-done((bf16[528,256]{1,0:T(8,128)(2,1)S(1)}, bf16[528,256]{1,0:T(8,128)(2,1)S(1)}, u32[]{:S(2)}, u32[]{:S(2)}) %collective-permute-start) | collective-permute-done | bytes 270368 | tf_op jit(solution)/shard_map/ppermute | solution.py:215
  19.0 0.0 collective-permute-done.4.refs_4_.refs_6_
  19.0 0.0 collective-permute-done.5.refs_5_.refs_7_
  19.0 0.8 %shard_map.47 = (f32[4,128]{1,0:T(4,128)S(1)}, f32[8,128]{1,0:T(8,128)S(1)}, f32[8,128]{1,0:T(8,128)S(1)}) custom-call(bf16[528,256]{1,0:T(8,128)(2,1)S(1)} %collective-permute-done.refs_0_, bf16[528,256]{1,0:T(8,128)(2,1)S(1)} %shard_map.46.refs_1_.refs_2_.refs_3_, bf16[528,256]{1,0:T(8,128)(2,1)S(1)} %collective-permute-done.2.refs_2_.refs_4_, ...), custom_call_target="tpu_custom_call" | custom-call | tf_op jit(solution)/shard_map/pallas_call | solution.py:176
  19.8 1.3 %collective-permute-start.6 = (f32[4,128]{1,0:T(4,128)S(1)}, f32[4,128]{1,0:T(4,128)S(1)}, u32[]{:S(2)}, u32[]{:S(2)}) collective-permute-start(f32[4,128]{1,0:T(4,128)S(1)} %get-tuple-element.14), channel_id=1, source_target_pairs={{8,0},{4,12},{9,1},{5,13},{10,2},{6,14},{11,3},{7,15},{24,16},{20,... | collective-permute-start | bytes 6152 | tf_op jit(solution)/shard_map/ppermute | solution.py:219
  21.1 5.0 %collective-permute-done.1.refs_0_.refs_1_ = bf16[528,256]{1,0:T(8,128)(2,1)S(1)} collective-permute-done((bf16[528,256]{1,0:T(8,128)(2,1)S(1)}, bf16[528,256]{1,0:T(8,128)(2,1)S(1)}, u32[]{:S(2)}, u32[]{:S(2)}) %collective-permute-start.1) | collective-permute-done | bytes 270368 | tf_op jit(solution)/shard_map/ppermute | solution.py:215
  26.2 0.8 %shard_map.48 = (f32[4,128]{1,0:T(4,128)S(1)}, f32[8,128]{1,0:T(8,128)S(1)}, f32[8,128]{1,0:T(8,128)S(1)}) custom-call(bf16[528,256]{1,0:T(8,128)(2,1)S(1)} %collective-permute-done.1.refs_0_.refs_1_, bf16[528,256]{1,0:T(8,128)(2,1)S(1)} %shard_map.46.refs_1_.refs_2_.refs_3_, bf16[528,256]{1,0:T(8,128)(2,1)S(1)} %collective-permute-done.2.refs_2_.refs_4_, ...), custom_call_target="tpu_custom_call" | custom-call | tf_op jit(solution)/shard_map/pallas_call | solution.py:176
  27.0 0.6 %collective-permute-start.7 = (f32[8,128]{1,0:T(8,128)S(1)}, f32[8,128]{1,0:T(8,128)S(1)}, u32[]{:S(2)}, u32[]{:S(2)}) collective-permute-start(f32[8,128]{1,0:T(8,128)S(1)} %get-tuple-element.15), channel_id=1, source_target_pairs={{0,2},{1,3},{2,0},{3,1},{4,6},{5,7},{6,4},{7,5},{8,10},{9,11},{10,... | collective-permute-start | bytes 12296 | tf_op jit(solution)/shard_map/ppermute | solution.py:205
  27.6 0.0 collective-permute-start.9
  27.6 0.0 collective-permute-done.6
  27.6 0.8 %shard_map.49 = f32[8,128]{1,0:T(8,128)S(1)} custom-call(bf16[528,256]{1,0:T(8,128)(2,1)S(1)} %collective-permute-done.refs_0_, bf16[528,256]{1,0:T(8,128)(2,1)S(1)} %collective-permute-done.1.refs_0_.refs_1_, bf16[528,256]{1,0:T(8,128)(2,1)S(1)} %shard_map.46.refs_1_.refs_2_.refs_3_, bf16[528,256]{1,0:T(8,128)(2,1)S(1)} %shard_map.46.refs_1_.refs_2_.refs_3_, ...), custom_call_target="tpu_custom_call" | custom-call | tf_op jit(solution)/shard_map/pallas_call | solution.py:176
  28.4 2.3 %collective-permute-done.7 = f32[8,128]{1,0:T(8,128)S(1)} collective-permute-done((f32[8,128]{1,0:T(8,128)S(1)}, f32[8,128]{1,0:T(8,128)S(1)}, u32[]{:S(2)}, u32[]{:S(2)}) %collective-permute-start.7) | collective-permute-done | bytes 4128 | tf_op jit(solution)/shard_map/ppermute | solution.py:205
  30.7 0.5 %collective-permute-done.9 = f32[4,128]{1,0:T(4,128)S(1)} collective-permute-done((f32[4,128]{1,0:T(4,128)S(1)}, f32[4,128]{1,0:T(4,128)S(1)}, u32[]{:S(2)}, u32[]{:S(2)}) %collective-permute-start.9) | collective-permute-done | bytes 2080 | tf_op jit(solution)/shard_map/ppermute | solution.py:219
  31.2 0.7 %collective-permute-done.8 = f32[4,128]{1,0:T(4,128)S(1)} collective-permute-done((f32[4,128]{1,0:T(4,128)S(1)}, f32[4,128]{1,0:T(4,128)S(1)}, u32[]{:S(2)}, u32[]{:S(2)}) %collective-permute-start.8) | collective-permute-done | bytes 2080 | tf_op jit(solution)/shard_map/ppermute | solution.py:205
  31.9 0.6 %maximum_bitcast_fusion = f32[512]{0:T(512)} fusion(f32[4,128]{1,0:T(4,128)S(1)} %collective-permute-done.9, f32[4,128]{1,0:T(4,128)S(1)} %collective-permute-done.8, f32[8,128]{1,0:T(8,128)S(1)} %max.15), kind=kLoop, calls=%fused_computation | loop fusion | flops 1536 | bytes 8192 | tf_op jit(solution)/shard_map/reshape | solution.py:231
  (6 shorter events, 0.0 us)
Async XLA Ops:
  4.7 9.5 %collective-permute-start.3 = (bf16[528,256]{1,0:T(8,128)(2,1)S(1)}, bf16[528,256]{1,0:T(8,128)(2,1)S(1)}, u32[]{:S(2)}, u32[]{:S(2)}) collective-permute-start(bf16[528,256]{1,0:T(8,128)(2,1)S(1)} %shard_map.46.refs_1_.refs_2_.refs_3_), channel_id=1, source_target_pairs={{0,2},{1,3},{2,0},{3,1},{4,6},{5,7},{6,4},{7,5},{8,10},{9,11},{10,... | collective-permute-start | bytes 811016 | tf_op jit(solution)/shard_map/ppermute | solution.py:205
  7.7 7.2 %collective-permute-start.2 = (bf16[528,256]{1,0:T(8,128)(2,1)S(1)}, bf16[528,256]{1,0:T(8,128)(2,1)S(1)}, u32[]{:S(2)}, u32[]{:S(2)}) collective-permute-start(bf16[528,256]{1,0:T(8,128)(2,1)S(1)} %shard_map.46.refs_1_.refs_2_.refs_3_), channel_id=1, source_target_pairs={{0,1},{1,0},{2,3},{3,2},{4,5},{5,4},{6,7},{7,6},{8,9},{9,8},{10,11... | collective-permute-start | bytes 811016 | tf_op jit(solution)/shard_map/ppermute | solution.py:205
  7.7 11.3 %collective-permute-start = (bf16[528,256]{1,0:T(8,128)(2,1)S(1)}, bf16[528,256]{1,0:T(8,128)(2,1)S(1)}, u32[]{:S(2)}, u32[]{:S(2)}) collective-permute-start(bf16[528,256]{1,0:T(8,128)(2,1)S(1)} %shard_map.46.refs_1_.refs_2_.refs_3_), channel_id=1, source_target_pairs={{0,8},{12,4},{1,9},{13,5},{2,10},{14,6},{3,11},{15,7},{16,24},{28,... | collective-permute-start | bytes 811016 | tf_op jit(solution)/shard_map/ppermute | solution.py:215
  12.2 14.0 %collective-permute-start.1 = (bf16[528,256]{1,0:T(8,128)(2,1)S(1)}, bf16[528,256]{1,0:T(8,128)(2,1)S(1)}, u32[]{:S(2)}, u32[]{:S(2)}) collective-permute-start(bf16[528,256]{1,0:T(8,128)(2,1)S(1)} %shard_map.46.refs_1_.refs_2_.refs_3_), channel_id=1, source_target_pairs={{0,4},{4,8},{8,12},{12,0},{1,5},{5,9},{9,13},{13,1},{2,6},{6,10},{... | collective-permute-start | bytes 811016 | tf_op jit(solution)/shard_map/ppermute | solution.py:215
  14.2 4.8 %collective-permute-start.5 = (bf16[272,256]{1,0:T(8,128)(2,1)S(1)}, bf16[272,256]{1,0:T(8,128)(2,1)S(1)}, u32[]{:S(2)}, u32[]{:S(2)}) collective-permute-start(bf16[272,256]{1,0:T(8,128)(2,1)S(1)} %slice.17), channel_id=1, source_target_pairs={{0,1},{1,0},{2,3},{3,2},{4,5},{5,4},{6,7},{7,6},{8,9},{9,8},{10,11... | collective-permute-start | bytes 417800 | tf_op jit(solution)/shard_map/ppermute | solution.py:205
  14.3 4.7 %collective-permute-start.4 = (bf16[256,256]{1,0:T(8,128)(2,1)S(1)}, bf16[256,256]{1,0:T(8,128)(2,1)S(1)}, u32[]{:S(2)}, u32[]{:S(2)}) collective-permute-start(bf16[256,256]{1,0:T(8,128)(2,1)S(1)} %slice.16), channel_id=1, source_target_pairs={{0,1},{1,0},{2,3},{3,2},{4,5},{5,4},{6,7},{7,6},{8,9},{9,8},{10,11... | collective-permute-start | bytes 393224 | tf_op jit(solution)/shard_map/ppermute | solution.py:205
  19.8 7.8 %collective-permute-start.6 = (f32[4,128]{1,0:T(4,128)S(1)}, f32[4,128]{1,0:T(4,128)S(1)}, u32[]{:S(2)}, u32[]{:S(2)}) collective-permute-start(f32[4,128]{1,0:T(4,128)S(1)} %get-tuple-element.14), channel_id=1, source_target_pairs={{8,0},{4,12},{9,1},{5,13},{10,2},{6,14},{11,3},{7,15},{24,16},{20,... | collective-permute-start | bytes 6152 | tf_op jit(solution)/shard_map/ppermute | solution.py:219
  27.0 3.7 %collective-permute-start.7 = (f32[8,128]{1,0:T(8,128)S(1)}, f32[8,128]{1,0:T(8,128)S(1)}, u32[]{:S(2)}, u32[]{:S(2)}) collective-permute-start(f32[8,128]{1,0:T(8,128)S(1)} %get-tuple-element.15), channel_id=1, source_target_pairs={{0,2},{1,3},{2,0},{3,1},{4,6},{5,7},{6,4},{7,5},{8,10},{9,11},{10,... | collective-permute-start | bytes 12296 | tf_op jit(solution)/shard_map/ppermute | solution.py:205
  27.6 3.6 %collective-permute-start.9 = (f32[4,128]{1,0:T(4,128)S(1)}, f32[4,128]{1,0:T(4,128)S(1)}, u32[]{:S(2)}, u32[]{:S(2)}) collective-permute-start(f32[4,128]{1,0:T(4,128)S(1)} %get-tuple-element.16), channel_id=1, source_target_pairs={{4,0},{8,4},{12,8},{0,12},{5,1},{9,5},{13,9},{1,13},{6,2},{10,6},{... | collective-permute-start | bytes 6152 | tf_op jit(solution)/shard_map/ppermute | solution.py:219
  30.7 1.2 %collective-permute-start.8 = (f32[4,128]{1,0:T(4,128)S(1)}, f32[4,128]{1,0:T(4,128)S(1)}, u32[]{:S(2)}, u32[]{:S(2)}) collective-permute-start(f32[4,128]{1,0:T(4,128)S(1)} %slice.15), channel_id=1, source_target_pairs={{0,1},{1,0},{2,3},{3,2},{4,5},{5,4},{6,7},{7,6},{8,9},{9,8},{10,11... | collective-permute-start | bytes 6152 | tf_op jit(solution)/shard_map/ppermute | solution.py:205

commit v6 on v5

--- a/solution.py
+++ b/solution.py
@@ -11,7 +11,7 @@
 LANES = 128
 TAG_ROWS = 16
 ABSENT = -2.0
-EIGHTHS = (2, 2, 2, 1, 1)
+STEPS = 16
 PARTS = 2
 VMEM_LIMIT = 48 * 1024 * 1024
 
@@ -20,8 +20,8 @@
     packed_refs, (source, basis, owner, sub, sems, tag_sems) = refs[:-6], refs[-6:]
     row_count, depth = source.shape
     width = basis.shape[1]
-    ends = [depth * sum(EIGHTHS[: step + 1]) // 8 for step in range(len(EIGHTHS))]
-    spans = list(zip([0] + ends, ends))
+    chunk = depth // STEPS
+    spans = [(chunk * step, chunk * (step + 1)) for step in range(STEPS)]
     tag_copies = [
         pltpu.make_async_copy(owner_hbm, owner, tag_sems.at[0]),
         pltpu.make_async_copy(sub_hbm, sub, tag_sems.at[1]),
@@ -86,7 +86,7 @@
             pltpu.VMEM((depth, width), jnp.bfloat16),
             pltpu.VMEM(tag_shape, jnp.int32),
             pltpu.VMEM(tag_shape, jnp.int32),
-            pltpu.SemaphoreType.DMA((2, len(EIGHTHS))),
+            pltpu.SemaphoreType.DMA((2, STEPS)),
             pltpu.SemaphoreType.DMA((2,)),
         ],
         compiler_params=pltpu.CompilerParams(vmem_limit_bytes=VMEM_LIMIT),

time: 32.6 us -> 32.5 us (level)
  no operation moved by 1% of the time
where the time goes in v6:
time: 32.5 us; the launch traced here: 32.3 us
  waiting for transfers between devices  14.6 us (45%)
  starting transfers between devices  10.1 us (31%)
  Pallas kernels  6.95 us (21%)
  other arithmetic  0.59 us (2%)
    ppermute x2, waiting for transfers between devices, per_device(): keys = [lax.ppermute(own, 'owners', step) for step in steps]  9.2 us
    ppermute x6, waiting for transfers between devices, swap(): lax.ppermute(block, 'split', [(s, s ^ offset) for s in range(split_count)])  4.86 us
    ppermute x2, starting transfers between devices, per_device(): keys = [lax.ppermute(own, 'owners', step) for step in steps]  4.56 us
    pallas_call x1, Pallas kernels, project(): pl.pallas_call(project_kernel, in_specs=[pl.BlockSpec(memory_space=pltpu....  4.52 us
    ppermute x6, starting transfers between devices, swap(): lax.ppermute(block, 'split', [(s, s ^ offset) for s in range(split_count)])  4.24 us
    pallas_call x3, Pallas kernels, score(): pl.pallas_call(functools.partial(score_kernel, [len(row) for row in parts...  2.43 us
    ppermute x2, starting transfers between devices, per_device(): back = lax.ppermute(found, 'owners', [(b, a) for a, b in step])  1.29 us
  transfers between devices with their start and end apart: 10, of which 6 were waited for; matrix products, arithmetic and copies ran while one was open for 0% of the time, Pallas kernels for 8%

profile of v6, /device:TPU:0, one launch (start us, length us, event | category | flops | bytes accessed | tf_op | source)
XLA Modules:
  0.0 32.3 jit_solution(10613686088953611694)
XLA Ops:
  0.0 4.5 %shard_map.46.refs_1_.refs_2_.refs_3_ = bf16[528,256]{1,0:T(8,128)(2,1)S(1)} custom-call(bf16[512,4096]{1,0:T(8,128)(2,1)} %source_hbm.1, bf16[4096,256]{1,0:T(8,128)(2,1)} %basis_hbm.1, s32[4,128]{1,0:T(4,128)} %bitcast.4, s32[4,128]{1,0:T(4,128)} %bitcast.5), custom_call_target="tpu_custom_call" | custom-call | flops 1073741824 | bytes 6291456 | tf_op jit(solution)/shard_map/pallas_call | solution.py:77
  4.5 3.0 %collective-permute-start.3 = (bf16[528,256]{1,0:T(8,128)(2,1)S(1)}, bf16[528,256]{1,0:T(8,128)(2,1)S(1)}, u32[]{:S(2)}, u32[]{:S(2)}) collective-permute-start(bf16[528,256]{1,0:T(8,128)(2,1)S(1)} %shard_map.46.refs_1_.refs_2_.refs_3_), channel_id=1, source_target_pairs={{0,2},{1,3},{2,0},{3,1},{4,6},{5,7},{6,4},{7,5},{8,10},{9,11},{10,... | collective-permute-start | bytes 811016 | tf_op jit(solution)/shard_map/ppermute | solution.py:205
  7.5 0.0 collective-permute-start.2
  7.5 4.5 %collective-permute-start = (bf16[528,256]{1,0:T(8,128)(2,1)S(1)}, bf16[528,256]{1,0:T(8,128)(2,1)S(1)}, u32[]{:S(2)}, u32[]{:S(2)}) collective-permute-start(bf16[528,256]{1,0:T(8,128)(2,1)S(1)} %shard_map.46.refs_1_.refs_2_.refs_3_), channel_id=1, source_target_pairs={{0,8},{12,4},{1,9},{13,5},{2,10},{14,6},{3,11},{15,7},{16,24},{28,... | collective-permute-start | bytes 811016 | tf_op jit(solution)/shard_map/ppermute | solution.py:215
  12.0 0.1 collective-permute-start.1
  12.1 1.9 %collective-permute-done.3.refs_3_.refs_5_ = bf16[528,256]{1,0:T(8,128)(2,1)S(1)} collective-permute-done((bf16[528,256]{1,0:T(8,128)(2,1)S(1)}, bf16[528,256]{1,0:T(8,128)(2,1)S(1)}, u32[]{:S(2)}, u32[]{:S(2)}) %collective-permute-start.3) | collective-permute-done | bytes 270368 | tf_op jit(solution)/shard_map/ppermute | solution.py:205
  14.0 0.1 collective-permute-start.5
  14.1 0.6 %collective-permute-start.4 = (bf16[256,256]{1,0:T(8,128)(2,1)S(1)}, bf16[256,256]{1,0:T(8,128)(2,1)S(1)}, u32[]{:S(2)}, u32[]{:S(2)}) collective-permute-start(bf16[256,256]{1,0:T(8,128)(2,1)S(1)} %slice.16), channel_id=1, source_target_pairs={{0,1},{1,0},{2,3},{3,2},{4,5},{5,4},{6,7},{7,6},{8,9},{9,8},{10,11... | collective-permute-start | bytes 393224 | tf_op jit(solution)/shard_map/ppermute | solution.py:205
  14.7 0.0 collective-permute-done.2.refs_2_.refs_4_
  14.7 4.2 %collective-permute-done.refs_0_ = bf16[528,256]{1,0:T(8,128)(2,1)S(1)} collective-permute-done((bf16[528,256]{1,0:T(8,128)(2,1)S(1)}, bf16[528,256]{1,0:T(8,128)(2,1)S(1)}, u32[]{:S(2)}, u32[]{:S(2)}) %collective-permute-start) | collective-permute-done | bytes 270368 | tf_op jit(solution)/shard_map/ppermute | solution.py:215
  18.8 0.0 collective-permute-done.4.refs_4_.refs_6_
  18.9 0.0 collective-permute-done.5.refs_5_.refs_7_
  18.9 0.8 %shard_map.47 = (f32[4,128]{1,0:T(4,128)S(1)}, f32[8,128]{1,0:T(8,128)S(1)}, f32[8,128]{1,0:T(8,128)S(1)}) custom-call(bf16[528,256]{1,0:T(8,128)(2,1)S(1)} %collective-permute-done.refs_0_, bf16[528,256]{1,0:T(8,128)(2,1)S(1)} %shard_map.46.refs_1_.refs_2_.refs_3_, bf16[528,256]{1,0:T(8,128)(2,1)S(1)} %collective-permute-done.2.refs_2_.refs_4_, ...), custom_call_target="tpu_custom_call" | custom-call | tf_op jit(solution)/shard_map/pallas_call | solution.py:176
  19.7 1.3 %collective-permute-start.6 = (f32[4,128]{1,0:T(4,128)S(1)}, f32[4,128]{1,0:T(4,128)S(1)}, u32[]{:S(2)}, u32[]{:S(2)}) collective-permute-start(f32[4,128]{1,0:T(4,128)S(1)} %get-tuple-element.14), channel_id=1, source_target_pairs={{8,0},{4,12},{9,1},{5,13},{10,2},{6,14},{11,3},{7,15},{24,16},{20,... | collective-permute-start | bytes 6152 | tf_op jit(solution)/shard_map/ppermute | solution.py:219
  21.0 5.0 %collective-permute-done.1.refs_0_.refs_1_ = bf16[528,256]{1,0:T(8,128)(2,1)S(1)} collective-permute-done((bf16[528,256]{1,0:T(8,128)(2,1)S(1)}, bf16[528,256]{1,0:T(8,128)(2,1)S(1)}, u32[]{:S(2)}, u32[]{:S(2)}) %collective-permute-start.1) | collective-permute-done | bytes 270368 | tf_op jit(solution)/shard_map/ppermute | solution.py:215
  26.0 0.8 %shard_map.48 = (f32[4,128]{1,0:T(4,128)S(1)}, f32[8,128]{1,0:T(8,128)S(1)}, f32[8,128]{1,0:T(8,128)S(1)}) custom-call(bf16[528,256]{1,0:T(8,128)(2,1)S(1)} %collective-permute-done.1.refs_0_.refs_1_, bf16[528,256]{1,0:T(8,128)(2,1)S(1)} %shard_map.46.refs_1_.refs_2_.refs_3_, bf16[528,256]{1,0:T(8,128)(2,1)S(1)} %collective-permute-done.2.refs_2_.refs_4_, ...), custom_call_target="tpu_custom_call" | custom-call | tf_op jit(solution)/shard_map/pallas_call | solution.py:176
  26.9 0.6 %collective-permute-start.7 = (f32[8,128]{1,0:T(8,128)S(1)}, f32[8,128]{1,0:T(8,128)S(1)}, u32[]{:S(2)}, u32[]{:S(2)}) collective-permute-start(f32[8,128]{1,0:T(8,128)S(1)} %get-tuple-element.15), channel_id=1, source_target_pairs={{0,2},{1,3},{2,0},{3,1},{4,6},{5,7},{6,4},{7,5},{8,10},{9,11},{10,... | collective-permute-start | bytes 12296 | tf_op jit(solution)/shard_map/ppermute | solution.py:205
  27.5 0.0 collective-permute-start.9
  27.5 0.0 collective-permute-done.6
  27.5 0.8 %shard_map.49 = f32[8,128]{1,0:T(8,128)S(1)} custom-call(bf16[528,256]{1,0:T(8,128)(2,1)S(1)} %collective-permute-done.refs_0_, bf16[528,256]{1,0:T(8,128)(2,1)S(1)} %collective-permute-done.1.refs_0_.refs_1_, bf16[528,256]{1,0:T(8,128)(2,1)S(1)} %shard_map.46.refs_1_.refs_2_.refs_3_, bf16[528,256]{1,0:T(8,128)(2,1)S(1)} %shard_map.46.refs_1_.refs_2_.refs_3_, ...), custom_call_target="tpu_custom_call" | custom-call | tf_op jit(solution)/shard_map/pallas_call | solution.py:176
  28.3 2.3 %collective-permute-done.7 = f32[8,128]{1,0:T(8,128)S(1)} collective-permute-done((f32[8,128]{1,0:T(8,128)S(1)}, f32[8,128]{1,0:T(8,128)S(1)}, u32[]{:S(2)}, u32[]{:S(2)}) %collective-permute-start.7) | collective-permute-done | bytes 4128 | tf_op jit(solution)/shard_map/ppermute | solution.py:205
  30.6 0.5 %collective-permute-done.9 = f32[4,128]{1,0:T(4,128)S(1)} collective-permute-done((f32[4,128]{1,0:T(4,128)S(1)}, f32[4,128]{1,0:T(4,128)S(1)}, u32[]{:S(2)}, u32[]{:S(2)}) %collective-permute-start.9) | collective-permute-done | bytes 2080 | tf_op jit(solution)/shard_map/ppermute | solution.py:219
  31.1 0.7 %collective-permute-done.8 = f32[4,128]{1,0:T(4,128)S(1)} collective-permute-done((f32[4,128]{1,0:T(4,128)S(1)}, f32[4,128]{1,0:T(4,128)S(1)}, u32[]{:S(2)}, u32[]{:S(2)}) %collective-permute-start.8) | collective-permute-done | bytes 2080 | tf_op jit(solution)/shard_map/ppermute | solution.py:205
  31.7 0.6 %maximum_bitcast_fusion = f32[512]{0:T(512)} fusion(f32[4,128]{1,0:T(4,128)S(1)} %collective-permute-done.9, f32[4,128]{1,0:T(4,128)S(1)} %collective-permute-done.8, f32[8,128]{1,0:T(8,128)S(1)} %max.15), kind=kLoop, calls=%fused_computation | loop fusion | flops 1536 | bytes 8192 | tf_op jit(solution)/shard_map/reshape | solution.py:231
  (6 shorter events, 0.0 us)
Async XLA Ops:
  4.5 9.5 %collective-permute-start.3 = (bf16[528,256]{1,0:T(8,128)(2,1)S(1)}, bf16[528,256]{1,0:T(8,128)(2,1)S(1)}, u32[]{:S(2)}, u32[]{:S(2)}) collective-permute-start(bf16[528,256]{1,0:T(8,128)(2,1)S(1)} %shard_map.46.refs_1_.refs_2_.refs_3_), channel_id=1, source_target_pairs={{0,2},{1,3},{2,0},{3,1},{4,6},{5,7},{6,4},{7,5},{8,10},{9,11},{10,... | collective-permute-start | bytes 811016 | tf_op jit(solution)/shard_map/ppermute | solution.py:205
  7.5 7.2 %collective-permute-start.2 = (bf16[528,256]{1,0:T(8,128)(2,1)S(1)}, bf16[528,256]{1,0:T(8,128)(2,1)S(1)}, u32[]{:S(2)}, u32[]{:S(2)}) collective-permute-start(bf16[528,256]{1,0:T(8,128)(2,1)S(1)} %shard_map.46.refs_1_.refs_2_.refs_3_), channel_id=1, source_target_pairs={{0,1},{1,0},{2,3},{3,2},{4,5},{5,4},{6,7},{7,6},{8,9},{9,8},{10,11... | collective-permute-start | bytes 811016 | tf_op jit(solution)/shard_map/ppermute | solution.py:205
  7.5 11.3 %collective-permute-start = (bf16[528,256]{1,0:T(8,128)(2,1)S(1)}, bf16[528,256]{1,0:T(8,128)(2,1)S(1)}, u32[]{:S(2)}, u32[]{:S(2)}) collective-permute-start(bf16[528,256]{1,0:T(8,128)(2,1)S(1)} %shard_map.46.refs_1_.refs_2_.refs_3_), channel_id=1, source_target_pairs={{0,8},{12,4},{1,9},{13,5},{2,10},{14,6},{3,11},{15,7},{16,24},{28,... | collective-permute-start | bytes 811016 | tf_op jit(solution)/shard_map/ppermute | solution.py:215
  12.0 14.0 %collective-permute-start.1 = (bf16[528,256]{1,0:T(8,128)(2,1)S(1)}, bf16[528,256]{1,0:T(8,128)(2,1)S(1)}, u32[]{:S(2)}, u32[]{:S(2)}) collective-permute-start(bf16[528,256]{1,0:T(8,128)(2,1)S(1)} %shard_map.46.refs_1_.refs_2_.refs_3_), channel_id=1, source_target_pairs={{0,4},{4,8},{8,12},{12,0},{1,5},{5,9},{9,13},{13,1},{2,6},{6,10},{... | collective-permute-start | bytes 811016 | tf_op jit(solution)/shard_map/ppermute | solution.py:215
  14.0 4.8 %collective-permute-start.5 = (bf16[272,256]{1,0:T(8,128)(2,1)S(1)}, bf16[272,256]{1,0:T(8,128)(2,1)S(1)}, u32[]{:S(2)}, u32[]{:S(2)}) collective-permute-start(bf16[272,256]{1,0:T(8,128)(2,1)S(1)} %slice.17), channel_id=1, source_target_pairs={{0,1},{1,0},{2,3},{3,2},{4,5},{5,4},{6,7},{7,6},{8,9},{9,8},{10,11... | collective-permute-start | bytes 417800 | tf_op jit(solution)/shard_map/ppermute | solution.py:205
  14.1 4.7 %collective-permute-start.4 = (bf16[256,256]{1,0:T(8,128)(2,1)S(1)}, bf16[256,256]{1,0:T(8,128)(2,1)S(1)}, u32[]{:S(2)}, u32[]{:S(2)}) collective-permute-start(bf16[256,256]{1,0:T(8,128)(2,1)S(1)} %slice.16), channel_id=1, source_target_pairs={{0,1},{1,0},{2,3},{3,2},{4,5},{5,4},{6,7},{7,6},{8,9},{9,8},{10,11... | collective-permute-start | bytes 393224 | tf_op jit(solution)/shard_map/ppermute | solution.py:205
  19.7 7.8 %collective-permute-start.6 = (f32[4,128]{1,0:T(4,128)S(1)}, f32[4,128]{1,0:T(4,128)S(1)}, u32[]{:S(2)}, u32[]{:S(2)}) collective-permute-start(f32[4,128]{1,0:T(4,128)S(1)} %get-tuple-element.14), channel_id=1, source_target_pairs={{8,0},{4,12},{9,1},{5,13},{10,2},{6,14},{11,3},{7,15},{24,16},{20,... | collective-permute-start | bytes 6152 | tf_op jit(solution)/shard_map/ppermute | solution.py:219
  26.9 3.7 %collective-permute-start.7 = (f32[8,128]{1,0:T(8,128)S(1)}, f32[8,128]{1,0:T(8,128)S(1)}, u32[]{:S(2)}, u32[]{:S(2)}) collective-permute-start(f32[8,128]{1,0:T(8,128)S(1)} %get-tuple-element.15), channel_id=1, source_target_pairs={{0,2},{1,3},{2,0},{3,1},{4,6},{5,7},{6,4},{7,5},{8,10},{9,11},{10,... | collective-permute-start | bytes 12296 | tf_op jit(solution)/shard_map/ppermute | solution.py:205
  27.5 3.6 %collective-permute-start.9 = (f32[4,128]{1,0:T(4,128)S(1)}, f32[4,128]{1,0:T(4,128)S(1)}, u32[]{:S(2)}, u32[]{:S(2)}) collective-permute-start(f32[4,128]{1,0:T(4,128)S(1)} %get-tuple-element.16), channel_id=1, source_target_pairs={{4,0},{8,4},{12,8},{0,12},{5,1},{9,5},{13,9},{1,13},{6,2},{10,6},{... | collective-permute-start | bytes 6152 | tf_op jit(solution)/shard_map/ppermute | solution.py:219
  30.6 1.2 %collective-permute-start.8 = (f32[4,128]{1,0:T(4,128)S(1)}, f32[4,128]{1,0:T(4,128)S(1)}, u32[]{:S(2)}, u32[]{:S(2)}) collective-permute-start(f32[4,128]{1,0:T(4,128)S(1)} %slice.15), channel_id=1, source_target_pairs={{0,1},{1,0},{2,3},{3,2},{4,5},{5,4},{6,7},{7,6},{8,9},{9,8},{10,11... | collective-permute-start | bytes 6152 | tf_op jit(solution)/shard_map/ppermute | solution.py:205

commit v7 on v6

v7 whole, which is shorter than its diff:
```python
import functools

import jax
import jax.numpy as jnp
from jax import lax
from jax.experimental import pallas as pl
from jax.experimental.pallas import tpu as pltpu
from jax.sharding import PartitionSpec as P

CPO = 8
LANES = 128
TAG_ROWS = 16
ABSENT = -2.0
BASIS_STEPS = 4
ROW_STEPS = 4
PARTS = 2
VMEM_LIMIT = 48 * 1024 * 1024


def project_kernel(source_hbm, basis_hbm, owner_hbm, sub_hbm, packed_ref, *scratch):
    source, basis, owner, sub, basis_sems, source_sems, tag_sems = scratch
    row_count, depth = source.shape
    width = basis.shape[1]
    basis_copies = [
        pltpu.make_async_copy(basis_hbm.at[span, :], basis.at[span, :], basis_sems.at[step])
        for step, span in enumerate(cut(depth, BASIS_STEPS))
    ]
    source_copies = [
        pltpu.make_async_copy(source_hbm.at[span, :], source.at[span, :], source_sems.at[step])
        for step, span in enumerate(cut(row_count, ROW_STEPS))
    ]
    tag_copies = [
        pltpu.make_async_copy(owner_hbm, owner, tag_sems.at[0]),
        pltpu.make_async_copy(sub_hbm, sub, tag_sems.at[1]),
    ]
    for copy in basis_copies + source_copies + tag_copies:
        copy.start()
    for copy in basis_copies:
        copy.wait()
    for copy, span in zip(source_copies, cut(row_count, ROW_STEPS)):
        copy.wait()
        projected = jnp.dot(source[span, :], basis[...], preferred_element_type=jnp.float32)
        norms = jnp.sum(projected * projected, axis=1, keepdims=True)
        packed_ref[span, :] = (projected * lax.rsqrt(norms + 1e-06)).astype(jnp.bfloat16)
    for copy in tag_copies:
        copy.wait()
    tags = (owner[...] * CPO + sub[...] + 1).astype(jnp.float32)
    tags = jnp.concatenate(
        [tags, jnp.zeros((TAG_ROWS - tags.shape[0], LANES), jnp.float32)], axis=0
    )
    tags = jnp.concatenate([tags, jnp.zeros((TAG_ROWS, width - LANES), jnp.float32)], axis=1)
    packed_ref[row_count:, :] = tags.astype(jnp.bfloat16)


def cut(size, steps):
    return [pl.ds(size // steps * step, size // steps) for step in range(steps)]


def project(embeddings, basis, owner_ids, sub_cluster):
    row_count, depth = embeddings.shape
    width = basis.shape[1]
    tag_shape = (row_count // LANES, LANES)
    return pl.pallas_call(
        project_kernel,
        in_specs=[pl.BlockSpec(memory_space=pltpu.HBM)] * 4,
        out_specs=pl.BlockSpec(memory_space=pltpu.VMEM),
        out_shape=jax.ShapeDtypeStruct((row_count + TAG_ROWS, width), jnp.bfloat16),
        scratch_shapes=[
            pltpu.VMEM((row_count, depth), jnp.bfloat16),
            pltpu.VMEM((depth, width), jnp.bfloat16),
            pltpu.VMEM(tag_shape, jnp.int32),
            pltpu.VMEM(tag_shape, jnp.int32),
            pltpu.SemaphoreType.DMA((BASIS_STEPS,)),
            pltpu.SemaphoreType.DMA((ROW_STEPS,)),
            pltpu.SemaphoreType.DMA((2,)),
        ],
        compiler_params=pltpu.CompilerParams(vmem_limit_bytes=VMEM_LIMIT),
        cost_estimate=pl.CostEstimate(
            flops=2 * row_count * depth * width,
            bytes_accessed=2 * depth * (row_count + width),
            transcendentals=0,
        ),
    )(
        *[
            pltpu.with_memory_space_constraint(array, pltpu.HBM)
            for array in (
                embeddings,
                basis,
                owner_ids.reshape(tag_shape),
                sub_cluster.reshape(tag_shape),
            )
        ]
    )


def score_kernel(row_parts, bases, want_cols, own_first, unread, *refs):
    refs = list(refs[unread:])
    key_ref = refs.pop(0)
    row_refs = [[refs.pop(0) for _ in range(parts)] for parts in row_parts]
    base_refs = [refs.pop(0) for _ in range(bases)]
    col_out = refs.pop(0) if want_cols else None
    row_outs = refs
    row_count = key_ref.shape[0] - TAG_ROWS
    tiles = row_count // LANES
    key_tags = key_ref[row_count:, :LANES].astype(jnp.float32)
    best = [jnp.full((8, LANES), ABSENT, jnp.float32) for _ in range(tiles)]
    for block, part_refs in enumerate(row_refs):
        tag_ref = part_refs[-1]
        row_tags = tag_ref[tag_ref.shape[0] - TAG_ROWS :, :LANES].astype(jnp.float32)
        place = 0
        for part_ref in part_refs:
            count = part_ref.shape[0] - (TAG_ROWS if part_ref is tag_ref else 0)
            scores = lax.dot_general(
                part_ref[:count, :],
                key_ref[:row_count, :],
                (((1,), (1,)), ((), ())),
                preferred_element_type=jnp.float32,
            )
            for start in range(0, count, LANES):
                tags = jnp.broadcast_to(row_tags[place : place + 1, :], (LANES, LANES)).T
                across = None
                for at in range(tiles):
                    same = tags == key_tags[at : at + 1, :]
                    if own_first and block == 0 and at == place:
                        same = same & (
                            lax.broadcasted_iota(jnp.int32, (LANES, LANES), 0)
                            != lax.broadcasted_iota(jnp.int32, (LANES, LANES), 1)
                        )
                    kept = scores[start : start + LANES, at * LANES : (at + 1) * LANES]
                    kept = jnp.where(same, kept, ABSENT)
                    if want_cols:
                        best[at] = jnp.maximum(
                            best[at], jnp.max(kept.reshape(LANES // 8, 8, LANES), axis=0)
                        )
                    if row_outs:
                        across = kept if across is None else jnp.maximum(across, kept)
                if row_outs:
                    found = jnp.max(across.T, axis=0, keepdims=True)
                    if base_refs:
                        found = jnp.maximum(found, base_refs[block][place : place + 1, :])
                    row_outs[block][place : place + 1, :] = found
                place += 1
    if want_cols:
        for at in range(tiles):
            col_out[at : at + 1, :] = jnp.max(best[at], axis=0, keepdims=True)


def score(key, rows, bases=(), want_cols=True, want_rows=True, own_first=False, after=()):
    best = jax.ShapeDtypeStruct(((key.shape[0] - TAG_ROWS) // LANES, LANES), jnp.float32)
    parts = [row if isinstance(row, tuple) else (row,) for row in rows]
    blocks = [part for row in parts for part in row]
    out_shape = [best] * (want_cols + want_rows * len(rows))
    whole = pl.BlockSpec(memory_space=pltpu.VMEM)
    found = pl.pallas_call(
        functools.partial(
            score_kernel,
            [len(row) for row in parts],
            len(bases),
            want_cols,
            own_first,
            len(after),
        ),
        in_specs=[pl.BlockSpec(memory_space=pl.ANY)] * len(after)
        + [whole] * (1 + len(blocks) + len(bases)),
        out_specs=[whole] * len(out_shape),
        out_shape=out_shape,
        compiler_params=pltpu.CompilerParams(vmem_limit_bytes=VMEM_LIMIT),
        cost_estimate=pl.CostEstimate(flops=0, bytes_accessed=0, transcendentals=0),
    )(*after, key, *blocks, *bases)
    return list(found[:want_cols]), list(found[want_cols:])


def owner_steps(count):
    half = count // 2
    circle = [count - 1 - 2 * i for i in range(half)] + [count - 2 - 2 * i for i in range(half)]
    return [
        [(circle[i], circle[(i + step) % count]) for i in range(count)]
        for step in range(1, half + 1)
    ]


def per_device(embeddings, basis, owner_ids, sub_cluster):
    row_count = embeddings.shape[0]
    split_count, owner_count = lax.axis_size("split"), lax.axis_size("owners")

    def swap(block, offset):
        return lax.ppermute(block, "split", [(s, s ^ offset) for s in range(split_count)])

    own = project(embeddings, basis, owner_ids, sub_cluster)
    rows = [own, swap(own, 1)]
    for offset in range(2, split_count, 2):
        beside = swap(own, offset)
        part = row_count // PARTS
        ends = [part * at for at in range(1, PARTS)] + [row_count + TAG_ROWS]
        rows += [beside, tuple(swap(beside[a:b], 1) for a, b in zip([0] + ends, ends))]
    *steps, last = owner_steps(owner_count)
    keys = [lax.ppermute(own, "owners", step) for step in steps]
    nearby = lax.ppermute(own, "owners", last)
    _, row_best = score(nearby, rows, want_cols=False)
    backs = []
    for key, step in zip(keys, steps):
        (found,), row_best = score(key, rows, row_best)
        backs.append(lax.ppermute(found, "owners", [(b, a) for a, b in step]))
    backs += [swap(found, offset) for offset, found in enumerate(row_best) if offset]
    (alone,), _ = score(own, rows, want_rows=False, own_first=True, after=[*keys, nearby])
    best = jnp.maximum(row_best[0], alone)
    for back in backs:
        best = jnp.maximum(best, back)
    return jnp.maximum(best, -1.0).reshape(row_count)


def solution(mesh):
    placed = (
        P(("groups", "owners", "split"), None),
        P(),
        P(("groups", "owners", "split"), None),
        P(("groups", "owners", "split")),
    )
    return jax.shard_map(
        per_device,
        mesh=mesh,
        in_specs=placed,
        out_specs=P(("groups", "owners", "split")),
        check_vma=False,
    )
```

time: 32.5 us -> 32.7 us (level)
  waiting for transfers between devices: 14.6 us -> 12.5 us
  Pallas kernels: 6.95 us -> 8.11 us
  starting transfers between devices: 10.1 us -> 11.2 us
    ppermute x2, waiting for transfers between devices: 0.5 us -> 8.55 us  [the longest x1 7.42 us: per_device(): nearby = lax.ppermute(own, 'owners', last)]
    ppermute x2 -> x1, waiting for transfers between devices: 9.2 us -> 1.52 us  [per_device(): keys = [lax.ppermute(own, 'owners', step) for step in steps]]
    ppermute x6 -> x7, waiting for transfers between devices: 4.86 us -> 2.44 us  [swap(): lax.ppermute(block, 'split', [(s, s ^ offset) for s in range(split_count)])]
    ppermute x2 -> x1, starting transfers between devices: 4.56 us -> 2.47 us  [per_device(): keys = [lax.ppermute(own, 'owners', step) for step in steps]]
    ppermute x2, starting transfers between devices: 1.29 us -> 3.26 us  [the longest x1 1.68 us: per_device(): backs.append(lax.ppermute(found, 'owners', [(b, a) for a, b in step]))]
    ppermute x6 -> x7, starting transfers between devices: 4.24 us -> 5.49 us  [swap(): lax.ppermute(block, 'split', [(s, s ^ offset) for s in range(split_count)])]
    pallas_call x1, Pallas kernels: 4.52 us -> 5.68 us  [project(): pl.pallas_call(project_kernel, in_specs=[pl.BlockSpec(memory_space=pltpu....]
  transfers between devices with their start and end apart: 10 -> 10, of which waited for: 6 -> 4; matrix products, arithmetic and copies ran while one was open for 0% -> 0% of each run, Pallas kernels for 8% -> 5%
where the time goes in v7:
time: 32.7 us; the launch traced here: 32.5 us
  waiting for transfers between devices  12.5 us (38%)
  starting transfers between devices  11.2 us (34%)
  Pallas kernels  8.11 us (25%)
  other arithmetic  0.59 us (2%)
    ppermute x1, waiting for transfers between devices, per_device(): nearby = lax.ppermute(own, 'owners', last)  7.42 us
    pallas_call x1, Pallas kernels, project(): pl.pallas_call(project_kernel, in_specs=[pl.BlockSpec(memory_space=pltpu....  5.68 us
    ppermute x7, starting transfers between devices, swap(): lax.ppermute(block, 'split', [(s, s ^ offset) for s in range(split_count)])  5.49 us
    ppermute x1, starting transfers between devices, per_device(): keys = [lax.ppermute(own, 'owners', step) for step in steps]  2.47 us
    ppermute x7, waiting for transfers between devices, swap(): lax.ppermute(block, 'split', [(s, s ^ offset) for s in range(split_count)])  2.44 us
    pallas_call x3, Pallas kernels, score(): pl.pallas_call(functools.partial(score_kernel, [len(row) for row in parts...  2.44 us
    ppermute x1, starting transfers between devices, per_device(): backs.append(lax.ppermute(found, 'owners', [(b, a) for a, b in step]))  1.68 us
    ppermute x1, starting transfers between devices, per_device(): nearby = lax.ppermute(own, 'owners', last)  1.58 us
  transfers between devices with their start and end apart: 10, of which 4 were waited for; matrix products, arithmetic and copies ran while one was open for 0% of the time, Pallas kernels for 5%

profile of v7, /device:TPU:0, one launch (start us, length us, event | category | flops | bytes accessed | tf_op | source)
XLA Modules:
  0.0 32.5 jit_solution(10464984225205144557)
XLA Ops:
  0.0 5.7 %shard_map.46.refs_1_.refs_2_.refs_3_ = bf16[528,256]{1,0:T(8,128)(2,1)S(1)} custom-call(bf16[512,4096]{1,0:T(8,128)(2,1)} %source_hbm.1, bf16[4096,256]{1,0:T(8,128)(2,1)} %basis_hbm.1, s32[4,128]{1,0:T(4,128)} %bitcast.4, s32[4,128]{1,0:T(4,128)} %bitcast.5), custom_call_target="tpu_custom_call" | custom-call | flops 1073741824 | bytes 6291456 | tf_op jit(solution)/shard_map/pallas_call | solution.py:63
  5.7 3.0 %collective-permute-start.2 = (bf16[528,256]{1,0:T(8,128)(2,1)S(1)}, bf16[528,256]{1,0:T(8,128)(2,1)S(1)}, u32[]{:S(2)}, u32[]{:S(2)}) collective-permute-start(bf16[528,256]{1,0:T(8,128)(2,1)S(1)} %shard_map.46.refs_1_.refs_2_.refs_3_), channel_id=1, source_target_pairs={{0,2},{1,3},{2,0},{3,1},{4,6},{5,7},{6,4},{7,5},{8,10},{9,11},{10,... | collective-permute-start | bytes 811016 | tf_op jit(solution)/shard_map/ppermute | solution.py:187
  8.7 0.0 collective-permute-start.1
  8.7 1.6 %collective-permute-start.5 = (bf16[528,256]{1,0:T(8,128)(2,1)S(1)}, bf16[528,256]{1,0:T(8,128)(2,1)S(1)}, u32[]{:S(2)}, u32[]{:S(2)}) collective-permute-start(bf16[528,256]{1,0:T(8,128)(2,1)S(1)} %shard_map.46.refs_1_.refs_2_.refs_3_), channel_id=1, source_target_pairs={{12,8},{4,0},{8,12},{0,4},{13,9},{5,1},{9,13},{1,5},{14,10},{6,2},... | collective-permute-start | bytes 811016 | tf_op jit(solution)/shard_map/ppermute | solution.py:198
  10.3 2.5 %collective-permute-start = (bf16[528,256]{1,0:T(8,128)(2,1)S(1)}, bf16[528,256]{1,0:T(8,128)(2,1)S(1)}, u32[]{:S(2)}, u32[]{:S(2)}) collective-permute-start(bf16[528,256]{1,0:T(8,128)(2,1)S(1)} %shard_map.46.refs_1_.refs_2_.refs_3_), channel_id=1, source_target_pairs={{12,4},{4,8},{8,0},{0,12},{13,5},{5,9},{9,1},{1,13},{14,6},{6,10},... | collective-permute-start | bytes 811016 | tf_op jit(solution)/shard_map/ppermute | solution.py:197
  12.7 2.4 %collective-permute-done.2.refs_3_.refs_5_ = bf16[528,256]{1,0:T(8,128)(2,1)S(1)} collective-permute-done((bf16[528,256]{1,0:T(8,128)(2,1)S(1)}, bf16[528,256]{1,0:T(8,128)(2,1)S(1)}, u32[]{:S(2)}, u32[]{:S(2)}) %collective-permute-start.2) | collective-permute-done | bytes 270368 | tf_op jit(solution)/shard_map/ppermute | solution.py:187
  15.2 0.1 collective-permute-start.4
  15.3 0.6 %collective-permute-start.3 = (bf16[256,256]{1,0:T(8,128)(2,1)S(1)}, bf16[256,256]{1,0:T(8,128)(2,1)S(1)}, u32[]{:S(2)}, u32[]{:S(2)}) collective-permute-start(bf16[256,256]{1,0:T(8,128)(2,1)S(1)} %slice.8), channel_id=1, source_target_pairs={{0,1},{1,0},{2,3},{3,2},{4,5},{5,4},{6,7},{7,6},{8,9},{9,8},{10,11... | collective-permute-start | bytes 393224 | tf_op jit(solution)/shard_map/ppermute | solution.py:187
  15.8 0.0 collective-permute-done.1.refs_2_.refs_4_
  15.8 7.4 %collective-permute-done.5.refs_0_.refs_1_ = bf16[528,256]{1,0:T(8,128)(2,1)S(1)} collective-permute-done((bf16[528,256]{1,0:T(8,128)(2,1)S(1)}, bf16[528,256]{1,0:T(8,128)(2,1)S(1)}, u32[]{:S(2)}, u32[]{:S(2)}) %collective-permute-start.5) | collective-permute-done | bytes 270368 | tf_op jit(solution)/shard_map/ppermute | solution.py:198
  23.3 0.0 collective-permute-done.3.refs_4_.refs_6_
  23.3 0.0 collective-permute-done.4.refs_5_.refs_7_
  23.3 0.8 %shard_map.47 = (f32[4,128]{1,0:T(4,128)S(1)}, f32[4,128]{1,0:T(4,128)S(1)}, f32[4,128]{1,0:T(4,128)S(1)}, f32[4,128]{1,0:T(4,128)S(1)}) custom-call(bf16[528,256]{1,0:T(8,128)(2,1)S(1)} %collective-permute-done.5.refs_0_.refs_1_, bf16[528,256]{1,0:T(8,128)(2,1)S(1)} %shard_map.46.refs_1_.refs_2_.refs_3_, ...), custom_call_target="tpu_custom_call" | custom-call | tf_op jit(solution)/shard_map/pallas_call | solution.py:154
  24.1 1.5 %collective-permute-done.refs_0_ = bf16[528,256]{1,0:T(8,128)(2,1)S(1)} collective-permute-done((bf16[528,256]{1,0:T(8,128)(2,1)S(1)}, bf16[528,256]{1,0:T(8,128)(2,1)S(1)}, u32[]{:S(2)}, u32[]{:S(2)}) %collective-permute-start) | collective-permute-done | bytes 270368 | tf_op jit(solution)/shard_map/ppermute | solution.py:197
  25.6 0.9 %shard_map.48 = (f32[4,128]{1,0:T(4,128)S(1)}, f32[4,128]{1,0:T(4,128)S(1)}, f32[4,128]{1,0:T(4,128)S(1)}, f32[4,128]{1,0:T(4,128)S(1)}, f32[4,128]{1,0:T(4,128)S(1)}) custom-call(bf16[528,256]{1,0:T(8,128)(2,1)S(1)} %collective-permute-done.refs_0_, bf16[528,256]{1,0:T(8,128)(2,1)S(1)} %shard_map.46.refs_1_.refs_2_.refs_3_, ...), custom_call_target="tpu_custom_call" | custom-call | tf_op jit(solution)/shard_map/pallas_call | solution.py:154
  26.5 1.7 %collective-permute-start.6 = (f32[4,128]{1,0:T(4,128)S(1)}, f32[4,128]{1,0:T(4,128)S(1)}, u32[]{:S(2)}, u32[]{:S(2)}) collective-permute-start(f32[4,128]{1,0:T(4,128)S(1)} %get-tuple-element.19), channel_id=1, source_target_pairs={{4,12},{8,4},{0,8},{12,0},{5,13},{9,5},{1,9},{13,1},{6,14},{10,6},... | collective-permute-start | bytes 6152 | tf_op jit(solution)/shard_map/ppermute | solution.py:203
  28.2 0.0 collective-permute-start.7
  28.2 0.5 %collective-permute-start.8 = (f32[4,128]{1,0:T(4,128)S(1)}, f32[4,128]{1,0:T(4,128)S(1)}, u32[]{:S(2)}, u32[]{:S(2)}) collective-permute-start(f32[4,128]{1,0:T(4,128)S(1)} %get-tuple-element.21), channel_id=1, source_target_pairs={{0,2},{1,3},{2,0},{3,1},{4,6},{5,7},{6,4},{7,5},{8,10},{9,11},{10,... | collective-permute-start | bytes 6152 | tf_op jit(solution)/shard_map/ppermute | solution.py:187
  28.7 1.3 %collective-permute-start.9 = (f32[4,128]{1,0:T(4,128)S(1)}, f32[4,128]{1,0:T(4,128)S(1)}, u32[]{:S(2)}, u32[]{:S(2)}) collective-permute-start(f32[4,128]{1,0:T(4,128)S(1)} %get-tuple-element.22), channel_id=1, source_target_pairs={{0,3},{1,2},{2,1},{3,0},{4,7},{5,6},{6,5},{7,4},{8,11},{9,10},{10,... | collective-permute-start | bytes 6152 | tf_op jit(solution)/shard_map/ppermute | solution.py:187
  30.0 0.8 %shard_map.49 = f32[4,128]{1,0:T(4,128)S(1)} custom-call(bf16[528,256]{1,0:T(8,128)(2,1)S(1)} %collective-permute-done.refs_0_, bf16[528,256]{1,0:T(8,128)(2,1)S(1)} %collective-permute-done.5.refs_0_.refs_1_, bf16[528,256]{1,0:T(8,128)(2,1)S(1)} %shard_map.46.refs_1_.refs_2_.refs_3_, bf16[528,256]{1,0:T(8,128)(2,1)S(1)} %shard_map.46.refs_1_.refs_2_.refs_3_, ...), custom_call_target="tpu_custom_call" | custom-call | tf_op jit(solution)/shard_map/pallas_call | solution.py:154
  30.8 1.1 %collective-permute-done.6 = f32[4,128]{1,0:T(4,128)S(1)} collective-permute-done((f32[4,128]{1,0:T(4,128)S(1)}, f32[4,128]{1,0:T(4,128)S(1)}, u32[]{:S(2)}, u32[]{:S(2)}) %collective-permute-start.6) | collective-permute-done | bytes 2080 | tf_op jit(solution)/shard_map/ppermute | solution.py:203
  31.9 0.0 collective-permute-done.7
  31.9 0.0 collective-permute-done.9
  31.9 0.6 %maximum_bitcast_fusion = f32[512]{0:T(512)} fusion(f32[4,128]{1,0:T(4,128)S(1)} %collective-permute-done.9, f32[4,128]{1,0:T(4,128)S(1)} %collective-permute-done.8, f32[4,128]{1,0:T(4,128)S(1)} %collective-permute-done.7, f32[4,128]{1,0:T(4,128)S(1)} %collective-permute-done.6, f32[4,128]{1,0:T(4,128)S(1)} %get-tuple-element.18, f32[4,128]{1,0:T(4,128)S(1)} %shard_map.49), kind=kLoop, calls=%fused_computation | loop fusion | flops 3072 | bytes 14336 | tf_op jit(solution)/shard_map/reshape | solution.py:209
  (3 shorter events, 0.0 us)
Async XLA Ops:
  5.7 9.5 %collective-permute-start.2 = (bf16[528,256]{1,0:T(8,128)(2,1)S(1)}, bf16[528,256]{1,0:T(8,128)(2,1)S(1)}, u32[]{:S(2)}, u32[]{:S(2)}) collective-permute-start(bf16[528,256]{1,0:T(8,128)(2,1)S(1)} %shard_map.46.refs_1_.refs_2_.refs_3_), channel_id=1, source_target_pairs={{0,2},{1,3},{2,0},{3,1},{4,6},{5,7},{6,4},{7,5},{8,10},{9,11},{10,... | collective-permute-start | bytes 811016 | tf_op jit(solution)/shard_map/ppermute | solution.py:187
  8.7 7.2 %collective-permute-start.1 = (bf16[528,256]{1,0:T(8,128)(2,1)S(1)}, bf16[528,256]{1,0:T(8,128)(2,1)S(1)}, u32[]{:S(2)}, u32[]{:S(2)}) collective-permute-start(bf16[528,256]{1,0:T(8,128)(2,1)S(1)} %shard_map.46.refs_1_.refs_2_.refs_3_), channel_id=1, source_target_pairs={{0,1},{1,0},{2,3},{3,2},{4,5},{5,4},{6,7},{7,6},{8,9},{9,8},{10,11... | collective-permute-start | bytes 811016 | tf_op jit(solution)/shard_map/ppermute | solution.py:187
  8.7 14.6 %collective-permute-start.5 = (bf16[528,256]{1,0:T(8,128)(2,1)S(1)}, bf16[528,256]{1,0:T(8,128)(2,1)S(1)}, u32[]{:S(2)}, u32[]{:S(2)}) collective-permute-start(bf16[528,256]{1,0:T(8,128)(2,1)S(1)} %shard_map.46.refs_1_.refs_2_.refs_3_), channel_id=1, source_target_pairs={{12,8},{4,0},{8,12},{0,4},{13,9},{5,1},{9,13},{1,5},{14,10},{6,2},... | collective-permute-start | bytes 811016 | tf_op jit(solution)/shard_map/ppermute | solution.py:198
  10.3 15.4 %collective-permute-start = (bf16[528,256]{1,0:T(8,128)(2,1)S(1)}, bf16[528,256]{1,0:T(8,128)(2,1)S(1)}, u32[]{:S(2)}, u32[]{:S(2)}) collective-permute-start(bf16[528,256]{1,0:T(8,128)(2,1)S(1)} %shard_map.46.refs_1_.refs_2_.refs_3_), channel_id=1, source_target_pairs={{12,4},{4,8},{8,0},{0,12},{13,5},{5,9},{9,1},{1,13},{14,6},{6,10},... | collective-permute-start | bytes 811016 | tf_op jit(solution)/shard_map/ppermute | solution.py:197
  15.2 8.1 %collective-permute-start.4 = (bf16[272,256]{1,0:T(8,128)(2,1)S(1)}, bf16[272,256]{1,0:T(8,128)(2,1)S(1)}, u32[]{:S(2)}, u32[]{:S(2)}) collective-permute-start(bf16[272,256]{1,0:T(8,128)(2,1)S(1)} %slice.9), channel_id=1, source_target_pairs={{0,1},{1,0},{2,3},{3,2},{4,5},{5,4},{6,7},{7,6},{8,9},{9,8},{10,11... | collective-permute-start | bytes 417800 | tf_op jit(solution)/shard_map/ppermute | solution.py:187
  15.3 8.0 %collective-permute-start.3 = (bf16[256,256]{1,0:T(8,128)(2,1)S(1)}, bf16[256,256]{1,0:T(8,128)(2,1)S(1)}, u32[]{:S(2)}, u32[]{:S(2)}) collective-permute-start(bf16[256,256]{1,0:T(8,128)(2,1)S(1)} %slice.8), channel_id=1, source_target_pairs={{0,1},{1,0},{2,3},{3,2},{4,5},{5,4},{6,7},{7,6},{8,9},{9,8},{10,11... | collective-permute-start | bytes 393224 | tf_op jit(solution)/shard_map/ppermute | solution.py:187
  26.5 5.4 %collective-permute-start.6 = (f32[4,128]{1,0:T(4,128)S(1)}, f32[4,128]{1,0:T(4,128)S(1)}, u32[]{:S(2)}, u32[]{:S(2)}) collective-permute-start(f32[4,128]{1,0:T(4,128)S(1)} %get-tuple-element.19), channel_id=1, source_target_pairs={{4,12},{8,4},{0,8},{12,0},{5,13},{9,5},{1,9},{13,1},{6,14},{10,6},... | collective-permute-start | bytes 6152 | tf_op jit(solution)/shard_map/ppermute | solution.py:203
  28.2 3.8 %collective-permute-start.7 = (f32[4,128]{1,0:T(4,128)S(1)}, f32[4,128]{1,0:T(4,128)S(1)}, u32[]{:S(2)}, u32[]{:S(2)}) collective-permute-start(f32[4,128]{1,0:T(4,128)S(1)} %get-tuple-element.20), channel_id=1, source_target_pairs={{0,1},{1,0},{2,3},{3,2},{4,5},{5,4},{6,7},{7,6},{8,9},{9,8},{10,11... | collective-permute-start | bytes 6152 | tf_op jit(solution)/shard_map/ppermute | solution.py:187
  28.2 3.8 %collective-permute-start.8 = (f32[4,128]{1,0:T(4,128)S(1)}, f32[4,128]{1,0:T(4,128)S(1)}, u32[]{:S(2)}, u32[]{:S(2)}) collective-permute-start(f32[4,128]{1,0:T(4,128)S(1)} %get-tuple-element.21), channel_id=1, source_target_pairs={{0,2},{1,3},{2,0},{3,1},{4,6},{5,7},{6,4},{7,5},{8,10},{9,11},{10,... | collective-permute-start | bytes 6152 | tf_op jit(solution)/shard_map/ppermute | solution.py:187
  28.7 3.2 %collective-permute-start.9 = (f32[4,128]{1,0:T(4,128)S(1)}, f32[4,128]{1,0:T(4,128)S(1)}, u32[]{:S(2)}, u32[]{:S(2)}) collective-permute-start(f32[4,128]{1,0:T(4,128)S(1)} %get-tuple-element.22), channel_id=1, source_target_pairs={{0,3},{1,2},{2,1},{3,0},{4,7},{5,6},{6,5},{7,4},{8,11},{9,10},{10,... | collective-permute-start | bytes 6152 | tf_op jit(solution)/shard_map/ppermute | solution.py:187

commit v8 on v7

v8 whole, which is shorter than its diff:
```python
import functools

import jax
import jax.numpy as jnp
from jax import lax
from jax.experimental import pallas as pl
from jax.experimental.pallas import tpu as pltpu
from jax.sharding import PartitionSpec as P

CPO = 8
LANES = 128
TAG_ROWS = 16
ABSENT = -2.0
STEPS = 8
ROW_PARTS = 2
VMEM_LIMIT = 48 * 1024 * 1024


def project_kernel(source_hbm, basis_hbm, owner_hbm, sub_hbm, packed_ref, *scratch):
    source, basis, owner, sub, sems, tag_sems = scratch
    row_count, depth = source.shape
    width = basis.shape[1]
    spans = cut(depth, STEPS)
    copies = [
        (
            pltpu.make_async_copy(basis_hbm.at[span, :], basis.at[span, :], sems.at[0, step]),
            pltpu.make_async_copy(source_hbm.at[:, span], source.at[:, span], sems.at[1, step]),
        )
        for step, span in enumerate(spans)
    ]
    tag_copies = [
        pltpu.make_async_copy(owner_hbm, owner, tag_sems.at[0]),
        pltpu.make_async_copy(sub_hbm, sub, tag_sems.at[1]),
    ]
    for copy in [copy for pair in copies for copy in pair] + tag_copies:
        copy.start()
    totals = [None] * ROW_PARTS
    for span, pair in zip(spans, copies):
        for copy in pair:
            copy.wait()
        for at, rows in enumerate(cut(row_count, ROW_PARTS)):
            part = jnp.dot(source[rows, span], basis[span, :], preferred_element_type=jnp.float32)
            totals[at] = part if totals[at] is None else totals[at] + part
    for projected, rows in zip(totals, cut(row_count, ROW_PARTS)):
        norms = jnp.sum(projected * projected, axis=1, keepdims=True)
        packed_ref[rows, :] = (projected * lax.rsqrt(norms + 1e-06)).astype(jnp.bfloat16)
    for copy in tag_copies:
        copy.wait()
    tags = (owner[...] * CPO + sub[...] + 1).astype(jnp.float32)
    tags = jnp.concatenate(
        [tags, jnp.zeros((TAG_ROWS - tags.shape[0], LANES), jnp.float32)], axis=0
    )
    tags = jnp.concatenate([tags, jnp.zeros((TAG_ROWS, width - LANES), jnp.float32)], axis=1)
    packed_ref[row_count:, :] = tags.astype(jnp.bfloat16)


def cut(size, steps):
    return [pl.ds(size // steps * step, size // steps) for step in range(steps)]


def project(embeddings, basis, owner_ids, sub_cluster):
    row_count, depth = embeddings.shape
    width = basis.shape[1]
    tag_shape = (row_count // LANES, LANES)
    return pl.pallas_call(
        project_kernel,
        in_specs=[pl.BlockSpec(memory_space=pltpu.HBM)] * 4,
        out_specs=pl.BlockSpec(memory_space=pltpu.VMEM),
        out_shape=jax.ShapeDtypeStruct((row_count + TAG_ROWS, width), jnp.bfloat16),
        scratch_shapes=[
            pltpu.VMEM((row_count, depth), jnp.bfloat16),
            pltpu.VMEM((depth, width), jnp.bfloat16),
            pltpu.VMEM(tag_shape, jnp.int32),
            pltpu.VMEM(tag_shape, jnp.int32),
            pltpu.SemaphoreType.DMA((2, STEPS)),
            pltpu.SemaphoreType.DMA((2,)),
        ],
        compiler_params=pltpu.CompilerParams(vmem_limit_bytes=VMEM_LIMIT),
        cost_estimate=pl.CostEstimate(
            flops=2 * row_count * depth * width,
            bytes_accessed=2 * depth * (row_count + width),
            transcendentals=0,
        ),
    )(
        *[
            pltpu.with_memory_space_constraint(array, pltpu.HBM)
            for array in (
                embeddings,
                basis,
                owner_ids.reshape(tag_shape),
                sub_cluster.reshape(tag_shape),
            )
        ]
    )


def score_kernel(key_parts, row_parts, bases, want_cols, own_first, unread, *refs):
    refs = list(refs[unread:])
    key_refs = [refs.pop(0) for _ in range(key_parts)]
    row_refs = [[refs.pop(0) for _ in range(parts)] for parts in row_parts]
    base_refs = [refs.pop(0) for _ in range(bases)]
    col_out = refs.pop(0) if want_cols else None
    row_outs = refs
    key_tag_ref = key_refs[-1]
    key_tags = key_tag_ref[key_tag_ref.shape[0] - TAG_ROWS :, :LANES].astype(jnp.float32)
    tiles = sum(key_ref.shape[0] for key_ref in key_refs) // LANES
    best = [jnp.full((8, LANES), ABSENT, jnp.float32) for _ in range(tiles)]
    for block, part_refs in enumerate(row_refs):
        tag_ref = part_refs[-1]
        row_tags = tag_ref[tag_ref.shape[0] - TAG_ROWS :, :LANES].astype(jnp.float32)
        place = 0
        for part_ref in part_refs:
            count = part_ref.shape[0] // LANES * LANES
            scores = [
                lax.dot_general(
                    part_ref[:count, :],
                    key_ref[: key_ref.shape[0] // LANES * LANES, :],
                    (((1,), (1,)), ((), ())),
                    preferred_element_type=jnp.float32,
                )
                for key_ref in key_refs
            ]
            scores = [
                part[:, start : start + LANES]
                for part in scores
                for start in range(0, part.shape[1], LANES)
            ]
            for start in range(0, count, LANES):
                tags = jnp.broadcast_to(row_tags[place : place + 1, :], (LANES, LANES)).T
                across = None
                for at in range(tiles):
                    same = tags == key_tags[at : at + 1, :]
                    if own_first and block == 0 and at == place:
                        same = same & (
                            lax.broadcasted_iota(jnp.int32, (LANES, LANES), 0)
                            != lax.broadcasted_iota(jnp.int32, (LANES, LANES), 1)
                        )
                    kept = jnp.where(same, scores[at][start : start + LANES, :], ABSENT)
                    if want_cols or own_first:
                        best[at] = jnp.maximum(
                            best[at], jnp.max(kept.reshape(LANES // 8, 8, LANES), axis=0)
                        )
                    if not own_first:
                        across = kept if across is None else jnp.maximum(across, kept)
                if not own_first:
                    at = block % 2 * tiles + place
                    found = jnp.max(across.T, axis=0, keepdims=True)
                    if base_refs:
                        found = jnp.maximum(found, base_refs[block // 2][at : at + 1, :])
                    row_outs[block // 2][at : at + 1, :] = found
                place += 1
    for at in range(tiles):
        found = jnp.max(best[at], axis=0, keepdims=True)
        if want_cols:
            col_out[at : at + 1, :] = found
        if own_first:
            row_outs[0][at : at + 1, :] = jnp.maximum(found, base_refs[0][at : at + 1, :])
    if own_first:
        row_outs[0][tiles:, :] = base_refs[0][tiles:, :]


def score(key, rows, bases=(), want_cols=True, own_first=False, after=()):
    whole = lambda block: block if isinstance(block, tuple) else (block,)
    key, parts = whole(key), [whole(row) for row in rows]
    blocks = [part for row in parts for part in row]
    tiles = sum(part.shape[0] for part in key) // LANES
    best = jax.ShapeDtypeStruct((tiles, LANES), jnp.float32)
    pair = jax.ShapeDtypeStruct((2 * tiles, LANES), jnp.float32)
    out_shape = [best] * want_cols + [pair] * (1 if own_first else len(rows) // 2)
    inside = pl.BlockSpec(memory_space=pltpu.VMEM)
    found = pl.pallas_call(
        functools.partial(
            score_kernel,
            len(key),
            [len(row) for row in parts],
            len(bases),
            want_cols,
            own_first,
            len(after),
        ),
        in_specs=[pl.BlockSpec(memory_space=pl.ANY)] * len(after)
        + [inside] * (len(key) + len(blocks) + len(bases)),
        out_specs=[inside] * len(out_shape),
        out_shape=out_shape,
        compiler_params=pltpu.CompilerParams(vmem_limit_bytes=VMEM_LIMIT),
        cost_estimate=pl.CostEstimate(flops=0, bytes_accessed=0, transcendentals=0),
    )(*after, *key, *blocks, *bases)
    return list(found[:want_cols]), list(found[want_cols:])


def owner_steps(count):
    half = count // 2
    circle = [count - 1 - 2 * i for i in range(half)] + [count - 2 - 2 * i for i in range(half)]
    return [
        [(circle[i], circle[(i + step) % count]) for i in range(count)]
        for step in range(1, half + 1)
    ]


def per_device(embeddings, basis, owner_ids, sub_cluster):
    row_count = embeddings.shape[0]
    tiles = row_count // LANES
    split_count, owner_count = lax.axis_size("split"), lax.axis_size("owners")

    def swap(block, offset):
        return lax.ppermute(block, "split", [(s, s ^ offset) for s in range(split_count)])

    def halves(block):
        return block[: row_count // 2], block[row_count // 2 :]

    own = project(embeddings, basis, owner_ids, sub_cluster)
    rows = [own, swap(own, 1)]
    for offset in range(2, split_count, 2):
        beside = swap(own, offset)
        rows += [beside, tuple(swap(part, 1) for part in halves(beside))]
    *steps, last = owner_steps(owner_count)
    keys = [lax.ppermute(own, "owners", step) for step in steps]
    nearby = tuple(lax.ppermute(part, "owners", last) for part in halves(own))
    _, row_best = score(nearby, rows, want_cols=False)
    backs = []
    for key, step in zip(keys, steps):
        (found,), row_best = score(key, rows, row_best)
        backs.append(lax.ppermute(found, "owners", [(b, a) for a, b in step]))
    others = [swap(found, 2 * at) for at, found in enumerate(row_best) if at]
    _, (local,) = score(
        own, rows, row_best[:1], want_cols=False, own_first=True, after=[*keys, *nearby]
    )
    for other in others:
        local = jnp.maximum(local, other)
    best = jnp.maximum(local[:tiles], swap(local[tiles:], 1))
    for back in backs:
        best = jnp.maximum(best, back)
    return jnp.maximum(best, -1.0).reshape(row_count)


def solution(mesh):
    placed = (
        P(("groups", "owners", "split"), None),
        P(),
        P(("groups", "owners", "split"), None),
        P(("groups", "owners", "split")),
    )
    return jax.shard_map(
        per_device,
        mesh=mesh,
        in_specs=placed,
        out_specs=P(("groups", "owners", "split")),
        check_vma=False,
    )
```

time: 32.7 us -> 31.7 us (0.969)
  waiting for transfers between devices: 12.5 us -> 15.4 us
  Pallas kernels: 8.11 us -> 5.79 us
  starting transfers between devices: 11.2 us -> 9.66 us
    ppermute x1 -> x2, waiting for transfers between devices: 7.42 us -> 10.4 us  [per_device(): nearby = tuple((lax.ppermute(part, 'owners', last) for part in halves(own)))]
    pallas_call x1, Pallas kernels: 5.68 us -> 3.37 us  [project(): pl.pallas_call(project_kernel, in_specs=[pl.BlockSpec(memory_space=pltpu....]
    ppermute x7 -> x6, starting transfers between devices: 5.49 us -> 3.65 us  [swap(): lax.ppermute(block, 'split', [(s, s ^ offset) for s in range(split_count)])]
    ppermute x1, waiting for transfers between devices: 1.52 us -> 0.01 us  [per_device(): keys = [lax.ppermute(own, 'owners', step) for step in steps]]
    ppermute x1, starting transfers between devices: 1.68 us -> 0.27 us  [per_device(): backs.append(lax.ppermute(found, 'owners', [(b, a) for a, b in step]))]
    ppermute x1, waiting for transfers between devices: 1.13 us -> 2.26 us  [per_device(): backs.append(lax.ppermute(found, 'owners', [(b, a) for a, b in step]))]
    ppermute x1, starting transfers between devices: 2.47 us -> 3.6 us  [per_device(): keys = [lax.ppermute(own, 'owners', step) for step in steps]]
    ppermute x1 -> x2, starting transfers between devices: 1.58 us -> 2.14 us  [per_device(): nearby = tuple((lax.ppermute(part, 'owners', last) for part in halves(own)))]
  transfers between devices with their start and end apart: 10 -> 10, of which waited for: 4 -> 5; matrix products, arithmetic and copies ran while one was open for 0% -> 0% of each run, Pallas kernels for 5% -> 5%
where the time goes in v8:
time: 31.7 us; the launch traced here: 31.6 us
  waiting for transfers between devices  15.4 us (49%)
  starting transfers between devices  9.66 us (30%)
  Pallas kernels  5.79 us (18%)
  other arithmetic  0.59 us (2%)
    ppermute x2, waiting for transfers between devices, per_device(): nearby = tuple((lax.ppermute(part, 'owners', last) for part in halves(own)))  10.4 us
    ppermute x6, starting transfers between devices, swap(): lax.ppermute(block, 'split', [(s, s ^ offset) for s in range(split_count)])  3.65 us
    ppermute x1, starting transfers between devices, per_device(): keys = [lax.ppermute(own, 'owners', step) for step in steps]  3.6 us
    pallas_call x1, Pallas kernels, project(): pl.pallas_call(project_kernel, in_specs=[pl.BlockSpec(memory_space=pltpu....  3.37 us
    ppermute x6, waiting for transfers between devices, swap(): lax.ppermute(block, 'split', [(s, s ^ offset) for s in range(split_count)])  2.78 us
    pallas_call x3, Pallas kernels, score(): pl.pallas_call(functools.partial(score_kernel, len(key), [len(row) for ro...  2.42 us
    ppermute x1, waiting for transfers between devices, per_device(): backs.append(lax.ppermute(found, 'owners', [(b, a) for a, b in step]))  2.26 us
    ppermute x2, starting transfers between devices, per_device(): nearby = tuple((lax.ppermute(part, 'owners', last) for part in halves(own)))  2.14 us
  transfers between devices with their start and end apart: 10, of which 5 were waited for; matrix products, arithmetic and copies ran while one was open for 0% of the time, Pallas kernels for 5%

profile of v8, /device:TPU:0, one launch (start us, length us, event | category | flops | bytes accessed | tf_op | source)
XLA Modules:
  0.0 31.6 jit_solution(9295653371929622478)
XLA Ops:
  0.0 3.4 %shard_map.46.refs_2_.refs_1_.refs_3_.refs_4_ = bf16[528,256]{1,0:T(8,128)(2,1)S(1)} custom-call(bf16[512,4096]{1,0:T(8,128)(2,1)} %source_hbm.1, bf16[4096,256]{1,0:T(8,128)(2,1)} %basis_hbm.1, s32[4,128]{1,0:T(4,128)} %bitcast.4, s32[4,128]{1,0:T(4,128)} %bitcast.5), custom_call_target="tpu_custom_call" | custom-call | flops 1073741824 | bytes 6291456 | tf_op jit(solution)/shard_map/pallas_call | solution.py:65
  3.4 3.0 %collective-permute-start.4 = (bf16[528,256]{1,0:T(8,128)(2,1)S(1)}, bf16[528,256]{1,0:T(8,128)(2,1)S(1)}, u32[]{:S(2)}, u32[]{:S(2)}) collective-permute-start(bf16[528,256]{1,0:T(8,128)(2,1)S(1)} %shard_map.46.refs_2_.refs_1_.refs_3_.refs_4_), channel_id=1, source_target_pairs={{0,2},{1,3},{2,0},{3,1},{4,6},{5,7},{6,4},{7,5},{8,10},{9,11},{10,... | collective-permute-start | bytes 811016 | tf_op jit(solution)/shard_map/ppermute | solution.py:206
  6.4 0.0 collective-permute-start.3
  6.4 3.6 %collective-permute-start = (bf16[528,256]{1,0:T(8,128)(2,1)S(1)}, bf16[528,256]{1,0:T(8,128)(2,1)S(1)}, u32[]{:S(2)}, u32[]{:S(2)}) collective-permute-start(bf16[528,256]{1,0:T(8,128)(2,1)S(1)} %shard_map.46.refs_2_.refs_1_.refs_3_.refs_4_), channel_id=1, source_target_pairs={{12,4},{4,8},{8,0},{0,12},{13,5},{5,9},{9,1},{1,13},{14,6},{6,10},... | collective-permute-start | bytes 811016 | tf_op jit(solution)/shard_map/ppermute | solution.py:217
  10.0 0.1 collective-permute-start.1
  10.1 2.1 %collective-permute-start.2 = (bf16[272,256]{1,0:T(8,128)(2,1)S(1)}, bf16[272,256]{1,0:T(8,128)(2,1)S(1)}, u32[]{:S(2)}, u32[]{:S(2)}) collective-permute-start(bf16[272,256]{1,0:T(8,128)(2,1)S(1)} %slice.25), channel_id=1, source_target_pairs={{12,8},{4,0},{8,12},{0,4},{13,9},{5,1},{9,13},{1,5},{14,10},{6,2},... | collective-permute-start | bytes 417800 | tf_op jit(solution)/shard_map/ppermute | solution.py:218
  12.2 0.7 %collective-permute-done.4.refs_4_.refs_3_.refs_6_ = bf16[528,256]{1,0:T(8,128)(2,1)S(1)} collective-permute-done((bf16[528,256]{1,0:T(8,128)(2,1)S(1)}, bf16[528,256]{1,0:T(8,128)(2,1)S(1)}, u32[]{:S(2)}, u32[]{:S(2)}) %collective-permute-start.4) | collective-permute-done | bytes 270368 | tf_op jit(solution)/shard_map/ppermute | solution.py:206
  12.9 0.1 collective-permute-start.6
  13.0 6.7 %collective-permute-done.1.refs_0_.refs_1_ = bf16[256,256]{1,0:T(8,128)(2,1)S(1)} collective-permute-done((bf16[256,256]{1,0:T(8,128)(2,1)S(1)}, bf16[256,256]{1,0:T(8,128)(2,1)S(1)}, u32[]{:S(2)}, u32[]{:S(2)}) %collective-permute-start.1) | collective-permute-done | bytes 131104 | tf_op jit(solution)/shard_map/ppermute | solution.py:218
  19.6 0.0 collective-permute-start.5
  19.6 3.7 %collective-permute-done.2.refs_1_.refs_2_ = bf16[272,256]{1,0:T(8,128)(2,1)S(1)} collective-permute-done((bf16[272,256]{1,0:T(8,128)(2,1)S(1)}, bf16[272,256]{1,0:T(8,128)(2,1)S(1)}, u32[]{:S(2)}, u32[]{:S(2)}) %collective-permute-start.2) | collective-permute-done | bytes 139296 | tf_op jit(solution)/shard_map/ppermute | solution.py:218
  23.4 0.0 collective-permute-done.3.refs_3_.refs_2_.refs_5_
  23.4 0.0 collective-permute-done.5.refs_5_.refs_4_.refs_7_
  23.4 0.0 collective-permute-done.6.refs_6_.refs_5_.refs_8_
  23.4 0.8 %shard_map.47 = (f32[8,128]{1,0:T(8,128)S(1)}, f32[8,128]{1,0:T(8,128)S(1)}) custom-call(bf16[256,256]{1,0:T(8,128)(2,1)S(1)} %collective-permute-done.1.refs_0_.refs_1_, bf16[272,256]{1,0:T(8,128)(2,1)S(1)} %collective-permute-done.2.refs_1_.refs_2_, bf16[528,256]{1,0:T(8,128)(2,1)S(1)} %shard_map.46.refs_2_.refs_1_.refs_3_.refs_4_, ...), custom_call_target="tpu_custom_call" | custom-call | tf_op jit(solution)/shard_map/pallas_call | solution.py:171
  24.2 0.0 collective-permute-done.refs_0_
  24.2 0.8 %shard_map.48 = (f32[4,128]{1,0:T(4,128)S(1)}, f32[8,128]{1,0:T(8,128)S(1)}, f32[8,128]{1,0:T(8,128)S(1)}) custom-call(bf16[528,256]{1,0:T(8,128)(2,1)S(1)} %collective-permute-done.refs_0_, bf16[528,256]{1,0:T(8,128)(2,1)S(1)} %shard_map.46.refs_2_.refs_1_.refs_3_.refs_4_, bf16[528,256]{1,0:T(8,128)(2,1)S(1)} %collective-permute-done.3.refs_3_.refs_2_.refs_5_, ...), custom_call_target="tpu_custom_call" | custom-call | tf_op jit(solution)/shard_map/pallas_call | solution.py:171
  25.1 0.6 %collective-permute-start.7 = (f32[8,128]{1,0:T(8,128)S(1)}, f32[8,128]{1,0:T(8,128)S(1)}, u32[]{:S(2)}, u32[]{:S(2)}) collective-permute-start(f32[8,128]{1,0:T(8,128)S(1)} %get-tuple-element.13), channel_id=1, source_target_pairs={{0,2},{1,3},{2,0},{3,1},{4,6},{5,7},{6,4},{7,5},{8,10},{9,11},{10,... | collective-permute-start | bytes 12296 | tf_op jit(solution)/shard_map/ppermute | solution.py:206
  25.6 0.3 collective-permute-start.9
  25.9 0.7 %shard_map.49 = f32[8,128]{1,0:T(8,128)S(1)} custom-call(bf16[528,256]{1,0:T(8,128)(2,1)S(1)} %collective-permute-done.refs_0_, bf16[256,256]{1,0:T(8,128)(2,1)S(1)} %collective-permute-done.1.refs_0_.refs_1_, bf16[272,256]{1,0:T(8,128)(2,1)S(1)} %collective-permute-done.2.refs_1_.refs_2_, bf16[528,256]{1,0:T(8,128)(2,1)S(1)} %shard_map.46.refs_2_.refs_1_.refs_3_.refs_4_, ...), custom_call_target="tpu_custom_call" | custom-call | tf_op jit(solution)/shard_map/pallas_call | solution.py:171
  26.6 2.1 %collective-permute-done.7 = f32[8,128]{1,0:T(8,128)S(1)} collective-permute-done((f32[8,128]{1,0:T(8,128)S(1)}, f32[8,128]{1,0:T(8,128)S(1)}, u32[]{:S(2)}, u32[]{:S(2)}) %collective-permute-start.7) | collective-permute-done | bytes 4128 | tf_op jit(solution)/shard_map/ppermute | solution.py:206
  28.7 2.3 %collective-permute-done.9 = f32[4,128]{1,0:T(4,128)S(1)} collective-permute-done((f32[4,128]{1,0:T(4,128)S(1)}, f32[4,128]{1,0:T(4,128)S(1)}, u32[]{:S(2)}, u32[]{:S(2)}) %collective-permute-start.9) | collective-permute-done | bytes 2080 | tf_op jit(solution)/shard_map/ppermute | solution.py:223
  31.0 0.0 collective-permute-done.8
  31.0 0.6 %maximum_bitcast_fusion = f32[512]{0:T(512)} fusion(f32[4,128]{1,0:T(4,128)S(1)} %collective-permute-done.9, f32[4,128]{1,0:T(4,128)S(1)} %collective-permute-done.8, f32[8,128]{1,0:T(8,128)S(1)} %max.15), kind=kLoop, calls=%fused_computation | loop fusion | flops 1536 | bytes 8192 | tf_op jit(solution)/shard_map/reshape | solution.py:233
  (7 shorter events, 0.1 us)
Async XLA Ops:
  3.4 9.5 %collective-permute-start.4 = (bf16[528,256]{1,0:T(8,128)(2,1)S(1)}, bf16[528,256]{1,0:T(8,128)(2,1)S(1)}, u32[]{:S(2)}, u32[]{:S(2)}) collective-permute-start(bf16[528,256]{1,0:T(8,128)(2,1)S(1)} %shard_map.46.refs_2_.refs_1_.refs_3_.refs_4_), channel_id=1, source_target_pairs={{0,2},{1,3},{2,0},{3,1},{4,6},{5,7},{6,4},{7,5},{8,10},{9,11},{10,... | collective-permute-start | bytes 811016 | tf_op jit(solution)/shard_map/ppermute | solution.py:206
  6.4 17.0 %collective-permute-start.3 = (bf16[528,256]{1,0:T(8,128)(2,1)S(1)}, bf16[528,256]{1,0:T(8,128)(2,1)S(1)}, u32[]{:S(2)}, u32[]{:S(2)}) collective-permute-start(bf16[528,256]{1,0:T(8,128)(2,1)S(1)} %shard_map.46.refs_2_.refs_1_.refs_3_.refs_4_), channel_id=1, source_target_pairs={{0,1},{1,0},{2,3},{3,2},{4,5},{5,4},{6,7},{7,6},{8,9},{9,8},{10,11... | collective-permute-start | bytes 811016 | tf_op jit(solution)/shard_map/ppermute | solution.py:206
  6.4 17.8 %collective-permute-start = (bf16[528,256]{1,0:T(8,128)(2,1)S(1)}, bf16[528,256]{1,0:T(8,128)(2,1)S(1)}, u32[]{:S(2)}, u32[]{:S(2)}) collective-permute-start(bf16[528,256]{1,0:T(8,128)(2,1)S(1)} %shard_map.46.refs_2_.refs_1_.refs_3_.refs_4_), channel_id=1, source_target_pairs={{12,4},{4,8},{8,0},{0,12},{13,5},{5,9},{9,1},{1,13},{14,6},{6,10},... | collective-permute-start | bytes 811016 | tf_op jit(solution)/shard_map/ppermute | solution.py:217
  10.0 9.6 %collective-permute-start.1 = (bf16[256,256]{1,0:T(8,128)(2,1)S(1)}, bf16[256,256]{1,0:T(8,128)(2,1)S(1)}, u32[]{:S(2)}, u32[]{:S(2)}) collective-permute-start(bf16[256,256]{1,0:T(8,128)(2,1)S(1)} %slice.24), channel_id=1, source_target_pairs={{12,8},{4,0},{8,12},{0,4},{13,9},{5,1},{9,13},{1,5},{14,10},{6,2},... | collective-permute-start | bytes 393224 | tf_op jit(solution)/shard_map/ppermute | solution.py:218
  10.1 13.3 %collective-permute-start.2 = (bf16[272,256]{1,0:T(8,128)(2,1)S(1)}, bf16[272,256]{1,0:T(8,128)(2,1)S(1)}, u32[]{:S(2)}, u32[]{:S(2)}) collective-permute-start(bf16[272,256]{1,0:T(8,128)(2,1)S(1)} %slice.25), channel_id=1, source_target_pairs={{12,8},{4,0},{8,12},{0,4},{13,9},{5,1},{9,13},{1,5},{14,10},{6,2},... | collective-permute-start | bytes 417800 | tf_op jit(solution)/shard_map/ppermute | solution.py:218
  12.9 10.5 %collective-permute-start.6 = (bf16[272,256]{1,0:T(8,128)(2,1)S(1)}, bf16[272,256]{1,0:T(8,128)(2,1)S(1)}, u32[]{:S(2)}, u32[]{:S(2)}) collective-permute-start(bf16[272,256]{1,0:T(8,128)(2,1)S(1)} %slice.27), channel_id=1, source_target_pairs={{0,1},{1,0},{2,3},{3,2},{4,5},{5,4},{6,7},{7,6},{8,9},{9,8},{10,11... | collective-permute-start | bytes 417800 | tf_op jit(solution)/shard_map/ppermute | solution.py:206
  19.6 3.7 %collective-permute-start.5 = (bf16[256,256]{1,0:T(8,128)(2,1)S(1)}, bf16[256,256]{1,0:T(8,128)(2,1)S(1)}, u32[]{:S(2)}, u32[]{:S(2)}) collective-permute-start(bf16[256,256]{1,0:T(8,128)(2,1)S(1)} %slice.26), channel_id=1, source_target_pairs={{0,1},{1,0},{2,3},{3,2},{4,5},{5,4},{6,7},{7,6},{8,9},{9,8},{10,11... | collective-permute-start | bytes 393224 | tf_op jit(solution)/shard_map/ppermute | solution.py:206
  25.1 3.7 %collective-permute-start.7 = (f32[8,128]{1,0:T(8,128)S(1)}, f32[8,128]{1,0:T(8,128)S(1)}, u32[]{:S(2)}, u32[]{:S(2)}) collective-permute-start(f32[8,128]{1,0:T(8,128)S(1)} %get-tuple-element.13), channel_id=1, source_target_pairs={{0,2},{1,3},{2,0},{3,1},{4,6},{5,7},{6,4},{7,5},{8,10},{9,11},{10,... | collective-permute-start | bytes 12296 | tf_op jit(solution)/shard_map/ppermute | solution.py:206
  25.6 5.4 %collective-permute-start.9 = (f32[4,128]{1,0:T(4,128)S(1)}, f32[4,128]{1,0:T(4,128)S(1)}, u32[]{:S(2)}, u32[]{:S(2)}) collective-permute-start(f32[4,128]{1,0:T(4,128)S(1)} %get-tuple-element.14), channel_id=1, source_target_pairs={{4,12},{8,4},{0,8},{12,0},{5,13},{9,5},{1,9},{13,1},{6,14},{10,6},... | collective-permute-start | bytes 6152 | tf_op jit(solution)/shard_map/ppermute | solution.py:223
  28.7 2.3 %collective-permute-start.8 = (f32[4,128]{1,0:T(4,128)S(1)}, f32[4,128]{1,0:T(4,128)S(1)}, u32[]{:S(2)}, u32[]{:S(2)}) collective-permute-start(f32[4,128]{1,0:T(4,128)S(1)} %slice.23), channel_id=1, source_target_pairs={{0,1},{1,0},{2,3},{3,2},{4,5},{5,4},{6,7},{7,6},{8,9},{9,8},{10,11... | collective-permute-start | bytes 6152 | tf_op jit(solution)/shard_map/ppermute | solution.py:206

commit v9 on v8

--- a/solution.py
+++ b/solution.py
@@ -12,7 +12,7 @@
 TAG_ROWS = 16
 ABSENT = -2.0
 STEPS = 8
-ROW_PARTS = 2
+ROW_PARTS = 4
 VMEM_LIMIT = 48 * 1024 * 1024
 
 
@@ -154,7 +154,9 @@
         if want_cols:
             col_out[at : at + 1, :] = found
         if own_first:
-            row_outs[0][at : at + 1, :] = jnp.maximum(found, base_refs[0][at : at + 1, :])
+            for base_ref in base_refs:
+                found = jnp.maximum(found, base_ref[at : at + 1, :])
+            row_outs[0][at : at + 1, :] = found
     if own_first:
         row_outs[0][tiles:, :] = base_refs[0][tiles:, :]
 
@@ -215,21 +217,24 @@
         rows += [beside, tuple(swap(part, 1) for part in halves(beside))]
     *steps, last = owner_steps(owner_count)
     keys = [lax.ppermute(own, "owners", step) for step in steps]
-    nearby = tuple(lax.ppermute(part, "owners", last) for part in halves(own))
-    _, row_best = score(nearby, rows, want_cols=False)
-    backs = []
+    nearby = lax.ppermute(own, "owners", last)
+    row_best, backs = [], []
     for key, step in zip(keys, steps):
         (found,), row_best = score(key, rows, row_best)
         backs.append(lax.ppermute(found, "owners", [(b, a) for a, b in step]))
+    _, row_best = score(nearby, rows, row_best, want_cols=False)
     others = [swap(found, 2 * at) for at, found in enumerate(row_best) if at]
     _, (local,) = score(
-        own, rows, row_best[:1], want_cols=False, own_first=True, after=[*keys, *nearby]
+        own,
+        rows,
+        [row_best[0], *(jnp.maximum(back, ABSENT) for back in backs)],
+        want_cols=False,
+        own_first=True,
+        after=[*keys, nearby],
     )
     for other in others:
         local = jnp.maximum(local, other)
     best = jnp.maximum(local[:tiles], swap(local[tiles:], 1))
-    for back in backs:
-        best = jnp.maximum(best, back)
     return jnp.maximum(best, -1.0).reshape(row_count)
 
 

time: 31.7 us -> 31.1 us (0.981)
  waiting for transfers between devices: 15.4 us -> 15 us
    ppermute x2 -> x1, waiting for transfers between devices: 10.4 us -> 0.01 us  [per_device(): nearby = lax.ppermute(own, 'owners', last)]
    ppermute x1, waiting for transfers between devices: 0.01 us -> 8.54 us  [per_device(): keys = [lax.ppermute(own, 'owners', step) for step in steps]]
    ppermute x2 -> x1, starting transfers between devices: 2.14 us -> 0.01 us  [per_device(): nearby = lax.ppermute(own, 'owners', last)]
    ppermute x1, starting transfers between devices: 0.27 us -> 1.64 us  [per_device(): backs.append(lax.ppermute(found, 'owners', [(b, a) for a, b in step]))]
    ppermute x6, waiting for transfers between devices: 2.78 us -> 4.03 us  [swap(): lax.ppermute(block, 'split', [(s, s ^ offset) for s in range(split_count)])]
    ppermute x6, starting transfers between devices: 3.65 us -> 4.29 us  [swap(): lax.ppermute(block, 'split', [(s, s ^ offset) for s in range(split_count)])]
  transfers between devices with their start and end apart: 10 -> 9, of which waited for: 5 -> 4; matrix products, arithmetic and copies ran while one was open for 0% -> 0% of each run, Pallas kernels for 5% -> 8%
where the time goes in v9:
time: 31.1 us; the launch traced here: 31 us
  waiting for transfers between devices  15 us (48%)
  starting transfers between devices  9.52 us (31%)
  Pallas kernels  5.82 us (19%)
  other arithmetic  0.59 us (2%)
    ppermute x1, waiting for transfers between devices, per_device(): keys = [lax.ppermute(own, 'owners', step) for step in steps]  8.54 us
    ppermute x6, starting transfers between devices, swap(): lax.ppermute(block, 'split', [(s, s ^ offset) for s in range(split_count)])  4.29 us
    ppermute x6, waiting for transfers between devices, swap(): lax.ppermute(block, 'split', [(s, s ^ offset) for s in range(split_count)])  4.03 us
    ppermute x1, starting transfers between devices, per_device(): keys = [lax.ppermute(own, 'owners', step) for step in steps]  3.6 us
    pallas_call x1, Pallas kernels, project(): pl.pallas_call(project_kernel, in_specs=[pl.BlockSpec(memory_space=pltpu....  3.38 us
    pallas_call x3, Pallas kernels, score(): pl.pallas_call(functools.partial(score_kernel, len(key), [len(row) for ro...  2.44 us
    ppermute x1, waiting for transfers between devices, per_device(): backs.append(lax.ppermute(found, 'owners', [(b, a) for a, b in step]))  2.38 us
    ppermute x1, starting transfers between devices, per_device(): backs.append(lax.ppermute(found, 'owners', [(b, a) for a, b in step]))  1.64 us
  transfers between devices with their start and end apart: 9, of which 4 were waited for; matrix products, arithmetic and copies ran while one was open for 0% of the time, Pallas kernels for 8%

profile of v9, /device:TPU:0, one launch (start us, length us, event | category | flops | bytes accessed | tf_op | source)
XLA Modules:
  0.0 31.0 jit_solution(3824478317058666782)
XLA Ops:
  0.0 3.4 %shard_map.46.refs_1_.refs_2_.refs_3_ = bf16[528,256]{1,0:T(8,128)(2,1)S(1)} custom-call(bf16[512,4096]{1,0:T(8,128)(2,1)} %source_hbm.1, bf16[4096,256]{1,0:T(8,128)(2,1)} %basis_hbm.1, s32[4,128]{1,0:T(4,128)} %bitcast.4, s32[4,128]{1,0:T(4,128)} %bitcast.5), custom_call_target="tpu_custom_call" | custom-call | flops 1073741824 | bytes 6291456 | tf_op jit(solution)/shard_map/pallas_call | solution.py:65
  3.4 3.0 %collective-permute-start.3 = (bf16[528,256]{1,0:T(8,128)(2,1)S(1)}, bf16[528,256]{1,0:T(8,128)(2,1)S(1)}, u32[]{:S(2)}, u32[]{:S(2)}) collective-permute-start(bf16[528,256]{1,0:T(8,128)(2,1)S(1)} %shard_map.46.refs_1_.refs_2_.refs_3_), channel_id=1, source_target_pairs={{0,2},{1,3},{2,0},{3,1},{4,6},{5,7},{6,4},{7,5},{8,10},{9,11},{10,... | collective-permute-start | bytes 811016 | tf_op jit(solution)/shard_map/ppermute | solution.py:208
  6.4 0.0 collective-permute-start.2
  6.4 3.6 %collective-permute-start = (bf16[528,256]{1,0:T(8,128)(2,1)S(1)}, bf16[528,256]{1,0:T(8,128)(2,1)S(1)}, u32[]{:S(2)}, u32[]{:S(2)}) collective-permute-start(bf16[528,256]{1,0:T(8,128)(2,1)S(1)} %shard_map.46.refs_1_.refs_2_.refs_3_), channel_id=1, source_target_pairs={{12,4},{4,8},{8,0},{0,12},{13,5},{5,9},{9,1},{1,13},{14,6},{6,10},... | collective-permute-start | bytes 811016 | tf_op jit(solution)/shard_map/ppermute | solution.py:219
  10.0 0.0 collective-permute-start.1
  10.0 2.9 %collective-permute-done.3.refs_3_.refs_5_ = bf16[528,256]{1,0:T(8,128)(2,1)S(1)} collective-permute-done((bf16[528,256]{1,0:T(8,128)(2,1)S(1)}, bf16[528,256]{1,0:T(8,128)(2,1)S(1)}, u32[]{:S(2)}, u32[]{:S(2)}) %collective-permute-start.3) | collective-permute-done | bytes 270368 | tf_op jit(solution)/shard_map/ppermute | solution.py:208
  12.9 0.1 collective-permute-start.5
  13.0 0.6 %collective-permute-start.4 = (bf16[256,256]{1,0:T(8,128)(2,1)S(1)}, bf16[256,256]{1,0:T(8,128)(2,1)S(1)}, u32[]{:S(2)}, u32[]{:S(2)}) collective-permute-start(bf16[256,256]{1,0:T(8,128)(2,1)S(1)} %slice.16), channel_id=1, source_target_pairs={{0,1},{1,0},{2,3},{3,2},{4,5},{5,4},{6,7},{7,6},{8,9},{9,8},{10,11... | collective-permute-start | bytes 393224 | tf_op jit(solution)/shard_map/ppermute | solution.py:208
  13.5 0.0 collective-permute-done.2.refs_2_.refs_4_
  13.5 8.5 %collective-permute-done.refs_0_ = bf16[528,256]{1,0:T(8,128)(2,1)S(1)} collective-permute-done((bf16[528,256]{1,0:T(8,128)(2,1)S(1)}, bf16[528,256]{1,0:T(8,128)(2,1)S(1)}, u32[]{:S(2)}, u32[]{:S(2)}) %collective-permute-start) | collective-permute-done | bytes 270368 | tf_op jit(solution)/shard_map/ppermute | solution.py:219
  22.1 0.0 collective-permute-done.4.refs_4_.refs_6_
  22.1 0.0 collective-permute-done.5.refs_5_.refs_7_
  22.1 0.9 %shard_map.47 = (f32[4,128]{1,0:T(4,128)S(1)}, f32[8,128]{1,0:T(8,128)S(1)}, f32[8,128]{1,0:T(8,128)S(1)}) custom-call(bf16[528,256]{1,0:T(8,128)(2,1)S(1)} %collective-permute-done.refs_0_, bf16[528,256]{1,0:T(8,128)(2,1)S(1)} %shard_map.46.refs_1_.refs_2_.refs_3_, bf16[528,256]{1,0:T(8,128)(2,1)S(1)} %collective-permute-done.2.refs_2_.refs_4_, ...), custom_call_target="tpu_custom_call" | custom-call | tf_op jit(solution)/shard_map/pallas_call | solution.py:173
  22.9 1.6 %collective-permute-start.6 = (f32[4,128]{1,0:T(4,128)S(1)}, f32[4,128]{1,0:T(4,128)S(1)}, u32[]{:S(2)}, u32[]{:S(2)}) collective-permute-start(f32[4,128]{1,0:T(4,128)S(1)} %get-tuple-element.13), channel_id=1, source_target_pairs={{4,12},{8,4},{0,8},{12,0},{5,13},{9,5},{1,9},{13,1},{6,14},{10,6},... | collective-permute-start | bytes 6152 | tf_op jit(solution)/shard_map/ppermute | solution.py:224
  24.6 0.0 collective-permute-done.1.refs_0_.refs_1_
  24.6 0.8 %shard_map.48 = (f32[8,128]{1,0:T(8,128)S(1)}, f32[8,128]{1,0:T(8,128)S(1)}) custom-call(bf16[528,256]{1,0:T(8,128)(2,1)S(1)} %collective-permute-done.1.refs_0_.refs_1_, bf16[528,256]{1,0:T(8,128)(2,1)S(1)} %shard_map.46.refs_1_.refs_2_.refs_3_, bf16[528,256]{1,0:T(8,128)(2,1)S(1)} %collective-permute-done.2.refs_2_.refs_4_, ...), custom_call_target="tpu_custom_call" | custom-call | tf_op jit(solution)/shard_map/pallas_call | solution.py:173
  25.4 0.6 %collective-permute-start.7 = (f32[8,128]{1,0:T(8,128)S(1)}, f32[8,128]{1,0:T(8,128)S(1)}, u32[]{:S(2)}, u32[]{:S(2)}) collective-permute-start(f32[8,128]{1,0:T(8,128)S(1)} %get-tuple-element.14), channel_id=1, source_target_pairs={{0,2},{1,3},{2,0},{3,1},{4,6},{5,7},{6,4},{7,5},{8,10},{9,11},{10,... | collective-permute-start | bytes 12296 | tf_op jit(solution)/shard_map/ppermute | solution.py:208
  26.0 2.4 %collective-permute-done.6 = f32[4,128]{1,0:T(4,128)S(1)} collective-permute-done((f32[4,128]{1,0:T(4,128)S(1)}, f32[4,128]{1,0:T(4,128)S(1)}, u32[]{:S(2)}, u32[]{:S(2)}) %collective-permute-start.6) | collective-permute-done | bytes 2080 | tf_op jit(solution)/shard_map/ppermute | solution.py:224
  28.4 0.8 %shard_map.49 = f32[8,128]{1,0:T(8,128)S(1)} custom-call(bf16[528,256]{1,0:T(8,128)(2,1)S(1)} %collective-permute-done.refs_0_, bf16[528,256]{1,0:T(8,128)(2,1)S(1)} %collective-permute-done.1.refs_0_.refs_1_, bf16[528,256]{1,0:T(8,128)(2,1)S(1)} %shard_map.46.refs_1_.refs_2_.refs_3_, bf16[528,256]{1,0:T(8,128)(2,1)S(1)} %shard_map.46.refs_1_.refs_2_.refs_3_, ...), custom_call_target="tpu_custom_call" | custom-call | tf_op jit(solution)/shard_map/pallas_call | solution.py:173
  29.2 0.0 collective-permute-done.7
  29.2 0.1 collective-permute-start.8
  29.3 1.1 %collective-permute-done.8 = f32[4,128]{1,0:T(4,128)S(1)} collective-permute-done((f32[4,128]{1,0:T(4,128)S(1)}, f32[4,128]{1,0:T(4,128)S(1)}, u32[]{:S(2)}, u32[]{:S(2)}) %collective-permute-start.8) | collective-permute-done | bytes 2080 | tf_op jit(solution)/shard_map/ppermute | solution.py:208
  30.4 0.6 %maximum_bitcast_fusion = f32[512]{0:T(512)} fusion(f32[4,128]{1,0:T(4,128)S(1)} %collective-permute-done.8, f32[8,128]{1,0:T(8,128)S(1)} %max.20), kind=kLoop, calls=%fused_computation | loop fusion | flops 1024 | bytes 6144 | tf_op jit(solution)/shard_map/reshape | solution.py:238
  (5 shorter events, 0.0 us)
Async XLA Ops:
  3.4 9.5 %collective-permute-start.3 = (bf16[528,256]{1,0:T(8,128)(2,1)S(1)}, bf16[528,256]{1,0:T(8,128)(2,1)S(1)}, u32[]{:S(2)}, u32[]{:S(2)}) collective-permute-start(bf16[528,256]{1,0:T(8,128)(2,1)S(1)} %shard_map.46.refs_1_.refs_2_.refs_3_), channel_id=1, source_target_pairs={{0,2},{1,3},{2,0},{3,1},{4,6},{5,7},{6,4},{7,5},{8,10},{9,11},{10,... | collective-permute-start | bytes 811016 | tf_op jit(solution)/shard_map/ppermute | solution.py:208
  6.4 7.2 %collective-permute-start.2 = (bf16[528,256]{1,0:T(8,128)(2,1)S(1)}, bf16[528,256]{1,0:T(8,128)(2,1)S(1)}, u32[]{:S(2)}, u32[]{:S(2)}) collective-permute-start(bf16[528,256]{1,0:T(8,128)(2,1)S(1)} %shard_map.46.refs_1_.refs_2_.refs_3_), channel_id=1, source_target_pairs={{0,1},{1,0},{2,3},{3,2},{4,5},{5,4},{6,7},{7,6},{8,9},{9,8},{10,11... | collective-permute-start | bytes 811016 | tf_op jit(solution)/shard_map/ppermute | solution.py:208
  6.4 15.7 %collective-permute-start = (bf16[528,256]{1,0:T(8,128)(2,1)S(1)}, bf16[528,256]{1,0:T(8,128)(2,1)S(1)}, u32[]{:S(2)}, u32[]{:S(2)}) collective-permute-start(bf16[528,256]{1,0:T(8,128)(2,1)S(1)} %shard_map.46.refs_1_.refs_2_.refs_3_), channel_id=1, source_target_pairs={{12,4},{4,8},{8,0},{0,12},{13,5},{5,9},{9,1},{1,13},{14,6},{6,10},... | collective-permute-start | bytes 811016 | tf_op jit(solution)/shard_map/ppermute | solution.py:219
  10.0 14.6 %collective-permute-start.1 = (bf16[528,256]{1,0:T(8,128)(2,1)S(1)}, bf16[528,256]{1,0:T(8,128)(2,1)S(1)}, u32[]{:S(2)}, u32[]{:S(2)}) collective-permute-start(bf16[528,256]{1,0:T(8,128)(2,1)S(1)} %shard_map.46.refs_1_.refs_2_.refs_3_), channel_id=1, source_target_pairs={{12,8},{4,0},{8,12},{0,4},{13,9},{5,1},{9,13},{1,5},{14,10},{6,2},... | collective-permute-start | bytes 811016 | tf_op jit(solution)/shard_map/ppermute | solution.py:220
  12.9 9.2 %collective-permute-start.5 = (bf16[272,256]{1,0:T(8,128)(2,1)S(1)}, bf16[272,256]{1,0:T(8,128)(2,1)S(1)}, u32[]{:S(2)}, u32[]{:S(2)}) collective-permute-start(bf16[272,256]{1,0:T(8,128)(2,1)S(1)} %slice.17), channel_id=1, source_target_pairs={{0,1},{1,0},{2,3},{3,2},{4,5},{5,4},{6,7},{7,6},{8,9},{9,8},{10,11... | collective-permute-start | bytes 417800 | tf_op jit(solution)/shard_map/ppermute | solution.py:208
  13.0 9.1 %collective-permute-start.4 = (bf16[256,256]{1,0:T(8,128)(2,1)S(1)}, bf16[256,256]{1,0:T(8,128)(2,1)S(1)}, u32[]{:S(2)}, u32[]{:S(2)}) collective-permute-start(bf16[256,256]{1,0:T(8,128)(2,1)S(1)} %slice.16), channel_id=1, source_target_pairs={{0,1},{1,0},{2,3},{3,2},{4,5},{5,4},{6,7},{7,6},{8,9},{9,8},{10,11... | collective-permute-start | bytes 393224 | tf_op jit(solution)/shard_map/ppermute | solution.py:208
  22.9 5.4 %collective-permute-start.6 = (f32[4,128]{1,0:T(4,128)S(1)}, f32[4,128]{1,0:T(4,128)S(1)}, u32[]{:S(2)}, u32[]{:S(2)}) collective-permute-start(f32[4,128]{1,0:T(4,128)S(1)} %get-tuple-element.13), channel_id=1, source_target_pairs={{4,12},{8,4},{0,8},{12,0},{5,13},{9,5},{1,9},{13,1},{6,14},{10,6},... | collective-permute-start | bytes 6152 | tf_op jit(solution)/shard_map/ppermute | solution.py:224
  25.4 3.7 %collective-permute-start.7 = (f32[8,128]{1,0:T(8,128)S(1)}, f32[8,128]{1,0:T(8,128)S(1)}, u32[]{:S(2)}, u32[]{:S(2)}) collective-permute-start(f32[8,128]{1,0:T(8,128)S(1)} %get-tuple-element.14), channel_id=1, source_target_pairs={{0,2},{1,3},{2,0},{3,1},{4,6},{5,7},{6,4},{7,5},{8,10},{9,11},{10,... | collective-permute-start | bytes 12296 | tf_op jit(solution)/shard_map/ppermute | solution.py:208
  29.2 1.2 %collective-permute-start.8 = (f32[4,128]{1,0:T(4,128)S(1)}, f32[4,128]{1,0:T(4,128)S(1)}, u32[]{:S(2)}, u32[]{:S(2)}) collective-permute-start(f32[4,128]{1,0:T(4,128)S(1)} %slice.15), channel_id=1, source_target_pairs={{0,1},{1,0},{2,3},{3,2},{4,5},{5,4},{6,7},{7,6},{8,9},{9,8},{10,11... | collective-permute-start | bytes 6152 | tf_op jit(solution)/shard_map/ppermute | solution.py:208

commit v10 on v8

--- a/solution.py
+++ b/solution.py
@@ -12,7 +12,7 @@
 TAG_ROWS = 16
 ABSENT = -2.0
 STEPS = 8
-ROW_PARTS = 2
+ROW_PARTS = 4
 VMEM_LIMIT = 48 * 1024 * 1024
 
 
@@ -154,7 +154,9 @@
         if want_cols:
             col_out[at : at + 1, :] = found
         if own_first:
-            row_outs[0][at : at + 1, :] = jnp.maximum(found, base_refs[0][at : at + 1, :])
+            for base_ref in base_refs:
+                found = jnp.maximum(found, base_ref[at : at + 1, :])
+            row_outs[0][at : at + 1, :] = found
     if own_first:
         row_outs[0][tiles:, :] = base_refs[0][tiles:, :]
 
@@ -192,7 +194,7 @@
     half = count // 2
     circle = [count - 1 - 2 * i for i in range(half)] + [count - 2 - 2 * i for i in range(half)]
     return [
-        [(circle[i], circle[(i + step) % count]) for i in range(count)]
+        [(circle[(i + step) % count], circle[i]) for i in range(count)]
         for step in range(1, half + 1)
     ]
 
@@ -215,7 +217,7 @@
         rows += [beside, tuple(swap(part, 1) for part in halves(beside))]
     *steps, last = owner_steps(owner_count)
     keys = [lax.ppermute(own, "owners", step) for step in steps]
-    nearby = tuple(lax.ppermute(part, "owners", last) for part in halves(own))
+    nearby = lax.ppermute(own, "owners", last)
     _, row_best = score(nearby, rows, want_cols=False)
     backs = []
     for key, step in zip(keys, steps):
@@ -223,7 +225,7 @@
         backs.append(lax.ppermute(found, "owners", [(b, a) for a, b in step]))
     others = [swap(found, 2 * at) for at, found in enumerate(row_best) if at]
     _, (local,) = score(
-        own, rows, row_best[:1], want_cols=False, own_first=True, after=[*keys, *nearby]
+        own, rows, row_best[:1], want_cols=False, own_first=True, after=[*keys, nearby]
     )
     for other in others:
         local = jnp.maximum(local, other)

time: 31.7 us -> 30 us (0.946)
  waiting for transfers between devices: 15.4 us -> 12.3 us
  starting transfers between devices: 9.66 us -> 11.1 us
    ppermute x2 -> x1, waiting for transfers between devices: 10.4 us -> 1.75 us  [per_device(): nearby = lax.ppermute(own, 'owners', last)]
    ppermute x1, waiting for transfers between devices: 0.01 us -> 7.08 us  [per_device(): keys = [lax.ppermute(own, 'owners', step) for step in steps]]
    ppermute x1, starting transfers between devices: 0.27 us -> 2.59 us  [per_device(): backs.append(lax.ppermute(found, 'owners', [(b, a) for a, b in step]))]
    ppermute x1, waiting for transfers between devices: 2.26 us -> 1.02 us  [per_device(): backs.append(lax.ppermute(found, 'owners', [(b, a) for a, b in step]))]
    ppermute x1, starting transfers between devices: 3.6 us -> 2.59 us  [per_device(): keys = [lax.ppermute(own, 'owners', step) for step in steps]]
    ppermute x6, starting transfers between devices: 3.65 us -> 4.3 us  [swap(): lax.ppermute(block, 'split', [(s, s ^ offset) for s in range(split_count)])]
    ppermute x2 -> x1, starting transfers between devices: 2.14 us -> 1.58 us  [per_device(): nearby = lax.ppermute(own, 'owners', last)]
    ppermute x6, waiting for transfers between devices: 2.78 us -> 2.44 us  [swap(): lax.ppermute(block, 'split', [(s, s ^ offset) for s in range(split_count)])]
  transfers between devices with their start and end apart: 10 -> 9, of which waited for: 5 -> 5; matrix products, arithmetic and copies ran while one was open for 0% -> 0% of each run, Pallas kernels for 5% -> 5%
where the time goes in v10:
time: 30 us; the launch traced here: 29.9 us
  waiting for transfers between devices  12.3 us (41%)
  starting transfers between devices  11.1 us (37%)
  Pallas kernels  5.81 us (19%)
  other arithmetic  0.59 us (2%)
    ppermute x1, waiting for transfers between devices, per_device(): keys = [lax.ppermute(own, 'owners', step) for step in steps]  7.08 us
    ppermute x6, starting transfers between devices, swap(): lax.ppermute(block, 'split', [(s, s ^ offset) for s in range(split_count)])  4.3 us
    pallas_call x1, Pallas kernels, project(): pl.pallas_call(project_kernel, in_specs=[pl.BlockSpec(memory_space=pltpu....  3.38 us
    ppermute x1, starting transfers between devices, per_device(): backs.append(lax.ppermute(found, 'owners', [(b, a) for a, b in step]))  2.59 us
    ppermute x1, starting transfers between devices, per_device(): keys = [lax.ppermute(own, 'owners', step) for step in steps]  2.59 us
    ppermute x6, waiting for transfers between devices, swap(): lax.ppermute(block, 'split', [(s, s ^ offset) for s in range(split_count)])  2.44 us
    pallas_call x3, Pallas kernels, score(): pl.pallas_call(functools.partial(score_kernel, len(key), [len(row) for ro...  2.43 us
    ppermute x1, waiting for transfers between devices, per_device(): nearby = lax.ppermute(own, 'owners', last)  1.75 us
  transfers between devices with their start and end apart: 9, of which 5 were waited for; matrix products, arithmetic and copies ran while one was open for 0% of the time, Pallas kernels for 5%

profile of v10, /device:TPU:0, one launch (start us, length us, event | category | flops | bytes accessed | tf_op | source)
XLA Modules:
  0.0 29.9 jit_solution(1104791428086118065)
XLA Ops:
  0.0 3.4 %shard_map.46.refs_1_.refs_2_.refs_3_ = bf16[528,256]{1,0:T(8,128)(2,1)S(1)} custom-call(bf16[512,4096]{1,0:T(8,128)(2,1)} %source_hbm.1, bf16[4096,256]{1,0:T(8,128)(2,1)} %basis_hbm.1, s32[4,128]{1,0:T(4,128)} %bitcast.4, s32[4,128]{1,0:T(4,128)} %bitcast.5), custom_call_target="tpu_custom_call" | custom-call | flops 1073741824 | bytes 6291456 | tf_op jit(solution)/shard_map/pallas_call | solution.py:65
  3.4 3.0 %collective-permute-start.3 = (bf16[528,256]{1,0:T(8,128)(2,1)S(1)}, bf16[528,256]{1,0:T(8,128)(2,1)S(1)}, u32[]{:S(2)}, u32[]{:S(2)}) collective-permute-start(bf16[528,256]{1,0:T(8,128)(2,1)S(1)} %shard_map.46.refs_1_.refs_2_.refs_3_), channel_id=1, source_target_pairs={{0,2},{1,3},{2,0},{3,1},{4,6},{5,7},{6,4},{7,5},{8,10},{9,11},{10,... | collective-permute-start | bytes 811016 | tf_op jit(solution)/shard_map/ppermute | solution.py:208
  6.4 0.0 collective-permute-start.2
  6.4 1.6 %collective-permute-start.1 = (bf16[528,256]{1,0:T(8,128)(2,1)S(1)}, bf16[528,256]{1,0:T(8,128)(2,1)S(1)}, u32[]{:S(2)}, u32[]{:S(2)}) collective-permute-start(bf16[528,256]{1,0:T(8,128)(2,1)S(1)} %shard_map.46.refs_1_.refs_2_.refs_3_), channel_id=1, source_target_pairs={{8,12},{0,4},{12,8},{4,0},{9,13},{1,5},{13,9},{5,1},{10,14},{2,6},... | collective-permute-start | bytes 811016 | tf_op jit(solution)/shard_map/ppermute | solution.py:220
  8.0 2.6 %collective-permute-start = (bf16[528,256]{1,0:T(8,128)(2,1)S(1)}, bf16[528,256]{1,0:T(8,128)(2,1)S(1)}, u32[]{:S(2)}, u32[]{:S(2)}) collective-permute-start(bf16[528,256]{1,0:T(8,128)(2,1)S(1)} %shard_map.46.refs_1_.refs_2_.refs_3_), channel_id=1, source_target_pairs={{4,12},{8,4},{0,8},{12,0},{5,13},{9,5},{1,9},{13,1},{6,14},{10,6},... | collective-permute-start | bytes 811016 | tf_op jit(solution)/shard_map/ppermute | solution.py:219
  10.6 2.3 %collective-permute-done.3.refs_3_.refs_5_ = bf16[528,256]{1,0:T(8,128)(2,1)S(1)} collective-permute-done((bf16[528,256]{1,0:T(8,128)(2,1)S(1)}, bf16[528,256]{1,0:T(8,128)(2,1)S(1)}, u32[]{:S(2)}, u32[]{:S(2)}) %collective-permute-start.3) | collective-permute-done | bytes 270368 | tf_op jit(solution)/shard_map/ppermute | solution.py:208
  12.9 0.1 collective-permute-start.5
  13.0 0.6 %collective-permute-start.4 = (bf16[256,256]{1,0:T(8,128)(2,1)S(1)}, bf16[256,256]{1,0:T(8,128)(2,1)S(1)}, u32[]{:S(2)}, u32[]{:S(2)}) collective-permute-start(bf16[256,256]{1,0:T(8,128)(2,1)S(1)} %slice.16), channel_id=1, source_target_pairs={{0,1},{1,0},{2,3},{3,2},{4,5},{5,4},{6,7},{7,6},{8,9},{9,8},{10,11... | collective-permute-start | bytes 393224 | tf_op jit(solution)/shard_map/ppermute | solution.py:208
  13.5 0.0 collective-permute-done.2.refs_2_.refs_4_
  13.5 1.7 %collective-permute-done.1.refs_0_.refs_1_ = bf16[528,256]{1,0:T(8,128)(2,1)S(1)} collective-permute-done((bf16[528,256]{1,0:T(8,128)(2,1)S(1)}, bf16[528,256]{1,0:T(8,128)(2,1)S(1)}, u32[]{:S(2)}, u32[]{:S(2)}) %collective-permute-start.1) | collective-permute-done | bytes 270368 | tf_op jit(solution)/shard_map/ppermute | solution.py:220
  15.3 0.0 collective-permute-done.4.refs_4_.refs_6_
  15.3 0.0 collective-permute-done.5.refs_5_.refs_7_
  15.3 0.8 %shard_map.47 = (f32[8,128]{1,0:T(8,128)S(1)}, f32[8,128]{1,0:T(8,128)S(1)}) custom-call(bf16[528,256]{1,0:T(8,128)(2,1)S(1)} %collective-permute-done.1.refs_0_.refs_1_, bf16[528,256]{1,0:T(8,128)(2,1)S(1)} %shard_map.46.refs_1_.refs_2_.refs_3_, bf16[528,256]{1,0:T(8,128)(2,1)S(1)} %collective-permute-done.2.refs_2_.refs_4_, ...), custom_call_target="tpu_custom_call" | custom-call | tf_op jit(solution)/shard_map/pallas_call | solution.py:173
  16.1 7.1 %collective-permute-done.refs_0_ = bf16[528,256]{1,0:T(8,128)(2,1)S(1)} collective-permute-done((bf16[528,256]{1,0:T(8,128)(2,1)S(1)}, bf16[528,256]{1,0:T(8,128)(2,1)S(1)}, u32[]{:S(2)}, u32[]{:S(2)}) %collective-permute-start) | collective-permute-done | bytes 270368 | tf_op jit(solution)/shard_map/ppermute | solution.py:219
  23.2 0.8 %shard_map.48 = (f32[4,128]{1,0:T(4,128)S(1)}, f32[8,128]{1,0:T(8,128)S(1)}, f32[8,128]{1,0:T(8,128)S(1)}) custom-call(bf16[528,256]{1,0:T(8,128)(2,1)S(1)} %collective-permute-done.refs_0_, bf16[528,256]{1,0:T(8,128)(2,1)S(1)} %shard_map.46.refs_1_.refs_2_.refs_3_, bf16[528,256]{1,0:T(8,128)(2,1)S(1)} %collective-permute-done.2.refs_2_.refs_4_, ...), custom_call_target="tpu_custom_call" | custom-call | tf_op jit(solution)/shard_map/pallas_call | solution.py:173
  24.1 0.6 %collective-permute-start.6 = (f32[8,128]{1,0:T(8,128)S(1)}, f32[8,128]{1,0:T(8,128)S(1)}, u32[]{:S(2)}, u32[]{:S(2)}) collective-permute-start(f32[8,128]{1,0:T(8,128)S(1)} %get-tuple-element.13), channel_id=1, source_target_pairs={{0,2},{1,3},{2,0},{3,1},{4,6},{5,7},{6,4},{7,5},{8,10},{9,11},{10,... | collective-permute-start | bytes 12296 | tf_op jit(solution)/shard_map/ppermute | solution.py:208
  24.7 2.6 %collective-permute-start.8 = (f32[4,128]{1,0:T(4,128)S(1)}, f32[4,128]{1,0:T(4,128)S(1)}, u32[]{:S(2)}, u32[]{:S(2)}) collective-permute-start(f32[4,128]{1,0:T(4,128)S(1)} %get-tuple-element.14), channel_id=1, source_target_pairs={{12,4},{4,8},{8,0},{0,12},{13,5},{5,9},{9,1},{1,13},{14,6},{6,10},... | collective-permute-start | bytes 6152 | tf_op jit(solution)/shard_map/ppermute | solution.py:225
  27.2 0.8 %shard_map.49 = f32[8,128]{1,0:T(8,128)S(1)} custom-call(bf16[528,256]{1,0:T(8,128)(2,1)S(1)} %collective-permute-done.refs_0_, bf16[528,256]{1,0:T(8,128)(2,1)S(1)} %collective-permute-done.1.refs_0_.refs_1_, bf16[528,256]{1,0:T(8,128)(2,1)S(1)} %shard_map.46.refs_1_.refs_2_.refs_3_, bf16[528,256]{1,0:T(8,128)(2,1)S(1)} %shard_map.46.refs_1_.refs_2_.refs_3_, ...), custom_call_target="tpu_custom_call" | custom-call | tf_op jit(solution)/shard_map/pallas_call | solution.py:173
  28.0 0.0 collective-permute-done.6
  28.0 0.1 collective-permute-start.7
  28.1 1.0 %collective-permute-done.8 = f32[4,128]{1,0:T(4,128)S(1)} collective-permute-done((f32[4,128]{1,0:T(4,128)S(1)}, f32[4,128]{1,0:T(4,128)S(1)}, u32[]{:S(2)}, u32[]{:S(2)}) %collective-permute-start.8) | collective-permute-done | bytes 2080 | tf_op jit(solution)/shard_map/ppermute | solution.py:225
  29.1 0.1 collective-permute-done.7
  29.3 0.6 %maximum_bitcast_fusion = f32[512]{0:T(512)} fusion(f32[4,128]{1,0:T(4,128)S(1)} %collective-permute-done.8, f32[4,128]{1,0:T(4,128)S(1)} %collective-permute-done.7, f32[8,128]{1,0:T(8,128)S(1)} %max.15), kind=kLoop, calls=%fused_computation | loop fusion | flops 1536 | bytes 8192 | tf_op jit(solution)/shard_map/reshape | solution.py:235
  (4 shorter events, 0.0 us)
Async XLA Ops:
  3.4 9.5 %collective-permute-start.3 = (bf16[528,256]{1,0:T(8,128)(2,1)S(1)}, bf16[528,256]{1,0:T(8,128)(2,1)S(1)}, u32[]{:S(2)}, u32[]{:S(2)}) collective-permute-start(bf16[528,256]{1,0:T(8,128)(2,1)S(1)} %shard_map.46.refs_1_.refs_2_.refs_3_), channel_id=1, source_target_pairs={{0,2},{1,3},{2,0},{3,1},{4,6},{5,7},{6,4},{7,5},{8,10},{9,11},{10,... | collective-permute-start | bytes 811016 | tf_op jit(solution)/shard_map/ppermute | solution.py:208
  6.4 7.2 %collective-permute-start.2 = (bf16[528,256]{1,0:T(8,128)(2,1)S(1)}, bf16[528,256]{1,0:T(8,128)(2,1)S(1)}, u32[]{:S(2)}, u32[]{:S(2)}) collective-permute-start(bf16[528,256]{1,0:T(8,128)(2,1)S(1)} %shard_map.46.refs_1_.refs_2_.refs_3_), channel_id=1, source_target_pairs={{0,1},{1,0},{2,3},{3,2},{4,5},{5,4},{6,7},{7,6},{8,9},{9,8},{10,11... | collective-permute-start | bytes 811016 | tf_op jit(solution)/shard_map/ppermute | solution.py:208
  6.4 8.9 %collective-permute-start.1 = (bf16[528,256]{1,0:T(8,128)(2,1)S(1)}, bf16[528,256]{1,0:T(8,128)(2,1)S(1)}, u32[]{:S(2)}, u32[]{:S(2)}) collective-permute-start(bf16[528,256]{1,0:T(8,128)(2,1)S(1)} %shard_map.46.refs_1_.refs_2_.refs_3_), channel_id=1, source_target_pairs={{8,12},{0,4},{12,8},{4,0},{9,13},{1,5},{13,9},{5,1},{10,14},{2,6},... | collective-permute-start | bytes 811016 | tf_op jit(solution)/shard_map/ppermute | solution.py:220
  8.0 15.2 %collective-permute-start = (bf16[528,256]{1,0:T(8,128)(2,1)S(1)}, bf16[528,256]{1,0:T(8,128)(2,1)S(1)}, u32[]{:S(2)}, u32[]{:S(2)}) collective-permute-start(bf16[528,256]{1,0:T(8,128)(2,1)S(1)} %shard_map.46.refs_1_.refs_2_.refs_3_), channel_id=1, source_target_pairs={{4,12},{8,4},{0,8},{12,0},{5,13},{9,5},{1,9},{13,1},{6,14},{10,6},... | collective-permute-start | bytes 811016 | tf_op jit(solution)/shard_map/ppermute | solution.py:219
  12.9 2.4 %collective-permute-start.5 = (bf16[272,256]{1,0:T(8,128)(2,1)S(1)}, bf16[272,256]{1,0:T(8,128)(2,1)S(1)}, u32[]{:S(2)}, u32[]{:S(2)}) collective-permute-start(bf16[272,256]{1,0:T(8,128)(2,1)S(1)} %slice.17), channel_id=1, source_target_pairs={{0,1},{1,0},{2,3},{3,2},{4,5},{5,4},{6,7},{7,6},{8,9},{9,8},{10,11... | collective-permute-start | bytes 417800 | tf_op jit(solution)/shard_map/ppermute | solution.py:208
  13.0 2.3 %collective-permute-start.4 = (bf16[256,256]{1,0:T(8,128)(2,1)S(1)}, bf16[256,256]{1,0:T(8,128)(2,1)S(1)}, u32[]{:S(2)}, u32[]{:S(2)}) collective-permute-start(bf16[256,256]{1,0:T(8,128)(2,1)S(1)} %slice.16), channel_id=1, source_target_pairs={{0,1},{1,0},{2,3},{3,2},{4,5},{5,4},{6,7},{7,6},{8,9},{9,8},{10,11... | collective-permute-start | bytes 393224 | tf_op jit(solution)/shard_map/ppermute | solution.py:208
  24.1 4.0 %collective-permute-start.6 = (f32[8,128]{1,0:T(8,128)S(1)}, f32[8,128]{1,0:T(8,128)S(1)}, u32[]{:S(2)}, u32[]{:S(2)}) collective-permute-start(f32[8,128]{1,0:T(8,128)S(1)} %get-tuple-element.13), channel_id=1, source_target_pairs={{0,2},{1,3},{2,0},{3,1},{4,6},{5,7},{6,4},{7,5},{8,10},{9,11},{10,... | collective-permute-start | bytes 12296 | tf_op jit(solution)/shard_map/ppermute | solution.py:208
  24.7 4.5 %collective-permute-start.8 = (f32[4,128]{1,0:T(4,128)S(1)}, f32[4,128]{1,0:T(4,128)S(1)}, u32[]{:S(2)}, u32[]{:S(2)}) collective-permute-start(f32[4,128]{1,0:T(4,128)S(1)} %get-tuple-element.14), channel_id=1, source_target_pairs={{12,4},{4,8},{8,0},{0,12},{13,5},{5,9},{9,1},{1,13},{14,6},{6,10},... | collective-permute-start | bytes 6152 | tf_op jit(solution)/shard_map/ppermute | solution.py:225
  28.0 1.2 %collective-permute-start.7 = (f32[4,128]{1,0:T(4,128)S(1)}, f32[4,128]{1,0:T(4,128)S(1)}, u32[]{:S(2)}, u32[]{:S(2)}) collective-permute-start(f32[4,128]{1,0:T(4,128)S(1)} %slice.15), channel_id=1, source_target_pairs={{0,1},{1,0},{2,3},{3,2},{4,5},{5,4},{6,7},{7,6},{8,9},{9,8},{10,11... | collective-permute-start | bytes 6152 | tf_op jit(solution)/shard_map/ppermute | solution.py:208

commit v11 on v10

--- a/solution.py
+++ b/solution.py
@@ -94,10 +94,13 @@
     )
 
 
-def score_kernel(key_parts, row_parts, bases, want_cols, own_first, unread, *refs):
+def score_kernel(key_parts, row_parts, bases, want_cols, own_first, unread, pass_on, *refs):
     refs = list(refs[unread:])
+    pass_refs = [refs.pop() for _ in range(pass_on)]
     key_refs = [refs.pop(0) for _ in range(key_parts)]
     row_refs = [[refs.pop(0) for _ in range(parts)] for parts in row_parts]
+    for pass_ref, (row_ref,) in zip(pass_refs, reversed(row_refs)):
+        pass_ref[...] = row_ref[...]
     base_refs = [refs.pop(0) for _ in range(bases)]
     col_out = refs.pop(0) if want_cols else None
     row_outs = refs
@@ -161,7 +164,7 @@
         row_outs[0][tiles:, :] = base_refs[0][tiles:, :]
 
 
-def score(key, rows, bases=(), want_cols=True, own_first=False, after=()):
+def score(key, rows, bases=(), want_cols=True, own_first=False, after=(), pass_on=0):
     whole = lambda block: block if isinstance(block, tuple) else (block,)
     key, parts = whole(key), [whole(row) for row in rows]
     blocks = [part for row in parts for part in row]
@@ -169,6 +172,8 @@
     best = jax.ShapeDtypeStruct((tiles, LANES), jnp.float32)
     pair = jax.ShapeDtypeStruct((2 * tiles, LANES), jnp.float32)
     out_shape = [best] * want_cols + [pair] * (1 if own_first else len(rows) // 2)
+    passed = blocks[len(blocks) - pass_on :]
+    out_shape += [jax.ShapeDtypeStruct(block.shape, block.dtype) for block in passed]
     inside = pl.BlockSpec(memory_space=pltpu.VMEM)
     found = pl.pallas_call(
         functools.partial(
@@ -179,6 +184,7 @@
             want_cols,
             own_first,
             len(after),
+            pass_on,
         ),
         in_specs=[pl.BlockSpec(memory_space=pl.ANY)] * len(after)
         + [inside] * (len(key) + len(blocks) + len(bases)),
@@ -187,7 +193,8 @@
         compiler_params=pltpu.CompilerParams(vmem_limit_bytes=VMEM_LIMIT),
         cost_estimate=pl.CostEstimate(flops=0, bytes_accessed=0, transcendentals=0),
     )(*after, *key, *blocks, *bases)
-    return list(found[:want_cols]), list(found[want_cols:])
+    best, passed = found[: len(found) - pass_on], found[len(found) - pass_on :]
+    return list(best[:want_cols]), list(best[want_cols:]), list(passed)
 
 
 def owner_steps(count):
@@ -211,20 +218,29 @@
         return block[: row_count // 2], block[row_count // 2 :]
 
     own = project(embeddings, basis, owner_ids, sub_cluster)
-    rows = [own, swap(own, 1)]
-    for offset in range(2, split_count, 2):
-        beside = swap(own, offset)
-        rows += [beside, tuple(swap(part, 1) for part in halves(beside))]
     *steps, last = owner_steps(owner_count)
     keys = [lax.ppermute(own, "owners", step) for step in steps]
     nearby = lax.ppermute(own, "owners", last)
-    _, row_best = score(nearby, rows, want_cols=False)
+    offsets = range(2, split_count, 2)
+
+    def gather_split(block):
+        besides = [swap(block, offset) for offset in offsets]
+        return [part for beside in besides for part in (beside, swap(beside, 1))]
+
+    gathered = lax.cond(
+        lax.axis_index("groups") < 1 << 16,
+        gather_split,
+        lambda block: [block] * (2 * len(offsets)),
+        own,
+    )
+    rows = [own, swap(own, 1), *gathered]
+    _, row_best, rows[2:] = score(nearby, rows, want_cols=False, pass_on=len(gathered))
     backs = []
     for key, step in zip(keys, steps):
-        (found,), row_best = score(key, rows, row_best)
+        (found,), row_best, _ = score(key, rows, row_best)
         backs.append(lax.ppermute(found, "owners", [(b, a) for a, b in step]))
     others = [swap(found, 2 * at) for at, found in enumerate(row_best) if at]
-    _, (local,) = score(
+    _, (local,), _ = score(
         own, rows, row_best[:1], want_cols=False, own_first=True, after=[*keys, nearby]
     )
     for other in others:

time: 30 us -> 29.5 us (0.983)
  waiting for transfers between devices: 12.3 us -> 10.3 us
  Pallas kernels: 5.81 us -> 6.86 us
  starting transfers between devices: 11.1 us -> 11.5 us
    ppermute x1, waiting for transfers between devices: 7.08 us -> 0.42 us  [per_device(): keys = [lax.ppermute(own, 'owners', step) for step in steps]]
    ppermute x6 -> x5, waiting for transfers between devices: 2.44 us -> 8.87 us  [swap(): lax.ppermute(block, 'split', [(s, s ^ offset) for s in range(split_count)])]
    ppermute x1, waiting for transfers between devices: 1.75 us -> 0.01 us  [per_device(): nearby = lax.ppermute(own, 'owners', last)]
    ppermute x1, starting transfers between devices: 1.58 us -> 2.65 us  [per_device(): nearby = lax.ppermute(own, 'owners', last)]
    pallas_call x3, Pallas kernels: 2.43 us -> 3.48 us  [score(): pl.pallas_call(functools.partial(score_kernel, len(key), [len(row) for ro...]
    ppermute x6 -> x5, starting transfers between devices: 4.3 us -> 3.66 us  [swap(): lax.ppermute(block, 'split', [(s, s ^ offset) for s in range(split_count)])]
  transfers between devices with their start and end apart: 9 -> 8, of which waited for: 5 -> 5; matrix products, arithmetic and copies ran while one was open for 0% -> 0% of each run, Pallas kernels for 5% -> 9%
where the time goes in v11:
time: 29.5 us; the launch traced here: 29.3 us
  starting transfers between devices  11.5 us (39%)
  waiting for transfers between devices  10.3 us (35%)
  Pallas kernels  6.86 us (23%)
  other arithmetic  0.59 us (2%)
    ppermute x5, waiting for transfers between devices, swap(): lax.ppermute(block, 'split', [(s, s ^ offset) for s in range(split_count)])  8.87 us
    ppermute x5, starting transfers between devices, swap(): lax.ppermute(block, 'split', [(s, s ^ offset) for s in range(split_count)])  3.66 us
    pallas_call x3, Pallas kernels, score(): pl.pallas_call(functools.partial(score_kernel, len(key), [len(row) for ro...  3.48 us
    pallas_call x1, Pallas kernels, project(): pl.pallas_call(project_kernel, in_specs=[pl.BlockSpec(memory_space=pltpu....  3.38 us
    ppermute x1, starting transfers between devices, per_device(): nearby = lax.ppermute(own, 'owners', last)  2.65 us
    ppermute x1, starting transfers between devices, per_device(): keys = [lax.ppermute(own, 'owners', step) for step in steps]  2.59 us
    ppermute x1, starting transfers between devices, per_device(): backs.append(lax.ppermute(found, 'owners', [(b, a) for a, b in step]))  2.57 us
    ppermute x1, waiting for transfers between devices, per_device(): backs.append(lax.ppermute(found, 'owners', [(b, a) for a, b in step]))  1.05 us
  transfers between devices with their start and end apart: 8, of which 5 were waited for; matrix products, arithmetic and copies ran while one was open for 0% of the time, Pallas kernels for 9%

profile of v11, /device:TPU:0, one launch (start us, length us, event | category | flops | bytes accessed | tf_op | source)
XLA Modules:
  0.0 29.3 jit_solution(11378459407444423778)
XLA Ops:
  0.0 3.4 %shard_map.46.refs_1_.refs_2_.refs_3_ = bf16[528,256]{1,0:T(8,128)(2,1)S(1)} custom-call(bf16[512,4096]{1,0:T(8,128)(2,1)} %source_hbm.1, bf16[4096,256]{1,0:T(8,128)(2,1)} %basis_hbm.1, s32[4,128]{1,0:T(4,128)} %bitcast.4, s32[4,128]{1,0:T(4,128)} %bitcast.5), custom_call_target="tpu_custom_call" | custom-call | flops 1073741824 | bytes 6291456 | tf_op jit(solution)/shard_map/pallas_call | solution.py:65
  3.4 0.5 %collective-permute-start.4 = (bf16[528,256]{1,0:T(8,128)(2,1)S(1)}, bf16[528,256]{1,0:T(8,128)(2,1)S(1)}, u32[]{:S(2)}, u32[]{:S(2)}) collective-permute-start(bf16[528,256]{1,0:T(8,128)(2,1)S(1)} %shard_map.46.refs_1_.refs_2_.refs_3_), channel_id=1, source_target_pairs={{0,1},{1,0},{2,3},{3,2},{4,5},{5,4},{6,7},{7,6},{8,9},{9,8},{10,11... | collective-permute-start | bytes 811016 | tf_op jit(solution)/shard_map/ppermute | solution.py:215
  3.9 2.6 %collective-permute-start.3 = (bf16[528,256]{1,0:T(8,128)(2,1)S(1)}, bf16[528,256]{1,0:T(8,128)(2,1)S(1)}, u32[]{:S(2)}, u32[]{:S(2)}) collective-permute-start(bf16[528,256]{1,0:T(8,128)(2,1)S(1)} %shard_map.46.refs_1_.refs_2_.refs_3_), channel_id=1, source_target_pairs={{8,12},{0,4},{12,8},{4,0},{9,13},{1,5},{13,9},{5,1},{10,14},{2,6},... | collective-permute-start | bytes 811016 | tf_op jit(solution)/shard_map/ppermute | solution.py:223
  6.6 2.6 %collective-permute-start.2 = (bf16[528,256]{1,0:T(8,128)(2,1)S(1)}, bf16[528,256]{1,0:T(8,128)(2,1)S(1)}, u32[]{:S(2)}, u32[]{:S(2)}) collective-permute-start(bf16[528,256]{1,0:T(8,128)(2,1)S(1)} %shard_map.46.refs_1_.refs_2_.refs_3_), channel_id=1, source_target_pairs={{4,12},{8,4},{0,8},{12,0},{5,13},{9,5},{1,9},{13,1},{6,14},{10,6},... | collective-permute-start | bytes 811016 | tf_op jit(solution)/shard_map/ppermute | solution.py:222
  9.1 10.3 %conditional.1 = (bf16[528,256]{1,0:T(8,128)(2,1)}, bf16[528,256]{1,0:T(8,128)(2,1)}) conditional(s32[]{:T(128)} %convert_element_type.3, bf16[528,256]{1,0:T(8,128)(2,1)S(1)} %shard_map.46.refs_1_.refs_2_.refs_3_, bf16[528,256]{1,0:T(8,128)(2,1)S(1)} %shard_map.46.refs_1_.refs_2_.refs_3_), branch_computations={%region_0.0_spmd, %region_1.0_spmd} | conditional | bytes 2162784 | solution.py:230
  9.1 1.5 %collective-permute-start = (bf16[528,256]{1,0:T(8,128)(2,1)S(1)}, bf16[528,256]{1,0:T(8,128)(2,1)}, u32[]{:S(2)}, u32[]{:S(2)}) collective-permute-start(bf16[528,256]{1,0:T(8,128)(2,1)S(1)} %param.1), channel_id=1, source_target_pairs={{0,2},{1,3},{2,0},{3,1},{4,6},{5,7},{6,4},{7,5},{8,10},{9,11},{10,... | collective-permute-start | bytes 811016 | tf_op jit(solution)/shard_map/cond/branch_1_fun/ppermute | solution.py:215
  10.6 6.9 %collective-permute-done = bf16[528,256]{1,0:T(8,128)(2,1)} collective-permute-done((bf16[528,256]{1,0:T(8,128)(2,1)S(1)}, bf16[528,256]{1,0:T(8,128)(2,1)}, u32[]{:S(2)}, u32[]{:S(2)}) %collective-permute-start) | collective-permute-done | bytes 270368 | tf_op jit(solution)/shard_map/cond/branch_1_fun/ppermute | solution.py:215
  17.5 0.0 collective-permute-start.1
  17.5 1.9 %collective-permute-done.1 = bf16[528,256]{1,0:T(8,128)(2,1)} collective-permute-done((bf16[528,256]{1,0:T(8,128)(2,1)}, bf16[528,256]{1,0:T(8,128)(2,1)}, u32[]{:S(2)}, u32[]{:S(2)}) %collective-permute-start.1) | collective-permute-done | bytes 270368 | tf_op jit(solution)/shard_map/cond/branch_1_fun/ppermute | solution.py:215
  19.4 0.0 collective-permute-done.4.refs_2_.refs_4_
  19.4 0.0 collective-permute-done.3.refs_0_.refs_1_
  19.4 1.9 %shard_map.47 = (f32[8,128]{1,0:T(8,128)S(1)}, f32[8,128]{1,0:T(8,128)S(1)}, bf16[528,256]{1,0:T(8,128)(2,1)S(1)}, bf16[528,256]{1,0:T(8,128)(2,1)S(1)}) custom-call(bf16[528,256]{1,0:T(8,128)(2,1)S(1)} %collective-permute-done.3.refs_0_.refs_1_, bf16[528,256]{1,0:T(8,128)(2,1)S(1)} %shard_map.46.refs_1_.refs_2_.refs_3_, ...), custom_call_target="tpu_custom_call" | custom-call | tf_op jit(solution)/shard_map/pallas_call | solution.py:178
  21.3 0.4 %collective-permute-done.2.refs_0_ = bf16[528,256]{1,0:T(8,128)(2,1)S(1)} collective-permute-done((bf16[528,256]{1,0:T(8,128)(2,1)S(1)}, bf16[528,256]{1,0:T(8,128)(2,1)S(1)}, u32[]{:S(2)}, u32[]{:S(2)}) %collective-permute-start.2) | collective-permute-done | bytes 270368 | tf_op jit(solution)/shard_map/ppermute | solution.py:222
  21.7 0.8 %shard_map.48 = (f32[4,128]{1,0:T(4,128)S(1)}, f32[8,128]{1,0:T(8,128)S(1)}, f32[8,128]{1,0:T(8,128)S(1)}) custom-call(bf16[528,256]{1,0:T(8,128)(2,1)S(1)} %collective-permute-done.2.refs_0_, bf16[528,256]{1,0:T(8,128)(2,1)S(1)} %shard_map.46.refs_1_.refs_2_.refs_3_, bf16[528,256]{1,0:T(8,128)(2,1)S(1)} %collective-permute-done.4.refs_2_.refs_4_, ...), custom_call_target="tpu_custom_call" | custom-call | tf_op jit(solution)/shard_map/pallas_call | solution.py:178
  22.6 1.6 %collective-permute-start.5 = (f32[8,128]{1,0:T(8,128)S(1)}, f32[8,128]{1,0:T(8,128)S(1)}, u32[]{:S(2)}, u32[]{:S(2)}) collective-permute-start(f32[8,128]{1,0:T(8,128)S(1)} %get-tuple-element.23), channel_id=1, source_target_pairs={{0,2},{1,3},{2,0},{3,1},{4,6},{5,7},{6,4},{7,5},{8,10},{9,11},{10,... | collective-permute-start | bytes 12296 | tf_op jit(solution)/shard_map/ppermute | solution.py:215
  24.1 2.6 %collective-permute-start.7 = (f32[4,128]{1,0:T(4,128)S(1)}, f32[4,128]{1,0:T(4,128)S(1)}, u32[]{:S(2)}, u32[]{:S(2)}) collective-permute-start(f32[4,128]{1,0:T(4,128)S(1)} %get-tuple-element.24), channel_id=1, source_target_pairs={{12,4},{4,8},{8,0},{0,12},{13,5},{5,9},{9,1},{1,13},{14,6},{6,10},... | collective-permute-start | bytes 6152 | tf_op jit(solution)/shard_map/ppermute | solution.py:241
  26.7 0.7 %shard_map.49 = f32[8,128]{1,0:T(8,128)S(1)} custom-call(bf16[528,256]{1,0:T(8,128)(2,1)S(1)} %collective-permute-done.2.refs_0_, bf16[528,256]{1,0:T(8,128)(2,1)S(1)} %collective-permute-done.3.refs_0_.refs_1_, bf16[528,256]{1,0:T(8,128)(2,1)S(1)} %shard_map.46.refs_1_.refs_2_.refs_3_, bf16[528,256]{1,0:T(8,128)(2,1)S(1)} %shard_map.46.refs_1_.refs_2_.refs_3_, ...), custom_call_target="tpu_custom_call" | custom-call | tf_op jit(solution)/shard_map/pallas_call | solution.py:178
  27.5 0.0 collective-permute-done.5
  27.5 0.1 collective-permute-start.6
  27.6 1.1 %collective-permute-done.7 = f32[4,128]{1,0:T(4,128)S(1)} collective-permute-done((f32[4,128]{1,0:T(4,128)S(1)}, f32[4,128]{1,0:T(4,128)S(1)}, u32[]{:S(2)}, u32[]{:S(2)}) %collective-permute-start.7) | collective-permute-done | bytes 2080 | tf_op jit(solution)/shard_map/ppermute | solution.py:241
  28.6 0.1 collective-permute-done.6
  28.7 0.6 %maximum_bitcast_fusion = f32[512]{0:T(512)} fusion(f32[4,128]{1,0:T(4,128)S(1)} %collective-permute-done.7, f32[4,128]{1,0:T(4,128)S(1)} %collective-permute-done.6, f32[8,128]{1,0:T(8,128)S(1)} %max.15), kind=kLoop, calls=%fused_computation | loop fusion | flops 1536 | bytes 8192 | tf_op jit(solution)/shard_map/reshape | solution.py:251
  (2 shorter events, 0.0 us)
Async XLA Ops:
  3.4 16.0 %collective-permute-start.4 = (bf16[528,256]{1,0:T(8,128)(2,1)S(1)}, bf16[528,256]{1,0:T(8,128)(2,1)S(1)}, u32[]{:S(2)}, u32[]{:S(2)}) collective-permute-start(bf16[528,256]{1,0:T(8,128)(2,1)S(1)} %shard_map.46.refs_1_.refs_2_.refs_3_), channel_id=1, source_target_pairs={{0,1},{1,0},{2,3},{3,2},{4,5},{5,4},{6,7},{7,6},{8,9},{9,8},{10,11... | collective-permute-start | bytes 811016 | tf_op jit(solution)/shard_map/ppermute | solution.py:215
  3.9 15.5 %collective-permute-start.3 = (bf16[528,256]{1,0:T(8,128)(2,1)S(1)}, bf16[528,256]{1,0:T(8,128)(2,1)S(1)}, u32[]{:S(2)}, u32[]{:S(2)}) collective-permute-start(bf16[528,256]{1,0:T(8,128)(2,1)S(1)} %shard_map.46.refs_1_.refs_2_.refs_3_), channel_id=1, source_target_pairs={{8,12},{0,4},{12,8},{4,0},{9,13},{1,5},{13,9},{5,1},{10,14},{2,6},... | collective-permute-start | bytes 811016 | tf_op jit(solution)/shard_map/ppermute | solution.py:223
  6.6 15.2 %collective-permute-start.2 = (bf16[528,256]{1,0:T(8,128)(2,1)S(1)}, bf16[528,256]{1,0:T(8,128)(2,1)S(1)}, u32[]{:S(2)}, u32[]{:S(2)}) collective-permute-start(bf16[528,256]{1,0:T(8,128)(2,1)S(1)} %shard_map.46.refs_1_.refs_2_.refs_3_), channel_id=1, source_target_pairs={{4,12},{8,4},{0,8},{12,0},{5,13},{9,5},{1,9},{13,1},{6,14},{10,6},... | collective-permute-start | bytes 811016 | tf_op jit(solution)/shard_map/ppermute | solution.py:222
  9.1 8.4 %collective-permute-start = (bf16[528,256]{1,0:T(8,128)(2,1)S(1)}, bf16[528,256]{1,0:T(8,128)(2,1)}, u32[]{:S(2)}, u32[]{:S(2)}) collective-permute-start(bf16[528,256]{1,0:T(8,128)(2,1)S(1)} %param.1), channel_id=1, source_target_pairs={{0,2},{1,3},{2,0},{3,1},{4,6},{5,7},{6,4},{7,5},{8,10},{9,11},{10,... | collective-permute-start | bytes 811016 | tf_op jit(solution)/shard_map/cond/branch_1_fun/ppermute | solution.py:215
  17.5 1.9 %collective-permute-start.1 = (bf16[528,256]{1,0:T(8,128)(2,1)}, bf16[528,256]{1,0:T(8,128)(2,1)}, u32[]{:S(2)}, u32[]{:S(2)}) collective-permute-start(bf16[528,256]{1,0:T(8,128)(2,1)} %collective-permute-done), channel_id=1, source_target_pairs={{0,1},{1,0},{2,3},{3,2},{4,5},{5,4},{6,7},{7,6},{8,9},{9,8},{10,11... | collective-permute-start | bytes 811016 | tf_op jit(solution)/shard_map/cond/branch_1_fun/ppermute | solution.py:215
  22.6 4.9 %collective-permute-start.5 = (f32[8,128]{1,0:T(8,128)S(1)}, f32[8,128]{1,0:T(8,128)S(1)}, u32[]{:S(2)}, u32[]{:S(2)}) collective-permute-start(f32[8,128]{1,0:T(8,128)S(1)} %get-tuple-element.23), channel_id=1, source_target_pairs={{0,2},{1,3},{2,0},{3,1},{4,6},{5,7},{6,4},{7,5},{8,10},{9,11},{10,... | collective-permute-start | bytes 12296 | tf_op jit(solution)/shard_map/ppermute | solution.py:215
  24.1 4.5 %collective-permute-start.7 = (f32[4,128]{1,0:T(4,128)S(1)}, f32[4,128]{1,0:T(4,128)S(1)}, u32[]{:S(2)}, u32[]{:S(2)}) collective-permute-start(f32[4,128]{1,0:T(4,128)S(1)} %get-tuple-element.24), channel_id=1, source_target_pairs={{12,4},{4,8},{8,0},{0,12},{13,5},{5,9},{9,1},{1,13},{14,6},{6,10},... | collective-permute-start | bytes 6152 | tf_op jit(solution)/shard_map/ppermute | solution.py:241
  27.5 1.2 %collective-permute-start.6 = (f32[4,128]{1,0:T(4,128)S(1)}, f32[4,128]{1,0:T(4,128)S(1)}, u32[]{:S(2)}, u32[]{:S(2)}) collective-permute-start(f32[4,128]{1,0:T(4,128)S(1)} %slice.7), channel_id=1, source_target_pairs={{0,1},{1,0},{2,3},{3,2},{4,5},{5,4},{6,7},{7,6},{8,9},{9,8},{10,11... | collective-permute-start | bytes 6152 | tf_op jit(solution)/shard_map/ppermute | solution.py:215

commit v12 on v10

--- a/solution.py
+++ b/solution.py
@@ -211,13 +211,19 @@
         return block[: row_count // 2], block[row_count // 2 :]
 
     own = project(embeddings, basis, owner_ids, sub_cluster)
-    rows = [own, swap(own, 1)]
-    for offset in range(2, split_count, 2):
-        beside = swap(own, offset)
-        rows += [beside, tuple(swap(part, 1) for part in halves(beside))]
     *steps, last = owner_steps(owner_count)
     keys = [lax.ppermute(own, "owners", step) for step in steps]
-    nearby = lax.ppermute(own, "owners", last)
+    nearby = tuple(lax.ppermute(part, "owners", last) for part in halves(own))
+    offsets = range(2, split_count, 2)
+    besides = lax.fori_loop(
+        0,
+        1 + (lax.axis_index("groups") >> 16),
+        lambda _, blocks: [swap(block, offset) for block, offset in zip(blocks, offsets)],
+        [own] * len(offsets),
+    )
+    rows = [own, swap(own, 1)]
+    for beside in besides:
+        rows += [beside, tuple(swap(part, 1) for part in halves(beside))]
     _, row_best = score(nearby, rows, want_cols=False)
     backs = []
     for key, step in zip(keys, steps):
@@ -225,7 +231,7 @@
         backs.append(lax.ppermute(found, "owners", [(b, a) for a, b in step]))
     others = [swap(found, 2 * at) for at, found in enumerate(row_best) if at]
     _, (local,) = score(
-        own, rows, row_best[:1], want_cols=False, own_first=True, after=[*keys, nearby]
+        own, rows, row_best[:1], want_cols=False, own_first=True, after=[*keys, *nearby]
     )
     for other in others:
         local = jnp.maximum(local, other)

time: 30 us -> 30 us (level)
    ppermute x1, waiting for transfers between devices: 7.08 us -> 0.01 us  [per_device(): keys = [lax.ppermute(own, 'owners', step) for step in steps]]
    ppermute x6, waiting for transfers between devices: 2.44 us -> 7.87 us  [swap(): lax.ppermute(block, 'split', [(s, s ^ offset) for s in range(split_count)])]
    ppermute x1, starting transfers between devices: 2.59 us -> 3.65 us  [per_device(): keys = [lax.ppermute(own, 'owners', step) for step in steps]]
    ppermute x1, starting transfers between devices: 2.59 us -> 1.58 us  [per_device(): backs.append(lax.ppermute(found, 'owners', [(b, a) for a, b in step]))]
    ppermute x1, waiting for transfers between devices: 1.02 us -> 2.03 us  [per_device(): backs.append(lax.ppermute(found, 'owners', [(b, a) for a, b in step]))]
    ppermute x1 -> x2, starting transfers between devices: 1.58 us -> 2.16 us  [per_device(): nearby = tuple((lax.ppermute(part, 'owners', last) for part in halves(own)))]
    ppermute x6, starting transfers between devices: 4.3 us -> 3.78 us  [swap(): lax.ppermute(block, 'split', [(s, s ^ offset) for s in range(split_count)])]
    ppermute x1 -> x2, waiting for transfers between devices: 1.75 us -> 2.2 us  [per_device(): nearby = tuple((lax.ppermute(part, 'owners', last) for part in halves(own)))]
  transfers between devices with their start and end apart: 9 -> 10, of which waited for: 5 -> 5; matrix products, arithmetic and copies ran while one was open for 0% -> 0% of each run, Pallas kernels for 5% -> 5%
where the time goes in v12:
time: 30 us; the launch traced here: 29.9 us
  waiting for transfers between devices  12.1 us (40%)
  starting transfers between devices  11.2 us (37%)
  Pallas kernels  5.8 us (19%)
  other arithmetic  0.59 us (2%)
    ppermute x6, waiting for transfers between devices, swap(): lax.ppermute(block, 'split', [(s, s ^ offset) for s in range(split_count)])  7.87 us
    ppermute x6, starting transfers between devices, swap(): lax.ppermute(block, 'split', [(s, s ^ offset) for s in range(split_count)])  3.78 us
    ppermute x1, starting transfers between devices, per_device(): keys = [lax.ppermute(own, 'owners', step) for step in steps]  3.65 us
    pallas_call x1, Pallas kernels, project(): pl.pallas_call(project_kernel, in_specs=[pl.BlockSpec(memory_space=pltpu....  3.38 us
    pallas_call x3, Pallas kernels, score(): pl.pallas_call(functools.partial(score_kernel, len(key), [len(row) for ro...  2.42 us
    ppermute x2, waiting for transfers between devices, per_device(): nearby = tuple((lax.ppermute(part, 'owners', last) for part in halves(own)))  2.2 us
    ppermute x2, starting transfers between devices, per_device(): nearby = tuple((lax.ppermute(part, 'owners', last) for part in halves(own)))  2.16 us
    ppermute x1, waiting for transfers between devices, per_device(): backs.append(lax.ppermute(found, 'owners', [(b, a) for a, b in step]))  2.03 us
  transfers between devices with their start and end apart: 10, of which 5 were waited for; matrix products, arithmetic and copies ran while one was open for 0% of the time, Pallas kernels for 5%

profile of v12, /device:TPU:0, one launch (start us, length us, event | category | flops | bytes accessed | tf_op | source)
XLA Modules:
  0.0 29.9 jit_solution(3854107926786295723)
XLA Ops:
  0.0 3.4 %shard_map.46.refs_2_.refs_1_.refs_3_.refs_4_ = bf16[528,256]{1,0:T(8,128)(2,1)S(1)} custom-call(bf16[512,4096]{1,0:T(8,128)(2,1)} %source_hbm.1, bf16[4096,256]{1,0:T(8,128)(2,1)} %basis_hbm.1, s32[4,128]{1,0:T(4,128)} %bitcast.4, s32[4,128]{1,0:T(4,128)} %bitcast.5), custom_call_target="tpu_custom_call" | custom-call | flops 1073741824 | bytes 6291456 | tf_op jit(solution)/shard_map/pallas_call | solution.py:65
  3.4 0.5 %collective-permute-start.4 = (bf16[528,256]{1,0:T(8,128)(2,1)S(1)}, bf16[528,256]{1,0:T(8,128)(2,1)S(1)}, u32[]{:S(2)}, u32[]{:S(2)}) collective-permute-start(bf16[528,256]{1,0:T(8,128)(2,1)S(1)} %shard_map.46.refs_2_.refs_1_.refs_3_.refs_4_), channel_id=1, source_target_pairs={{0,1},{1,0},{2,3},{3,2},{4,5},{5,4},{6,7},{7,6},{8,9},{9,8},{10,11... | collective-permute-start | bytes 811016 | tf_op jit(solution)/shard_map/ppermute | solution.py:208
  3.9 3.6 %collective-permute-start.1 = (bf16[528,256]{1,0:T(8,128)(2,1)S(1)}, bf16[528,256]{1,0:T(8,128)(2,1)S(1)}, u32[]{:S(2)}, u32[]{:S(2)}) collective-permute-start(bf16[528,256]{1,0:T(8,128)(2,1)S(1)} %shard_map.46.refs_2_.refs_1_.refs_3_.refs_4_), channel_id=1, source_target_pairs={{4,12},{8,4},{0,8},{12,0},{5,13},{9,5},{1,9},{13,1},{6,14},{10,6},... | collective-permute-start | bytes 811016 | tf_op jit(solution)/shard_map/ppermute | solution.py:215
  7.6 1.6 %collective-permute-start.2 = (bf16[256,256]{1,0:T(8,128)(2,1)S(1)}, bf16[256,256]{1,0:T(8,128)(2,1)S(1)}, u32[]{:S(2)}, u32[]{:S(2)}) collective-permute-start(bf16[256,256]{1,0:T(8,128)(2,1)S(1)} %slice.24), channel_id=1, source_target_pairs={{8,12},{0,4},{12,8},{4,0},{9,13},{1,5},{13,9},{5,1},{10,14},{2,6},... | collective-permute-start | bytes 393224 | tf_op jit(solution)/shard_map/ppermute | solution.py:216
  9.2 0.5 %collective-permute-start.3 = (bf16[272,256]{1,0:T(8,128)(2,1)S(1)}, bf16[272,256]{1,0:T(8,128)(2,1)S(1)}, u32[]{:S(2)}, u32[]{:S(2)}) collective-permute-start(bf16[272,256]{1,0:T(8,128)(2,1)S(1)} %slice.25), channel_id=1, source_target_pairs={{8,12},{0,4},{12,8},{4,0},{9,13},{1,5},{13,9},{5,1},{10,14},{2,6},... | collective-permute-start | bytes 417800 | tf_op jit(solution)/shard_map/ppermute | solution.py:216
  9.8 8.1 %while.10 = (s32[]{:T(128)}, bf16[528,256]{1,0:T(8,128)(2,1)S(1)}, s32[]{:T(128)}, s32[]{:T(128)}) while((s32[]{:T(128)}, bf16[528,256]{1,0:T(8,128)(2,1)S(1)}, s32[]{:T(128)}, s32[]{:T(128)}) %tuple.18), condition=%wide.region_1.0_spmd, body=%wide.region_0.0_spmd.sunk | while | flops 2 | bytes 1622109 | solution.py:218
  9.8 1.6 %collective-permute-start = (bf16[528,256]{1,0:T(8,128)(2,1)S(1)}, bf16[528,256]{1,0:T(8,128)(2,1)S(1)}, u32[]{:S(2)}, u32[]{:S(2)}) collective-permute-start(bf16[528,256]{1,0:T(8,128)(2,1)S(1)} %get-tuple-element.65), channel_id=1, source_target_pairs={{0,2},{1,3},{2,0},{3,1},{4,6},{5,7},{6,4},{7,5},{8,10},{9,11},{10,... | collective-permute-start | bytes 811016 | tf_op jit(solution)/shard_map/while/body/ppermute | solution.py:208
  11.3 6.5 %collective-permute-done = bf16[528,256]{1,0:T(8,128)(2,1)S(1)} collective-permute-done((bf16[528,256]{1,0:T(8,128)(2,1)S(1)}, bf16[528,256]{1,0:T(8,128)(2,1)S(1)}, u32[]{:S(2)}, u32[]{:S(2)}) %collective-permute-start) | collective-permute-done | bytes 270368 | tf_op jit(solution)/shard_map/while/body/ppermute | solution.py:208
  17.9 0.1 collective-permute-start.6
  18.0 0.6 %collective-permute-done.2.refs_0_.refs_1_ = bf16[256,256]{1,0:T(8,128)(2,1)S(1)} collective-permute-done((bf16[256,256]{1,0:T(8,128)(2,1)S(1)}, bf16[256,256]{1,0:T(8,128)(2,1)S(1)}, u32[]{:S(2)}, u32[]{:S(2)}) %collective-permute-start.2) | collective-permute-done | bytes 131104 | tf_op jit(solution)/shard_map/ppermute | solution.py:216
  18.6 0.0 collective-permute-start.5
  18.6 1.3 %collective-permute-done.5.refs_5_.refs_4_.refs_7_ = bf16[256,256]{1,0:T(8,128)(2,1)S(1)} collective-permute-done((bf16[256,256]{1,0:T(8,128)(2,1)S(1)}, bf16[256,256]{1,0:T(8,128)(2,1)S(1)}, u32[]{:S(2)}, u32[]{:S(2)}) %collective-permute-start.5) | collective-permute-done | bytes 131104 | tf_op jit(solution)/shard_map/ppermute | solution.py:208
  20.0 1.6 %collective-permute-done.3.refs_1_.refs_2_ = bf16[272,256]{1,0:T(8,128)(2,1)S(1)} collective-permute-done((bf16[272,256]{1,0:T(8,128)(2,1)S(1)}, bf16[272,256]{1,0:T(8,128)(2,1)S(1)}, u32[]{:S(2)}, u32[]{:S(2)}) %collective-permute-start.3) | collective-permute-done | bytes 139296 | tf_op jit(solution)/shard_map/ppermute | solution.py:216
  21.5 0.0 collective-permute-done.6.refs_6_.refs_5_.refs_8_
  21.6 0.0 collective-permute-done.4.refs_3_.refs_2_.refs_5_
  21.6 0.8 %shard_map.47 = (f32[8,128]{1,0:T(8,128)S(1)}, f32[8,128]{1,0:T(8,128)S(1)}) custom-call(bf16[256,256]{1,0:T(8,128)(2,1)S(1)} %collective-permute-done.2.refs_0_.refs_1_, bf16[272,256]{1,0:T(8,128)(2,1)S(1)} %collective-permute-done.3.refs_1_.refs_2_, bf16[528,256]{1,0:T(8,128)(2,1)S(1)} %shard_map.46.refs_2_.refs_1_.refs_3_.refs_4_, ...), custom_call_target="tpu_custom_call" | custom-call | tf_op jit(solution)/shard_map/pallas_call | solution.py:173
  22.4 0.0 collective-permute-done.1.refs_0_
  22.4 0.8 %shard_map.48 = (f32[4,128]{1,0:T(4,128)S(1)}, f32[8,128]{1,0:T(8,128)S(1)}, f32[8,128]{1,0:T(8,128)S(1)}) custom-call(bf16[528,256]{1,0:T(8,128)(2,1)S(1)} %collective-permute-done.1.refs_0_, bf16[528,256]{1,0:T(8,128)(2,1)S(1)} %shard_map.46.refs_2_.refs_1_.refs_3_.refs_4_, bf16[528,256]{1,0:T(8,128)(2,1)S(1)} %collective-permute-done.4.refs_3_.refs_2_.refs_5_, ...), custom_call_target="tpu_custom_call" | custom-call | tf_op jit(solution)/shard_map/pallas_call | solution.py:173
  23.2 1.6 %collective-permute-start.7 = (f32[8,128]{1,0:T(8,128)S(1)}, f32[8,128]{1,0:T(8,128)S(1)}, u32[]{:S(2)}, u32[]{:S(2)}) collective-permute-start(f32[8,128]{1,0:T(8,128)S(1)} %get-tuple-element.32), channel_id=1, source_target_pairs={{0,2},{1,3},{2,0},{3,1},{4,6},{5,7},{6,4},{7,5},{8,10},{9,11},{10,... | collective-permute-start | bytes 12296 | tf_op jit(solution)/shard_map/ppermute | solution.py:208
  24.8 1.6 %collective-permute-start.9 = (f32[4,128]{1,0:T(4,128)S(1)}, f32[4,128]{1,0:T(4,128)S(1)}, u32[]{:S(2)}, u32[]{:S(2)}) collective-permute-start(f32[4,128]{1,0:T(4,128)S(1)} %get-tuple-element.33), channel_id=1, source_target_pairs={{12,4},{4,8},{8,0},{0,12},{13,5},{5,9},{9,1},{1,13},{14,6},{6,10},... | collective-permute-start | bytes 6152 | tf_op jit(solution)/shard_map/ppermute | solution.py:231
  26.4 0.8 %shard_map.49 = f32[8,128]{1,0:T(8,128)S(1)} custom-call(bf16[528,256]{1,0:T(8,128)(2,1)S(1)} %collective-permute-done.1.refs_0_, bf16[256,256]{1,0:T(8,128)(2,1)S(1)} %collective-permute-done.2.refs_0_.refs_1_, bf16[272,256]{1,0:T(8,128)(2,1)S(1)} %collective-permute-done.3.refs_1_.refs_2_, bf16[528,256]{1,0:T(8,128)(2,1)S(1)} %shard_map.46.refs_2_.refs_1_.refs_3_.refs_4_, ...), custom_call_target="tpu_custom_call" | custom-call | tf_op jit(solution)/shard_map/pallas_call | solution.py:173
  27.2 0.1 collective-permute-start.8
  27.2 2.0 %collective-permute-done.9 = f32[4,128]{1,0:T(4,128)S(1)} collective-permute-done((f32[4,128]{1,0:T(4,128)S(1)}, f32[4,128]{1,0:T(4,128)S(1)}, u32[]{:S(2)}, u32[]{:S(2)}) %collective-permute-start.9) | collective-permute-done | bytes 2080 | tf_op jit(solution)/shard_map/ppermute | solution.py:231
  29.3 0.6 %maximum_bitcast_fusion = f32[512]{0:T(512)} fusion(f32[4,128]{1,0:T(4,128)S(1)} %collective-permute-done.9, f32[4,128]{1,0:T(4,128)S(1)} %collective-permute-done.8, f32[8,128]{1,0:T(8,128)S(1)} %max.15), kind=kLoop, calls=%fused_computation | loop fusion | flops 1536 | bytes 8192 | tf_op jit(solution)/shard_map/reshape | solution.py:241
  (10 shorter events, 0.1 us)
Async XLA Ops:
  3.4 18.2 %collective-permute-start.4 = (bf16[528,256]{1,0:T(8,128)(2,1)S(1)}, bf16[528,256]{1,0:T(8,128)(2,1)S(1)}, u32[]{:S(2)}, u32[]{:S(2)}) collective-permute-start(bf16[528,256]{1,0:T(8,128)(2,1)S(1)} %shard_map.46.refs_2_.refs_1_.refs_3_.refs_4_), channel_id=1, source_target_pairs={{0,1},{1,0},{2,3},{3,2},{4,5},{5,4},{6,7},{7,6},{8,9},{9,8},{10,11... | collective-permute-start | bytes 811016 | tf_op jit(solution)/shard_map/ppermute | solution.py:208
  3.9 18.5 %collective-permute-start.1 = (bf16[528,256]{1,0:T(8,128)(2,1)S(1)}, bf16[528,256]{1,0:T(8,128)(2,1)S(1)}, u32[]{:S(2)}, u32[]{:S(2)}) collective-permute-start(bf16[528,256]{1,0:T(8,128)(2,1)S(1)} %shard_map.46.refs_2_.refs_1_.refs_3_.refs_4_), channel_id=1, source_target_pairs={{4,12},{8,4},{0,8},{12,0},{5,13},{9,5},{1,9},{13,1},{6,14},{10,6},... | collective-permute-start | bytes 811016 | tf_op jit(solution)/shard_map/ppermute | solution.py:215
  7.6 11.1 %collective-permute-start.2 = (bf16[256,256]{1,0:T(8,128)(2,1)S(1)}, bf16[256,256]{1,0:T(8,128)(2,1)S(1)}, u32[]{:S(2)}, u32[]{:S(2)}) collective-permute-start(bf16[256,256]{1,0:T(8,128)(2,1)S(1)} %slice.24), channel_id=1, source_target_pairs={{8,12},{0,4},{12,8},{4,0},{9,13},{1,5},{13,9},{5,1},{10,14},{2,6},... | collective-permute-start | bytes 393224 | tf_op jit(solution)/shard_map/ppermute | solution.py:216
  9.2 12.3 %collective-permute-start.3 = (bf16[272,256]{1,0:T(8,128)(2,1)S(1)}, bf16[272,256]{1,0:T(8,128)(2,1)S(1)}, u32[]{:S(2)}, u32[]{:S(2)}) collective-permute-start(bf16[272,256]{1,0:T(8,128)(2,1)S(1)} %slice.25), channel_id=1, source_target_pairs={{8,12},{0,4},{12,8},{4,0},{9,13},{1,5},{13,9},{5,1},{10,14},{2,6},... | collective-permute-start | bytes 417800 | tf_op jit(solution)/shard_map/ppermute | solution.py:216
  9.8 8.1 %collective-permute-start = (bf16[528,256]{1,0:T(8,128)(2,1)S(1)}, bf16[528,256]{1,0:T(8,128)(2,1)S(1)}, u32[]{:S(2)}, u32[]{:S(2)}) collective-permute-start(bf16[528,256]{1,0:T(8,128)(2,1)S(1)} %get-tuple-element.65), channel_id=1, source_target_pairs={{0,2},{1,3},{2,0},{3,1},{4,6},{5,7},{6,4},{7,5},{8,10},{9,11},{10,... | collective-permute-start | bytes 811016 | tf_op jit(solution)/shard_map/while/body/ppermute | solution.py:208
  17.9 3.7 %collective-permute-start.6 = (bf16[272,256]{1,0:T(8,128)(2,1)S(1)}, bf16[272,256]{1,0:T(8,128)(2,1)S(1)}, u32[]{:S(2)}, u32[]{:S(2)}) collective-permute-start(bf16[272,256]{1,0:T(8,128)(2,1)S(1)} %slice.21), channel_id=1, source_target_pairs={{0,1},{1,0},{2,3},{3,2},{4,5},{5,4},{6,7},{7,6},{8,9},{9,8},{10,11... | collective-permute-start | bytes 417800 | tf_op jit(solution)/shard_map/ppermute | solution.py:208
  18.6 1.3 %collective-permute-start.5 = (bf16[256,256]{1,0:T(8,128)(2,1)S(1)}, bf16[256,256]{1,0:T(8,128)(2,1)S(1)}, u32[]{:S(2)}, u32[]{:S(2)}) collective-permute-start(bf16[256,256]{1,0:T(8,128)(2,1)S(1)} %slice.20), channel_id=1, source_target_pairs={{0,1},{1,0},{2,3},{3,2},{4,5},{5,4},{6,7},{7,6},{8,9},{9,8},{10,11... | collective-permute-start | bytes 393224 | tf_op jit(solution)/shard_map/ppermute | solution.py:208
  23.2 3.9 %collective-permute-start.7 = (f32[8,128]{1,0:T(8,128)S(1)}, f32[8,128]{1,0:T(8,128)S(1)}, u32[]{:S(2)}, u32[]{:S(2)}) collective-permute-start(f32[8,128]{1,0:T(8,128)S(1)} %get-tuple-element.32), channel_id=1, source_target_pairs={{0,2},{1,3},{2,0},{3,1},{4,6},{5,7},{6,4},{7,5},{8,10},{9,11},{10,... | collective-permute-start | bytes 12296 | tf_op jit(solution)/shard_map/ppermute | solution.py:208
  24.8 4.5 %collective-permute-start.9 = (f32[4,128]{1,0:T(4,128)S(1)}, f32[4,128]{1,0:T(4,128)S(1)}, u32[]{:S(2)}, u32[]{:S(2)}) collective-permute-start(f32[4,128]{1,0:T(4,128)S(1)} %get-tuple-element.33), channel_id=1, source_target_pairs={{12,4},{4,8},{8,0},{0,12},{13,5},{5,9},{9,1},{1,13},{14,6},{6,10},... | collective-permute-start | bytes 6152 | tf_op jit(solution)/shard_map/ppermute | solution.py:231
  27.2 2.1 %collective-permute-start.8 = (f32[4,128]{1,0:T(4,128)S(1)}, f32[4,128]{1,0:T(4,128)S(1)}, u32[]{:S(2)}, u32[]{:S(2)}) collective-permute-start(f32[4,128]{1,0:T(4,128)S(1)} %slice.23), channel_id=1, source_target_pairs={{0,1},{1,0},{2,3},{3,2},{4,5},{5,4},{6,7},{7,6},{8,9},{9,8},{10,11... | collective-permute-start | bytes 6152 | tf_op jit(solution)/shard_map/ppermute | solution.py:208

commit v13 on v12

--- a/solution.py
+++ b/solution.py
@@ -94,100 +94,100 @@
     )
 
 
-def score_kernel(key_parts, row_parts, bases, want_cols, own_first, unread, *refs):
+def score_kernel(key_count, cols, row_parts, own_first, unread, *refs):
     refs = list(refs[unread:])
-    key_refs = [refs.pop(0) for _ in range(key_parts)]
+    key_refs = [refs.pop(0) for _ in range(key_count)]
     row_refs = [[refs.pop(0) for _ in range(parts)] for parts in row_parts]
-    base_refs = [refs.pop(0) for _ in range(bases)]
-    col_out = refs.pop(0) if want_cols else None
+    base_ref = refs.pop(0) if own_first else None
+    col_refs = [refs.pop(0) for _ in range(cols)]
     row_outs = refs
-    key_tag_ref = key_refs[-1]
-    key_tags = key_tag_ref[key_tag_ref.shape[0] - TAG_ROWS :, :LANES].astype(jnp.float32)
-    tiles = sum(key_ref.shape[0] for key_ref in key_refs) // LANES
-    best = [jnp.full((8, LANES), ABSENT, jnp.float32) for _ in range(tiles)]
+    row_count = key_refs[0].shape[0] - TAG_ROWS
+    tiles = row_count // LANES
+    best = [
+        [jnp.full((8, LANES), ABSENT, jnp.float32) for _ in range(tiles)]
+        for _ in range(key_count if own_first else cols)
+    ]
     for block, part_refs in enumerate(row_refs):
         tag_ref = part_refs[-1]
         row_tags = tag_ref[tag_ref.shape[0] - TAG_ROWS :, :LANES].astype(jnp.float32)
         place = 0
         for part_ref in part_refs:
             count = part_ref.shape[0] // LANES * LANES
-            scores = [
-                lax.dot_general(
+            tags = [
+                jnp.broadcast_to(row_tags[at : at + 1, :], (LANES, LANES)).T
+                for at in range(place, place + count // LANES)
+            ]
+            across = [None] * len(tags)
+            for key, key_ref in enumerate(key_refs):
+                key_tags = key_ref[row_count:, :LANES].astype(jnp.float32)
+                scores = lax.dot_general(
                     part_ref[:count, :],
-                    key_ref[: key_ref.shape[0] // LANES * LANES, :],
+                    key_ref[:row_count, :],
                     (((1,), (1,)), ((), ())),
                     preferred_element_type=jnp.float32,
                 )
-                for key_ref in key_refs
-            ]
-            scores = [
-                part[:, start : start + LANES]
-                for part in scores
-                for start in range(0, part.shape[1], LANES)
-            ]
-            for start in range(0, count, LANES):
-                tags = jnp.broadcast_to(row_tags[place : place + 1, :], (LANES, LANES)).T
-                across = None
-                for at in range(tiles):
-                    same = tags == key_tags[at : at + 1, :]
-                    if own_first and block == 0 and at == place:
-                        same = same & (
-                            lax.broadcasted_iota(jnp.int32, (LANES, LANES), 0)
-                            != lax.broadcasted_iota(jnp.int32, (LANES, LANES), 1)
-                        )
-                    kept = jnp.where(same, scores[at][start : start + LANES, :], ABSENT)
-                    if want_cols or own_first:
-                        best[at] = jnp.maximum(
-                            best[at], jnp.max(kept.reshape(LANES // 8, 8, LANES), axis=0)
-                        )
-                    if not own_first:
-                        across = kept if across is None else jnp.maximum(across, kept)
-                if not own_first:
-                    at = block % 2 * tiles + place
-                    found = jnp.max(across.T, axis=0, keepdims=True)
-                    if base_refs:
-                        found = jnp.maximum(found, base_refs[block // 2][at : at + 1, :])
+                for tile, tag in enumerate(tags):
+                    for at in range(tiles):
+                        same = tag == key_tags[at : at + 1, :]
+                        if own_first and block == 0 and at == place + tile:
+                            same = same & (
+                                lax.broadcasted_iota(jnp.int32, (LANES, LANES), 0)
+                                != lax.broadcasted_iota(jnp.int32, (LANES, LANES), 1)
+                            )
+                        kept = scores[
+                            tile * LANES : (tile + 1) * LANES, at * LANES : (at + 1) * LANES
+                        ]
+                        kept = jnp.where(same, kept, ABSENT)
+                        if key < len(best):
+                            best[key][at] = jnp.maximum(
+                                best[key][at], jnp.max(kept.reshape(LANES // 8, 8, LANES), axis=0)
+                            )
+                        if not own_first:
+                            across[tile] = (
+                                kept if across[tile] is None else jnp.maximum(across[tile], kept)
+                            )
+            if not own_first:
+                for tile in range(len(tags)):
+                    at = block % 2 * tiles + place + tile
+                    found = jnp.max(across[tile].T, axis=0, keepdims=True)
                     row_outs[block // 2][at : at + 1, :] = found
-                place += 1
-    for at in range(tiles):
-        found = jnp.max(best[at], axis=0, keepdims=True)
-        if want_cols:
-            col_out[at : at + 1, :] = found
-        if own_first:
-            for base_ref in base_refs:
-                found = jnp.maximum(found, base_ref[at : at + 1, :])
-            row_outs[0][at : at + 1, :] = found
+            place += len(tags)
+    for key, found in enumerate(best):
+        for at in range(tiles):
+            highest = jnp.max(found[at], axis=0, keepdims=True)
+            if own_first:
+                row_outs[0][at : at + 1, :] = jnp.maximum(highest, base_ref[at : at + 1, :])
+            else:
+                col_refs[key][at : at + 1, :] = highest
     if own_first:
-        row_outs[0][tiles:, :] = base_refs[0][tiles:, :]
-
-
-def score(key, rows, bases=(), want_cols=True, own_first=False, after=()):
-    whole = lambda block: block if isinstance(block, tuple) else (block,)
-    key, parts = whole(key), [whole(row) for row in rows]
-    blocks = [part for row in parts for part in row]
-    tiles = sum(part.shape[0] for part in key) // LANES
+        row_outs[0][tiles:, :] = base_ref[tiles:, :]
+
+
+def score(keys, rows, cols=0, base=None, after=()):
+    parts = [row if isinstance(row, tuple) else (row,) for row in rows]
+    operands = [*keys, *(part for row in parts for part in row)]
+    operands += [] if base is None else [base]
+    tiles = keys[0].shape[0] // LANES
     best = jax.ShapeDtypeStruct((tiles, LANES), jnp.float32)
     pair = jax.ShapeDtypeStruct((2 * tiles, LANES), jnp.float32)
-    out_shape = [best] * want_cols + [pair] * (1 if own_first else len(rows) // 2)
+    out_shape = [best] * cols + [pair] * (len(rows) // 2 if base is None else 1)
     inside = pl.BlockSpec(memory_space=pltpu.VMEM)
     found = pl.pallas_call(
         functools.partial(
             score_kernel,
-            len(key),
+            len(keys),
+            cols,
             [len(row) for row in parts],
-            len(bases),
-            want_cols,
-            own_first,
+            base is not None,
             len(after),
         ),
-        in_specs=[pl.BlockSpec(memory_space=pl.ANY)] * len(after)
-        + [inside] * (len(key) + len(blocks) + len(bases)),
+        in_specs=[pl.BlockSpec(memory_space=pl.ANY)] * len(after) + [inside] * len(operands),
         out_specs=[inside] * len(out_shape),
         out_shape=out_shape,
         compiler_params=pltpu.CompilerParams(vmem_limit_bytes=VMEM_LIMIT),
         cost_estimate=pl.CostEstimate(flops=0, bytes_accessed=0, transcendentals=0),
-    )(*after, *key, *blocks, *bases)
-    return list(found[:want_cols]), list(found[want_cols:])
+    )(*after, *operands)
+    return list(found[:cols]), list(found[cols:])
 
 
 def owner_steps(count):
@@ -213,7 +213,7 @@
     own = project(embeddings, basis, owner_ids, sub_cluster)
     *steps, last = owner_steps(owner_count)
     keys = [lax.ppermute(own, "owners", step) for step in steps]
-    nearby = tuple(lax.ppermute(part, "owners", last) for part in halves(own))
+    nearby = lax.ppermute(own, "owners", last)
     offsets = range(2, split_count, 2)
     besides = lax.fori_loop(
         0,
@@ -224,15 +224,13 @@
     rows = [own, swap(own, 1)]
     for beside in besides:
         rows += [beside, tuple(swap(part, 1) for part in halves(beside))]
-    _, row_best = score(nearby, rows, want_cols=False)
-    backs = []
-    for key, step in zip(keys, steps):
-        (found,), row_best = score(key, rows, row_best)
-        backs.append(lax.ppermute(found, "owners", [(b, a) for a, b in step]))
+    col_best, row_best = score([*keys, nearby], rows, cols=len(keys))
+    backs = [
+        lax.ppermute(found, "owners", [(b, a) for a, b in step])
+        for found, step in zip(col_best, steps)
+    ]
     others = [swap(found, 2 * at) for at, found in enumerate(row_best) if at]
-    _, (local,) = score(
-        own, rows, row_best[:1], want_cols=False, own_first=True, after=[*keys, *nearby]
-    )
+    _, (local,) = score([own], rows, base=row_best[0], after=[nearby, *keys])
     for other in others:
         local = jnp.maximum(local, other)
     best = jnp.maximum(local[:tiles], swap(local[tiles:], 1))

time: 30 us -> 29.8 us (level)
  starting transfers between devices: 11.2 us -> 12 us
  waiting for transfers between devices: 12.1 us -> 11.3 us
    ppermute x3 -> x2, waiting for transfers between devices: 4.23 us -> 3.49 us  [the longest x1 2.34 us: per_device(): nearby = lax.ppermute(own, 'owners', last)]
    ppermute x6, starting transfers between devices: 3.78 us -> 4.33 us  [swap(): lax.ppermute(block, 'split', [(s, s ^ offset) for s in range(split_count)])]
    ppermute x3 -> x2, starting transfers between devices: 3.74 us -> 4.03 us  [the longest x1 2.45 us: per_device(): lax.ppermute(found, 'owners', [(b, a) for a, b in step])]
    pallas_call x3 -> x2, Pallas kernels: 2.42 us -> 2.19 us  [score(): pl.pallas_call(functools.partial(score_kernel, len(keys), cols, [len(row)...]
  transfers between devices with their start and end apart: 10 -> 9, of which waited for: 5 -> 4; matrix products, arithmetic and copies ran while one was open for 0% -> 0% of each run, Pallas kernels for 5% -> 3%
where the time goes in v13:
time: 29.8 us; the launch traced here: 29.6 us
  starting transfers between devices  12 us (40%)
  waiting for transfers between devices  11.3 us (38%)
  Pallas kernels  5.57 us (19%)
  other arithmetic  0.59 us (2%)
    ppermute x6, waiting for transfers between devices, swap(): lax.ppermute(block, 'split', [(s, s ^ offset) for s in range(split_count)])  7.78 us
    ppermute x6, starting transfers between devices, swap(): lax.ppermute(block, 'split', [(s, s ^ offset) for s in range(split_count)])  4.33 us
    ppermute x1, starting transfers between devices, per_device(): keys = [lax.ppermute(own, 'owners', step) for step in steps]  3.65 us
    pallas_call x1, Pallas kernels, project(): pl.pallas_call(project_kernel, in_specs=[pl.BlockSpec(memory_space=pltpu....  3.38 us
    ppermute x1, starting transfers between devices, per_device(): lax.ppermute(found, 'owners', [(b, a) for a, b in step])  2.45 us
    ppermute x1, waiting for transfers between devices, per_device(): nearby = lax.ppermute(own, 'owners', last)  2.34 us
    pallas_call x2, Pallas kernels, score(): pl.pallas_call(functools.partial(score_kernel, len(keys), cols, [len(row)...  2.19 us
    ppermute x1, starting transfers between devices, per_device(): nearby = lax.ppermute(own, 'owners', last)  1.58 us
  transfers between devices with their start and end apart: 9, of which 4 were waited for; matrix products, arithmetic and copies ran while one was open for 0% of the time, Pallas kernels for 3%

profile of v13, /device:TPU:0, one launch (start us, length us, event | category | flops | bytes accessed | tf_op | source)
XLA Modules:
  0.0 29.6 jit_solution(1431134355946515557)
XLA Ops:
  0.0 3.4 %shard_map.46.refs_2_.refs_3_ = bf16[528,256]{1,0:T(8,128)(2,1)S(1)} custom-call(bf16[512,4096]{1,0:T(8,128)(2,1)} %source_hbm.1, bf16[4096,256]{1,0:T(8,128)(2,1)} %basis_hbm.1, s32[4,128]{1,0:T(4,128)} %bitcast.4, s32[4,128]{1,0:T(4,128)} %bitcast.5), custom_call_target="tpu_custom_call" | custom-call | flops 1073741824 | bytes 6291456 | tf_op jit(solution)/shard_map/pallas_call | solution.py:65
  3.4 0.5 %collective-permute-start.3 = (bf16[528,256]{1,0:T(8,128)(2,1)S(1)}, bf16[528,256]{1,0:T(8,128)(2,1)S(1)}, u32[]{:S(2)}, u32[]{:S(2)}) collective-permute-start(bf16[528,256]{1,0:T(8,128)(2,1)S(1)} %shard_map.46.refs_2_.refs_3_), channel_id=1, source_target_pairs={{0,1},{1,0},{2,3},{3,2},{4,5},{5,4},{6,7},{7,6},{8,9},{9,8},{10,11... | collective-permute-start | bytes 811016 | tf_op jit(solution)/shard_map/ppermute | solution.py:208
  3.9 3.6 %collective-permute-start.2 = (bf16[528,256]{1,0:T(8,128)(2,1)S(1)}, bf16[528,256]{1,0:T(8,128)(2,1)S(1)}, u32[]{:S(2)}, u32[]{:S(2)}) collective-permute-start(bf16[528,256]{1,0:T(8,128)(2,1)S(1)} %shard_map.46.refs_2_.refs_3_), channel_id=1, source_target_pairs={{4,12},{8,4},{0,8},{12,0},{5,13},{9,5},{1,9},{13,1},{6,14},{10,6},... | collective-permute-start | bytes 811016 | tf_op jit(solution)/shard_map/ppermute | solution.py:215
  7.6 1.6 %collective-permute-start.1 = (bf16[528,256]{1,0:T(8,128)(2,1)S(1)}, bf16[528,256]{1,0:T(8,128)(2,1)S(1)}, u32[]{:S(2)}, u32[]{:S(2)}) collective-permute-start(bf16[528,256]{1,0:T(8,128)(2,1)S(1)} %shard_map.46.refs_2_.refs_3_), channel_id=1, source_target_pairs={{8,12},{0,4},{12,8},{4,0},{9,13},{1,5},{13,9},{5,1},{10,14},{2,6},... | collective-permute-start | bytes 811016 | tf_op jit(solution)/shard_map/ppermute | solution.py:216
  9.2 8.4 %while.10 = (s32[]{:T(128)}, bf16[528,256]{1,0:T(8,128)(2,1)S(1)}, s32[]{:T(128)}, s32[]{:T(128)}) while((s32[]{:T(128)}, bf16[528,256]{1,0:T(8,128)(2,1)S(1)}, s32[]{:T(128)}, s32[]{:T(128)}) %tuple.18), condition=%wide.region_1.0_spmd, body=%wide.region_0.0_spmd.sunk | while | flops 2 | bytes 1622109 | solution.py:218
  9.2 1.6 %collective-permute-start = (bf16[528,256]{1,0:T(8,128)(2,1)S(1)}, bf16[528,256]{1,0:T(8,128)(2,1)S(1)}, u32[]{:S(2)}, u32[]{:S(2)}) collective-permute-start(bf16[528,256]{1,0:T(8,128)(2,1)S(1)} %get-tuple-element.61), channel_id=1, source_target_pairs={{0,2},{1,3},{2,0},{3,1},{4,6},{5,7},{6,4},{7,5},{8,10},{9,11},{10,... | collective-permute-start | bytes 811016 | tf_op jit(solution)/shard_map/while/body/ppermute | solution.py:208
  10.7 6.8 %collective-permute-done = bf16[528,256]{1,0:T(8,128)(2,1)S(1)} collective-permute-done((bf16[528,256]{1,0:T(8,128)(2,1)S(1)}, bf16[528,256]{1,0:T(8,128)(2,1)S(1)}, u32[]{:S(2)}, u32[]{:S(2)}) %collective-permute-start) | collective-permute-done | bytes 270368 | tf_op jit(solution)/shard_map/while/body/ppermute | solution.py:208
  17.6 0.1 collective-permute-start.5
  17.7 0.6 %collective-permute-start.4 = (bf16[256,256]{1,0:T(8,128)(2,1)S(1)}, bf16[256,256]{1,0:T(8,128)(2,1)S(1)}, u32[]{:S(2)}, u32[]{:S(2)}) collective-permute-start(bf16[256,256]{1,0:T(8,128)(2,1)S(1)} %slice.12), channel_id=1, source_target_pairs={{0,1},{1,0},{2,3},{3,2},{4,5},{5,4},{6,7},{7,6},{8,9},{9,8},{10,11... | collective-permute-start | bytes 393224 | tf_op jit(solution)/shard_map/ppermute | solution.py:208
  18.2 1.0 %collective-permute-done.4.refs_5_.refs_6_ = bf16[256,256]{1,0:T(8,128)(2,1)S(1)} collective-permute-done((bf16[256,256]{1,0:T(8,128)(2,1)S(1)}, bf16[256,256]{1,0:T(8,128)(2,1)S(1)}, u32[]{:S(2)}, u32[]{:S(2)}) %collective-permute-start.4) | collective-permute-done | bytes 131104 | tf_op jit(solution)/shard_map/ppermute | solution.py:208
  19.2 0.0 collective-permute-done.5.refs_6_.refs_7_
  19.2 0.0 collective-permute-done.3.refs_3_.refs_4_
  19.2 0.0 collective-permute-done.2.refs_0_.refs_1_
  19.2 2.3 %collective-permute-done.1.refs_1_.refs_0_ = bf16[528,256]{1,0:T(8,128)(2,1)S(1)} collective-permute-done((bf16[528,256]{1,0:T(8,128)(2,1)S(1)}, bf16[528,256]{1,0:T(8,128)(2,1)S(1)}, u32[]{:S(2)}, u32[]{:S(2)}) %collective-permute-start.1) | collective-permute-done | bytes 270368 | tf_op jit(solution)/shard_map/ppermute | solution.py:216
  21.5 1.4 %shard_map.47 = (f32[4,128]{1,0:T(4,128)S(1)}, f32[8,128]{1,0:T(8,128)S(1)}, f32[8,128]{1,0:T(8,128)S(1)}) custom-call(bf16[528,256]{1,0:T(8,128)(2,1)S(1)} %collective-permute-done.2.refs_0_.refs_1_, bf16[528,256]{1,0:T(8,128)(2,1)S(1)} %collective-permute-done.1.refs_1_.refs_0_, bf16[528,256]{1,0:T(8,128)(2,1)S(1)} %shard_map.46.refs_2_.refs_3_, ...), custom_call_target="tpu_custom_call" | custom-call | tf_op jit(solution)/shard_map/pallas_call | solution.py:175
  23.0 1.6 %collective-permute-start.6 = (f32[8,128]{1,0:T(8,128)S(1)}, f32[8,128]{1,0:T(8,128)S(1)}, u32[]{:S(2)}, u32[]{:S(2)}) collective-permute-start(f32[8,128]{1,0:T(8,128)S(1)} %get-tuple-element.28), channel_id=1, source_target_pairs={{0,2},{1,3},{2,0},{3,1},{4,6},{5,7},{6,4},{7,5},{8,10},{9,11},{10,... | collective-permute-start | bytes 12296 | tf_op jit(solution)/shard_map/ppermute | solution.py:208
  24.5 2.5 %collective-permute-start.8 = (f32[4,128]{1,0:T(4,128)S(1)}, f32[4,128]{1,0:T(4,128)S(1)}, u32[]{:S(2)}, u32[]{:S(2)}) collective-permute-start(f32[4,128]{1,0:T(4,128)S(1)} %get-tuple-element.29), channel_id=1, source_target_pairs={{12,4},{4,8},{8,0},{0,12},{13,5},{5,9},{9,1},{1,13},{14,6},{6,10},... | collective-permute-start | bytes 6152 | tf_op jit(solution)/shard_map/ppermute | solution.py:229
  27.0 0.8 %shard_map.48 = f32[8,128]{1,0:T(8,128)S(1)} custom-call(bf16[528,256]{1,0:T(8,128)(2,1)S(1)} %collective-permute-done.1.refs_1_.refs_0_, bf16[528,256]{1,0:T(8,128)(2,1)S(1)} %collective-permute-done.2.refs_0_.refs_1_, bf16[528,256]{1,0:T(8,128)(2,1)S(1)} %shard_map.46.refs_2_.refs_3_, bf16[528,256]{1,0:T(8,128)(2,1)S(1)} %shard_map.46.refs_2_.refs_3_, ...), custom_call_target="tpu_custom_call" | custom-call | tf_op jit(solution)/shard_map/pallas_call | solution.py:175
  27.8 0.0 collective-permute-done.6
  27.8 0.1 collective-permute-start.7
  27.9 1.2 %collective-permute-done.8 = f32[4,128]{1,0:T(4,128)S(1)} collective-permute-done((f32[4,128]{1,0:T(4,128)S(1)}, f32[4,128]{1,0:T(4,128)S(1)}, u32[]{:S(2)}, u32[]{:S(2)}) %collective-permute-start.8) | collective-permute-done | bytes 2080 | tf_op jit(solution)/shard_map/ppermute | solution.py:229
  29.0 0.0 collective-permute-done.7
  29.0 0.6 %maximum_bitcast_fusion = f32[512]{0:T(512)} fusion(f32[4,128]{1,0:T(4,128)S(1)} %collective-permute-done.8, f32[4,128]{1,0:T(4,128)S(1)} %collective-permute-done.7, f32[8,128]{1,0:T(8,128)S(1)} %max.15), kind=kLoop, calls=%fused_computation | loop fusion | flops 1536 | bytes 8192 | tf_op jit(solution)/shard_map/reshape | solution.py:239
  (6 shorter events, 0.1 us)
Async XLA Ops:
  3.4 15.8 %collective-permute-start.3 = (bf16[528,256]{1,0:T(8,128)(2,1)S(1)}, bf16[528,256]{1,0:T(8,128)(2,1)S(1)}, u32[]{:S(2)}, u32[]{:S(2)}) collective-permute-start(bf16[528,256]{1,0:T(8,128)(2,1)S(1)} %shard_map.46.refs_2_.refs_3_), channel_id=1, source_target_pairs={{0,1},{1,0},{2,3},{3,2},{4,5},{5,4},{6,7},{7,6},{8,9},{9,8},{10,11... | collective-permute-start | bytes 811016 | tf_op jit(solution)/shard_map/ppermute | solution.py:208
  3.9 15.3 %collective-permute-start.2 = (bf16[528,256]{1,0:T(8,128)(2,1)S(1)}, bf16[528,256]{1,0:T(8,128)(2,1)S(1)}, u32[]{:S(2)}, u32[]{:S(2)}) collective-permute-start(bf16[528,256]{1,0:T(8,128)(2,1)S(1)} %shard_map.46.refs_2_.refs_3_), channel_id=1, source_target_pairs={{4,12},{8,4},{0,8},{12,0},{5,13},{9,5},{1,9},{13,1},{6,14},{10,6},... | collective-permute-start | bytes 811016 | tf_op jit(solution)/shard_map/ppermute | solution.py:215
  7.6 14.0 %collective-permute-start.1 = (bf16[528,256]{1,0:T(8,128)(2,1)S(1)}, bf16[528,256]{1,0:T(8,128)(2,1)S(1)}, u32[]{:S(2)}, u32[]{:S(2)}) collective-permute-start(bf16[528,256]{1,0:T(8,128)(2,1)S(1)} %shard_map.46.refs_2_.refs_3_), channel_id=1, source_target_pairs={{8,12},{0,4},{12,8},{4,0},{9,13},{1,5},{13,9},{5,1},{10,14},{2,6},... | collective-permute-start | bytes 811016 | tf_op jit(solution)/shard_map/ppermute | solution.py:216
  9.2 8.3 %collective-permute-start = (bf16[528,256]{1,0:T(8,128)(2,1)S(1)}, bf16[528,256]{1,0:T(8,128)(2,1)S(1)}, u32[]{:S(2)}, u32[]{:S(2)}) collective-permute-start(bf16[528,256]{1,0:T(8,128)(2,1)S(1)} %get-tuple-element.61), channel_id=1, source_target_pairs={{0,2},{1,3},{2,0},{3,1},{4,6},{5,7},{6,4},{7,5},{8,10},{9,11},{10,... | collective-permute-start | bytes 811016 | tf_op jit(solution)/shard_map/while/body/ppermute | solution.py:208
  17.6 1.6 %collective-permute-start.5 = (bf16[272,256]{1,0:T(8,128)(2,1)S(1)}, bf16[272,256]{1,0:T(8,128)(2,1)S(1)}, u32[]{:S(2)}, u32[]{:S(2)}) collective-permute-start(bf16[272,256]{1,0:T(8,128)(2,1)S(1)} %slice.13), channel_id=1, source_target_pairs={{0,1},{1,0},{2,3},{3,2},{4,5},{5,4},{6,7},{7,6},{8,9},{9,8},{10,11... | collective-permute-start | bytes 417800 | tf_op jit(solution)/shard_map/ppermute | solution.py:208
  17.7 1.5 %collective-permute-start.4 = (bf16[256,256]{1,0:T(8,128)(2,1)S(1)}, bf16[256,256]{1,0:T(8,128)(2,1)S(1)}, u32[]{:S(2)}, u32[]{:S(2)}) collective-permute-start(bf16[256,256]{1,0:T(8,128)(2,1)S(1)} %slice.12), channel_id=1, source_target_pairs={{0,1},{1,0},{2,3},{3,2},{4,5},{5,4},{6,7},{7,6},{8,9},{9,8},{10,11... | collective-permute-start | bytes 393224 | tf_op jit(solution)/shard_map/ppermute | solution.py:208
  23.0 4.8 %collective-permute-start.6 = (f32[8,128]{1,0:T(8,128)S(1)}, f32[8,128]{1,0:T(8,128)S(1)}, u32[]{:S(2)}, u32[]{:S(2)}) collective-permute-start(f32[8,128]{1,0:T(8,128)S(1)} %get-tuple-element.28), channel_id=1, source_target_pairs={{0,2},{1,3},{2,0},{3,1},{4,6},{5,7},{6,4},{7,5},{8,10},{9,11},{10,... | collective-permute-start | bytes 12296 | tf_op jit(solution)/shard_map/ppermute | solution.py:208
  24.5 4.5 %collective-permute-start.8 = (f32[4,128]{1,0:T(4,128)S(1)}, f32[4,128]{1,0:T(4,128)S(1)}, u32[]{:S(2)}, u32[]{:S(2)}) collective-permute-start(f32[4,128]{1,0:T(4,128)S(1)} %get-tuple-element.29), channel_id=1, source_target_pairs={{12,4},{4,8},{8,0},{0,12},{13,5},{5,9},{9,1},{1,13},{14,6},{6,10},... | collective-permute-start | bytes 6152 | tf_op jit(solution)/shard_map/ppermute | solution.py:229
  27.8 1.2 %collective-permute-start.7 = (f32[4,128]{1,0:T(4,128)S(1)}, f32[4,128]{1,0:T(4,128)S(1)}, u32[]{:S(2)}, u32[]{:S(2)}) collective-permute-start(f32[4,128]{1,0:T(4,128)S(1)} %slice.15), channel_id=1, source_target_pairs={{0,1},{1,0},{2,3},{3,2},{4,5},{5,4},{6,7},{7,6},{8,9},{9,8},{10,11... | collective-permute-start | bytes 6152 | tf_op jit(solution)/shard_map/ppermute | solution.py:208

commit v14 on v13

--- a/solution.py
+++ b/solution.py
@@ -94,10 +94,11 @@
     )
 
 
-def score_kernel(key_count, cols, row_parts, own_first, unread, *refs):
-    refs = list(refs[unread:])
+def score_kernel(key_count, cols, row_parts, known, own_first, *refs):
+    refs = list(refs)
     key_refs = [refs.pop(0) for _ in range(key_count)]
     row_refs = [[refs.pop(0) for _ in range(parts)] for parts in row_parts]
+    known_refs = [refs.pop(0) for _ in range(known)]
     base_ref = refs.pop(0) if own_first else None
     col_refs = [refs.pop(0) for _ in range(cols)]
     row_outs = refs
@@ -150,6 +151,8 @@
                 for tile in range(len(tags)):
                     at = block % 2 * tiles + place + tile
                     found = jnp.max(across[tile].T, axis=0, keepdims=True)
+                    if known_refs:
+                        found = jnp.maximum(found, known_refs[block // 2][at : at + 1, :])
                     row_outs[block // 2][at : at + 1, :] = found
             place += len(tags)
     for key, found in enumerate(best):
@@ -163,10 +166,10 @@
         row_outs[0][tiles:, :] = base_ref[tiles:, :]
 
 
-def score(keys, rows, cols=0, base=None, after=()):
+def score(keys, rows, cols=0, known=(), base=None):
     parts = [row if isinstance(row, tuple) else (row,) for row in rows]
     operands = [*keys, *(part for row in parts for part in row)]
-    operands += [] if base is None else [base]
+    operands += known if base is None else [base]
     tiles = keys[0].shape[0] // LANES
     best = jax.ShapeDtypeStruct((tiles, LANES), jnp.float32)
     pair = jax.ShapeDtypeStruct((2 * tiles, LANES), jnp.float32)
@@ -178,15 +181,15 @@
             len(keys),
             cols,
             [len(row) for row in parts],
+            len(known),
             base is not None,
-            len(after),
         ),
-        in_specs=[pl.BlockSpec(memory_space=pl.ANY)] * len(after) + [inside] * len(operands),
+        in_specs=[inside] * len(operands),
         out_specs=[inside] * len(out_shape),
         out_shape=out_shape,
         compiler_params=pltpu.CompilerParams(vmem_limit_bytes=VMEM_LIMIT),
         cost_estimate=pl.CostEstimate(flops=0, bytes_accessed=0, transcendentals=0),
-    )(*after, *operands)
+    )(*operands)
     return list(found[:cols]), list(found[cols:])
 
 
@@ -194,7 +197,7 @@
     half = count // 2
     circle = [count - 1 - 2 * i for i in range(half)] + [count - 2 - 2 * i for i in range(half)]
     return [
-        [(circle[(i + step) % count], circle[i]) for i in range(count)]
+        [(circle[i], circle[(i + step) % count]) for i in range(count)]
         for step in range(1, half + 1)
     ]
 
@@ -215,25 +218,31 @@
     keys = [lax.ppermute(own, "owners", step) for step in steps]
     nearby = lax.ppermute(own, "owners", last)
     offsets = range(2, split_count, 2)
+    one_turn = 1 + (lax.axis_index("groups") >> 16)
     besides = lax.fori_loop(
         0,
-        1 + (lax.axis_index("groups") >> 16),
+        one_turn,
         lambda _, blocks: [swap(block, offset) for block, offset in zip(blocks, offsets)],
         [own] * len(offsets),
     )
     rows = [own, swap(own, 1)]
     for beside in besides:
         rows += [beside, tuple(swap(part, 1) for part in halves(beside))]
-    col_best, row_best = score([*keys, nearby], rows, cols=len(keys))
-    backs = [
-        lax.ppermute(found, "owners", [(b, a) for a, b in step])
-        for found, step in zip(col_best, steps)
-    ]
-    others = [swap(found, 2 * at) for at, found in enumerate(row_best) if at]
-    _, (local,) = score([own], rows, base=row_best[0], after=[nearby, *keys])
-    for other in others:
-        local = jnp.maximum(local, other)
-    best = jnp.maximum(local[:tiles], swap(local[tiles:], 1))
+    _, row_best = score([nearby], rows)
+    backs = []
+    for key, step in zip(keys, steps):
+        (found,), row_best = score([key], rows, cols=1, known=row_best)
+        backs.append(lax.ppermute(found, "owners", [(b, a) for a, b in step]))
+
+    def exchange_split(_, carried):
+        (first, *more), _ = carried
+        more = [swap(found, offset) for found, offset in zip(more, offsets)]
+        _, (local,) = score([own], rows, base=first)
+        for other in more:
+            local = jnp.maximum(local, other)
+        return [local, *more], jnp.maximum(local[:tiles], swap(local[tiles:], 1))
+
+    _, best = lax.fori_loop(0, one_turn, exchange_split, (row_best, row_best[0][:tiles]))
     for back in backs:
         best = jnp.maximum(best, back)
     return jnp.maximum(best, -1.0).reshape(row_count)

time: 29.8 us -> 31.9 us (1.070)
  other arithmetic: 0.59 us -> 1.8 us
  waiting for transfers between devices: 11.3 us -> 12.5 us
  starting transfers between devices: 12 us -> 10.9 us
  local copies, waits for them, and re-layouts: 0.06 us -> 0.64 us
    ppermute x6, waiting for transfers between devices: 7.78 us -> 10.6 us  [swap(): lax.ppermute(block, 'split', [(s, s ^ offset) for s in range(split_count)])]
    ppermute x1, waiting for transfers between devices: 2.34 us -> 0.01 us  [per_device(): nearby = lax.ppermute(own, 'owners', last)]
    ppermute x1, waiting for transfers between devices: 0.01 us -> 1.9 us  [per_device(): keys = [lax.ppermute(own, 'owners', step) for step in steps]]
    ppermute x1, starting transfers between devices: 1.58 us -> 3.09 us  [per_device(): nearby = lax.ppermute(own, 'owners', last)]
    ppermute x1, starting transfers between devices: 3.65 us -> 2.47 us  [per_device(): keys = [lax.ppermute(own, 'owners', step) for step in steps]]
    ppermute x1, waiting for transfers between devices: 1.16 us -> 0.01 us  [per_device(): backs.append(lax.ppermute(found, 'owners', [(b, a) for a, b in step]))]
    ppermute x1, starting transfers between devices: 2.45 us -> 1.64 us  [per_device(): backs.append(lax.ppermute(found, 'owners', [(b, a) for a, b in step]))]
    reshape x1, other arithmetic: 0.58 us -> 1.24 us  [per_device(): return jnp.maximum(best, -1.0).reshape(row_count)]
  transfers between devices with their start and end apart: 9 -> 9, of which waited for: 4 -> 5; matrix products, arithmetic and copies ran while one was open for 0% -> 2% of each run, Pallas kernels for 3% -> 5%
where the time goes in v14:
time: 31.9 us; the launch traced here: 31.7 us
  waiting for transfers between devices  12.5 us (39%)
  starting transfers between devices  10.9 us (34%)
  Pallas kernels  5.82 us (18%)
  other arithmetic  1.8 us (6%)
  local copies, waits for them, and re-layouts  0.64 us (2%)
    ppermute x6, waiting for transfers between devices, swap(): lax.ppermute(block, 'split', [(s, s ^ offset) for s in range(split_count)])  10.6 us
    ppermute x6, starting transfers between devices, swap(): lax.ppermute(block, 'split', [(s, s ^ offset) for s in range(split_count)])  3.68 us
    pallas_call x1, Pallas kernels, project(): pl.pallas_call(project_kernel, in_specs=[pl.BlockSpec(memory_space=pltpu....  3.38 us
    ppermute x1, starting transfers between devices, per_device(): nearby = lax.ppermute(own, 'owners', last)  3.09 us
    ppermute x1, starting transfers between devices, per_device(): keys = [lax.ppermute(own, 'owners', step) for step in steps]  2.47 us
    pallas_call x3, Pallas kernels, score(): pl.pallas_call(functools.partial(score_kernel, len(keys), cols, [len(row)...  2.44 us
    ppermute x1, waiting for transfers between devices, per_device(): keys = [lax.ppermute(own, 'owners', step) for step in steps]  1.9 us
    ppermute x1, starting transfers between devices, per_device(): backs.append(lax.ppermute(found, 'owners', [(b, a) for a, b in step]))  1.64 us
  transfers between devices with their start and end apart: 9, of which 5 were waited for; matrix products, arithmetic and copies ran while one was open for 2% of the time, Pallas kernels for 5%

profile of v14, /device:TPU:0, one launch (start us, length us, event | category | flops | bytes accessed | tf_op | source)
XLA Modules:
  0.0 31.7 jit_solution(12842764732744157165)
XLA Ops:
  0.0 3.4 %shard_map.46.refs_1_ = bf16[528,256]{1,0:T(8,128)(2,1)S(1)} custom-call(bf16[512,4096]{1,0:T(8,128)(2,1)} %source_hbm.1, bf16[4096,256]{1,0:T(8,128)(2,1)} %basis_hbm.1, s32[4,128]{1,0:T(4,128)} %bitcast.4, s32[4,128]{1,0:T(4,128)} %bitcast.5), custom_call_target="tpu_custom_call" | custom-call | flops 1073741824 | bytes 6291456 | tf_op jit(solution)/shard_map/pallas_call | solution.py:65
  3.4 3.1 %collective-permute-start.7 = (bf16[528,256]{1,0:T(8,128)(2,1)S(1)}, bf16[528,256]{1,0:T(8,128)(2,1)S(1)}, u32[]{:S(2)}, u32[]{:S(2)}) collective-permute-start(bf16[528,256]{1,0:T(8,128)(2,1)S(1)} %shard_map.46.refs_1_), channel_id=1, source_target_pairs={{12,8},{4,0},{8,12},{0,4},{13,9},{5,1},{9,13},{1,5},{14,10},{6,2},... | collective-permute-start | bytes 811016 | tf_op jit(solution)/shard_map/ppermute | solution.py:219
  6.5 2.5 %collective-permute-start.3 = (bf16[528,256]{1,0:T(8,128)(2,1)S(1)}, bf16[528,256]{1,0:T(8,128)(2,1)S(1)}, u32[]{:S(2)}, u32[]{:S(2)}) collective-permute-start(bf16[528,256]{1,0:T(8,128)(2,1)S(1)} %shard_map.46.refs_1_), channel_id=1, source_target_pairs={{12,4},{4,8},{8,0},{0,12},{13,5},{5,9},{9,1},{1,13},{14,6},{6,10},... | collective-permute-start | bytes 811016 | tf_op jit(solution)/shard_map/ppermute | solution.py:218
  9.0 8.7 %while.24 = (s32[]{:T(128)}, bf16[528,256]{1,0:T(8,128)(2,1)S(1)}, s32[]{:T(128)}, s32[]{:T(128)}) while((s32[]{:T(128)}, bf16[528,256]{1,0:T(8,128)(2,1)S(1)}, s32[]{:T(128)}, s32[]{:T(128)}) %tuple.31), condition=%wide.region_1.0_spmd, body=%wide.region_0.0_spmd.sunk | while | flops 2 | bytes 1622109 | solution.py:222
  9.0 1.6 %collective-permute-start = (bf16[528,256]{1,0:T(8,128)(2,1)S(1)}, bf16[528,256]{1,0:T(8,128)(2,1)S(1)}, u32[]{:S(2)}, u32[]{:S(2)}) collective-permute-start(bf16[528,256]{1,0:T(8,128)(2,1)S(1)} %get-tuple-element.198), channel_id=1, source_target_pairs={{0,2},{1,3},{2,0},{3,1},{4,6},{5,7},{6,4},{7,5},{8,10},{9,11},{10,... | collective-permute-start | bytes 811016 | tf_op jit(solution)/shard_map/while/body/ppermute | solution.py:211
  10.6 7.1 %collective-permute-done = bf16[528,256]{1,0:T(8,128)(2,1)S(1)} collective-permute-done((bf16[528,256]{1,0:T(8,128)(2,1)S(1)}, bf16[528,256]{1,0:T(8,128)(2,1)S(1)}, u32[]{:S(2)}, u32[]{:S(2)}) %collective-permute-start) | collective-permute-done | bytes 270368 | tf_op jit(solution)/shard_map/while/body/ppermute | solution.py:211
  17.7 0.1 collective-permute-start.6
  17.8 0.6 %collective-permute-start.5 = (bf16[256,256]{1,0:T(8,128)(2,1)S(1)}, bf16[256,256]{1,0:T(8,128)(2,1)S(1)}, u32[]{:S(2)}, u32[]{:S(2)}) collective-permute-start(bf16[256,256]{1,0:T(8,128)(2,1)S(1)} %slice.15), channel_id=1, source_target_pairs={{0,1},{1,0},{2,3},{3,2},{4,5},{5,4},{6,7},{7,6},{8,9},{9,8},{10,11... | collective-permute-start | bytes 393224 | tf_op jit(solution)/shard_map/ppermute | solution.py:211
  18.4 1.0 %collective-permute-done.5.refs_4_ = bf16[256,256]{1,0:T(8,128)(2,1)S(1)} collective-permute-done((bf16[256,256]{1,0:T(8,128)(2,1)S(1)}, bf16[256,256]{1,0:T(8,128)(2,1)S(1)}, u32[]{:S(2)}, u32[]{:S(2)}) %collective-permute-start.5) | collective-permute-done | bytes 131104 | tf_op jit(solution)/shard_map/ppermute | solution.py:211
  19.4 0.0 collective-permute-done.7.refs_0_
  19.4 0.0 collective-permute-done.4.refs_2_
  19.4 0.8 %shard_map.47 = (f32[8,128]{1,0:T(8,128)S(1)}, f32[8,128]{1,0:T(8,128)S(1)}) custom-call(bf16[528,256]{1,0:T(8,128)(2,1)S(1)} %collective-permute-done.7.refs_0_, bf16[528,256]{1,0:T(8,128)(2,1)S(1)} %shard_map.46.refs_1_, bf16[528,256]{1,0:T(8,128)(2,1)S(1)} %collective-permute-done.4.refs_2_, bf16[528,256]{1,0:T(8,128)(2,1)S(1)} %get-tuple-element.212.refs_3_, ...), custom_call_target="tpu_custom_call" | custom-call | tf_op jit(solution)/shard_map/pallas_call | solution.py:178
  20.2 1.9 %collective-permute-done.3.refs_0_ = bf16[528,256]{1,0:T(8,128)(2,1)S(1)} collective-permute-done((bf16[528,256]{1,0:T(8,128)(2,1)S(1)}, bf16[528,256]{1,0:T(8,128)(2,1)S(1)}, u32[]{:S(2)}, u32[]{:S(2)}) %collective-permute-start.3) | collective-permute-done | bytes 270368 | tf_op jit(solution)/shard_map/ppermute | solution.py:218
  22.1 0.8 %shard_map.48 = (f32[4,128]{1,0:T(4,128)S(1)}, f32[8,128]{1,0:T(8,128)S(1)}, f32[8,128]{1,0:T(8,128)S(1)}) custom-call(bf16[528,256]{1,0:T(8,128)(2,1)S(1)} %collective-permute-done.3.refs_0_, bf16[528,256]{1,0:T(8,128)(2,1)S(1)} %shard_map.46.refs_1_, bf16[528,256]{1,0:T(8,128)(2,1)S(1)} %collective-permute-done.4.refs_2_, ...), custom_call_target="tpu_custom_call" | custom-call | tf_op jit(solution)/shard_map/pallas_call | solution.py:178
  23.0 0.6 %slice.17 = f32[4,128]{1,0:T(4,128)} slice(f32[8,128]{1,0:T(8,128)S(1)} %get-tuple-element.206), slice={[0:4], [0:128]} | slice | bytes 4096 | tf_op jit(solution)/shard_map/slice | solution.py:245
  23.5 1.6 %collective-permute-start.8 = (f32[4,128]{1,0:T(4,128)S(1)}, f32[4,128]{1,0:T(4,128)S(1)}, u32[]{:S(2)}, u32[]{:S(2)}) collective-permute-start(f32[4,128]{1,0:T(4,128)S(1)} %get-tuple-element.86), channel_id=1, source_target_pairs={{4,12},{8,4},{0,8},{12,0},{5,13},{9,5},{1,9},{13,1},{6,14},{10,6},... | collective-permute-start | bytes 6152 | tf_op jit(solution)/shard_map/ppermute | solution.py:235
  25.2 5.3 %while.25 = (s32[]{:T(128)}, f32[8,128]{1,0:T(8,128)S(1)}, f32[8,128]{1,0:T(8,128)S(1)}, f32[4,128]{1,0:T(4,128)}, s32[]{:T(128)}, /*index=5*/bf16[528,256]{1,0:...) while((s32[]{:T(128)}, f32[8,128]{1,0:T(8,128)S(1)}, ...), condition=%wide.region_3.0_spmd, body=%wide.region_2.0_spmd.sunk | while | flops 1538 | bytes 55485 | solution.py:245
  25.2 1.5 %collective-permute-start.1 = (f32[8,128]{1,0:T(8,128)S(1)}, f32[8,128]{1,0:T(8,128)S(1)}, u32[]{:S(2)}, u32[]{:S(2)}) collective-permute-start(f32[8,128]{1,0:T(8,128)S(1)} %get-tuple-element.218), channel_id=1, source_target_pairs={{0,2},{1,3},{2,0},{3,1},{4,6},{5,7},{6,4},{7,5},{8,10},{9,11},{10,... | collective-permute-start | bytes 12296 | tf_op jit(solution)/shard_map/while/body/ppermute | solution.py:211
  26.7 0.8 %body.1 = f32[8,128]{1,0:T(8,128)S(1)} custom-call(bf16[528,256]{1,0:T(8,128)(2,1)S(1)} %get-tuple-element.232.refs_0_.refs_1_, bf16[528,256]{1,0:T(8,128)(2,1)S(1)} %get-tuple-element.232.refs_0_.refs_1_, bf16[528,256]{1,0:T(8,128)(2,1)S(1)} %get-tuple-element.233.refs_2_, bf16[528,256]{1,0:T(8,128)(2,1)S(1)} %get-tuple-element.234.refs_3_, ...), custom_call_target="tpu_custom_call" | custom-call | tf_op jit(solution)/shard_map/while/body/pallas_call | solution.py:178
  27.4 1.4 %collective-permute-done.1 = f32[8,128]{1,0:T(8,128)S(1)} collective-permute-done((f32[8,128]{1,0:T(8,128)S(1)}, f32[8,128]{1,0:T(8,128)S(1)}, u32[]{:S(2)}, u32[]{:S(2)}) %collective-permute-start.1) | collective-permute-done | bytes 4128 | tf_op jit(solution)/shard_map/while/body/ppermute | solution.py:211
  28.8 0.0 collective-permute-start.2
  28.8 1.1 %collective-permute-done.2 = f32[4,128]{1,0:T(4,128)S(1)} collective-permute-done((f32[4,128]{1,0:T(4,128)S(1)}, f32[4,128]{1,0:T(4,128)S(1)}, u32[]{:S(2)}, u32[]{:S(2)}) %collective-permute-start.2) | collective-permute-done | bytes 2080 | tf_op jit(solution)/shard_map/while/body/ppermute | solution.py:211
  29.9 0.6 %slice_maximum_fusion.2 = f32[4,128]{1,0:T(4,128)} fusion(f32[4,128]{1,0:T(4,128)S(1)} %collective-permute-done.2, f32[8,128]{1,0:T(8,128)S(1)} %max.25), kind=kLoop, calls=%fused_computation.clone.1 | loop fusion | flops 512 | bytes 6144 | tf_op jit(solution)/shard_map/while/body/max | solution.py:243
  30.5 1.2 %maximum_bitcast_fusion = f32[512]{0:T(512)} fusion(f32[4,128]{1,0:T(4,128)} %get-tuple-element.85, f32[4,128]{1,0:T(4,128)S(1)} %collective-permute-done.8), kind=kLoop, calls=%fused_computation.1 | loop fusion | flops 1024 | bytes 6144 | tf_op jit(solution)/shard_map/reshape | solution.py:248
  (10 shorter events, 0.1 us)
Async XLA Ops:
  3.4 16.0 %collective-permute-start.7 = (bf16[528,256]{1,0:T(8,128)(2,1)S(1)}, bf16[528,256]{1,0:T(8,128)(2,1)S(1)}, u32[]{:S(2)}, u32[]{:S(2)}) collective-permute-start(bf16[528,256]{1,0:T(8,128)(2,1)S(1)} %shard_map.46.refs_1_), channel_id=1, source_target_pairs={{12,8},{4,0},{8,12},{0,4},{13,9},{5,1},{9,13},{1,5},{14,10},{6,2},... | collective-permute-start | bytes 811016 | tf_op jit(solution)/shard_map/ppermute | solution.py:219
  6.5 12.9 %collective-permute-start.4 = (bf16[528,256]{1,0:T(8,128)(2,1)S(1)}, bf16[528,256]{1,0:T(8,128)(2,1)S(1)}, u32[]{:S(2)}, u32[]{:S(2)}) collective-permute-start(bf16[528,256]{1,0:T(8,128)(2,1)S(1)} %shard_map.46.refs_1_), channel_id=1, source_target_pairs={{0,1},{1,0},{2,3},{3,2},{4,5},{5,4},{6,7},{7,6},{8,9},{9,8},{10,11... | collective-permute-start | bytes 811016 | tf_op jit(solution)/shard_map/ppermute | solution.py:211
  6.5 15.6 %collective-permute-start.3 = (bf16[528,256]{1,0:T(8,128)(2,1)S(1)}, bf16[528,256]{1,0:T(8,128)(2,1)S(1)}, u32[]{:S(2)}, u32[]{:S(2)}) collective-permute-start(bf16[528,256]{1,0:T(8,128)(2,1)S(1)} %shard_map.46.refs_1_), channel_id=1, source_target_pairs={{12,4},{4,8},{8,0},{0,12},{13,5},{5,9},{9,1},{1,13},{14,6},{6,10},... | collective-permute-start | bytes 811016 | tf_op jit(solution)/shard_map/ppermute | solution.py:218
  9.0 8.7 %collective-permute-start = (bf16[528,256]{1,0:T(8,128)(2,1)S(1)}, bf16[528,256]{1,0:T(8,128)(2,1)S(1)}, u32[]{:S(2)}, u32[]{:S(2)}) collective-permute-start(bf16[528,256]{1,0:T(8,128)(2,1)S(1)} %get-tuple-element.198), channel_id=1, source_target_pairs={{0,2},{1,3},{2,0},{3,1},{4,6},{5,7},{6,4},{7,5},{8,10},{9,11},{10,... | collective-permute-start | bytes 811016 | tf_op jit(solution)/shard_map/while/body/ppermute | solution.py:211
  17.7 1.6 %collective-permute-start.6 = (bf16[272,256]{1,0:T(8,128)(2,1)S(1)}, bf16[272,256]{1,0:T(8,128)(2,1)S(1)}, u32[]{:S(2)}, u32[]{:S(2)}) collective-permute-start(bf16[272,256]{1,0:T(8,128)(2,1)S(1)} %slice.16), channel_id=1, source_target_pairs={{0,1},{1,0},{2,3},{3,2},{4,5},{5,4},{6,7},{7,6},{8,9},{9,8},{10,11... | collective-permute-start | bytes 417800 | tf_op jit(solution)/shard_map/ppermute | solution.py:211
  17.8 1.5 %collective-permute-start.5 = (bf16[256,256]{1,0:T(8,128)(2,1)S(1)}, bf16[256,256]{1,0:T(8,128)(2,1)S(1)}, u32[]{:S(2)}, u32[]{:S(2)}) collective-permute-start(bf16[256,256]{1,0:T(8,128)(2,1)S(1)} %slice.15), channel_id=1, source_target_pairs={{0,1},{1,0},{2,3},{3,2},{4,5},{5,4},{6,7},{7,6},{8,9},{9,8},{10,11... | collective-permute-start | bytes 393224 | tf_op jit(solution)/shard_map/ppermute | solution.py:211
  23.5 7.0 %collective-permute-start.8 = (f32[4,128]{1,0:T(4,128)S(1)}, f32[4,128]{1,0:T(4,128)S(1)}, u32[]{:S(2)}, u32[]{:S(2)}) collective-permute-start(f32[4,128]{1,0:T(4,128)S(1)} %get-tuple-element.86), channel_id=1, source_target_pairs={{4,12},{8,4},{0,8},{12,0},{5,13},{9,5},{1,9},{13,1},{6,14},{10,6},... | collective-permute-start | bytes 6152 | tf_op jit(solution)/shard_map/ppermute | solution.py:235
  25.2 3.6 %collective-permute-start.1 = (f32[8,128]{1,0:T(8,128)S(1)}, f32[8,128]{1,0:T(8,128)S(1)}, u32[]{:S(2)}, u32[]{:S(2)}) collective-permute-start(f32[8,128]{1,0:T(8,128)S(1)} %get-tuple-element.218), channel_id=1, source_target_pairs={{0,2},{1,3},{2,0},{3,1},{4,6},{5,7},{6,4},{7,5},{8,10},{9,11},{10,... | collective-permute-start | bytes 12296 | tf_op jit(solution)/shard_map/while/body/ppermute | solution.py:211
  28.8 1.2 %collective-permute-start.2 = (f32[4,128]{1,0:T(4,128)S(1)}, f32[4,128]{1,0:T(4,128)S(1)}, u32[]{:S(2)}, u32[]{:S(2)}) collective-permute-start(f32[4,128]{1,0:T(4,128)S(1)} %slice.22), channel_id=1, source_target_pairs={{0,1},{1,0},{2,3},{3,2},{4,5},{5,4},{6,7},{7,6},{8,9},{9,8},{10,11... | collective-permute-start | bytes 6152 | tf_op jit(solution)/shard_map/while/body/ppermute | solution.py:211

commit v15 on v14

--- a/solution.py
+++ b/solution.py
@@ -197,7 +197,7 @@
     half = count // 2
     circle = [count - 1 - 2 * i for i in range(half)] + [count - 2 - 2 * i for i in range(half)]
     return [
-        [(circle[i], circle[(i + step) % count]) for i in range(count)]
+        [(circle[(i + step) % count], circle[i]) for i in range(count)]
         for step in range(1, half + 1)
     ]
 
@@ -228,21 +228,16 @@
     rows = [own, swap(own, 1)]
     for beside in besides:
         rows += [beside, tuple(swap(part, 1) for part in halves(beside))]
-    _, row_best = score([nearby], rows)
-    backs = []
+    row_best, backs = [], []
     for key, step in zip(keys, steps):
         (found,), row_best = score([key], rows, cols=1, known=row_best)
         backs.append(lax.ppermute(found, "owners", [(b, a) for a, b in step]))
-
-    def exchange_split(_, carried):
-        (first, *more), _ = carried
-        more = [swap(found, offset) for found, offset in zip(more, offsets)]
-        _, (local,) = score([own], rows, base=first)
-        for other in more:
-            local = jnp.maximum(local, other)
-        return [local, *more], jnp.maximum(local[:tiles], swap(local[tiles:], 1))
-
-    _, best = lax.fori_loop(0, one_turn, exchange_split, (row_best, row_best[0][:tiles]))
+    _, row_best = score([nearby], rows, known=row_best)
+    others = [swap(found, offset) for found, offset in zip(row_best[1:], offsets)]
+    _, (local,) = score([own], rows, base=row_best[0])
+    for other in others:
+        local = jnp.maximum(local, other)
+    best = jnp.maximum(local[:tiles], swap(local[tiles:], 1))
     for back in backs:
         best = jnp.maximum(best, back)
     return jnp.maximum(best, -1.0).reshape(row_count)

time: 31.9 us -> 30 us (0.940)
  waiting for transfers between devices: 12.5 us -> 10.4 us
  starting transfers between devices: 10.9 us -> 12.8 us
  other arithmetic: 1.8 us -> 0.59 us
  local copies, waits for them, and re-layouts: 0.64 us -> 0.06 us
    ppermute x6, waiting for transfers between devices: 10.6 us -> 8.48 us  [swap(): lax.ppermute(block, 'split', [(s, s ^ offset) for s in range(split_count)])]
    ppermute x1, waiting for transfers between devices: 1.9 us -> 0.01 us  [per_device(): keys = [lax.ppermute(own, 'owners', step) for step in steps]]
    ppermute x1, starting transfers between devices: 1.64 us -> 3.29 us  [per_device(): backs.append(lax.ppermute(found, 'owners', [(b, a) for a, b in step]))]
    ppermute x1, starting transfers between devices: 3.09 us -> 1.58 us  [per_device(): nearby = lax.ppermute(own, 'owners', last)]
    ppermute x1, waiting for transfers between devices: 0.01 us -> 1.49 us  [per_device(): nearby = lax.ppermute(own, 'owners', last)]
    ppermute x1, starting transfers between devices: 2.47 us -> 3.65 us  [per_device(): keys = [lax.ppermute(own, 'owners', step) for step in steps]]
    reshape x1, other arithmetic: 1.24 us -> 0.58 us  [per_device(): return jnp.maximum(best, -1.0).reshape(row_count)]
    ppermute x6, starting transfers between devices: 3.68 us -> 4.33 us  [swap(): lax.ppermute(block, 'split', [(s, s ^ offset) for s in range(split_count)])]
  transfers between devices with their start and end apart: 9 -> 9, of which waited for: 5 -> 5; matrix products, arithmetic and copies ran while one was open for 2% -> 0% of each run, Pallas kernels for 5% -> 5%
where the time goes in v15:
time: 30 us; the launch traced here: 29.8 us
  starting transfers between devices  12.8 us (43%)
  waiting for transfers between devices  10.4 us (35%)
  Pallas kernels  5.82 us (19%)
  other arithmetic  0.59 us (2%)
    ppermute x6, waiting for transfers between devices, swap(): lax.ppermute(block, 'split', [(s, s ^ offset) for s in range(split_count)])  8.48 us
    ppermute x6, starting transfers between devices, swap(): lax.ppermute(block, 'split', [(s, s ^ offset) for s in range(split_count)])  4.33 us
    ppermute x1, starting transfers between devices, per_device(): keys = [lax.ppermute(own, 'owners', step) for step in steps]  3.65 us
    pallas_call x1, Pallas kernels, project(): pl.pallas_call(project_kernel, in_specs=[pl.BlockSpec(memory_space=pltpu....  3.38 us
    ppermute x1, starting transfers between devices, per_device(): backs.append(lax.ppermute(found, 'owners', [(b, a) for a, b in step]))  3.29 us
    pallas_call x3, Pallas kernels, score(): pl.pallas_call(functools.partial(score_kernel, len(keys), cols, [len(row)...  2.44 us
    ppermute x1, starting transfers between devices, per_device(): nearby = lax.ppermute(own, 'owners', last)  1.58 us
    ppermute x1, waiting for transfers between devices, per_device(): nearby = lax.ppermute(own, 'owners', last)  1.49 us
  transfers between devices with their start and end apart: 9, of which 5 were waited for; matrix products, arithmetic and copies ran while one was open for 0% of the time, Pallas kernels for 5%

profile of v15, /device:TPU:0, one launch (start us, length us, event | category | flops | bytes accessed | tf_op | source)
XLA Modules:
  0.0 29.8 jit_solution(17609401200268527030)
XLA Ops:
  0.0 3.4 %shard_map.46.refs_1_.refs_0_ = bf16[528,256]{1,0:T(8,128)(2,1)S(1)} custom-call(bf16[512,4096]{1,0:T(8,128)(2,1)} %source_hbm.1, bf16[4096,256]{1,0:T(8,128)(2,1)} %basis_hbm.1, s32[4,128]{1,0:T(4,128)} %bitcast.4, s32[4,128]{1,0:T(4,128)} %bitcast.5), custom_call_target="tpu_custom_call" | custom-call | flops 1073741824 | bytes 6291456 | tf_op jit(solution)/shard_map/pallas_call | solution.py:65
  3.4 0.5 %collective-permute-start.1 = (bf16[528,256]{1,0:T(8,128)(2,1)S(1)}, bf16[528,256]{1,0:T(8,128)(2,1)S(1)}, u32[]{:S(2)}, u32[]{:S(2)}) collective-permute-start(bf16[528,256]{1,0:T(8,128)(2,1)S(1)} %shard_map.46.refs_1_.refs_0_), channel_id=1, source_target_pairs={{0,1},{1,0},{2,3},{3,2},{4,5},{5,4},{6,7},{7,6},{8,9},{9,8},{10,11... | collective-permute-start | bytes 811016 | tf_op jit(solution)/shard_map/ppermute | solution.py:211
  3.9 3.6 %collective-permute-start.5 = (bf16[528,256]{1,0:T(8,128)(2,1)S(1)}, bf16[528,256]{1,0:T(8,128)(2,1)S(1)}, u32[]{:S(2)}, u32[]{:S(2)}) collective-permute-start(bf16[528,256]{1,0:T(8,128)(2,1)S(1)} %shard_map.46.refs_1_.refs_0_), channel_id=1, source_target_pairs={{4,12},{8,4},{0,8},{12,0},{5,13},{9,5},{1,9},{13,1},{6,14},{10,6},... | collective-permute-start | bytes 811016 | tf_op jit(solution)/shard_map/ppermute | solution.py:218
  7.6 1.6 %collective-permute-start.4 = (bf16[528,256]{1,0:T(8,128)(2,1)S(1)}, bf16[528,256]{1,0:T(8,128)(2,1)S(1)}, u32[]{:S(2)}, u32[]{:S(2)}) collective-permute-start(bf16[528,256]{1,0:T(8,128)(2,1)S(1)} %shard_map.46.refs_1_.refs_0_), channel_id=1, source_target_pairs={{8,12},{0,4},{12,8},{4,0},{9,13},{1,5},{13,9},{5,1},{10,14},{2,6},... | collective-permute-start | bytes 811016 | tf_op jit(solution)/shard_map/ppermute | solution.py:219
  9.2 8.4 %while.10 = (s32[]{:T(128)}, bf16[528,256]{1,0:T(8,128)(2,1)S(1)}, s32[]{:T(128)}, s32[]{:T(128)}) while((s32[]{:T(128)}, bf16[528,256]{1,0:T(8,128)(2,1)S(1)}, s32[]{:T(128)}, s32[]{:T(128)}) %tuple.18), condition=%wide.region_1.0_spmd, body=%wide.region_0.0_spmd.sunk | while | flops 2 | bytes 1622109 | solution.py:222
  9.2 1.6 %collective-permute-start = (bf16[528,256]{1,0:T(8,128)(2,1)S(1)}, bf16[528,256]{1,0:T(8,128)(2,1)S(1)}, u32[]{:S(2)}, u32[]{:S(2)}) collective-permute-start(bf16[528,256]{1,0:T(8,128)(2,1)S(1)} %get-tuple-element.65), channel_id=1, source_target_pairs={{0,2},{1,3},{2,0},{3,1},{4,6},{5,7},{6,4},{7,5},{8,10},{9,11},{10,... | collective-permute-start | bytes 811016 | tf_op jit(solution)/shard_map/while/body/ppermute | solution.py:211
  10.7 6.8 %collective-permute-done = bf16[528,256]{1,0:T(8,128)(2,1)S(1)} collective-permute-done((bf16[528,256]{1,0:T(8,128)(2,1)S(1)}, bf16[528,256]{1,0:T(8,128)(2,1)S(1)}, u32[]{:S(2)}, u32[]{:S(2)}) %collective-permute-start) | collective-permute-done | bytes 270368 | tf_op jit(solution)/shard_map/while/body/ppermute | solution.py:211
  17.6 0.1 collective-permute-start.3
  17.7 0.6 %collective-permute-start.2 = (bf16[256,256]{1,0:T(8,128)(2,1)S(1)}, bf16[256,256]{1,0:T(8,128)(2,1)S(1)}, u32[]{:S(2)}, u32[]{:S(2)}) collective-permute-start(bf16[256,256]{1,0:T(8,128)(2,1)S(1)} %slice.12), channel_id=1, source_target_pairs={{0,1},{1,0},{2,3},{3,2},{4,5},{5,4},{6,7},{7,6},{8,9},{9,8},{10,11... | collective-permute-start | bytes 393224 | tf_op jit(solution)/shard_map/ppermute | solution.py:211
  18.2 1.0 %collective-permute-done.2.refs_4_ = bf16[256,256]{1,0:T(8,128)(2,1)S(1)} collective-permute-done((bf16[256,256]{1,0:T(8,128)(2,1)S(1)}, bf16[256,256]{1,0:T(8,128)(2,1)S(1)}, u32[]{:S(2)}, u32[]{:S(2)}) %collective-permute-start.2) | collective-permute-done | bytes 131104 | tf_op jit(solution)/shard_map/ppermute | solution.py:211
  19.2 0.0 collective-permute-done.3.refs_5_
  19.2 0.0 collective-permute-done.1.refs_2_
  19.2 0.0 collective-permute-done.5.refs_0_
  19.2 0.9 %shard_map.47 = (f32[4,128]{1,0:T(4,128)S(1)}, f32[8,128]{1,0:T(8,128)S(1)}, f32[8,128]{1,0:T(8,128)S(1)}) custom-call(bf16[528,256]{1,0:T(8,128)(2,1)S(1)} %collective-permute-done.5.refs_0_, bf16[528,256]{1,0:T(8,128)(2,1)S(1)} %shard_map.46.refs_1_.refs_0_, bf16[528,256]{1,0:T(8,128)(2,1)S(1)} %collective-permute-done.1.refs_2_, ...), custom_call_target="tpu_custom_call" | custom-call | tf_op jit(solution)/shard_map/pallas_call | solution.py:178
  20.1 1.5 %collective-permute-done.4.refs_0_ = bf16[528,256]{1,0:T(8,128)(2,1)S(1)} collective-permute-done((bf16[528,256]{1,0:T(8,128)(2,1)S(1)}, bf16[528,256]{1,0:T(8,128)(2,1)S(1)}, u32[]{:S(2)}, u32[]{:S(2)}) %collective-permute-start.4) | collective-permute-done | bytes 270368 | tf_op jit(solution)/shard_map/ppermute | solution.py:219
  21.5 0.8 %shard_map.48 = (f32[8,128]{1,0:T(8,128)S(1)}, f32[8,128]{1,0:T(8,128)S(1)}) custom-call(bf16[528,256]{1,0:T(8,128)(2,1)S(1)} %collective-permute-done.4.refs_0_, bf16[528,256]{1,0:T(8,128)(2,1)S(1)} %shard_map.46.refs_1_.refs_0_, bf16[528,256]{1,0:T(8,128)(2,1)S(1)} %collective-permute-done.1.refs_2_, bf16[528,256]{1,0:T(8,128)(2,1)S(1)} %get-tuple-element.28.refs_3_, ...), custom_call_target="tpu_custom_call" | custom-call | tf_op jit(solution)/shard_map/pallas_call | solution.py:178
  22.4 1.6 %collective-permute-start.6 = (f32[8,128]{1,0:T(8,128)S(1)}, f32[8,128]{1,0:T(8,128)S(1)}, u32[]{:S(2)}, u32[]{:S(2)}) collective-permute-start(f32[8,128]{1,0:T(8,128)S(1)} %get-tuple-element.32), channel_id=1, source_target_pairs={{0,2},{1,3},{2,0},{3,1},{4,6},{5,7},{6,4},{7,5},{8,10},{9,11},{10,... | collective-permute-start | bytes 12296 | tf_op jit(solution)/shard_map/ppermute | solution.py:211
  23.9 3.3 %collective-permute-start.8 = (f32[4,128]{1,0:T(4,128)S(1)}, f32[4,128]{1,0:T(4,128)S(1)}, u32[]{:S(2)}, u32[]{:S(2)}) collective-permute-start(f32[4,128]{1,0:T(4,128)S(1)} %get-tuple-element.33), channel_id=1, source_target_pairs={{12,4},{4,8},{8,0},{0,12},{13,5},{5,9},{9,1},{1,13},{14,6},{6,10},... | collective-permute-start | bytes 6152 | tf_op jit(solution)/shard_map/ppermute | solution.py:234
  27.2 0.8 %shard_map.49 = f32[8,128]{1,0:T(8,128)S(1)} custom-call(bf16[528,256]{1,0:T(8,128)(2,1)S(1)} %shard_map.46.refs_1_.refs_0_, bf16[528,256]{1,0:T(8,128)(2,1)S(1)} %shard_map.46.refs_1_.refs_0_, bf16[528,256]{1,0:T(8,128)(2,1)S(1)} %collective-permute-done.1.refs_2_, bf16[528,256]{1,0:T(8,128)(2,1)S(1)} %get-tuple-element.28.refs_3_, ...), custom_call_target="tpu_custom_call" | custom-call | tf_op jit(solution)/shard_map/pallas_call | solution.py:178
  28.0 0.0 collective-permute-done.6
  28.0 0.1 collective-permute-start.7
  28.1 0.4 %collective-permute-done.8 = f32[4,128]{1,0:T(4,128)S(1)} collective-permute-done((f32[4,128]{1,0:T(4,128)S(1)}, f32[4,128]{1,0:T(4,128)S(1)}, u32[]{:S(2)}, u32[]{:S(2)}) %collective-permute-start.8) | collective-permute-done | bytes 2080 | tf_op jit(solution)/shard_map/ppermute | solution.py:234
  28.5 0.7 %collective-permute-done.7 = f32[4,128]{1,0:T(4,128)S(1)} collective-permute-done((f32[4,128]{1,0:T(4,128)S(1)}, f32[4,128]{1,0:T(4,128)S(1)}, u32[]{:S(2)}, u32[]{:S(2)}) %collective-permute-start.7) | collective-permute-done | bytes 2080 | tf_op jit(solution)/shard_map/ppermute | solution.py:211
  29.3 0.6 %maximum_bitcast_fusion = f32[512]{0:T(512)} fusion(f32[4,128]{1,0:T(4,128)S(1)} %collective-permute-done.8, f32[4,128]{1,0:T(4,128)S(1)} %collective-permute-done.7, f32[8,128]{1,0:T(8,128)S(1)} %max.15), kind=kLoop, calls=%fused_computation | loop fusion | flops 1536 | bytes 8192 | tf_op jit(solution)/shard_map/reshape | solution.py:243
  (6 shorter events, 0.1 us)
Async XLA Ops:
  3.4 15.8 %collective-permute-start.1 = (bf16[528,256]{1,0:T(8,128)(2,1)S(1)}, bf16[528,256]{1,0:T(8,128)(2,1)S(1)}, u32[]{:S(2)}, u32[]{:S(2)}) collective-permute-start(bf16[528,256]{1,0:T(8,128)(2,1)S(1)} %shard_map.46.refs_1_.refs_0_), channel_id=1, source_target_pairs={{0,1},{1,0},{2,3},{3,2},{4,5},{5,4},{6,7},{7,6},{8,9},{9,8},{10,11... | collective-permute-start | bytes 811016 | tf_op jit(solution)/shard_map/ppermute | solution.py:211
  3.9 15.3 %collective-permute-start.5 = (bf16[528,256]{1,0:T(8,128)(2,1)S(1)}, bf16[528,256]{1,0:T(8,128)(2,1)S(1)}, u32[]{:S(2)}, u32[]{:S(2)}) collective-permute-start(bf16[528,256]{1,0:T(8,128)(2,1)S(1)} %shard_map.46.refs_1_.refs_0_), channel_id=1, source_target_pairs={{4,12},{8,4},{0,8},{12,0},{5,13},{9,5},{1,9},{13,1},{6,14},{10,6},... | collective-permute-start | bytes 811016 | tf_op jit(solution)/shard_map/ppermute | solution.py:218
  7.6 14.0 %collective-permute-start.4 = (bf16[528,256]{1,0:T(8,128)(2,1)S(1)}, bf16[528,256]{1,0:T(8,128)(2,1)S(1)}, u32[]{:S(2)}, u32[]{:S(2)}) collective-permute-start(bf16[528,256]{1,0:T(8,128)(2,1)S(1)} %shard_map.46.refs_1_.refs_0_), channel_id=1, source_target_pairs={{8,12},{0,4},{12,8},{4,0},{9,13},{1,5},{13,9},{5,1},{10,14},{2,6},... | collective-permute-start | bytes 811016 | tf_op jit(solution)/shard_map/ppermute | solution.py:219
  9.2 8.3 %collective-permute-start = (bf16[528,256]{1,0:T(8,128)(2,1)S(1)}, bf16[528,256]{1,0:T(8,128)(2,1)S(1)}, u32[]{:S(2)}, u32[]{:S(2)}) collective-permute-start(bf16[528,256]{1,0:T(8,128)(2,1)S(1)} %get-tuple-element.65), channel_id=1, source_target_pairs={{0,2},{1,3},{2,0},{3,1},{4,6},{5,7},{6,4},{7,5},{8,10},{9,11},{10,... | collective-permute-start | bytes 811016 | tf_op jit(solution)/shard_map/while/body/ppermute | solution.py:211
  17.6 1.6 %collective-permute-start.3 = (bf16[272,256]{1,0:T(8,128)(2,1)S(1)}, bf16[272,256]{1,0:T(8,128)(2,1)S(1)}, u32[]{:S(2)}, u32[]{:S(2)}) collective-permute-start(bf16[272,256]{1,0:T(8,128)(2,1)S(1)} %slice.13), channel_id=1, source_target_pairs={{0,1},{1,0},{2,3},{3,2},{4,5},{5,4},{6,7},{7,6},{8,9},{9,8},{10,11... | collective-permute-start | bytes 417800 | tf_op jit(solution)/shard_map/ppermute | solution.py:211
  17.7 1.5 %collective-permute-start.2 = (bf16[256,256]{1,0:T(8,128)(2,1)S(1)}, bf16[256,256]{1,0:T(8,128)(2,1)S(1)}, u32[]{:S(2)}, u32[]{:S(2)}) collective-permute-start(bf16[256,256]{1,0:T(8,128)(2,1)S(1)} %slice.12), channel_id=1, source_target_pairs={{0,1},{1,0},{2,3},{3,2},{4,5},{5,4},{6,7},{7,6},{8,9},{9,8},{10,11... | collective-permute-start | bytes 393224 | tf_op jit(solution)/shard_map/ppermute | solution.py:211
  22.4 5.6 %collective-permute-start.6 = (f32[8,128]{1,0:T(8,128)S(1)}, f32[8,128]{1,0:T(8,128)S(1)}, u32[]{:S(2)}, u32[]{:S(2)}) collective-permute-start(f32[8,128]{1,0:T(8,128)S(1)} %get-tuple-element.32), channel_id=1, source_target_pairs={{0,2},{1,3},{2,0},{3,1},{4,6},{5,7},{6,4},{7,5},{8,10},{9,11},{10,... | collective-permute-start | bytes 12296 | tf_op jit(solution)/shard_map/ppermute | solution.py:211
  23.9 4.6 %collective-permute-start.8 = (f32[4,128]{1,0:T(4,128)S(1)}, f32[4,128]{1,0:T(4,128)S(1)}, u32[]{:S(2)}, u32[]{:S(2)}) collective-permute-start(f32[4,128]{1,0:T(4,128)S(1)} %get-tuple-element.33), channel_id=1, source_target_pairs={{12,4},{4,8},{8,0},{0,12},{13,5},{5,9},{9,1},{1,13},{14,6},{6,10},... | collective-permute-start | bytes 6152 | tf_op jit(solution)/shard_map/ppermute | solution.py:234
  28.0 1.2 %collective-permute-start.7 = (f32[4,128]{1,0:T(4,128)S(1)}, f32[4,128]{1,0:T(4,128)S(1)}, u32[]{:S(2)}, u32[]{:S(2)}) collective-permute-start(f32[4,128]{1,0:T(4,128)S(1)} %slice.15), channel_id=1, source_target_pairs={{0,1},{1,0},{2,3},{3,2},{4,5},{5,4},{6,7},{7,6},{8,9},{9,8},{10,11... | collective-permute-start | bytes 6152 | tf_op jit(solution)/shard_map/ppermute | solution.py:211

commit v16 on v15

--- a/solution.py
+++ b/solution.py
@@ -11,7 +11,7 @@
 LANES = 128
 TAG_ROWS = 16
 ABSENT = -2.0
-STEPS = 8
+STEPS = 4
 ROW_PARTS = 4
 VMEM_LIMIT = 48 * 1024 * 1024
 
@@ -99,7 +99,6 @@
     key_refs = [refs.pop(0) for _ in range(key_count)]
     row_refs = [[refs.pop(0) for _ in range(parts)] for parts in row_parts]
     known_refs = [refs.pop(0) for _ in range(known)]
-    base_ref = refs.pop(0) if own_first else None
     col_refs = [refs.pop(0) for _ in range(cols)]
     row_outs = refs
     row_count = key_refs[0].shape[0] - TAG_ROWS
@@ -151,7 +150,7 @@
                 for tile in range(len(tags)):
                     at = block % 2 * tiles + place + tile
                     found = jnp.max(across[tile].T, axis=0, keepdims=True)
-                    if known_refs:
+                    if block // 2 < known:
                         found = jnp.maximum(found, known_refs[block // 2][at : at + 1, :])
                     row_outs[block // 2][at : at + 1, :] = found
             place += len(tags)
@@ -159,21 +158,21 @@
         for at in range(tiles):
             highest = jnp.max(found[at], axis=0, keepdims=True)
             if own_first:
-                row_outs[0][at : at + 1, :] = jnp.maximum(highest, base_ref[at : at + 1, :])
+                row_outs[0][at : at + 1, :] = highest
             else:
                 col_refs[key][at : at + 1, :] = highest
     if own_first:
-        row_outs[0][tiles:, :] = base_ref[tiles:, :]
-
-
-def score(keys, rows, cols=0, known=(), base=None):
+        row_outs[0][tiles:, :] = jnp.full((tiles, LANES), ABSENT, jnp.float32)
+
+
+def score(keys, rows, cols=0, known=(), own_first=False):
     parts = [row if isinstance(row, tuple) else (row,) for row in rows]
     operands = [*keys, *(part for row in parts for part in row)]
-    operands += known if base is None else [base]
+    operands += known
     tiles = keys[0].shape[0] // LANES
     best = jax.ShapeDtypeStruct((tiles, LANES), jnp.float32)
     pair = jax.ShapeDtypeStruct((2 * tiles, LANES), jnp.float32)
-    out_shape = [best] * cols + [pair] * (len(rows) // 2 if base is None else 1)
+    out_shape = [best] * cols + [pair] * (1 if own_first else len(rows) // 2)
     inside = pl.BlockSpec(memory_space=pltpu.VMEM)
     found = pl.pallas_call(
         functools.partial(
@@ -182,7 +181,7 @@
             cols,
             [len(row) for row in parts],
             len(known),
-            base is not None,
+            own_first,
         ),
         in_specs=[inside] * len(operands),
         out_specs=[inside] * len(out_shape),
@@ -228,13 +227,14 @@
     rows = [own, swap(own, 1)]
     for beside in besides:
         rows += [beside, tuple(swap(part, 1) for part in halves(beside))]
-    row_best, backs = [], []
+    _, row_best = score([own], rows, own_first=True)
+    backs = []
     for key, step in zip(keys, steps):
         (found,), row_best = score([key], rows, cols=1, known=row_best)
         backs.append(lax.ppermute(found, "owners", [(b, a) for a, b in step]))
     _, row_best = score([nearby], rows, known=row_best)
     others = [swap(found, offset) for found, offset in zip(row_best[1:], offsets)]
-    _, (local,) = score([own], rows, base=row_best[0])
+    local = row_best[0]
     for other in others:
         local = jnp.maximum(local, other)
     best = jnp.maximum(local[:tiles], swap(local[tiles:], 1))

time: 30 us -> 29.4 us (0.980)
  waiting for transfers between devices: 10.4 us -> 9.72 us
    ppermute x1, waiting for transfers between devices: 0.43 us -> 1.22 us  [per_device(): backs.append(lax.ppermute(found, 'owners', [(b, a) for a, b in step]))]
    ppermute x1, waiting for transfers between devices: 1.49 us -> 0.72 us  [per_device(): nearby = lax.ppermute(own, 'owners', last)]
    ppermute x6, waiting for transfers between devices: 8.48 us -> 7.78 us  [swap(): lax.ppermute(block, 'split', [(s, s ^ offset) for s in range(split_count)])]
  transfers between devices with their start and end apart: 9 -> 9, of which waited for: 5 -> 4; matrix products, arithmetic and copies ran while one was open for 0% -> 0% of each run, Pallas kernels for 5% -> 5%
where the time goes in v16:
time: 29.4 us; the launch traced here: 29.2 us
  starting transfers between devices  12.8 us (44%)
  waiting for transfers between devices  9.72 us (33%)
  Pallas kernels  5.91 us (20%)
  other arithmetic  0.59 us (2%)
    ppermute x6, waiting for transfers between devices, swap(): lax.ppermute(block, 'split', [(s, s ^ offset) for s in range(split_count)])  7.78 us
    ppermute x6, starting transfers between devices, swap(): lax.ppermute(block, 'split', [(s, s ^ offset) for s in range(split_count)])  4.32 us
    ppermute x1, starting transfers between devices, per_device(): keys = [lax.ppermute(own, 'owners', step) for step in steps]  3.65 us
    pallas_call x1, Pallas kernels, project(): pl.pallas_call(project_kernel, in_specs=[pl.BlockSpec(memory_space=pltpu....  3.47 us
    ppermute x1, starting transfers between devices, per_device(): backs.append(lax.ppermute(found, 'owners', [(b, a) for a, b in step]))  3.29 us
    pallas_call x3, Pallas kernels, score(): pl.pallas_call(functools.partial(score_kernel, len(keys), cols, [len(row)...  2.44 us
    ppermute x1, starting transfers between devices, per_device(): nearby = lax.ppermute(own, 'owners', last)  1.58 us
    ppermute x1, waiting for transfers between devices, per_device(): backs.append(lax.ppermute(found, 'owners', [(b, a) for a, b in step]))  1.22 us
  transfers between devices with their start and end apart: 9, of which 4 were waited for; matrix products, arithmetic and copies ran while one was open for 0% of the time, Pallas kernels for 5%

profile of v16, /device:TPU:0, one launch (start us, length us, event | category | flops | bytes accessed | tf_op | source)
XLA Modules:
  0.0 29.2 jit_solution(12655297270561242656)
XLA Ops:
  0.0 3.5 %shard_map.46.refs_0_.refs_1_ = bf16[528,256]{1,0:T(8,128)(2,1)S(1)} custom-call(bf16[512,4096]{1,0:T(8,128)(2,1)} %source_hbm.1, bf16[4096,256]{1,0:T(8,128)(2,1)} %basis_hbm.1, s32[4,128]{1,0:T(4,128)} %bitcast.4, s32[4,128]{1,0:T(4,128)} %bitcast.5), custom_call_target="tpu_custom_call" | custom-call | flops 1073741824 | bytes 6291456 | tf_op jit(solution)/shard_map/pallas_call | solution.py:65
  3.5 0.5 %collective-permute-start.2 = (bf16[528,256]{1,0:T(8,128)(2,1)S(1)}, bf16[528,256]{1,0:T(8,128)(2,1)S(1)}, u32[]{:S(2)}, u32[]{:S(2)}) collective-permute-start(bf16[528,256]{1,0:T(8,128)(2,1)S(1)} %shard_map.46.refs_0_.refs_1_), channel_id=1, source_target_pairs={{0,1},{1,0},{2,3},{3,2},{4,5},{5,4},{6,7},{7,6},{8,9},{9,8},{10,11... | collective-permute-start | bytes 811016 | tf_op jit(solution)/shard_map/ppermute | solution.py:210
  4.0 3.6 %collective-permute-start.5 = (bf16[528,256]{1,0:T(8,128)(2,1)S(1)}, bf16[528,256]{1,0:T(8,128)(2,1)S(1)}, u32[]{:S(2)}, u32[]{:S(2)}) collective-permute-start(bf16[528,256]{1,0:T(8,128)(2,1)S(1)} %shard_map.46.refs_0_.refs_1_), channel_id=1, source_target_pairs={{4,12},{8,4},{0,8},{12,0},{5,13},{9,5},{1,9},{13,1},{6,14},{10,6},... | collective-permute-start | bytes 811016 | tf_op jit(solution)/shard_map/ppermute | solution.py:217
  7.6 1.6 %collective-permute-start.1 = (bf16[528,256]{1,0:T(8,128)(2,1)S(1)}, bf16[528,256]{1,0:T(8,128)(2,1)S(1)}, u32[]{:S(2)}, u32[]{:S(2)}) collective-permute-start(bf16[528,256]{1,0:T(8,128)(2,1)S(1)} %shard_map.46.refs_0_.refs_1_), channel_id=1, source_target_pairs={{8,12},{0,4},{12,8},{4,0},{9,13},{1,5},{13,9},{5,1},{10,14},{2,6},... | collective-permute-start | bytes 811016 | tf_op jit(solution)/shard_map/ppermute | solution.py:218
  9.3 8.4 %while.10 = (s32[]{:T(128)}, bf16[528,256]{1,0:T(8,128)(2,1)S(1)}, s32[]{:T(128)}, s32[]{:T(128)}) while((s32[]{:T(128)}, bf16[528,256]{1,0:T(8,128)(2,1)S(1)}, s32[]{:T(128)}, s32[]{:T(128)}) %tuple.18), condition=%wide.region_1.0_spmd, body=%wide.region_0.0_spmd.sunk | while | flops 2 | bytes 1622109 | solution.py:221
  9.3 1.6 %collective-permute-start = (bf16[528,256]{1,0:T(8,128)(2,1)S(1)}, bf16[528,256]{1,0:T(8,128)(2,1)S(1)}, u32[]{:S(2)}, u32[]{:S(2)}) collective-permute-start(bf16[528,256]{1,0:T(8,128)(2,1)S(1)} %get-tuple-element.65), channel_id=1, source_target_pairs={{0,2},{1,3},{2,0},{3,1},{4,6},{5,7},{6,4},{7,5},{8,10},{9,11},{10,... | collective-permute-start | bytes 811016 | tf_op jit(solution)/shard_map/while/body/ppermute | solution.py:210
  10.8 6.8 %collective-permute-done = bf16[528,256]{1,0:T(8,128)(2,1)S(1)} collective-permute-done((bf16[528,256]{1,0:T(8,128)(2,1)S(1)}, bf16[528,256]{1,0:T(8,128)(2,1)S(1)}, u32[]{:S(2)}, u32[]{:S(2)}) %collective-permute-start) | collective-permute-done | bytes 270368 | tf_op jit(solution)/shard_map/while/body/ppermute | solution.py:210
  17.7 0.1 collective-permute-start.4
  17.8 0.6 %collective-permute-start.3 = (bf16[256,256]{1,0:T(8,128)(2,1)S(1)}, bf16[256,256]{1,0:T(8,128)(2,1)S(1)}, u32[]{:S(2)}, u32[]{:S(2)}) collective-permute-start(bf16[256,256]{1,0:T(8,128)(2,1)S(1)} %slice.12), channel_id=1, source_target_pairs={{0,1},{1,0},{2,3},{3,2},{4,5},{5,4},{6,7},{7,6},{8,9},{9,8},{10,11... | collective-permute-start | bytes 393224 | tf_op jit(solution)/shard_map/ppermute | solution.py:210
  18.3 1.0 %collective-permute-done.3.refs_4_ = bf16[256,256]{1,0:T(8,128)(2,1)S(1)} collective-permute-done((bf16[256,256]{1,0:T(8,128)(2,1)S(1)}, bf16[256,256]{1,0:T(8,128)(2,1)S(1)}, u32[]{:S(2)}, u32[]{:S(2)}) %collective-permute-start.3) | collective-permute-done | bytes 131104 | tf_op jit(solution)/shard_map/ppermute | solution.py:210
  19.3 0.0 collective-permute-done.4.refs_5_
  19.3 0.0 collective-permute-done.2.refs_2_
  19.3 0.8 %shard_map.47.refs_6_ = f32[8,128]{1,0:T(8,128)S(1)} custom-call(bf16[528,256]{1,0:T(8,128)(2,1)S(1)} %shard_map.46.refs_0_.refs_1_, bf16[528,256]{1,0:T(8,128)(2,1)S(1)} %shard_map.46.refs_0_.refs_1_, bf16[528,256]{1,0:T(8,128)(2,1)S(1)} %collective-permute-done.2.refs_2_, bf16[528,256]{1,0:T(8,128)(2,1)S(1)} %get-tuple-element.28.refs_3_, ...), custom_call_target="tpu_custom_call" | custom-call | tf_op jit(solution)/shard_map/pallas_call | solution.py:177
  20.1 0.0 collective-permute-done.5.refs_0_
  20.1 0.9 %shard_map.48 = (f32[4,128]{1,0:T(4,128)S(1)}, f32[8,128]{1,0:T(8,128)S(1)}, f32[8,128]{1,0:T(8,128)S(1)}) custom-call(bf16[528,256]{1,0:T(8,128)(2,1)S(1)} %collective-permute-done.5.refs_0_, bf16[528,256]{1,0:T(8,128)(2,1)S(1)} %shard_map.46.refs_0_.refs_1_, bf16[528,256]{1,0:T(8,128)(2,1)S(1)} %collective-permute-done.2.refs_2_, ...), custom_call_target="tpu_custom_call" | custom-call | tf_op jit(solution)/shard_map/pallas_call | solution.py:177
  20.9 0.7 %collective-permute-done.1.refs_0_ = bf16[528,256]{1,0:T(8,128)(2,1)S(1)} collective-permute-done((bf16[528,256]{1,0:T(8,128)(2,1)S(1)}, bf16[528,256]{1,0:T(8,128)(2,1)S(1)}, u32[]{:S(2)}, u32[]{:S(2)}) %collective-permute-start.1) | collective-permute-done | bytes 270368 | tf_op jit(solution)/shard_map/ppermute | solution.py:218
  21.6 0.8 %shard_map.49 = (f32[8,128]{1,0:T(8,128)S(1)}, f32[8,128]{1,0:T(8,128)S(1)}) custom-call(bf16[528,256]{1,0:T(8,128)(2,1)S(1)} %collective-permute-done.1.refs_0_, bf16[528,256]{1,0:T(8,128)(2,1)S(1)} %shard_map.46.refs_0_.refs_1_, bf16[528,256]{1,0:T(8,128)(2,1)S(1)} %collective-permute-done.2.refs_2_, bf16[528,256]{1,0:T(8,128)(2,1)S(1)} %get-tuple-element.28.refs_3_, ...), custom_call_target="tpu_custom_call" | custom-call | tf_op jit(solution)/shard_map/pallas_call | solution.py:177
  22.5 1.6 %collective-permute-start.6 = (f32[8,128]{1,0:T(8,128)S(1)}, f32[8,128]{1,0:T(8,128)S(1)}, u32[]{:S(2)}, u32[]{:S(2)}) collective-permute-start(f32[8,128]{1,0:T(8,128)S(1)} %get-tuple-element.32), channel_id=1, source_target_pairs={{0,2},{1,3},{2,0},{3,1},{4,6},{5,7},{6,4},{7,5},{8,10},{9,11},{10,... | collective-permute-start | bytes 12296 | tf_op jit(solution)/shard_map/ppermute | solution.py:210
  24.0 3.3 %collective-permute-start.8 = (f32[4,128]{1,0:T(4,128)S(1)}, f32[4,128]{1,0:T(4,128)S(1)}, u32[]{:S(2)}, u32[]{:S(2)}) collective-permute-start(f32[4,128]{1,0:T(4,128)S(1)} %get-tuple-element.33), channel_id=1, source_target_pairs={{12,4},{4,8},{8,0},{0,12},{13,5},{5,9},{9,1},{1,13},{14,6},{6,10},... | collective-permute-start | bytes 6152 | tf_op jit(solution)/shard_map/ppermute | solution.py:234
  27.3 0.0 collective-permute-done.6
  27.3 0.1 collective-permute-start.7
  27.4 1.2 %collective-permute-done.8 = f32[4,128]{1,0:T(4,128)S(1)} collective-permute-done((f32[4,128]{1,0:T(4,128)S(1)}, f32[4,128]{1,0:T(4,128)S(1)}, u32[]{:S(2)}, u32[]{:S(2)}) %collective-permute-start.8) | collective-permute-done | bytes 2080 | tf_op jit(solution)/shard_map/ppermute | solution.py:234
  28.6 0.0 collective-permute-done.7
  28.6 0.6 %maximum_bitcast_fusion = f32[512]{0:T(512)} fusion(f32[4,128]{1,0:T(4,128)S(1)} %collective-permute-done.8, f32[4,128]{1,0:T(4,128)S(1)} %collective-permute-done.7, f32[8,128]{1,0:T(8,128)S(1)} %max.15), kind=kLoop, calls=%fused_computation | loop fusion | flops 1536 | bytes 8192 | tf_op jit(solution)/shard_map/reshape | solution.py:243
  (6 shorter events, 0.1 us)
Async XLA Ops:
  3.5 15.8 %collective-permute-start.2 = (bf16[528,256]{1,0:T(8,128)(2,1)S(1)}, bf16[528,256]{1,0:T(8,128)(2,1)S(1)}, u32[]{:S(2)}, u32[]{:S(2)}) collective-permute-start(bf16[528,256]{1,0:T(8,128)(2,1)S(1)} %shard_map.46.refs_0_.refs_1_), channel_id=1, source_target_pairs={{0,1},{1,0},{2,3},{3,2},{4,5},{5,4},{6,7},{7,6},{8,9},{9,8},{10,11... | collective-permute-start | bytes 811016 | tf_op jit(solution)/shard_map/ppermute | solution.py:210
  4.0 16.1 %collective-permute-start.5 = (bf16[528,256]{1,0:T(8,128)(2,1)S(1)}, bf16[528,256]{1,0:T(8,128)(2,1)S(1)}, u32[]{:S(2)}, u32[]{:S(2)}) collective-permute-start(bf16[528,256]{1,0:T(8,128)(2,1)S(1)} %shard_map.46.refs_0_.refs_1_), channel_id=1, source_target_pairs={{4,12},{8,4},{0,8},{12,0},{5,13},{9,5},{1,9},{13,1},{6,14},{10,6},... | collective-permute-start | bytes 811016 | tf_op jit(solution)/shard_map/ppermute | solution.py:217
  7.6 14.0 %collective-permute-start.1 = (bf16[528,256]{1,0:T(8,128)(2,1)S(1)}, bf16[528,256]{1,0:T(8,128)(2,1)S(1)}, u32[]{:S(2)}, u32[]{:S(2)}) collective-permute-start(bf16[528,256]{1,0:T(8,128)(2,1)S(1)} %shard_map.46.refs_0_.refs_1_), channel_id=1, source_target_pairs={{8,12},{0,4},{12,8},{4,0},{9,13},{1,5},{13,9},{5,1},{10,14},{2,6},... | collective-permute-start | bytes 811016 | tf_op jit(solution)/shard_map/ppermute | solution.py:218
  9.3 8.3 %collective-permute-start = (bf16[528,256]{1,0:T(8,128)(2,1)S(1)}, bf16[528,256]{1,0:T(8,128)(2,1)S(1)}, u32[]{:S(2)}, u32[]{:S(2)}) collective-permute-start(bf16[528,256]{1,0:T(8,128)(2,1)S(1)} %get-tuple-element.65), channel_id=1, source_target_pairs={{0,2},{1,3},{2,0},{3,1},{4,6},{5,7},{6,4},{7,5},{8,10},{9,11},{10,... | collective-permute-start | bytes 811016 | tf_op jit(solution)/shard_map/while/body/ppermute | solution.py:210
  17.7 1.6 %collective-permute-start.4 = (bf16[272,256]{1,0:T(8,128)(2,1)S(1)}, bf16[272,256]{1,0:T(8,128)(2,1)S(1)}, u32[]{:S(2)}, u32[]{:S(2)}) collective-permute-start(bf16[272,256]{1,0:T(8,128)(2,1)S(1)} %slice.13), channel_id=1, source_target_pairs={{0,1},{1,0},{2,3},{3,2},{4,5},{5,4},{6,7},{7,6},{8,9},{9,8},{10,11... | collective-permute-start | bytes 417800 | tf_op jit(solution)/shard_map/ppermute | solution.py:210
  17.8 1.5 %collective-permute-start.3 = (bf16[256,256]{1,0:T(8,128)(2,1)S(1)}, bf16[256,256]{1,0:T(8,128)(2,1)S(1)}, u32[]{:S(2)}, u32[]{:S(2)}) collective-permute-start(bf16[256,256]{1,0:T(8,128)(2,1)S(1)} %slice.12), channel_id=1, source_target_pairs={{0,1},{1,0},{2,3},{3,2},{4,5},{5,4},{6,7},{7,6},{8,9},{9,8},{10,11... | collective-permute-start | bytes 393224 | tf_op jit(solution)/shard_map/ppermute | solution.py:210
  22.5 4.8 %collective-permute-start.6 = (f32[8,128]{1,0:T(8,128)S(1)}, f32[8,128]{1,0:T(8,128)S(1)}, u32[]{:S(2)}, u32[]{:S(2)}) collective-permute-start(f32[8,128]{1,0:T(8,128)S(1)} %get-tuple-element.32), channel_id=1, source_target_pairs={{0,2},{1,3},{2,0},{3,1},{4,6},{5,7},{6,4},{7,5},{8,10},{9,11},{10,... | collective-permute-start | bytes 12296 | tf_op jit(solution)/shard_map/ppermute | solution.py:210
  24.0 4.6 %collective-permute-start.8 = (f32[4,128]{1,0:T(4,128)S(1)}, f32[4,128]{1,0:T(4,128)S(1)}, u32[]{:S(2)}, u32[]{:S(2)}) collective-permute-start(f32[4,128]{1,0:T(4,128)S(1)} %get-tuple-element.33), channel_id=1, source_target_pairs={{12,4},{4,8},{8,0},{0,12},{13,5},{5,9},{9,1},{1,13},{14,6},{6,10},... | collective-permute-start | bytes 6152 | tf_op jit(solution)/shard_map/ppermute | solution.py:234
  27.3 1.3 %collective-permute-start.7 = (f32[4,128]{1,0:T(4,128)S(1)}, f32[4,128]{1,0:T(4,128)S(1)}, u32[]{:S(2)}, u32[]{:S(2)}) collective-permute-start(f32[4,128]{1,0:T(4,128)S(1)} %slice.15), channel_id=1, source_target_pairs={{0,1},{1,0},{2,3},{3,2},{4,5},{5,4},{6,7},{7,6},{8,9},{9,8},{10,11... | collective-permute-start | bytes 6152 | tf_op jit(solution)/shard_map/ppermute | solution.py:210

commit v17 on v16

--- a/solution.py
+++ b/solution.py
@@ -11,7 +11,7 @@
 LANES = 128
 TAG_ROWS = 16
 ABSENT = -2.0
-STEPS = 4
+STEPS = 8
 ROW_PARTS = 4
 VMEM_LIMIT = 48 * 1024 * 1024
 
@@ -228,11 +228,11 @@
     for beside in besides:
         rows += [beside, tuple(swap(part, 1) for part in halves(beside))]
     _, row_best = score([own], rows, own_first=True)
+    _, row_best = score([nearby], rows, known=row_best)
     backs = []
     for key, step in zip(keys, steps):
         (found,), row_best = score([key], rows, cols=1, known=row_best)
         backs.append(lax.ppermute(found, "owners", [(b, a) for a, b in step]))
-    _, row_best = score([nearby], rows, known=row_best)
     others = [swap(found, offset) for found, offset in zip(row_best[1:], offsets)]
     local = row_best[0]
     for other in others:

time: 29.4 us -> 29.4 us (level)
  waiting for transfers between devices: 9.72 us -> 10.5 us
  starting transfers between devices: 12.8 us -> 12.2 us
    ppermute x1, starting transfers between devices: 1.58 us -> 2.65 us  [per_device(): nearby = lax.ppermute(own, 'owners', last)]
    ppermute x1, starting transfers between devices: 3.65 us -> 2.59 us  [per_device(): keys = [lax.ppermute(own, 'owners', step) for step in steps]]
    ppermute x1, waiting for transfers between devices: 0.01 us -> 0.9 us  [per_device(): keys = [lax.ppermute(own, 'owners', step) for step in steps]]
    ppermute x1, waiting for transfers between devices: 0.72 us -> 0.01 us  [per_device(): nearby = lax.ppermute(own, 'owners', last)]
    ppermute x1, starting transfers between devices: 3.29 us -> 2.58 us  [per_device(): backs.append(lax.ppermute(found, 'owners', [(b, a) for a, b in step]))]
    ppermute x1, waiting for transfers between devices: 1.22 us -> 1.82 us  [per_device(): backs.append(lax.ppermute(found, 'owners', [(b, a) for a, b in step]))]
where the time goes in v17:
time: 29.4 us; the launch traced here: 29.2 us
  starting transfers between devices  12.2 us (41%)
  waiting for transfers between devices  10.5 us (36%)
  Pallas kernels  5.82 us (20%)
  other arithmetic  0.59 us (2%)
    ppermute x6, waiting for transfers between devices, swap(): lax.ppermute(block, 'split', [(s, s ^ offset) for s in range(split_count)])  7.78 us
    ppermute x6, starting transfers between devices, swap(): lax.ppermute(block, 'split', [(s, s ^ offset) for s in range(split_count)])  4.33 us
    pallas_call x1, Pallas kernels, project(): pl.pallas_call(project_kernel, in_specs=[pl.BlockSpec(memory_space=pltpu....  3.38 us
    ppermute x1, starting transfers between devices, per_device(): nearby = lax.ppermute(own, 'owners', last)  2.65 us
    ppermute x1, starting transfers between devices, per_device(): keys = [lax.ppermute(own, 'owners', step) for step in steps]  2.59 us
    ppermute x1, starting transfers between devices, per_device(): backs.append(lax.ppermute(found, 'owners', [(b, a) for a, b in step]))  2.58 us
    pallas_call x3, Pallas kernels, score(): pl.pallas_call(functools.partial(score_kernel, len(keys), cols, [len(row)...  2.44 us
    ppermute x1, waiting for transfers between devices, per_device(): backs.append(lax.ppermute(found, 'owners', [(b, a) for a, b in step]))  1.82 us
  transfers between devices with their start and end apart: 9, of which 4 were waited for; matrix products, arithmetic and copies ran while one was open for 0% of the time, Pallas kernels for 5%

profile of v17, /device:TPU:0, one launch (start us, length us, event | category | flops | bytes accessed | tf_op | source)
XLA Modules:
  0.0 29.2 jit_solution(15604636118093661991)
XLA Ops:
  0.0 3.4 %shard_map.46.refs_0_.refs_1_ = bf16[528,256]{1,0:T(8,128)(2,1)S(1)} custom-call(bf16[512,4096]{1,0:T(8,128)(2,1)} %source_hbm.1, bf16[4096,256]{1,0:T(8,128)(2,1)} %basis_hbm.1, s32[4,128]{1,0:T(4,128)} %bitcast.4, s32[4,128]{1,0:T(4,128)} %bitcast.5), custom_call_target="tpu_custom_call" | custom-call | flops 1073741824 | bytes 6291456 | tf_op jit(solution)/shard_map/pallas_call | solution.py:65
  3.4 0.5 %collective-permute-start.2 = (bf16[528,256]{1,0:T(8,128)(2,1)S(1)}, bf16[528,256]{1,0:T(8,128)(2,1)S(1)}, u32[]{:S(2)}, u32[]{:S(2)}) collective-permute-start(bf16[528,256]{1,0:T(8,128)(2,1)S(1)} %shard_map.46.refs_0_.refs_1_), channel_id=1, source_target_pairs={{0,1},{1,0},{2,3},{3,2},{4,5},{5,4},{6,7},{7,6},{8,9},{9,8},{10,11... | collective-permute-start | bytes 811016 | tf_op jit(solution)/shard_map/ppermute | solution.py:210
  3.9 2.6 %collective-permute-start.5 = (bf16[528,256]{1,0:T(8,128)(2,1)S(1)}, bf16[528,256]{1,0:T(8,128)(2,1)S(1)}, u32[]{:S(2)}, u32[]{:S(2)}) collective-permute-start(bf16[528,256]{1,0:T(8,128)(2,1)S(1)} %shard_map.46.refs_0_.refs_1_), channel_id=1, source_target_pairs={{8,12},{0,4},{12,8},{4,0},{9,13},{1,5},{13,9},{5,1},{10,14},{2,6},... | collective-permute-start | bytes 811016 | tf_op jit(solution)/shard_map/ppermute | solution.py:218
  6.6 2.6 %collective-permute-start.1 = (bf16[528,256]{1,0:T(8,128)(2,1)S(1)}, bf16[528,256]{1,0:T(8,128)(2,1)S(1)}, u32[]{:S(2)}, u32[]{:S(2)}) collective-permute-start(bf16[528,256]{1,0:T(8,128)(2,1)S(1)} %shard_map.46.refs_0_.refs_1_), channel_id=1, source_target_pairs={{4,12},{8,4},{0,8},{12,0},{5,13},{9,5},{1,9},{13,1},{6,14},{10,6},... | collective-permute-start | bytes 811016 | tf_op jit(solution)/shard_map/ppermute | solution.py:217
  9.2 8.4 %while.10 = (s32[]{:T(128)}, bf16[528,256]{1,0:T(8,128)(2,1)S(1)}, s32[]{:T(128)}, s32[]{:T(128)}) while((s32[]{:T(128)}, bf16[528,256]{1,0:T(8,128)(2,1)S(1)}, s32[]{:T(128)}, s32[]{:T(128)}) %tuple.18), condition=%wide.region_1.0_spmd, body=%wide.region_0.0_spmd.sunk | while | flops 2 | bytes 1622109 | solution.py:221
  9.2 1.6 %collective-permute-start = (bf16[528,256]{1,0:T(8,128)(2,1)S(1)}, bf16[528,256]{1,0:T(8,128)(2,1)S(1)}, u32[]{:S(2)}, u32[]{:S(2)}) collective-permute-start(bf16[528,256]{1,0:T(8,128)(2,1)S(1)} %get-tuple-element.65), channel_id=1, source_target_pairs={{0,2},{1,3},{2,0},{3,1},{4,6},{5,7},{6,4},{7,5},{8,10},{9,11},{10,... | collective-permute-start | bytes 811016 | tf_op jit(solution)/shard_map/while/body/ppermute | solution.py:210
  10.7 6.8 %collective-permute-done = bf16[528,256]{1,0:T(8,128)(2,1)S(1)} collective-permute-done((bf16[528,256]{1,0:T(8,128)(2,1)S(1)}, bf16[528,256]{1,0:T(8,128)(2,1)S(1)}, u32[]{:S(2)}, u32[]{:S(2)}) %collective-permute-start) | collective-permute-done | bytes 270368 | tf_op jit(solution)/shard_map/while/body/ppermute | solution.py:210
  17.6 0.1 collective-permute-start.4
  17.7 0.6 %collective-permute-start.3 = (bf16[256,256]{1,0:T(8,128)(2,1)S(1)}, bf16[256,256]{1,0:T(8,128)(2,1)S(1)}, u32[]{:S(2)}, u32[]{:S(2)}) collective-permute-start(bf16[256,256]{1,0:T(8,128)(2,1)S(1)} %slice.12), channel_id=1, source_target_pairs={{0,1},{1,0},{2,3},{3,2},{4,5},{5,4},{6,7},{7,6},{8,9},{9,8},{10,11... | collective-permute-start | bytes 393224 | tf_op jit(solution)/shard_map/ppermute | solution.py:210
  18.2 1.0 %collective-permute-done.3.refs_4_ = bf16[256,256]{1,0:T(8,128)(2,1)S(1)} collective-permute-done((bf16[256,256]{1,0:T(8,128)(2,1)S(1)}, bf16[256,256]{1,0:T(8,128)(2,1)S(1)}, u32[]{:S(2)}, u32[]{:S(2)}) %collective-permute-start.3) | collective-permute-done | bytes 131104 | tf_op jit(solution)/shard_map/ppermute | solution.py:210
  19.2 0.0 collective-permute-done.4.refs_5_
  19.2 0.0 collective-permute-done.2.refs_2_
  19.2 0.8 %shard_map.47.refs_6_ = f32[8,128]{1,0:T(8,128)S(1)} custom-call(bf16[528,256]{1,0:T(8,128)(2,1)S(1)} %shard_map.46.refs_0_.refs_1_, bf16[528,256]{1,0:T(8,128)(2,1)S(1)} %shard_map.46.refs_0_.refs_1_, bf16[528,256]{1,0:T(8,128)(2,1)S(1)} %collective-permute-done.2.refs_2_, bf16[528,256]{1,0:T(8,128)(2,1)S(1)} %get-tuple-element.28.refs_3_, ...), custom_call_target="tpu_custom_call" | custom-call | tf_op jit(solution)/shard_map/pallas_call | solution.py:177
  20.0 0.0 collective-permute-done.5.refs_0_
  20.0 0.8 %shard_map.48 = (f32[8,128]{1,0:T(8,128)S(1)}, f32[8,128]{1,0:T(8,128)S(1)}) custom-call(bf16[528,256]{1,0:T(8,128)(2,1)S(1)} %collective-permute-done.5.refs_0_, bf16[528,256]{1,0:T(8,128)(2,1)S(1)} %shard_map.46.refs_0_.refs_1_, bf16[528,256]{1,0:T(8,128)(2,1)S(1)} %collective-permute-done.2.refs_2_, bf16[528,256]{1,0:T(8,128)(2,1)S(1)} %get-tuple-element.28.refs_3_, ...), custom_call_target="tpu_custom_call" | custom-call | tf_op jit(solution)/shard_map/pallas_call | solution.py:177
  20.8 0.9 %collective-permute-done.1.refs_0_ = bf16[528,256]{1,0:T(8,128)(2,1)S(1)} collective-permute-done((bf16[528,256]{1,0:T(8,128)(2,1)S(1)}, bf16[528,256]{1,0:T(8,128)(2,1)S(1)}, u32[]{:S(2)}, u32[]{:S(2)}) %collective-permute-start.1) | collective-permute-done | bytes 270368 | tf_op jit(solution)/shard_map/ppermute | solution.py:217
  21.7 0.8 %shard_map.49 = (f32[4,128]{1,0:T(4,128)S(1)}, f32[8,128]{1,0:T(8,128)S(1)}, f32[8,128]{1,0:T(8,128)S(1)}) custom-call(bf16[528,256]{1,0:T(8,128)(2,1)S(1)} %collective-permute-done.1.refs_0_, bf16[528,256]{1,0:T(8,128)(2,1)S(1)} %shard_map.46.refs_0_.refs_1_, bf16[528,256]{1,0:T(8,128)(2,1)S(1)} %collective-permute-done.2.refs_2_, ...), custom_call_target="tpu_custom_call" | custom-call | tf_op jit(solution)/shard_map/pallas_call | solution.py:177
  22.6 1.6 %collective-permute-start.6 = (f32[8,128]{1,0:T(8,128)S(1)}, f32[8,128]{1,0:T(8,128)S(1)}, u32[]{:S(2)}, u32[]{:S(2)}) collective-permute-start(f32[8,128]{1,0:T(8,128)S(1)} %get-tuple-element.32), channel_id=1, source_target_pairs={{0,2},{1,3},{2,0},{3,1},{4,6},{5,7},{6,4},{7,5},{8,10},{9,11},{10,... | collective-permute-start | bytes 12296 | tf_op jit(solution)/shard_map/ppermute | solution.py:210
  24.1 2.6 %collective-permute-start.8 = (f32[4,128]{1,0:T(4,128)S(1)}, f32[4,128]{1,0:T(4,128)S(1)}, u32[]{:S(2)}, u32[]{:S(2)}) collective-permute-start(f32[4,128]{1,0:T(4,128)S(1)} %get-tuple-element.33), channel_id=1, source_target_pairs={{12,4},{4,8},{8,0},{0,12},{13,5},{5,9},{9,1},{1,13},{14,6},{6,10},... | collective-permute-start | bytes 6152 | tf_op jit(solution)/shard_map/ppermute | solution.py:235
  26.7 0.0 collective-permute-done.6
  26.7 0.1 collective-permute-start.7
  26.8 1.8 %collective-permute-done.8 = f32[4,128]{1,0:T(4,128)S(1)} collective-permute-done((f32[4,128]{1,0:T(4,128)S(1)}, f32[4,128]{1,0:T(4,128)S(1)}, u32[]{:S(2)}, u32[]{:S(2)}) %collective-permute-start.8) | collective-permute-done | bytes 2080 | tf_op jit(solution)/shard_map/ppermute | solution.py:235
  28.6 0.0 collective-permute-done.7
  28.6 0.6 %maximum_bitcast_fusion = f32[512]{0:T(512)} fusion(f32[4,128]{1,0:T(4,128)S(1)} %collective-permute-done.8, f32[4,128]{1,0:T(4,128)S(1)} %collective-permute-done.7, f32[8,128]{1,0:T(8,128)S(1)} %max.15), kind=kLoop, calls=%fused_computation | loop fusion | flops 1536 | bytes 8192 | tf_op jit(solution)/shard_map/reshape | solution.py:243
  (6 shorter events, 0.1 us)
Async XLA Ops:
  3.4 15.8 %collective-permute-start.2 = (bf16[528,256]{1,0:T(8,128)(2,1)S(1)}, bf16[528,256]{1,0:T(8,128)(2,1)S(1)}, u32[]{:S(2)}, u32[]{:S(2)}) collective-permute-start(bf16[528,256]{1,0:T(8,128)(2,1)S(1)} %shard_map.46.refs_0_.refs_1_), channel_id=1, source_target_pairs={{0,1},{1,0},{2,3},{3,2},{4,5},{5,4},{6,7},{7,6},{8,9},{9,8},{10,11... | collective-permute-start | bytes 811016 | tf_op jit(solution)/shard_map/ppermute | solution.py:210
  3.9 16.1 %collective-permute-start.5 = (bf16[528,256]{1,0:T(8,128)(2,1)S(1)}, bf16[528,256]{1,0:T(8,128)(2,1)S(1)}, u32[]{:S(2)}, u32[]{:S(2)}) collective-permute-start(bf16[528,256]{1,0:T(8,128)(2,1)S(1)} %shard_map.46.refs_0_.refs_1_), channel_id=1, source_target_pairs={{8,12},{0,4},{12,8},{4,0},{9,13},{1,5},{13,9},{5,1},{10,14},{2,6},... | collective-permute-start | bytes 811016 | tf_op jit(solution)/shard_map/ppermute | solution.py:218
  6.6 15.2 %collective-permute-start.1 = (bf16[528,256]{1,0:T(8,128)(2,1)S(1)}, bf16[528,256]{1,0:T(8,128)(2,1)S(1)}, u32[]{:S(2)}, u32[]{:S(2)}) collective-permute-start(bf16[528,256]{1,0:T(8,128)(2,1)S(1)} %shard_map.46.refs_0_.refs_1_), channel_id=1, source_target_pairs={{4,12},{8,4},{0,8},{12,0},{5,13},{9,5},{1,9},{13,1},{6,14},{10,6},... | collective-permute-start | bytes 811016 | tf_op jit(solution)/shard_map/ppermute | solution.py:217
  9.2 8.3 %collective-permute-start = (bf16[528,256]{1,0:T(8,128)(2,1)S(1)}, bf16[528,256]{1,0:T(8,128)(2,1)S(1)}, u32[]{:S(2)}, u32[]{:S(2)}) collective-permute-start(bf16[528,256]{1,0:T(8,128)(2,1)S(1)} %get-tuple-element.65), channel_id=1, source_target_pairs={{0,2},{1,3},{2,0},{3,1},{4,6},{5,7},{6,4},{7,5},{8,10},{9,11},{10,... | collective-permute-start | bytes 811016 | tf_op jit(solution)/shard_map/while/body/ppermute | solution.py:210
  17.6 1.6 %collective-permute-start.4 = (bf16[272,256]{1,0:T(8,128)(2,1)S(1)}, bf16[272,256]{1,0:T(8,128)(2,1)S(1)}, u32[]{:S(2)}, u32[]{:S(2)}) collective-permute-start(bf16[272,256]{1,0:T(8,128)(2,1)S(1)} %slice.13), channel_id=1, source_target_pairs={{0,1},{1,0},{2,3},{3,2},{4,5},{5,4},{6,7},{7,6},{8,9},{9,8},{10,11... | collective-permute-start | bytes 417800 | tf_op jit(solution)/shard_map/ppermute | solution.py:210
  17.7 1.5 %collective-permute-start.3 = (bf16[256,256]{1,0:T(8,128)(2,1)S(1)}, bf16[256,256]{1,0:T(8,128)(2,1)S(1)}, u32[]{:S(2)}, u32[]{:S(2)}) collective-permute-start(bf16[256,256]{1,0:T(8,128)(2,1)S(1)} %slice.12), channel_id=1, source_target_pairs={{0,1},{1,0},{2,3},{3,2},{4,5},{5,4},{6,7},{7,6},{8,9},{9,8},{10,11... | collective-permute-start | bytes 393224 | tf_op jit(solution)/shard_map/ppermute | solution.py:210
  22.6 4.1 %collective-permute-start.6 = (f32[8,128]{1,0:T(8,128)S(1)}, f32[8,128]{1,0:T(8,128)S(1)}, u32[]{:S(2)}, u32[]{:S(2)}) collective-permute-start(f32[8,128]{1,0:T(8,128)S(1)} %get-tuple-element.32), channel_id=1, source_target_pairs={{0,2},{1,3},{2,0},{3,1},{4,6},{5,7},{6,4},{7,5},{8,10},{9,11},{10,... | collective-permute-start | bytes 12296 | tf_op jit(solution)/shard_map/ppermute | solution.py:210
  24.1 4.5 %collective-permute-start.8 = (f32[4,128]{1,0:T(4,128)S(1)}, f32[4,128]{1,0:T(4,128)S(1)}, u32[]{:S(2)}, u32[]{:S(2)}) collective-permute-start(f32[4,128]{1,0:T(4,128)S(1)} %get-tuple-element.33), channel_id=1, source_target_pairs={{12,4},{4,8},{8,0},{0,12},{13,5},{5,9},{9,1},{1,13},{14,6},{6,10},... | collective-permute-start | bytes 6152 | tf_op jit(solution)/shard_map/ppermute | solution.py:235
  26.7 1.9 %collective-permute-start.7 = (f32[4,128]{1,0:T(4,128)S(1)}, f32[4,128]{1,0:T(4,128)S(1)}, u32[]{:S(2)}, u32[]{:S(2)}) collective-permute-start(f32[4,128]{1,0:T(4,128)S(1)} %slice.15), channel_id=1, source_target_pairs={{0,1},{1,0},{2,3},{3,2},{4,5},{5,4},{6,7},{7,6},{8,9},{9,8},{10,11... | collective-permute-start | bytes 6152 | tf_op jit(solution)/shard_map/ppermute | solution.py:210

commit v18 on v17

--- a/solution.py
+++ b/solution.py
@@ -96,6 +96,7 @@
 
 def score_kernel(key_count, cols, row_parts, known, own_first, *refs):
     refs = list(refs)
+    group = len(row_parts) // 2
     key_refs = [refs.pop(0) for _ in range(key_count)]
     row_refs = [[refs.pop(0) for _ in range(parts)] for parts in row_parts]
     known_refs = [refs.pop(0) for _ in range(known)]
@@ -148,11 +149,11 @@
                             )
             if not own_first:
                 for tile in range(len(tags)):
-                    at = block % 2 * tiles + place + tile
+                    at = block % group * tiles + place + tile
                     found = jnp.max(across[tile].T, axis=0, keepdims=True)
-                    if block // 2 < known:
-                        found = jnp.maximum(found, known_refs[block // 2][at : at + 1, :])
-                    row_outs[block // 2][at : at + 1, :] = found
+                    if block // group < known:
+                        found = jnp.maximum(found, known_refs[block // group][at : at + 1, :])
+                    row_outs[block // group][at : at + 1, :] = found
             place += len(tags)
     for key, found in enumerate(best):
         for at in range(tiles):
@@ -162,7 +163,8 @@
             else:
                 col_refs[key][at : at + 1, :] = highest
     if own_first:
-        row_outs[0][tiles:, :] = jnp.full((tiles, LANES), ABSENT, jnp.float32)
+        rest = row_outs[0].shape[0] - tiles
+        row_outs[0][tiles:, :] = jnp.full((rest, LANES), ABSENT, jnp.float32)
 
 
 def score(keys, rows, cols=0, known=(), own_first=False):
@@ -171,8 +173,8 @@
     operands += known
     tiles = keys[0].shape[0] // LANES
     best = jax.ShapeDtypeStruct((tiles, LANES), jnp.float32)
-    pair = jax.ShapeDtypeStruct((2 * tiles, LANES), jnp.float32)
-    out_shape = [best] * cols + [pair] * (1 if own_first else len(rows) // 2)
+    group = jax.ShapeDtypeStruct((len(rows) // 2 * tiles, LANES), jnp.float32)
+    out_shape = [best] * cols + [group] * (1 if own_first else 2)
     inside = pl.BlockSpec(memory_space=pltpu.VMEM)
     found = pl.pallas_call(
         functools.partial(
@@ -224,20 +226,18 @@
         lambda _, blocks: [swap(block, offset) for block, offset in zip(blocks, offsets)],
         [own] * len(offsets),
     )
-    rows = [own, swap(own, 1)]
-    for beside in besides:
-        rows += [beside, tuple(swap(part, 1) for part in halves(beside))]
+    rows = [own, *besides, swap(own, 1)]
+    rows += [tuple(swap(part, 1) for part in halves(beside)) for beside in besides]
     _, row_best = score([own], rows, own_first=True)
     _, row_best = score([nearby], rows, known=row_best)
     backs = []
     for key, step in zip(keys, steps):
         (found,), row_best = score([key], rows, cols=1, known=row_best)
         backs.append(lax.ppermute(found, "owners", [(b, a) for a, b in step]))
-    others = [swap(found, offset) for found, offset in zip(row_best[1:], offsets)]
-    local = row_best[0]
-    for other in others:
-        local = jnp.maximum(local, other)
-    best = jnp.maximum(local[:tiles], swap(local[tiles:], 1))
+    local = jnp.maximum(row_best[0], swap(row_best[1], 1))
+    best = local[:tiles]
+    for at, offset in enumerate(offsets, start=1):
+        best = jnp.maximum(best, swap(local[at * tiles : (at + 1) * tiles], offset))
     for back in backs:
         best = jnp.maximum(best, back)
     return jnp.maximum(best, -1.0).reshape(row_count)

time: 29.4 us -> 29.7 us (1.010)
  waiting for transfers between devices: 10.5 us -> 10.8 us
    ppermute x6, waiting for transfers between devices: 7.78 us -> 9.53 us  [swap(): lax.ppermute(block, 'split', [(s, s ^ offset) for s in range(split_count)])]
    ppermute x1, waiting for transfers between devices: 1.82 us -> 0.34 us  [per_device(): backs.append(lax.ppermute(found, 'owners', [(b, a) for a, b in step]))]
  transfers between devices with their start and end apart: 9 -> 9, of which waited for: 4 -> 5; matrix products, arithmetic and copies ran while one was open for 0% -> 0% of each run, Pallas kernels for 5% -> 5%
where the time goes in v18:
time: 29.7 us; the launch traced here: 29.5 us
  starting transfers between devices  12.2 us (41%)
  waiting for transfers between devices  10.8 us (36%)
  Pallas kernels  5.82 us (20%)
  other arithmetic  0.59 us (2%)
    ppermute x6, waiting for transfers between devices, swap(): lax.ppermute(block, 'split', [(s, s ^ offset) for s in range(split_count)])  9.53 us
    ppermute x6, starting transfers between devices, swap(): lax.ppermute(block, 'split', [(s, s ^ offset) for s in range(split_count)])  4.33 us
    pallas_call x1, Pallas kernels, project(): pl.pallas_call(project_kernel, in_specs=[pl.BlockSpec(memory_space=pltpu....  3.38 us
    ppermute x1, starting transfers between devices, per_device(): nearby = lax.ppermute(own, 'owners', last)  2.65 us
    ppermute x1, starting transfers between devices, per_device(): backs.append(lax.ppermute(found, 'owners', [(b, a) for a, b in step]))  2.63 us
    ppermute x1, starting transfers between devices, per_device(): keys = [lax.ppermute(own, 'owners', step) for step in steps]  2.59 us
    pallas_call x3, Pallas kernels, score(): pl.pallas_call(functools.partial(score_kernel, len(keys), cols, [len(row)...  2.44 us
    ppermute x1, waiting for transfers between devices, per_device(): keys = [lax.ppermute(own, 'owners', step) for step in steps]  0.9 us
  transfers between devices with their start and end apart: 9, of which 5 were waited for; matrix products, arithmetic and copies ran while one was open for 0% of the time, Pallas kernels for 5%

profile of v18, /device:TPU:0, one launch (start us, length us, event | category | flops | bytes accessed | tf_op | source)
XLA Modules:
  0.0 29.5 jit_solution(14266117233584442236)
XLA Ops:
  0.0 3.4 %shard_map.46.refs_0_.refs_1_ = bf16[528,256]{1,0:T(8,128)(2,1)S(1)} custom-call(bf16[512,4096]{1,0:T(8,128)(2,1)} %source_hbm.1, bf16[4096,256]{1,0:T(8,128)(2,1)} %basis_hbm.1, s32[4,128]{1,0:T(4,128)} %bitcast.4, s32[4,128]{1,0:T(4,128)} %bitcast.5), custom_call_target="tpu_custom_call" | custom-call | flops 1073741824 | bytes 6291456 | tf_op jit(solution)/shard_map/pallas_call | solution.py:65
  3.4 0.5 %collective-permute-start.2 = (bf16[528,256]{1,0:T(8,128)(2,1)S(1)}, bf16[528,256]{1,0:T(8,128)(2,1)S(1)}, u32[]{:S(2)}, u32[]{:S(2)}) collective-permute-start(bf16[528,256]{1,0:T(8,128)(2,1)S(1)} %shard_map.46.refs_0_.refs_1_), channel_id=1, source_target_pairs={{0,1},{1,0},{2,3},{3,2},{4,5},{5,4},{6,7},{7,6},{8,9},{9,8},{10,11... | collective-permute-start | bytes 811016 | tf_op jit(solution)/shard_map/ppermute | solution.py:212
  3.9 2.6 %collective-permute-start.5 = (bf16[528,256]{1,0:T(8,128)(2,1)S(1)}, bf16[528,256]{1,0:T(8,128)(2,1)S(1)}, u32[]{:S(2)}, u32[]{:S(2)}) collective-permute-start(bf16[528,256]{1,0:T(8,128)(2,1)S(1)} %shard_map.46.refs_0_.refs_1_), channel_id=1, source_target_pairs={{8,12},{0,4},{12,8},{4,0},{9,13},{1,5},{13,9},{5,1},{10,14},{2,6},... | collective-permute-start | bytes 811016 | tf_op jit(solution)/shard_map/ppermute | solution.py:220
  6.6 2.6 %collective-permute-start.1 = (bf16[528,256]{1,0:T(8,128)(2,1)S(1)}, bf16[528,256]{1,0:T(8,128)(2,1)S(1)}, u32[]{:S(2)}, u32[]{:S(2)}) collective-permute-start(bf16[528,256]{1,0:T(8,128)(2,1)S(1)} %shard_map.46.refs_0_.refs_1_), channel_id=1, source_target_pairs={{4,12},{8,4},{0,8},{12,0},{5,13},{9,5},{1,9},{13,1},{6,14},{10,6},... | collective-permute-start | bytes 811016 | tf_op jit(solution)/shard_map/ppermute | solution.py:219
  9.2 8.4 %while.10 = (s32[]{:T(128)}, bf16[528,256]{1,0:T(8,128)(2,1)S(1)}, s32[]{:T(128)}, s32[]{:T(128)}) while((s32[]{:T(128)}, bf16[528,256]{1,0:T(8,128)(2,1)S(1)}, s32[]{:T(128)}, s32[]{:T(128)}) %tuple.18), condition=%wide.region_1.0_spmd, body=%wide.region_0.0_spmd.sunk | while | flops 2 | bytes 1622109 | solution.py:223
  9.2 1.6 %collective-permute-start = (bf16[528,256]{1,0:T(8,128)(2,1)S(1)}, bf16[528,256]{1,0:T(8,128)(2,1)S(1)}, u32[]{:S(2)}, u32[]{:S(2)}) collective-permute-start(bf16[528,256]{1,0:T(8,128)(2,1)S(1)} %get-tuple-element.65), channel_id=1, source_target_pairs={{0,2},{1,3},{2,0},{3,1},{4,6},{5,7},{6,4},{7,5},{8,10},{9,11},{10,... | collective-permute-start | bytes 811016 | tf_op jit(solution)/shard_map/while/body/ppermute | solution.py:212
  10.7 6.8 %collective-permute-done = bf16[528,256]{1,0:T(8,128)(2,1)S(1)} collective-permute-done((bf16[528,256]{1,0:T(8,128)(2,1)S(1)}, bf16[528,256]{1,0:T(8,128)(2,1)S(1)}, u32[]{:S(2)}, u32[]{:S(2)}) %collective-permute-start) | collective-permute-done | bytes 270368 | tf_op jit(solution)/shard_map/while/body/ppermute | solution.py:212
  17.6 0.1 collective-permute-start.4
  17.7 0.6 %collective-permute-start.3 = (bf16[256,256]{1,0:T(8,128)(2,1)S(1)}, bf16[256,256]{1,0:T(8,128)(2,1)S(1)}, u32[]{:S(2)}, u32[]{:S(2)}) collective-permute-start(bf16[256,256]{1,0:T(8,128)(2,1)S(1)} %slice.12), channel_id=1, source_target_pairs={{0,1},{1,0},{2,3},{3,2},{4,5},{5,4},{6,7},{7,6},{8,9},{9,8},{10,11... | collective-permute-start | bytes 393224 | tf_op jit(solution)/shard_map/ppermute | solution.py:212
  18.2 1.0 %collective-permute-done.3.refs_4_ = bf16[256,256]{1,0:T(8,128)(2,1)S(1)} collective-permute-done((bf16[256,256]{1,0:T(8,128)(2,1)S(1)}, bf16[256,256]{1,0:T(8,128)(2,1)S(1)}, u32[]{:S(2)}, u32[]{:S(2)}) %collective-permute-start.3) | collective-permute-done | bytes 131104 | tf_op jit(solution)/shard_map/ppermute | solution.py:212
  19.2 0.0 collective-permute-done.4.refs_5_
  19.2 0.0 collective-permute-done.2.refs_3_
  19.2 0.8 %shard_map.47.refs_6_ = f32[8,128]{1,0:T(8,128)S(1)} custom-call(bf16[528,256]{1,0:T(8,128)(2,1)S(1)} %shard_map.46.refs_0_.refs_1_, bf16[528,256]{1,0:T(8,128)(2,1)S(1)} %shard_map.46.refs_0_.refs_1_, bf16[528,256]{1,0:T(8,128)(2,1)S(1)} %get-tuple-element.28.refs_2_, bf16[528,256]{1,0:T(8,128)(2,1)S(1)} %collective-permute-done.2.refs_3_, ...), custom_call_target="tpu_custom_call" | custom-call | tf_op jit(solution)/shard_map/pallas_call | solution.py:179
  20.0 0.0 collective-permute-done.5.refs_0_
  20.0 0.8 %shard_map.48 = (f32[8,128]{1,0:T(8,128)S(1)}, f32[8,128]{1,0:T(8,128)S(1)}) custom-call(bf16[528,256]{1,0:T(8,128)(2,1)S(1)} %collective-permute-done.5.refs_0_, bf16[528,256]{1,0:T(8,128)(2,1)S(1)} %shard_map.46.refs_0_.refs_1_, bf16[528,256]{1,0:T(8,128)(2,1)S(1)} %get-tuple-element.28.refs_2_, bf16[528,256]{1,0:T(8,128)(2,1)S(1)} %collective-permute-done.2.refs_3_, ...), custom_call_target="tpu_custom_call" | custom-call | tf_op jit(solution)/shard_map/pallas_call | solution.py:179
  20.8 0.9 %collective-permute-done.1.refs_0_ = bf16[528,256]{1,0:T(8,128)(2,1)S(1)} collective-permute-done((bf16[528,256]{1,0:T(8,128)(2,1)S(1)}, bf16[528,256]{1,0:T(8,128)(2,1)S(1)}, u32[]{:S(2)}, u32[]{:S(2)}) %collective-permute-start.1) | collective-permute-done | bytes 270368 | tf_op jit(solution)/shard_map/ppermute | solution.py:219
  21.7 0.8 %shard_map.49 = (f32[4,128]{1,0:T(4,128)S(1)}, f32[8,128]{1,0:T(8,128)S(1)}, f32[8,128]{1,0:T(8,128)S(1)}) custom-call(bf16[528,256]{1,0:T(8,128)(2,1)S(1)} %collective-permute-done.1.refs_0_, bf16[528,256]{1,0:T(8,128)(2,1)S(1)} %shard_map.46.refs_0_.refs_1_, bf16[528,256]{1,0:T(8,128)(2,1)S(1)} %get-tuple-element.28.refs_2_, ...), custom_call_target="tpu_custom_call" | custom-call | tf_op jit(solution)/shard_map/pallas_call | solution.py:179
  22.6 0.1 collective-permute-start.6
  22.7 2.6 %collective-permute-start.8 = (f32[4,128]{1,0:T(4,128)S(1)}, f32[4,128]{1,0:T(4,128)S(1)}, u32[]{:S(2)}, u32[]{:S(2)}) collective-permute-start(f32[4,128]{1,0:T(4,128)S(1)} %get-tuple-element.33), channel_id=1, source_target_pairs={{12,4},{4,8},{8,0},{0,12},{13,5},{5,9},{9,1},{1,13},{14,6},{6,10},... | collective-permute-start | bytes 6152 | tf_op jit(solution)/shard_map/ppermute | solution.py:236
  25.3 0.0 collective-permute-done.6
  25.3 1.6 %collective-permute-start.7 = (f32[4,128]{1,0:T(4,128)S(1)}, f32[4,128]{1,0:T(4,128)S(1)}, u32[]{:S(2)}, u32[]{:S(2)}) collective-permute-start(f32[4,128]{1,0:T(4,128)S(1)} %slice.15), channel_id=1, source_target_pairs={{0,2},{1,3},{2,0},{3,1},{4,6},{5,7},{6,4},{7,5},{8,10},{9,11},{10,... | collective-permute-start | bytes 6152 | tf_op jit(solution)/shard_map/ppermute | solution.py:212
  26.9 0.3 %collective-permute-done.8 = f32[4,128]{1,0:T(4,128)S(1)} collective-permute-done((f32[4,128]{1,0:T(4,128)S(1)}, f32[4,128]{1,0:T(4,128)S(1)}, u32[]{:S(2)}, u32[]{:S(2)}) %collective-permute-start.8) | collective-permute-done | bytes 2080 | tf_op jit(solution)/shard_map/ppermute | solution.py:236
  27.2 1.7 %collective-permute-done.7 = f32[4,128]{1,0:T(4,128)S(1)} collective-permute-done((f32[4,128]{1,0:T(4,128)S(1)}, f32[4,128]{1,0:T(4,128)S(1)}, u32[]{:S(2)}, u32[]{:S(2)}) %collective-permute-start.7) | collective-permute-done | bytes 2080 | tf_op jit(solution)/shard_map/ppermute | solution.py:212
  29.0 0.6 %maximum_bitcast_fusion = f32[512]{0:T(512)} fusion(f32[4,128]{1,0:T(4,128)S(1)} %collective-permute-done.8, f32[4,128]{1,0:T(4,128)S(1)} %collective-permute-done.7, f32[8,128]{1,0:T(8,128)S(1)} %max.15), kind=kLoop, calls=%fused_computation | loop fusion | flops 1536 | bytes 8192 | tf_op jit(solution)/shard_map/reshape | solution.py:243
  (6 shorter events, 0.1 us)
Async XLA Ops:
  3.4 15.8 %collective-permute-start.2 = (bf16[528,256]{1,0:T(8,128)(2,1)S(1)}, bf16[528,256]{1,0:T(8,128)(2,1)S(1)}, u32[]{:S(2)}, u32[]{:S(2)}) collective-permute-start(bf16[528,256]{1,0:T(8,128)(2,1)S(1)} %shard_map.46.refs_0_.refs_1_), channel_id=1, source_target_pairs={{0,1},{1,0},{2,3},{3,2},{4,5},{5,4},{6,7},{7,6},{8,9},{9,8},{10,11... | collective-permute-start | bytes 811016 | tf_op jit(solution)/shard_map/ppermute | solution.py:212
  3.9 16.1 %collective-permute-start.5 = (bf16[528,256]{1,0:T(8,128)(2,1)S(1)}, bf16[528,256]{1,0:T(8,128)(2,1)S(1)}, u32[]{:S(2)}, u32[]{:S(2)}) collective-permute-start(bf16[528,256]{1,0:T(8,128)(2,1)S(1)} %shard_map.46.refs_0_.refs_1_), channel_id=1, source_target_pairs={{8,12},{0,4},{12,8},{4,0},{9,13},{1,5},{13,9},{5,1},{10,14},{2,6},... | collective-permute-start | bytes 811016 | tf_op jit(solution)/shard_map/ppermute | solution.py:220
  6.6 15.2 %collective-permute-start.1 = (bf16[528,256]{1,0:T(8,128)(2,1)S(1)}, bf16[528,256]{1,0:T(8,128)(2,1)S(1)}, u32[]{:S(2)}, u32[]{:S(2)}) collective-permute-start(bf16[528,256]{1,0:T(8,128)(2,1)S(1)} %shard_map.46.refs_0_.refs_1_), channel_id=1, source_target_pairs={{4,12},{8,4},{0,8},{12,0},{5,13},{9,5},{1,9},{13,1},{6,14},{10,6},... | collective-permute-start | bytes 811016 | tf_op jit(solution)/shard_map/ppermute | solution.py:219
  9.2 8.3 %collective-permute-start = (bf16[528,256]{1,0:T(8,128)(2,1)S(1)}, bf16[528,256]{1,0:T(8,128)(2,1)S(1)}, u32[]{:S(2)}, u32[]{:S(2)}) collective-permute-start(bf16[528,256]{1,0:T(8,128)(2,1)S(1)} %get-tuple-element.65), channel_id=1, source_target_pairs={{0,2},{1,3},{2,0},{3,1},{4,6},{5,7},{6,4},{7,5},{8,10},{9,11},{10,... | collective-permute-start | bytes 811016 | tf_op jit(solution)/shard_map/while/body/ppermute | solution.py:212
  17.6 1.6 %collective-permute-start.4 = (bf16[272,256]{1,0:T(8,128)(2,1)S(1)}, bf16[272,256]{1,0:T(8,128)(2,1)S(1)}, u32[]{:S(2)}, u32[]{:S(2)}) collective-permute-start(bf16[272,256]{1,0:T(8,128)(2,1)S(1)} %slice.13), channel_id=1, source_target_pairs={{0,1},{1,0},{2,3},{3,2},{4,5},{5,4},{6,7},{7,6},{8,9},{9,8},{10,11... | collective-permute-start | bytes 417800 | tf_op jit(solution)/shard_map/ppermute | solution.py:212
  17.7 1.5 %collective-permute-start.3 = (bf16[256,256]{1,0:T(8,128)(2,1)S(1)}, bf16[256,256]{1,0:T(8,128)(2,1)S(1)}, u32[]{:S(2)}, u32[]{:S(2)}) collective-permute-start(bf16[256,256]{1,0:T(8,128)(2,1)S(1)} %slice.12), channel_id=1, source_target_pairs={{0,1},{1,0},{2,3},{3,2},{4,5},{5,4},{6,7},{7,6},{8,9},{9,8},{10,11... | collective-permute-start | bytes 393224 | tf_op jit(solution)/shard_map/ppermute | solution.py:212
  22.6 2.7 %collective-permute-start.6 = (f32[8,128]{1,0:T(8,128)S(1)}, f32[8,128]{1,0:T(8,128)S(1)}, u32[]{:S(2)}, u32[]{:S(2)}) collective-permute-start(f32[8,128]{1,0:T(8,128)S(1)} %get-tuple-element.32), channel_id=1, source_target_pairs={{0,1},{1,0},{2,3},{3,2},{4,5},{5,4},{6,7},{7,6},{8,9},{9,8},{10,11... | collective-permute-start | bytes 12296 | tf_op jit(solution)/shard_map/ppermute | solution.py:212
  22.7 4.5 %collective-permute-start.8 = (f32[4,128]{1,0:T(4,128)S(1)}, f32[4,128]{1,0:T(4,128)S(1)}, u32[]{:S(2)}, u32[]{:S(2)}) collective-permute-start(f32[4,128]{1,0:T(4,128)S(1)} %get-tuple-element.33), channel_id=1, source_target_pairs={{12,4},{4,8},{8,0},{0,12},{13,5},{5,9},{9,1},{1,13},{14,6},{6,10},... | collective-permute-start | bytes 6152 | tf_op jit(solution)/shard_map/ppermute | solution.py:236
  25.3 3.6 %collective-permute-start.7 = (f32[4,128]{1,0:T(4,128)S(1)}, f32[4,128]{1,0:T(4,128)S(1)}, u32[]{:S(2)}, u32[]{:S(2)}) collective-permute-start(f32[4,128]{1,0:T(4,128)S(1)} %slice.15), channel_id=1, source_target_pairs={{0,2},{1,3},{2,0},{3,1},{4,6},{5,7},{6,4},{7,5},{8,10},{9,11},{10,... | collective-permute-start | bytes 6152 | tf_op jit(solution)/shard_map/ppermute | solution.py:212

commit v19 on v18

--- a/solution.py
+++ b/solution.py
@@ -198,7 +198,7 @@
     half = count // 2
     circle = [count - 1 - 2 * i for i in range(half)] + [count - 2 - 2 * i for i in range(half)]
     return [
-        [(circle[(i + step) % count], circle[i]) for i in range(count)]
+        [(circle[i], circle[(i + step) % count]) for i in range(count)]
         for step in range(1, half + 1)
     ]
 

time: 29.7 us -> 28.9 us (0.973)
  starting transfers between devices: 12.2 us -> 11.1 us
  waiting for transfers between devices: 10.8 us -> 11.1 us
    ppermute x1, waiting for transfers between devices: 0.34 us -> 2.17 us  [per_device(): backs.append(lax.ppermute(found, 'owners', [(b, a) for a, b in step]))]
    ppermute x6, waiting for transfers between devices: 9.53 us -> 7.77 us  [swap(): lax.ppermute(block, 'split', [(s, s ^ offset) for s in range(split_count)])]
    ppermute x1, starting transfers between devices: 2.63 us -> 1.7 us  [per_device(): backs.append(lax.ppermute(found, 'owners', [(b, a) for a, b in step]))]
  transfers between devices with their start and end apart: 9 -> 9, of which waited for: 5 -> 4; matrix products, arithmetic and copies ran while one was open for 0% -> 0% of each run, Pallas kernels for 5% -> 6%
where the time goes in v19:
time: 28.9 us; the launch traced here: 28.8 us
  starting transfers between devices  11.1 us (38%)
  waiting for transfers between devices  11.1 us (38%)
  Pallas kernels  5.82 us (20%)
  other arithmetic  0.59 us (2%)
    ppermute x6, waiting for transfers between devices, swap(): lax.ppermute(block, 'split', [(s, s ^ offset) for s in range(split_count)])  7.77 us
    ppermute x6, starting transfers between devices, swap(): lax.ppermute(block, 'split', [(s, s ^ offset) for s in range(split_count)])  4.33 us
    pallas_call x1, Pallas kernels, project(): pl.pallas_call(project_kernel, in_specs=[pl.BlockSpec(memory_space=pltpu....  3.38 us
    ppermute x1, starting transfers between devices, per_device(): nearby = lax.ppermute(own, 'owners', last)  2.65 us
    ppermute x1, starting transfers between devices, per_device(): keys = [lax.ppermute(own, 'owners', step) for step in steps]  2.47 us
    pallas_call x3, Pallas kernels, score(): pl.pallas_call(functools.partial(score_kernel, len(keys), cols, [len(row)...  2.44 us
    ppermute x1, waiting for transfers between devices, per_device(): backs.append(lax.ppermute(found, 'owners', [(b, a) for a, b in step]))  2.17 us
    ppermute x1, starting transfers between devices, per_device(): backs.append(lax.ppermute(found, 'owners', [(b, a) for a, b in step]))  1.7 us
  transfers between devices with their start and end apart: 9, of which 4 were waited for; matrix products, arithmetic and copies ran while one was open for 0% of the time, Pallas kernels for 6%

profile of v19, /device:TPU:0, one launch (start us, length us, event | category | flops | bytes accessed | tf_op | source)
XLA Modules:
  0.0 28.8 jit_solution(56272554487948592)
XLA Ops:
  0.0 3.4 %shard_map.46.refs_0_.refs_1_ = bf16[528,256]{1,0:T(8,128)(2,1)S(1)} custom-call(bf16[512,4096]{1,0:T(8,128)(2,1)} %source_hbm.1, bf16[4096,256]{1,0:T(8,128)(2,1)} %basis_hbm.1, s32[4,128]{1,0:T(4,128)} %bitcast.4, s32[4,128]{1,0:T(4,128)} %bitcast.5), custom_call_target="tpu_custom_call" | custom-call | flops 1073741824 | bytes 6291456 | tf_op jit(solution)/shard_map/pallas_call | solution.py:65
  3.4 0.5 %collective-permute-start.2 = (bf16[528,256]{1,0:T(8,128)(2,1)S(1)}, bf16[528,256]{1,0:T(8,128)(2,1)S(1)}, u32[]{:S(2)}, u32[]{:S(2)}) collective-permute-start(bf16[528,256]{1,0:T(8,128)(2,1)S(1)} %shard_map.46.refs_0_.refs_1_), channel_id=1, source_target_pairs={{0,1},{1,0},{2,3},{3,2},{4,5},{5,4},{6,7},{7,6},{8,9},{9,8},{10,11... | collective-permute-start | bytes 811016 | tf_op jit(solution)/shard_map/ppermute | solution.py:212
  3.9 2.6 %collective-permute-start.5 = (bf16[528,256]{1,0:T(8,128)(2,1)S(1)}, bf16[528,256]{1,0:T(8,128)(2,1)S(1)}, u32[]{:S(2)}, u32[]{:S(2)}) collective-permute-start(bf16[528,256]{1,0:T(8,128)(2,1)S(1)} %shard_map.46.refs_0_.refs_1_), channel_id=1, source_target_pairs={{12,8},{4,0},{8,12},{0,4},{13,9},{5,1},{9,13},{1,5},{14,10},{6,2},... | collective-permute-start | bytes 811016 | tf_op jit(solution)/shard_map/ppermute | solution.py:220
  6.6 2.5 %collective-permute-start.1 = (bf16[528,256]{1,0:T(8,128)(2,1)S(1)}, bf16[528,256]{1,0:T(8,128)(2,1)S(1)}, u32[]{:S(2)}, u32[]{:S(2)}) collective-permute-start(bf16[528,256]{1,0:T(8,128)(2,1)S(1)} %shard_map.46.refs_0_.refs_1_), channel_id=1, source_target_pairs={{12,4},{4,8},{8,0},{0,12},{13,5},{5,9},{9,1},{1,13},{14,6},{6,10},... | collective-permute-start | bytes 811016 | tf_op jit(solution)/shard_map/ppermute | solution.py:219
  9.1 8.4 %while.10 = (s32[]{:T(128)}, bf16[528,256]{1,0:T(8,128)(2,1)S(1)}, s32[]{:T(128)}, s32[]{:T(128)}) while((s32[]{:T(128)}, bf16[528,256]{1,0:T(8,128)(2,1)S(1)}, s32[]{:T(128)}, s32[]{:T(128)}) %tuple.18), condition=%wide.region_1.0_spmd, body=%wide.region_0.0_spmd.sunk | while | flops 2 | bytes 1622109 | solution.py:223
  9.1 1.6 %collective-permute-start = (bf16[528,256]{1,0:T(8,128)(2,1)S(1)}, bf16[528,256]{1,0:T(8,128)(2,1)S(1)}, u32[]{:S(2)}, u32[]{:S(2)}) collective-permute-start(bf16[528,256]{1,0:T(8,128)(2,1)S(1)} %get-tuple-element.65), channel_id=1, source_target_pairs={{0,2},{1,3},{2,0},{3,1},{4,6},{5,7},{6,4},{7,5},{8,10},{9,11},{10,... | collective-permute-start | bytes 811016 | tf_op jit(solution)/shard_map/while/body/ppermute | solution.py:212
  10.6 6.8 %collective-permute-done = bf16[528,256]{1,0:T(8,128)(2,1)S(1)} collective-permute-done((bf16[528,256]{1,0:T(8,128)(2,1)S(1)}, bf16[528,256]{1,0:T(8,128)(2,1)S(1)}, u32[]{:S(2)}, u32[]{:S(2)}) %collective-permute-start) | collective-permute-done | bytes 270368 | tf_op jit(solution)/shard_map/while/body/ppermute | solution.py:212
  17.5 0.1 collective-permute-start.4
  17.6 0.6 %collective-permute-start.3 = (bf16[256,256]{1,0:T(8,128)(2,1)S(1)}, bf16[256,256]{1,0:T(8,128)(2,1)S(1)}, u32[]{:S(2)}, u32[]{:S(2)}) collective-permute-start(bf16[256,256]{1,0:T(8,128)(2,1)S(1)} %slice.12), channel_id=1, source_target_pairs={{0,1},{1,0},{2,3},{3,2},{4,5},{5,4},{6,7},{7,6},{8,9},{9,8},{10,11... | collective-permute-start | bytes 393224 | tf_op jit(solution)/shard_map/ppermute | solution.py:212
  18.1 1.0 %collective-permute-done.3.refs_4_ = bf16[256,256]{1,0:T(8,128)(2,1)S(1)} collective-permute-done((bf16[256,256]{1,0:T(8,128)(2,1)S(1)}, bf16[256,256]{1,0:T(8,128)(2,1)S(1)}, u32[]{:S(2)}, u32[]{:S(2)}) %collective-permute-start.3) | collective-permute-done | bytes 131104 | tf_op jit(solution)/shard_map/ppermute | solution.py:212
  19.1 0.0 collective-permute-done.4.refs_5_
  19.1 0.0 collective-permute-done.2.refs_3_
  19.1 0.8 %shard_map.47.refs_6_ = f32[8,128]{1,0:T(8,128)S(1)} custom-call(bf16[528,256]{1,0:T(8,128)(2,1)S(1)} %shard_map.46.refs_0_.refs_1_, bf16[528,256]{1,0:T(8,128)(2,1)S(1)} %shard_map.46.refs_0_.refs_1_, bf16[528,256]{1,0:T(8,128)(2,1)S(1)} %get-tuple-element.28.refs_2_, bf16[528,256]{1,0:T(8,128)(2,1)S(1)} %collective-permute-done.2.refs_3_, ...), custom_call_target="tpu_custom_call" | custom-call | tf_op jit(solution)/shard_map/pallas_call | solution.py:179
  19.9 0.0 collective-permute-done.5.refs_0_
  19.9 0.8 %shard_map.48 = (f32[8,128]{1,0:T(8,128)S(1)}, f32[8,128]{1,0:T(8,128)S(1)}) custom-call(bf16[528,256]{1,0:T(8,128)(2,1)S(1)} %collective-permute-done.5.refs_0_, bf16[528,256]{1,0:T(8,128)(2,1)S(1)} %shard_map.46.refs_0_.refs_1_, bf16[528,256]{1,0:T(8,128)(2,1)S(1)} %get-tuple-element.28.refs_2_, bf16[528,256]{1,0:T(8,128)(2,1)S(1)} %collective-permute-done.2.refs_3_, ...), custom_call_target="tpu_custom_call" | custom-call | tf_op jit(solution)/shard_map/pallas_call | solution.py:179
  20.7 1.1 %collective-permute-done.1.refs_0_ = bf16[528,256]{1,0:T(8,128)(2,1)S(1)} collective-permute-done((bf16[528,256]{1,0:T(8,128)(2,1)S(1)}, bf16[528,256]{1,0:T(8,128)(2,1)S(1)}, u32[]{:S(2)}, u32[]{:S(2)}) %collective-permute-start.1) | collective-permute-done | bytes 270368 | tf_op jit(solution)/shard_map/ppermute | solution.py:219
  21.8 0.8 %shard_map.49 = (f32[4,128]{1,0:T(4,128)S(1)}, f32[8,128]{1,0:T(8,128)S(1)}, f32[8,128]{1,0:T(8,128)S(1)}) custom-call(bf16[528,256]{1,0:T(8,128)(2,1)S(1)} %collective-permute-done.1.refs_0_, bf16[528,256]{1,0:T(8,128)(2,1)S(1)} %shard_map.46.refs_0_.refs_1_, bf16[528,256]{1,0:T(8,128)(2,1)S(1)} %get-tuple-element.28.refs_2_, ...), custom_call_target="tpu_custom_call" | custom-call | tf_op jit(solution)/shard_map/pallas_call | solution.py:179
  22.7 0.1 collective-permute-start.6
  22.8 1.7 %collective-permute-start.8 = (f32[4,128]{1,0:T(4,128)S(1)}, f32[4,128]{1,0:T(4,128)S(1)}, u32[]{:S(2)}, u32[]{:S(2)}) collective-permute-start(f32[4,128]{1,0:T(4,128)S(1)} %get-tuple-element.33), channel_id=1, source_target_pairs={{4,12},{8,4},{0,8},{12,0},{5,13},{9,5},{1,9},{13,1},{6,14},{10,6},... | collective-permute-start | bytes 6152 | tf_op jit(solution)/shard_map/ppermute | solution.py:236
  24.5 0.0 collective-permute-done.6
  24.5 1.6 %collective-permute-start.7 = (f32[4,128]{1,0:T(4,128)S(1)}, f32[4,128]{1,0:T(4,128)S(1)}, u32[]{:S(2)}, u32[]{:S(2)}) collective-permute-start(f32[4,128]{1,0:T(4,128)S(1)} %slice.15), channel_id=1, source_target_pairs={{0,2},{1,3},{2,0},{3,1},{4,6},{5,7},{6,4},{7,5},{8,10},{9,11},{10,... | collective-permute-start | bytes 6152 | tf_op jit(solution)/shard_map/ppermute | solution.py:212
  26.0 2.2 %collective-permute-done.8 = f32[4,128]{1,0:T(4,128)S(1)} collective-permute-done((f32[4,128]{1,0:T(4,128)S(1)}, f32[4,128]{1,0:T(4,128)S(1)}, u32[]{:S(2)}, u32[]{:S(2)}) %collective-permute-start.8) | collective-permute-done | bytes 2080 | tf_op jit(solution)/shard_map/ppermute | solution.py:236
  28.2 0.0 collective-permute-done.7
  28.2 0.6 %maximum_bitcast_fusion = f32[512]{0:T(512)} fusion(f32[4,128]{1,0:T(4,128)S(1)} %collective-permute-done.8, f32[4,128]{1,0:T(4,128)S(1)} %collective-permute-done.7, f32[8,128]{1,0:T(8,128)S(1)} %max.15), kind=kLoop, calls=%fused_computation | loop fusion | flops 1536 | bytes 8192 | tf_op jit(solution)/shard_map/reshape | solution.py:243
  (6 shorter events, 0.1 us)
Async XLA Ops:
  3.4 15.7 %collective-permute-start.2 = (bf16[528,256]{1,0:T(8,128)(2,1)S(1)}, bf16[528,256]{1,0:T(8,128)(2,1)S(1)}, u32[]{:S(2)}, u32[]{:S(2)}) collective-permute-start(bf16[528,256]{1,0:T(8,128)(2,1)S(1)} %shard_map.46.refs_0_.refs_1_), channel_id=1, source_target_pairs={{0,1},{1,0},{2,3},{3,2},{4,5},{5,4},{6,7},{7,6},{8,9},{9,8},{10,11... | collective-permute-start | bytes 811016 | tf_op jit(solution)/shard_map/ppermute | solution.py:212
  3.9 16.0 %collective-permute-start.5 = (bf16[528,256]{1,0:T(8,128)(2,1)S(1)}, bf16[528,256]{1,0:T(8,128)(2,1)S(1)}, u32[]{:S(2)}, u32[]{:S(2)}) collective-permute-start(bf16[528,256]{1,0:T(8,128)(2,1)S(1)} %shard_map.46.refs_0_.refs_1_), channel_id=1, source_target_pairs={{12,8},{4,0},{8,12},{0,4},{13,9},{5,1},{9,13},{1,5},{14,10},{6,2},... | collective-permute-start | bytes 811016 | tf_op jit(solution)/shard_map/ppermute | solution.py:220
  6.6 15.3 %collective-permute-start.1 = (bf16[528,256]{1,0:T(8,128)(2,1)S(1)}, bf16[528,256]{1,0:T(8,128)(2,1)S(1)}, u32[]{:S(2)}, u32[]{:S(2)}) collective-permute-start(bf16[528,256]{1,0:T(8,128)(2,1)S(1)} %shard_map.46.refs_0_.refs_1_), channel_id=1, source_target_pairs={{12,4},{4,8},{8,0},{0,12},{13,5},{5,9},{9,1},{1,13},{14,6},{6,10},... | collective-permute-start | bytes 811016 | tf_op jit(solution)/shard_map/ppermute | solution.py:219
  9.1 8.3 %collective-permute-start = (bf16[528,256]{1,0:T(8,128)(2,1)S(1)}, bf16[528,256]{1,0:T(8,128)(2,1)S(1)}, u32[]{:S(2)}, u32[]{:S(2)}) collective-permute-start(bf16[528,256]{1,0:T(8,128)(2,1)S(1)} %get-tuple-element.65), channel_id=1, source_target_pairs={{0,2},{1,3},{2,0},{3,1},{4,6},{5,7},{6,4},{7,5},{8,10},{9,11},{10,... | collective-permute-start | bytes 811016 | tf_op jit(solution)/shard_map/while/body/ppermute | solution.py:212
  17.5 1.6 %collective-permute-start.4 = (bf16[272,256]{1,0:T(8,128)(2,1)S(1)}, bf16[272,256]{1,0:T(8,128)(2,1)S(1)}, u32[]{:S(2)}, u32[]{:S(2)}) collective-permute-start(bf16[272,256]{1,0:T(8,128)(2,1)S(1)} %slice.13), channel_id=1, source_target_pairs={{0,1},{1,0},{2,3},{3,2},{4,5},{5,4},{6,7},{7,6},{8,9},{9,8},{10,11... | collective-permute-start | bytes 417800 | tf_op jit(solution)/shard_map/ppermute | solution.py:212
  17.6 1.5 %collective-permute-start.3 = (bf16[256,256]{1,0:T(8,128)(2,1)S(1)}, bf16[256,256]{1,0:T(8,128)(2,1)S(1)}, u32[]{:S(2)}, u32[]{:S(2)}) collective-permute-start(bf16[256,256]{1,0:T(8,128)(2,1)S(1)} %slice.12), channel_id=1, source_target_pairs={{0,1},{1,0},{2,3},{3,2},{4,5},{5,4},{6,7},{7,6},{8,9},{9,8},{10,11... | collective-permute-start | bytes 393224 | tf_op jit(solution)/shard_map/ppermute | solution.py:212
  22.7 1.8 %collective-permute-start.6 = (f32[8,128]{1,0:T(8,128)S(1)}, f32[8,128]{1,0:T(8,128)S(1)}, u32[]{:S(2)}, u32[]{:S(2)}) collective-permute-start(f32[8,128]{1,0:T(8,128)S(1)} %get-tuple-element.32), channel_id=1, source_target_pairs={{0,1},{1,0},{2,3},{3,2},{4,5},{5,4},{6,7},{7,6},{8,9},{9,8},{10,11... | collective-permute-start | bytes 12296 | tf_op jit(solution)/shard_map/ppermute | solution.py:212
  22.8 5.4 %collective-permute-start.8 = (f32[4,128]{1,0:T(4,128)S(1)}, f32[4,128]{1,0:T(4,128)S(1)}, u32[]{:S(2)}, u32[]{:S(2)}) collective-permute-start(f32[4,128]{1,0:T(4,128)S(1)} %get-tuple-element.33), channel_id=1, source_target_pairs={{4,12},{8,4},{0,8},{12,0},{5,13},{9,5},{1,9},{13,1},{6,14},{10,6},... | collective-permute-start | bytes 6152 | tf_op jit(solution)/shard_map/ppermute | solution.py:236
  24.5 3.7 %collective-permute-start.7 = (f32[4,128]{1,0:T(4,128)S(1)}, f32[4,128]{1,0:T(4,128)S(1)}, u32[]{:S(2)}, u32[]{:S(2)}) collective-permute-start(f32[4,128]{1,0:T(4,128)S(1)} %slice.15), channel_id=1, source_target_pairs={{0,2},{1,3},{2,0},{3,1},{4,6},{5,7},{6,4},{7,5},{8,10},{9,11},{10,... | collective-permute-start | bytes 6152 | tf_op jit(solution)/shard_map/ppermute | solution.py:212

commit v20 on v19

--- a/solution.py
+++ b/solution.py
@@ -100,8 +100,9 @@
     key_refs = [refs.pop(0) for _ in range(key_count)]
     row_refs = [[refs.pop(0) for _ in range(parts)] for parts in row_parts]
     known_refs = [refs.pop(0) for _ in range(known)]
+    row_tag_refs = [] if own_first else [refs.pop(0) for _ in row_parts]
     col_refs = [refs.pop(0) for _ in range(cols)]
-    row_outs = refs
+    row_outs, row_tag_outs = refs[: 2 - own_first], refs[2 - own_first :]
     row_count = key_refs[0].shape[0] - TAG_ROWS
     tiles = row_count // LANES
     best = [
@@ -114,10 +115,15 @@
         place = 0
         for part_ref in part_refs:
             count = part_ref.shape[0] // LANES * LANES
-            tags = [
-                jnp.broadcast_to(row_tags[at : at + 1, :], (LANES, LANES)).T
-                for at in range(place, place + count // LANES)
-            ]
+            tags = []
+            for at in range(place, place + count // LANES):
+                span = slice(at * LANES, (at + 1) * LANES)
+                if own_first:
+                    tag = jnp.broadcast_to(row_tags[at : at + 1, :], (LANES, LANES)).T
+                    row_tag_outs[block][span, :] = tag
+                else:
+                    tag = row_tag_refs[block][span, :]
+                tags.append(tag)
             across = [None] * len(tags)
             for key, key_ref in enumerate(key_refs):
                 key_tags = key_ref[row_count:, :LANES].astype(jnp.float32)
@@ -167,14 +173,16 @@
         row_outs[0][tiles:, :] = jnp.full((rest, LANES), ABSENT, jnp.float32)
 
 
-def score(keys, rows, cols=0, known=(), own_first=False):
+def score(keys, rows, cols=0, known=(), row_tags=None):
     parts = [row if isinstance(row, tuple) else (row,) for row in rows]
     operands = [*keys, *(part for row in parts for part in row)]
-    operands += known
+    operands += known if row_tags is None else [*known, *row_tags]
+    own_first = row_tags is None
     tiles = keys[0].shape[0] // LANES
     best = jax.ShapeDtypeStruct((tiles, LANES), jnp.float32)
     group = jax.ShapeDtypeStruct((len(rows) // 2 * tiles, LANES), jnp.float32)
-    out_shape = [best] * cols + [group] * (1 if own_first else 2)
+    row_tag = jax.ShapeDtypeStruct((tiles * LANES, LANES), jnp.float32)
+    out_shape = [best] * cols + ([group] + [row_tag] * len(rows) if own_first else [group] * 2)
     inside = pl.BlockSpec(memory_space=pltpu.VMEM)
     found = pl.pallas_call(
         functools.partial(
@@ -228,11 +236,11 @@
     )
     rows = [own, *besides, swap(own, 1)]
     rows += [tuple(swap(part, 1) for part in halves(beside)) for beside in besides]
-    _, row_best = score([own], rows, own_first=True)
-    _, row_best = score([nearby], rows, known=row_best)
+    _, (own_best, *row_tags) = score([own], rows)
+    _, row_best = score([nearby], rows, known=[own_best], row_tags=row_tags)
     backs = []
     for key, step in zip(keys, steps):
-        (found,), row_best = score([key], rows, cols=1, known=row_best)
+        (found,), row_best = score([key], rows, cols=1, known=row_best, row_tags=row_tags)
         backs.append(lax.ppermute(found, "owners", [(b, a) for a, b in step]))
     local = jnp.maximum(row_best[0], swap(row_best[1], 1))
     best = local[:tiles]

time: 28.9 us -> 28.9 us (level)
  no operation moved by 1% of the time
where the time goes in v20:
time: 28.9 us; the launch traced here: 28.8 us
  starting transfers between devices  11.2 us (39%)
  waiting for transfers between devices  11.1 us (38%)
  Pallas kernels  5.84 us (20%)
  other arithmetic  0.59 us (2%)
    ppermute x6, waiting for transfers between devices, swap(): lax.ppermute(block, 'split', [(s, s ^ offset) for s in range(split_count)])  7.77 us
    ppermute x6, starting transfers between devices, swap(): lax.ppermute(block, 'split', [(s, s ^ offset) for s in range(split_count)])  4.33 us
    pallas_call x1, Pallas kernels, project(): pl.pallas_call(project_kernel, in_specs=[pl.BlockSpec(memory_space=pltpu....  3.38 us
    ppermute x1, starting transfers between devices, per_device(): nearby = lax.ppermute(own, 'owners', last)  2.65 us
    ppermute x1, starting transfers between devices, per_device(): keys = [lax.ppermute(own, 'owners', step) for step in steps]  2.47 us
    pallas_call x3, Pallas kernels, score(): pl.pallas_call(functools.partial(score_kernel, len(keys), cols, [len(row)...  2.46 us
    ppermute x1, waiting for transfers between devices, per_device(): backs.append(lax.ppermute(found, 'owners', [(b, a) for a, b in step]))  2.17 us
    ppermute x1, starting transfers between devices, per_device(): backs.append(lax.ppermute(found, 'owners', [(b, a) for a, b in step]))  1.7 us
  transfers between devices with their start and end apart: 9, of which 4 were waited for; matrix products, arithmetic and copies ran while one was open for 0% of the time, Pallas kernels for 6%

profile of v20, /device:TPU:0, one launch (start us, length us, event | category | flops | bytes accessed | tf_op | source)
XLA Modules:
  0.0 28.8 jit_solution(6532661760937368221)
XLA Ops:
  0.0 3.4 %shard_map.46.refs_0_.refs_1_ = bf16[528,256]{1,0:T(8,128)(2,1)S(1)} custom-call(bf16[512,4096]{1,0:T(8,128)(2,1)} %source_hbm.1, bf16[4096,256]{1,0:T(8,128)(2,1)} %basis_hbm.1, s32[4,128]{1,0:T(4,128)} %bitcast.4, s32[4,128]{1,0:T(4,128)} %bitcast.5), custom_call_target="tpu_custom_call" | custom-call | flops 1073741824 | bytes 6291456 | tf_op jit(solution)/shard_map/pallas_call | solution.py:65
  3.4 0.5 %collective-permute-start.2 = (bf16[528,256]{1,0:T(8,128)(2,1)S(1)}, bf16[528,256]{1,0:T(8,128)(2,1)S(1)}, u32[]{:S(2)}, u32[]{:S(2)}) collective-permute-start(bf16[528,256]{1,0:T(8,128)(2,1)S(1)} %shard_map.46.refs_0_.refs_1_), channel_id=1, source_target_pairs={{0,1},{1,0},{2,3},{3,2},{4,5},{5,4},{6,7},{7,6},{8,9},{9,8},{10,11... | collective-permute-start | bytes 811016 | tf_op jit(solution)/shard_map/ppermute | solution.py:220
  3.9 2.6 %collective-permute-start.5 = (bf16[528,256]{1,0:T(8,128)(2,1)S(1)}, bf16[528,256]{1,0:T(8,128)(2,1)S(1)}, u32[]{:S(2)}, u32[]{:S(2)}) collective-permute-start(bf16[528,256]{1,0:T(8,128)(2,1)S(1)} %shard_map.46.refs_0_.refs_1_), channel_id=1, source_target_pairs={{12,8},{4,0},{8,12},{0,4},{13,9},{5,1},{9,13},{1,5},{14,10},{6,2},... | collective-permute-start | bytes 811016 | tf_op jit(solution)/shard_map/ppermute | solution.py:228
  6.6 2.5 %collective-permute-start.1 = (bf16[528,256]{1,0:T(8,128)(2,1)S(1)}, bf16[528,256]{1,0:T(8,128)(2,1)S(1)}, u32[]{:S(2)}, u32[]{:S(2)}) collective-permute-start(bf16[528,256]{1,0:T(8,128)(2,1)S(1)} %shard_map.46.refs_0_.refs_1_), channel_id=1, source_target_pairs={{12,4},{4,8},{8,0},{0,12},{13,5},{5,9},{9,1},{1,13},{14,6},{6,10},... | collective-permute-start | bytes 811016 | tf_op jit(solution)/shard_map/ppermute | solution.py:227
  9.1 8.4 %while.10 = (s32[]{:T(128)}, bf16[528,256]{1,0:T(8,128)(2,1)S(1)}, s32[]{:T(128)}, s32[]{:T(128)}) while((s32[]{:T(128)}, bf16[528,256]{1,0:T(8,128)(2,1)S(1)}, s32[]{:T(128)}, s32[]{:T(128)}) %tuple.18), condition=%wide.region_1.0_spmd, body=%wide.region_0.0_spmd.sunk | while | flops 2 | bytes 1622109 | solution.py:231
  9.1 1.6 %collective-permute-start = (bf16[528,256]{1,0:T(8,128)(2,1)S(1)}, bf16[528,256]{1,0:T(8,128)(2,1)S(1)}, u32[]{:S(2)}, u32[]{:S(2)}) collective-permute-start(bf16[528,256]{1,0:T(8,128)(2,1)S(1)} %get-tuple-element.75), channel_id=1, source_target_pairs={{0,2},{1,3},{2,0},{3,1},{4,6},{5,7},{6,4},{7,5},{8,10},{9,11},{10,... | collective-permute-start | bytes 811016 | tf_op jit(solution)/shard_map/while/body/ppermute | solution.py:220
  10.6 6.8 %collective-permute-done = bf16[528,256]{1,0:T(8,128)(2,1)S(1)} collective-permute-done((bf16[528,256]{1,0:T(8,128)(2,1)S(1)}, bf16[528,256]{1,0:T(8,128)(2,1)S(1)}, u32[]{:S(2)}, u32[]{:S(2)}) %collective-permute-start) | collective-permute-done | bytes 270368 | tf_op jit(solution)/shard_map/while/body/ppermute | solution.py:220
  17.5 0.1 collective-permute-start.4
  17.6 0.6 %collective-permute-start.3 = (bf16[256,256]{1,0:T(8,128)(2,1)S(1)}, bf16[256,256]{1,0:T(8,128)(2,1)S(1)}, u32[]{:S(2)}, u32[]{:S(2)}) collective-permute-start(bf16[256,256]{1,0:T(8,128)(2,1)S(1)} %slice.12), channel_id=1, source_target_pairs={{0,1},{1,0},{2,3},{3,2},{4,5},{5,4},{6,7},{7,6},{8,9},{9,8},{10,11... | collective-permute-start | bytes 393224 | tf_op jit(solution)/shard_map/ppermute | solution.py:220
  18.1 1.0 %collective-permute-done.3.refs_4_ = bf16[256,256]{1,0:T(8,128)(2,1)S(1)} collective-permute-done((bf16[256,256]{1,0:T(8,128)(2,1)S(1)}, bf16[256,256]{1,0:T(8,128)(2,1)S(1)}, u32[]{:S(2)}, u32[]{:S(2)}) %collective-permute-start.3) | collective-permute-done | bytes 131104 | tf_op jit(solution)/shard_map/ppermute | solution.py:220
  19.1 0.0 collective-permute-done.4.refs_5_
  19.1 0.0 collective-permute-done.2.refs_3_
  19.1 0.8 %shard_map.47 = (f32[8,128]{1,0:T(8,128)S(1)}, f32[512,128]{1,0:T(8,128)S(1)}, f32[512,128]{1,0:T(8,128)S(1)}, f32[512,128]{1,0:T(8,128)S(1)}, f32[512,128]{1,0:T(8,128)S(1)}) custom-call(bf16[528,256]{1,0:T(8,128)(2,1)S(1)} %shard_map.46.refs_0_.refs_1_, bf16[528,256]{1,0:T(8,128)(2,1)S(1)} %shard_map.46.refs_0_.refs_1_, ...), custom_call_target="tpu_custom_call" | custom-call | tf_op jit(solution)/shard_map/pallas_call | solution.py:187
  19.9 0.0 collective-permute-done.5.refs_0_
  19.9 0.8 %shard_map.48 = (f32[8,128]{1,0:T(8,128)S(1)}, f32[8,128]{1,0:T(8,128)S(1)}) custom-call(bf16[528,256]{1,0:T(8,128)(2,1)S(1)} %collective-permute-done.5.refs_0_, bf16[528,256]{1,0:T(8,128)(2,1)S(1)} %shard_map.46.refs_0_.refs_1_, bf16[528,256]{1,0:T(8,128)(2,1)S(1)} %get-tuple-element.33.refs_2_, bf16[528,256]{1,0:T(8,128)(2,1)S(1)} %collective-permute-done.2.refs_3_, ...), custom_call_target="tpu_custom_call" | custom-call | tf_op jit(solution)/shard_map/pallas_call | solution.py:187
  20.7 1.1 %collective-permute-done.1.refs_0_ = bf16[528,256]{1,0:T(8,128)(2,1)S(1)} collective-permute-done((bf16[528,256]{1,0:T(8,128)(2,1)S(1)}, bf16[528,256]{1,0:T(8,128)(2,1)S(1)}, u32[]{:S(2)}, u32[]{:S(2)}) %collective-permute-start.1) | collective-permute-done | bytes 270368 | tf_op jit(solution)/shard_map/ppermute | solution.py:227
  21.8 0.8 %shard_map.49 = (f32[4,128]{1,0:T(4,128)S(1)}, f32[8,128]{1,0:T(8,128)S(1)}, f32[8,128]{1,0:T(8,128)S(1)}) custom-call(bf16[528,256]{1,0:T(8,128)(2,1)S(1)} %collective-permute-done.1.refs_0_, bf16[528,256]{1,0:T(8,128)(2,1)S(1)} %shard_map.46.refs_0_.refs_1_, bf16[528,256]{1,0:T(8,128)(2,1)S(1)} %get-tuple-element.33.refs_2_, ...), custom_call_target="tpu_custom_call" | custom-call | tf_op jit(solution)/shard_map/pallas_call | solution.py:187
  22.7 0.1 collective-permute-start.6
  22.8 1.7 %collective-permute-start.8 = (f32[4,128]{1,0:T(4,128)S(1)}, f32[4,128]{1,0:T(4,128)S(1)}, u32[]{:S(2)}, u32[]{:S(2)}) collective-permute-start(f32[4,128]{1,0:T(4,128)S(1)} %get-tuple-element.43), channel_id=1, source_target_pairs={{4,12},{8,4},{0,8},{12,0},{5,13},{9,5},{1,9},{13,1},{6,14},{10,6},... | collective-permute-start | bytes 6152 | tf_op jit(solution)/shard_map/ppermute | solution.py:244
  24.5 0.0 collective-permute-done.6
  24.5 1.6 %collective-permute-start.7 = (f32[4,128]{1,0:T(4,128)S(1)}, f32[4,128]{1,0:T(4,128)S(1)}, u32[]{:S(2)}, u32[]{:S(2)}) collective-permute-start(f32[4,128]{1,0:T(4,128)S(1)} %slice.15), channel_id=1, source_target_pairs={{0,2},{1,3},{2,0},{3,1},{4,6},{5,7},{6,4},{7,5},{8,10},{9,11},{10,... | collective-permute-start | bytes 6152 | tf_op jit(solution)/shard_map/ppermute | solution.py:220
  26.0 2.2 %collective-permute-done.8 = f32[4,128]{1,0:T(4,128)S(1)} collective-permute-done((f32[4,128]{1,0:T(4,128)S(1)}, f32[4,128]{1,0:T(4,128)S(1)}, u32[]{:S(2)}, u32[]{:S(2)}) %collective-permute-start.8) | collective-permute-done | bytes 2080 | tf_op jit(solution)/shard_map/ppermute | solution.py:244
  28.2 0.0 collective-permute-done.7
  28.2 0.6 %maximum_bitcast_fusion = f32[512]{0:T(512)} fusion(f32[4,128]{1,0:T(4,128)S(1)} %collective-permute-done.8, f32[4,128]{1,0:T(4,128)S(1)} %collective-permute-done.7, f32[8,128]{1,0:T(8,128)S(1)} %max.15), kind=kLoop, calls=%fused_computation | loop fusion | flops 1536 | bytes 8192 | tf_op jit(solution)/shard_map/reshape | solution.py:251
  (6 shorter events, 0.1 us)
Async XLA Ops:
  3.4 15.7 %collective-permute-start.2 = (bf16[528,256]{1,0:T(8,128)(2,1)S(1)}, bf16[528,256]{1,0:T(8,128)(2,1)S(1)}, u32[]{:S(2)}, u32[]{:S(2)}) collective-permute-start(bf16[528,256]{1,0:T(8,128)(2,1)S(1)} %shard_map.46.refs_0_.refs_1_), channel_id=1, source_target_pairs={{0,1},{1,0},{2,3},{3,2},{4,5},{5,4},{6,7},{7,6},{8,9},{9,8},{10,11... | collective-permute-start | bytes 811016 | tf_op jit(solution)/shard_map/ppermute | solution.py:220
  3.9 16.0 %collective-permute-start.5 = (bf16[528,256]{1,0:T(8,128)(2,1)S(1)}, bf16[528,256]{1,0:T(8,128)(2,1)S(1)}, u32[]{:S(2)}, u32[]{:S(2)}) collective-permute-start(bf16[528,256]{1,0:T(8,128)(2,1)S(1)} %shard_map.46.refs_0_.refs_1_), channel_id=1, source_target_pairs={{12,8},{4,0},{8,12},{0,4},{13,9},{5,1},{9,13},{1,5},{14,10},{6,2},... | collective-permute-start | bytes 811016 | tf_op jit(solution)/shard_map/ppermute | solution.py:228
  6.6 15.3 %collective-permute-start.1 = (bf16[528,256]{1,0:T(8,128)(2,1)S(1)}, bf16[528,256]{1,0:T(8,128)(2,1)S(1)}, u32[]{:S(2)}, u32[]{:S(2)}) collective-permute-start(bf16[528,256]{1,0:T(8,128)(2,1)S(1)} %shard_map.46.refs_0_.refs_1_), channel_id=1, source_target_pairs={{12,4},{4,8},{8,0},{0,12},{13,5},{5,9},{9,1},{1,13},{14,6},{6,10},... | collective-permute-start | bytes 811016 | tf_op jit(solution)/shard_map/ppermute | solution.py:227
  9.1 8.3 %collective-permute-start = (bf16[528,256]{1,0:T(8,128)(2,1)S(1)}, bf16[528,256]{1,0:T(8,128)(2,1)S(1)}, u32[]{:S(2)}, u32[]{:S(2)}) collective-permute-start(bf16[528,256]{1,0:T(8,128)(2,1)S(1)} %get-tuple-element.75), channel_id=1, source_target_pairs={{0,2},{1,3},{2,0},{3,1},{4,6},{5,7},{6,4},{7,5},{8,10},{9,11},{10,... | collective-permute-start | bytes 811016 | tf_op jit(solution)/shard_map/while/body/ppermute | solution.py:220
  17.5 1.6 %collective-permute-start.4 = (bf16[272,256]{1,0:T(8,128)(2,1)S(1)}, bf16[272,256]{1,0:T(8,128)(2,1)S(1)}, u32[]{:S(2)}, u32[]{:S(2)}) collective-permute-start(bf16[272,256]{1,0:T(8,128)(2,1)S(1)} %slice.13), channel_id=1, source_target_pairs={{0,1},{1,0},{2,3},{3,2},{4,5},{5,4},{6,7},{7,6},{8,9},{9,8},{10,11... | collective-permute-start | bytes 417800 | tf_op jit(solution)/shard_map/ppermute | solution.py:220
  17.6 1.5 %collective-permute-start.3 = (bf16[256,256]{1,0:T(8,128)(2,1)S(1)}, bf16[256,256]{1,0:T(8,128)(2,1)S(1)}, u32[]{:S(2)}, u32[]{:S(2)}) collective-permute-start(bf16[256,256]{1,0:T(8,128)(2,1)S(1)} %slice.12), channel_id=1, source_target_pairs={{0,1},{1,0},{2,3},{3,2},{4,5},{5,4},{6,7},{7,6},{8,9},{9,8},{10,11... | collective-permute-start | bytes 393224 | tf_op jit(solution)/shard_map/ppermute | solution.py:220
  22.7 1.8 %collective-permute-start.6 = (f32[8,128]{1,0:T(8,128)S(1)}, f32[8,128]{1,0:T(8,128)S(1)}, u32[]{:S(2)}, u32[]{:S(2)}) collective-permute-start(f32[8,128]{1,0:T(8,128)S(1)} %get-tuple-element.42), channel_id=1, source_target_pairs={{0,1},{1,0},{2,3},{3,2},{4,5},{5,4},{6,7},{7,6},{8,9},{9,8},{10,11... | collective-permute-start | bytes 12296 | tf_op jit(solution)/shard_map/ppermute | solution.py:220
  22.8 5.4 %collective-permute-start.8 = (f32[4,128]{1,0:T(4,128)S(1)}, f32[4,128]{1,0:T(4,128)S(1)}, u32[]{:S(2)}, u32[]{:S(2)}) collective-permute-start(f32[4,128]{1,0:T(4,128)S(1)} %get-tuple-element.43), channel_id=1, source_target_pairs={{4,12},{8,4},{0,8},{12,0},{5,13},{9,5},{1,9},{13,1},{6,14},{10,6},... | collective-permute-start | bytes 6152 | tf_op jit(solution)/shard_map/ppermute | solution.py:244
  24.5 3.7 %collective-permute-start.7 = (f32[4,128]{1,0:T(4,128)S(1)}, f32[4,128]{1,0:T(4,128)S(1)}, u32[]{:S(2)}, u32[]{:S(2)}) collective-permute-start(f32[4,128]{1,0:T(4,128)S(1)} %slice.15), channel_id=1, source_target_pairs={{0,2},{1,3},{2,0},{3,1},{4,6},{5,7},{6,4},{7,5},{8,10},{9,11},{10,... | collective-permute-start | bytes 6152 | tf_op jit(solution)/shard_map/ppermute | solution.py:220

commit v21 on v19

--- a/solution.py
+++ b/solution.py
@@ -228,14 +228,14 @@
     )
     rows = [own, *besides, swap(own, 1)]
     rows += [tuple(swap(part, 1) for part in halves(beside)) for beside in besides]
-    _, row_best = score([own], rows, own_first=True)
-    _, row_best = score([nearby], rows, known=row_best)
-    backs = []
+    row_best, backs = [], []
     for key, step in zip(keys, steps):
         (found,), row_best = score([key], rows, cols=1, known=row_best)
         backs.append(lax.ppermute(found, "owners", [(b, a) for a, b in step]))
+    _, row_best = score([nearby], rows, known=row_best)
+    _, (own_best,) = score([own], rows, own_first=True)
     local = jnp.maximum(row_best[0], swap(row_best[1], 1))
-    best = local[:tiles]
+    best = jnp.maximum(local[:tiles], own_best[:tiles])
     for at, offset in enumerate(offsets, start=1):
         best = jnp.maximum(best, swap(local[at * tiles : (at + 1) * tiles], offset))
     for back in backs:

time: 28.9 us -> 28.8 us (level)
  starting transfers between devices: 11.1 us -> 10.3 us
  waiting for transfers between devices: 11.1 us -> 11.8 us
    ppermute x1, starting transfers between devices: 2.65 us -> 0.01 us  [per_device(): nearby = lax.ppermute(own, 'owners', last)]
    ppermute x1, starting transfers between devices: 2.47 us -> 4.66 us  [per_device(): keys = [lax.ppermute(own, 'owners', step) for step in steps]]
    ppermute x1, waiting for transfers between devices: 1.12 us -> 1.62 us  [per_device(): keys = [lax.ppermute(own, 'owners', step) for step in steps]]
    ppermute x1, waiting for transfers between devices: 2.17 us -> 1.75 us  [per_device(): backs.append(lax.ppermute(found, 'owners', [(b, a) for a, b in step]))]
    ppermute x1, starting transfers between devices: 1.7 us -> 1.35 us  [per_device(): backs.append(lax.ppermute(found, 'owners', [(b, a) for a, b in step]))]
    ppermute x1, waiting for transfers between devices: 0.01 us -> 0.35 us  [per_device(): nearby = lax.ppermute(own, 'owners', last)]
  transfers between devices with their start and end apart: 9 -> 9, of which waited for: 4 -> 5; matrix products, arithmetic and copies ran while one was open for 0% -> 0% of each run, Pallas kernels for 6% -> 6%
where the time goes in v21:
time: 28.8 us; the launch traced here: 28.7 us
  waiting for transfers between devices  11.8 us (41%)
  starting transfers between devices  10.3 us (36%)
  Pallas kernels  5.82 us (20%)
  other arithmetic  0.59 us (2%)
    ppermute x6, waiting for transfers between devices, swap(): lax.ppermute(block, 'split', [(s, s ^ offset) for s in range(split_count)])  8.06 us
    ppermute x1, starting transfers between devices, per_device(): keys = [lax.ppermute(own, 'owners', step) for step in steps]  4.66 us
    ppermute x6, starting transfers between devices, swap(): lax.ppermute(block, 'split', [(s, s ^ offset) for s in range(split_count)])  4.33 us
    pallas_call x1, Pallas kernels, project(): pl.pallas_call(project_kernel, in_specs=[pl.BlockSpec(memory_space=pltpu....  3.38 us
    pallas_call x3, Pallas kernels, score(): pl.pallas_call(functools.partial(score_kernel, len(keys), cols, [len(row)...  2.44 us
    ppermute x1, waiting for transfers between devices, per_device(): backs.append(lax.ppermute(found, 'owners', [(b, a) for a, b in step]))  1.75 us
    ppermute x1, waiting for transfers between devices, per_device(): keys = [lax.ppermute(own, 'owners', step) for step in steps]  1.62 us
    ppermute x1, starting transfers between devices, per_device(): backs.append(lax.ppermute(found, 'owners', [(b, a) for a, b in step]))  1.35 us
  transfers between devices with their start and end apart: 9, of which 5 were waited for; matrix products, arithmetic and copies ran while one was open for 0% of the time, Pallas kernels for 6%

profile of v21, /device:TPU:0, one launch (start us, length us, event | category | flops | bytes accessed | tf_op | source)
XLA Modules:
  0.0 28.7 jit_solution(8380221929028623210)
XLA Ops:
  0.0 3.4 %shard_map.46.refs_1_.refs_0_ = bf16[528,256]{1,0:T(8,128)(2,1)S(1)} custom-call(bf16[512,4096]{1,0:T(8,128)(2,1)} %source_hbm.1, bf16[4096,256]{1,0:T(8,128)(2,1)} %basis_hbm.1, s32[4,128]{1,0:T(4,128)} %bitcast.4, s32[4,128]{1,0:T(4,128)} %bitcast.5), custom_call_target="tpu_custom_call" | custom-call | flops 1073741824 | bytes 6291456 | tf_op jit(solution)/shard_map/pallas_call | solution.py:65
  3.4 0.5 %collective-permute-start.2 = (bf16[528,256]{1,0:T(8,128)(2,1)S(1)}, bf16[528,256]{1,0:T(8,128)(2,1)S(1)}, u32[]{:S(2)}, u32[]{:S(2)}) collective-permute-start(bf16[528,256]{1,0:T(8,128)(2,1)S(1)} %shard_map.46.refs_1_.refs_0_), channel_id=1, source_target_pairs={{0,1},{1,0},{2,3},{3,2},{4,5},{5,4},{6,7},{7,6},{8,9},{9,8},{10,11... | collective-permute-start | bytes 811016 | tf_op jit(solution)/shard_map/ppermute | solution.py:212
  3.9 4.7 %collective-permute-start.5 = (bf16[528,256]{1,0:T(8,128)(2,1)S(1)}, bf16[528,256]{1,0:T(8,128)(2,1)S(1)}, u32[]{:S(2)}, u32[]{:S(2)}) collective-permute-start(bf16[528,256]{1,0:T(8,128)(2,1)S(1)} %shard_map.46.refs_1_.refs_0_), channel_id=1, source_target_pairs={{12,4},{4,8},{8,0},{0,12},{13,5},{5,9},{9,1},{1,13},{14,6},{6,10},... | collective-permute-start | bytes 811016 | tf_op jit(solution)/shard_map/ppermute | solution.py:219
  8.6 0.0 collective-permute-start.1
  8.6 8.7 %while.10 = (s32[]{:T(128)}, bf16[528,256]{1,0:T(8,128)(2,1)S(1)}, s32[]{:T(128)}, s32[]{:T(128)}) while((s32[]{:T(128)}, bf16[528,256]{1,0:T(8,128)(2,1)S(1)}, s32[]{:T(128)}, s32[]{:T(128)}) %tuple.18), condition=%wide.region_1.0_spmd, body=%wide.region_0.0_spmd.sunk | while | flops 2 | bytes 1622109 | solution.py:223
  8.6 1.6 %collective-permute-start = (bf16[528,256]{1,0:T(8,128)(2,1)S(1)}, bf16[528,256]{1,0:T(8,128)(2,1)S(1)}, u32[]{:S(2)}, u32[]{:S(2)}) collective-permute-start(bf16[528,256]{1,0:T(8,128)(2,1)S(1)} %get-tuple-element.65), channel_id=1, source_target_pairs={{0,2},{1,3},{2,0},{3,1},{4,6},{5,7},{6,4},{7,5},{8,10},{9,11},{10,... | collective-permute-start | bytes 811016 | tf_op jit(solution)/shard_map/while/body/ppermute | solution.py:212
  10.2 7.1 %collective-permute-done = bf16[528,256]{1,0:T(8,128)(2,1)S(1)} collective-permute-done((bf16[528,256]{1,0:T(8,128)(2,1)S(1)}, bf16[528,256]{1,0:T(8,128)(2,1)S(1)}, u32[]{:S(2)}, u32[]{:S(2)}) %collective-permute-start) | collective-permute-done | bytes 270368 | tf_op jit(solution)/shard_map/while/body/ppermute | solution.py:212
  17.3 0.1 collective-permute-start.4
  17.4 0.6 %collective-permute-start.3 = (bf16[256,256]{1,0:T(8,128)(2,1)S(1)}, bf16[256,256]{1,0:T(8,128)(2,1)S(1)}, u32[]{:S(2)}, u32[]{:S(2)}) collective-permute-start(bf16[256,256]{1,0:T(8,128)(2,1)S(1)} %slice.15), channel_id=1, source_target_pairs={{0,1},{1,0},{2,3},{3,2},{4,5},{5,4},{6,7},{7,6},{8,9},{9,8},{10,11... | collective-permute-start | bytes 393224 | tf_op jit(solution)/shard_map/ppermute | solution.py:212
  17.9 1.0 %collective-permute-done.3.refs_4_ = bf16[256,256]{1,0:T(8,128)(2,1)S(1)} collective-permute-done((bf16[256,256]{1,0:T(8,128)(2,1)S(1)}, bf16[256,256]{1,0:T(8,128)(2,1)S(1)}, u32[]{:S(2)}, u32[]{:S(2)}) %collective-permute-start.3) | collective-permute-done | bytes 131104 | tf_op jit(solution)/shard_map/ppermute | solution.py:212
  18.9 0.0 collective-permute-done.4.refs_5_
  18.9 0.0 collective-permute-done.2.refs_3_
  18.9 1.6 %collective-permute-done.5.refs_0_ = bf16[528,256]{1,0:T(8,128)(2,1)S(1)} collective-permute-done((bf16[528,256]{1,0:T(8,128)(2,1)S(1)}, bf16[528,256]{1,0:T(8,128)(2,1)S(1)}, u32[]{:S(2)}, u32[]{:S(2)}) %collective-permute-start.5) | collective-permute-done | bytes 270368 | tf_op jit(solution)/shard_map/ppermute | solution.py:219
  20.5 0.9 %shard_map.47 = (f32[4,128]{1,0:T(4,128)S(1)}, f32[8,128]{1,0:T(8,128)S(1)}, f32[8,128]{1,0:T(8,128)S(1)}) custom-call(bf16[528,256]{1,0:T(8,128)(2,1)S(1)} %collective-permute-done.5.refs_0_, bf16[528,256]{1,0:T(8,128)(2,1)S(1)} %shard_map.46.refs_1_.refs_0_, bf16[528,256]{1,0:T(8,128)(2,1)S(1)} %get-tuple-element.28.refs_2_, ...), custom_call_target="tpu_custom_call" | custom-call | tf_op jit(solution)/shard_map/pallas_call | solution.py:179
  21.4 0.3 %collective-permute-done.1.refs_0_ = bf16[528,256]{1,0:T(8,128)(2,1)S(1)} collective-permute-done((bf16[528,256]{1,0:T(8,128)(2,1)S(1)}, bf16[528,256]{1,0:T(8,128)(2,1)S(1)}, u32[]{:S(2)}, u32[]{:S(2)}) %collective-permute-start.1) | collective-permute-done | bytes 270368 | tf_op jit(solution)/shard_map/ppermute | solution.py:220
  21.7 0.8 %shard_map.48 = (f32[8,128]{1,0:T(8,128)S(1)}, f32[8,128]{1,0:T(8,128)S(1)}) custom-call(bf16[528,256]{1,0:T(8,128)(2,1)S(1)} %collective-permute-done.1.refs_0_, bf16[528,256]{1,0:T(8,128)(2,1)S(1)} %shard_map.46.refs_1_.refs_0_, bf16[528,256]{1,0:T(8,128)(2,1)S(1)} %get-tuple-element.28.refs_2_, bf16[528,256]{1,0:T(8,128)(2,1)S(1)} %collective-permute-done.2.refs_3_, ...), custom_call_target="tpu_custom_call" | custom-call | tf_op jit(solution)/shard_map/pallas_call | solution.py:179
  22.6 0.1 collective-permute-start.6
  22.7 1.3 %collective-permute-start.8 = (f32[4,128]{1,0:T(4,128)S(1)}, f32[4,128]{1,0:T(4,128)S(1)}, u32[]{:S(2)}, u32[]{:S(2)}) collective-permute-start(f32[4,128]{1,0:T(4,128)S(1)} %get-tuple-element.33), channel_id=1, source_target_pairs={{4,12},{8,4},{0,8},{12,0},{5,13},{9,5},{1,9},{13,1},{6,14},{10,6},... | collective-permute-start | bytes 6152 | tf_op jit(solution)/shard_map/ppermute | solution.py:234
  24.0 0.0 collective-permute-done.6
  24.0 1.6 %collective-permute-start.7 = (f32[4,128]{1,0:T(4,128)S(1)}, f32[4,128]{1,0:T(4,128)S(1)}, u32[]{:S(2)}, u32[]{:S(2)}) collective-permute-start(f32[4,128]{1,0:T(4,128)S(1)} %slice.19), channel_id=1, source_target_pairs={{0,2},{1,3},{2,0},{3,1},{4,6},{5,7},{6,4},{7,5},{8,10},{9,11},{10,... | collective-permute-start | bytes 6152 | tf_op jit(solution)/shard_map/ppermute | solution.py:212
  25.6 0.8 %shard_map.49 = f32[8,128]{1,0:T(8,128)S(1)} custom-call(bf16[528,256]{1,0:T(8,128)(2,1)S(1)} %shard_map.46.refs_1_.refs_0_, bf16[528,256]{1,0:T(8,128)(2,1)S(1)} %shard_map.46.refs_1_.refs_0_, bf16[528,256]{1,0:T(8,128)(2,1)S(1)} %get-tuple-element.28.refs_2_, bf16[528,256]{1,0:T(8,128)(2,1)S(1)} %collective-permute-done.2.refs_3_, ...), custom_call_target="tpu_custom_call" | custom-call | tf_op jit(solution)/shard_map/pallas_call | solution.py:179
  26.3 1.8 %collective-permute-done.8 = f32[4,128]{1,0:T(4,128)S(1)} collective-permute-done((f32[4,128]{1,0:T(4,128)S(1)}, f32[4,128]{1,0:T(4,128)S(1)}, u32[]{:S(2)}, u32[]{:S(2)}) %collective-permute-start.8) | collective-permute-done | bytes 2080 | tf_op jit(solution)/shard_map/ppermute | solution.py:234
  28.1 0.0 collective-permute-done.7
  28.1 0.6 %maximum_bitcast_fusion = f32[512]{0:T(512)} fusion(f32[4,128]{1,0:T(4,128)S(1)} %collective-permute-done.8, f32[4,128]{1,0:T(4,128)S(1)} %collective-permute-done.7, f32[8,128]{1,0:T(8,128)S(1)} %shard_map.49, f32[8,128]{1,0:T(8,128)S(1)} %max.18), kind=kLoop, calls=%fused_computation | loop fusion | flops 2048 | bytes 10240 | tf_op jit(solution)/shard_map/reshape | solution.py:243
  (6 shorter events, 0.1 us)
Async XLA Ops:
  3.4 15.5 %collective-permute-start.2 = (bf16[528,256]{1,0:T(8,128)(2,1)S(1)}, bf16[528,256]{1,0:T(8,128)(2,1)S(1)}, u32[]{:S(2)}, u32[]{:S(2)}) collective-permute-start(bf16[528,256]{1,0:T(8,128)(2,1)S(1)} %shard_map.46.refs_1_.refs_0_), channel_id=1, source_target_pairs={{0,1},{1,0},{2,3},{3,2},{4,5},{5,4},{6,7},{7,6},{8,9},{9,8},{10,11... | collective-permute-start | bytes 811016 | tf_op jit(solution)/shard_map/ppermute | solution.py:212
  3.9 16.6 %collective-permute-start.5 = (bf16[528,256]{1,0:T(8,128)(2,1)S(1)}, bf16[528,256]{1,0:T(8,128)(2,1)S(1)}, u32[]{:S(2)}, u32[]{:S(2)}) collective-permute-start(bf16[528,256]{1,0:T(8,128)(2,1)S(1)} %shard_map.46.refs_1_.refs_0_), channel_id=1, source_target_pairs={{12,4},{4,8},{8,0},{0,12},{13,5},{5,9},{9,1},{1,13},{14,6},{6,10},... | collective-permute-start | bytes 811016 | tf_op jit(solution)/shard_map/ppermute | solution.py:219
  8.6 13.2 %collective-permute-start.1 = (bf16[528,256]{1,0:T(8,128)(2,1)S(1)}, bf16[528,256]{1,0:T(8,128)(2,1)S(1)}, u32[]{:S(2)}, u32[]{:S(2)}) collective-permute-start(bf16[528,256]{1,0:T(8,128)(2,1)S(1)} %shard_map.46.refs_1_.refs_0_), channel_id=1, source_target_pairs={{12,8},{4,0},{8,12},{0,4},{13,9},{5,1},{9,13},{1,5},{14,10},{6,2},... | collective-permute-start | bytes 811016 | tf_op jit(solution)/shard_map/ppermute | solution.py:220
  8.6 8.6 %collective-permute-start = (bf16[528,256]{1,0:T(8,128)(2,1)S(1)}, bf16[528,256]{1,0:T(8,128)(2,1)S(1)}, u32[]{:S(2)}, u32[]{:S(2)}) collective-permute-start(bf16[528,256]{1,0:T(8,128)(2,1)S(1)} %get-tuple-element.65), channel_id=1, source_target_pairs={{0,2},{1,3},{2,0},{3,1},{4,6},{5,7},{6,4},{7,5},{8,10},{9,11},{10,... | collective-permute-start | bytes 811016 | tf_op jit(solution)/shard_map/while/body/ppermute | solution.py:212
  17.3 1.6 %collective-permute-start.4 = (bf16[272,256]{1,0:T(8,128)(2,1)S(1)}, bf16[272,256]{1,0:T(8,128)(2,1)S(1)}, u32[]{:S(2)}, u32[]{:S(2)}) collective-permute-start(bf16[272,256]{1,0:T(8,128)(2,1)S(1)} %slice.16), channel_id=1, source_target_pairs={{0,1},{1,0},{2,3},{3,2},{4,5},{5,4},{6,7},{7,6},{8,9},{9,8},{10,11... | collective-permute-start | bytes 417800 | tf_op jit(solution)/shard_map/ppermute | solution.py:212
  17.4 1.5 %collective-permute-start.3 = (bf16[256,256]{1,0:T(8,128)(2,1)S(1)}, bf16[256,256]{1,0:T(8,128)(2,1)S(1)}, u32[]{:S(2)}, u32[]{:S(2)}) collective-permute-start(bf16[256,256]{1,0:T(8,128)(2,1)S(1)} %slice.15), channel_id=1, source_target_pairs={{0,1},{1,0},{2,3},{3,2},{4,5},{5,4},{6,7},{7,6},{8,9},{9,8},{10,11... | collective-permute-start | bytes 393224 | tf_op jit(solution)/shard_map/ppermute | solution.py:212
  22.6 1.4 %collective-permute-start.6 = (f32[8,128]{1,0:T(8,128)S(1)}, f32[8,128]{1,0:T(8,128)S(1)}, u32[]{:S(2)}, u32[]{:S(2)}) collective-permute-start(f32[8,128]{1,0:T(8,128)S(1)} %get-tuple-element.32), channel_id=1, source_target_pairs={{0,1},{1,0},{2,3},{3,2},{4,5},{5,4},{6,7},{7,6},{8,9},{9,8},{10,11... | collective-permute-start | bytes 12296 | tf_op jit(solution)/shard_map/ppermute | solution.py:212
  22.7 5.4 %collective-permute-start.8 = (f32[4,128]{1,0:T(4,128)S(1)}, f32[4,128]{1,0:T(4,128)S(1)}, u32[]{:S(2)}, u32[]{:S(2)}) collective-permute-start(f32[4,128]{1,0:T(4,128)S(1)} %get-tuple-element.33), channel_id=1, source_target_pairs={{4,12},{8,4},{0,8},{12,0},{5,13},{9,5},{1,9},{13,1},{6,14},{10,6},... | collective-permute-start | bytes 6152 | tf_op jit(solution)/shard_map/ppermute | solution.py:234
  24.0 4.1 %collective-permute-start.7 = (f32[4,128]{1,0:T(4,128)S(1)}, f32[4,128]{1,0:T(4,128)S(1)}, u32[]{:S(2)}, u32[]{:S(2)}) collective-permute-start(f32[4,128]{1,0:T(4,128)S(1)} %slice.19), channel_id=1, source_target_pairs={{0,2},{1,3},{2,0},{3,1},{4,6},{5,7},{6,4},{7,5},{8,10},{9,11},{10,... | collective-permute-start | bytes 6152 | tf_op jit(solution)/shard_map/ppermute | solution.py:212

commit v22 on v19

--- a/solution.py
+++ b/solution.py
@@ -11,8 +11,8 @@
 LANES = 128
 TAG_ROWS = 16
 ABSENT = -2.0
-STEPS = 8
-ROW_PARTS = 4
+STEPS = 16
+ROW_PARTS = 2
 VMEM_LIMIT = 48 * 1024 * 1024
 
 
@@ -229,15 +229,20 @@
     rows = [own, *besides, swap(own, 1)]
     rows += [tuple(swap(part, 1) for part in halves(beside)) for beside in besides]
     _, row_best = score([own], rows, own_first=True)
-    _, row_best = score([nearby], rows, known=row_best)
     backs = []
     for key, step in zip(keys, steps):
         (found,), row_best = score([key], rows, cols=1, known=row_best)
         backs.append(lax.ppermute(found, "owners", [(b, a) for a, b in step]))
-    local = jnp.maximum(row_best[0], swap(row_best[1], 1))
-    best = local[:tiles]
-    for at, offset in enumerate(offsets, start=1):
-        best = jnp.maximum(best, swap(local[at * tiles : (at + 1) * tiles], offset))
+    _, row_best = score([nearby], rows, known=row_best)
+
+    def exchange_split(_, row_best):
+        local = jnp.maximum(row_best[0], swap(row_best[1], 1))
+        best = local[:tiles]
+        for at, offset in enumerate(offsets, start=1):
+            best = jnp.maximum(best, swap(local[at * tiles : (at + 1) * tiles], offset))
+        return [jnp.concatenate([best, local[tiles:]]), local]
+
+    best = lax.fori_loop(0, one_turn, exchange_split, row_best)[0][:tiles]
     for back in backs:
         best = jnp.maximum(best, back)
     return jnp.maximum(best, -1.0).reshape(row_count)

time: 28.9 us -> 29.6 us (1.024)
  waiting for transfers between devices: 11.1 us -> 12.2 us
  starting transfers between devices: 11.1 us -> 10.6 us
    ppermute x6, waiting for transfers between devices: 7.77 us -> 11.3 us  [swap(): lax.ppermute(block, 'split', [(s, s ^ offset) for s in range(split_count)])]
    ppermute x1, starting transfers between devices: 2.65 us -> 0.01 us  [per_device(): nearby = lax.ppermute(own, 'owners', last)]
    ppermute x1, starting transfers between devices: 2.47 us -> 4.67 us  [per_device(): keys = [lax.ppermute(own, 'owners', step) for step in steps]]
    ppermute x1, waiting for transfers between devices: 2.17 us -> 0.01 us  [per_device(): backs.append(lax.ppermute(found, 'owners', [(b, a) for a, b in step]))]
  transfers between devices with their start and end apart: 9 -> 9, of which waited for: 4 -> 5; matrix products, arithmetic and copies ran while one was open for 0% -> 0% of each run, Pallas kernels for 6% -> 8%
where the time goes in v22:
time: 29.6 us; the launch traced here: 29.5 us
  waiting for transfers between devices  12.2 us (41%)
  starting transfers between devices  10.6 us (36%)
  Pallas kernels  5.93 us (20%)
  other arithmetic  0.6 us (2%)
    ppermute x6, waiting for transfers between devices, swap(): lax.ppermute(block, 'split', [(s, s ^ offset) for s in range(split_count)])  11.3 us
    ppermute x1, starting transfers between devices, per_device(): keys = [lax.ppermute(own, 'owners', step) for step in steps]  4.67 us
    ppermute x6, starting transfers between devices, swap(): lax.ppermute(block, 'split', [(s, s ^ offset) for s in range(split_count)])  4.25 us
    pallas_call x1, Pallas kernels, project(): pl.pallas_call(project_kernel, in_specs=[pl.BlockSpec(memory_space=pltpu....  3.5 us
    pallas_call x3, Pallas kernels, score(): pl.pallas_call(functools.partial(score_kernel, len(keys), cols, [len(row)...  2.43 us
    ppermute x1, starting transfers between devices, per_device(): backs.append(lax.ppermute(found, 'owners', [(b, a) for a, b in step]))  1.69 us
    ppermute x1, waiting for transfers between devices, per_device(): keys = [lax.ppermute(own, 'owners', step) for step in steps]  0.86 us
  transfers between devices with their start and end apart: 9, of which 5 were waited for; matrix products, arithmetic and copies ran while one was open for 0% of the time, Pallas kernels for 8%

profile of v22, /device:TPU:0, one launch (start us, length us, event | category | flops | bytes accessed | tf_op | source)
XLA Modules:
  0.0 29.5 jit_solution(16563550350838222011)
XLA Ops:
  0.0 3.5 %shard_map.46.refs_0_.refs_1_ = bf16[528,256]{1,0:T(8,128)(2,1)S(1)} custom-call(bf16[512,4096]{1,0:T(8,128)(2,1)} %source_hbm.1, bf16[4096,256]{1,0:T(8,128)(2,1)} %basis_hbm.1, s32[4,128]{1,0:T(4,128)} %bitcast.4, s32[4,128]{1,0:T(4,128)} %bitcast.5), custom_call_target="tpu_custom_call" | custom-call | flops 1073741824 | bytes 6291456 | tf_op jit(solution)/shard_map/pallas_call | solution.py:65
  3.5 0.5 %collective-permute-start.4 = (bf16[528,256]{1,0:T(8,128)(2,1)S(1)}, bf16[528,256]{1,0:T(8,128)(2,1)S(1)}, u32[]{:S(2)}, u32[]{:S(2)}) collective-permute-start(bf16[528,256]{1,0:T(8,128)(2,1)S(1)} %shard_map.46.refs_0_.refs_1_), channel_id=1, source_target_pairs={{0,1},{1,0},{2,3},{3,2},{4,5},{5,4},{6,7},{7,6},{8,9},{9,8},{10,11... | collective-permute-start | bytes 811016 | tf_op jit(solution)/shard_map/ppermute | solution.py:212
  4.0 4.7 %collective-permute-start.7 = (bf16[528,256]{1,0:T(8,128)(2,1)S(1)}, bf16[528,256]{1,0:T(8,128)(2,1)S(1)}, u32[]{:S(2)}, u32[]{:S(2)}) collective-permute-start(bf16[528,256]{1,0:T(8,128)(2,1)S(1)} %shard_map.46.refs_0_.refs_1_), channel_id=1, source_target_pairs={{12,4},{4,8},{8,0},{0,12},{13,5},{5,9},{9,1},{1,13},{14,6},{6,10},... | collective-permute-start | bytes 811016 | tf_op jit(solution)/shard_map/ppermute | solution.py:219
  8.7 0.0 collective-permute-start.3
  8.7 8.7 %while.22 = (s32[]{:T(128)}, bf16[528,256]{1,0:T(8,128)(2,1)S(1)}, s32[]{:T(128)}, s32[]{:T(128)}) while((s32[]{:T(128)}, bf16[528,256]{1,0:T(8,128)(2,1)S(1)}, s32[]{:T(128)}, s32[]{:T(128)}) %tuple.31), condition=%wide.region_1.0_spmd, body=%wide.region_0.0_spmd.sunk | while | flops 2 | bytes 1622109 | solution.py:223
  8.7 1.6 %collective-permute-start = (bf16[528,256]{1,0:T(8,128)(2,1)S(1)}, bf16[528,256]{1,0:T(8,128)(2,1)S(1)}, u32[]{:S(2)}, u32[]{:S(2)}) collective-permute-start(bf16[528,256]{1,0:T(8,128)(2,1)S(1)} %get-tuple-element.123), channel_id=1, source_target_pairs={{0,2},{1,3},{2,0},{3,1},{4,6},{5,7},{6,4},{7,5},{8,10},{9,11},{10,... | collective-permute-start | bytes 811016 | tf_op jit(solution)/shard_map/while/body/ppermute | solution.py:212
  10.3 7.1 %collective-permute-done = bf16[528,256]{1,0:T(8,128)(2,1)S(1)} collective-permute-done((bf16[528,256]{1,0:T(8,128)(2,1)S(1)}, bf16[528,256]{1,0:T(8,128)(2,1)S(1)}, u32[]{:S(2)}, u32[]{:S(2)}) %collective-permute-start) | collective-permute-done | bytes 270368 | tf_op jit(solution)/shard_map/while/body/ppermute | solution.py:212
  17.4 0.1 collective-permute-start.6
  17.5 0.6 %collective-permute-start.5 = (bf16[256,256]{1,0:T(8,128)(2,1)S(1)}, bf16[256,256]{1,0:T(8,128)(2,1)S(1)}, u32[]{:S(2)}, u32[]{:S(2)}) collective-permute-start(bf16[256,256]{1,0:T(8,128)(2,1)S(1)} %slice.16), channel_id=1, source_target_pairs={{0,1},{1,0},{2,3},{3,2},{4,5},{5,4},{6,7},{7,6},{8,9},{9,8},{10,11... | collective-permute-start | bytes 393224 | tf_op jit(solution)/shard_map/ppermute | solution.py:212
  18.1 1.0 %collective-permute-done.5.refs_4_ = bf16[256,256]{1,0:T(8,128)(2,1)S(1)} collective-permute-done((bf16[256,256]{1,0:T(8,128)(2,1)S(1)}, bf16[256,256]{1,0:T(8,128)(2,1)S(1)}, u32[]{:S(2)}, u32[]{:S(2)}) %collective-permute-start.5) | collective-permute-done | bytes 131104 | tf_op jit(solution)/shard_map/ppermute | solution.py:212
  19.0 0.0 collective-permute-done.6.refs_5_
  19.1 0.0 collective-permute-done.4.refs_3_
  19.1 0.8 %shard_map.47.refs_6_ = f32[8,128]{1,0:T(8,128)S(1)} custom-call(bf16[528,256]{1,0:T(8,128)(2,1)S(1)} %shard_map.46.refs_0_.refs_1_, bf16[528,256]{1,0:T(8,128)(2,1)S(1)} %shard_map.46.refs_0_.refs_1_, bf16[528,256]{1,0:T(8,128)(2,1)S(1)} %get-tuple-element.51.refs_2_, bf16[528,256]{1,0:T(8,128)(2,1)S(1)} %collective-permute-done.4.refs_3_, ...), custom_call_target="tpu_custom_call" | custom-call | tf_op jit(solution)/shard_map/pallas_call | solution.py:179
  19.8 0.9 %collective-permute-done.7.refs_0_ = bf16[528,256]{1,0:T(8,128)(2,1)S(1)} collective-permute-done((bf16[528,256]{1,0:T(8,128)(2,1)S(1)}, bf16[528,256]{1,0:T(8,128)(2,1)S(1)}, u32[]{:S(2)}, u32[]{:S(2)}) %collective-permute-start.7) | collective-permute-done | bytes 270368 | tf_op jit(solution)/shard_map/ppermute | solution.py:219
  20.7 0.9 %shard_map.48 = (f32[4,128]{1,0:T(4,128)S(1)}, f32[8,128]{1,0:T(8,128)S(1)}, f32[8,128]{1,0:T(8,128)S(1)}) custom-call(bf16[528,256]{1,0:T(8,128)(2,1)S(1)} %collective-permute-done.7.refs_0_, bf16[528,256]{1,0:T(8,128)(2,1)S(1)} %shard_map.46.refs_0_.refs_1_, bf16[528,256]{1,0:T(8,128)(2,1)S(1)} %get-tuple-element.51.refs_2_, ...), custom_call_target="tpu_custom_call" | custom-call | tf_op jit(solution)/shard_map/pallas_call | solution.py:179
  21.5 1.7 %collective-permute-start.8 = (f32[4,128]{1,0:T(4,128)S(1)}, f32[4,128]{1,0:T(4,128)S(1)}, u32[]{:S(2)}, u32[]{:S(2)}) collective-permute-start(f32[4,128]{1,0:T(4,128)S(1)} %get-tuple-element.57), channel_id=1, source_target_pairs={{4,12},{8,4},{0,8},{12,0},{5,13},{9,5},{1,9},{13,1},{6,14},{10,6},... | collective-permute-start | bytes 6152 | tf_op jit(solution)/shard_map/ppermute | solution.py:235
  23.2 0.0 collective-permute-done.3.refs_0_
  23.2 0.8 %shard_map.49 = (f32[8,128]{1,0:T(8,128)S(1)}, f32[8,128]{1,0:T(8,128)S(1)}) custom-call(bf16[528,256]{1,0:T(8,128)(2,1)S(1)} %collective-permute-done.3.refs_0_, bf16[528,256]{1,0:T(8,128)(2,1)S(1)} %shard_map.46.refs_0_.refs_1_, bf16[528,256]{1,0:T(8,128)(2,1)S(1)} %get-tuple-element.51.refs_2_, bf16[528,256]{1,0:T(8,128)(2,1)S(1)} %collective-permute-done.4.refs_3_, ...), custom_call_target="tpu_custom_call" | custom-call | tf_op jit(solution)/shard_map/pallas_call | solution.py:179
  24.1 4.9 %while.23 = (s32[]{:T(128)}, f32[8,128]{1,0:T(8,128)S(1)}, f32[8,128]{1,0:T(8,128)S(1)}, s32[]{:T(128)}, s32[]{:T(128)}) while((s32[]{:T(128)}, f32[8,128]{1,0:T(8,128)S(1)}, f32[8,128]{1,0:T(8,128)S(1)}, s32[]{:T(128)}, s32[]{:T(128)}) %tuple.34), condition=%wide.region_3.0_spmd, body=%wide.region_2.0_spmd.sunk | while | flops 2562 | bytes 55437 | solution.py:245
  24.1 0.1 collective-permute-start.1
  24.1 1.2 %collective-permute-done.1 = f32[8,128]{1,0:T(8,128)S(1)} collective-permute-done((f32[8,128]{1,0:T(8,128)S(1)}, f32[8,128]{1,0:T(8,128)S(1)}, u32[]{:S(2)}, u32[]{:S(2)}) %collective-permute-start.1) | collective-permute-done | bytes 4128 | tf_op jit(solution)/shard_map/while/body/ppermute | solution.py:212
  25.3 1.5 %collective-permute-start.2 = (f32[4,128]{1,0:T(4,128)S(1)}, f32[4,128]{1,0:T(4,128)S(1)}, u32[]{:S(2)}, u32[]{:S(2)}) collective-permute-start(f32[4,128]{1,0:T(4,128)S(1)} %slice.24), channel_id=1, source_target_pairs={{0,2},{1,3},{2,0},{3,1},{4,6},{5,7},{6,4},{7,5},{8,10},{9,11},{10,... | collective-permute-start | bytes 6152 | tf_op jit(solution)/shard_map/while/body/ppermute | solution.py:212
  26.8 2.1 %collective-permute-done.2 = f32[4,128]{1,0:T(4,128)S(1)} collective-permute-done((f32[4,128]{1,0:T(4,128)S(1)}, f32[4,128]{1,0:T(4,128)S(1)}, u32[]{:S(2)}, u32[]{:S(2)}) %collective-permute-start.2) | collective-permute-done | bytes 2080 | tf_op jit(solution)/shard_map/while/body/ppermute | solution.py:212
  28.9 0.6 %maximum_bitcast_fusion = f32[512]{0:T(512)} fusion(f32[4,128]{1,0:T(4,128)S(1)} %collective-permute-done.8, f32[8,128]{1,0:T(8,128)S(1)} %get-tuple-element.56), kind=kLoop, calls=%fused_computation.2 | loop fusion | flops 1024 | bytes 6144 | tf_op jit(solution)/shard_map/reshape | solution.py:248
  (9 shorter events, 0.1 us)
Async XLA Ops:
  3.5 15.6 %collective-permute-start.4 = (bf16[528,256]{1,0:T(8,128)(2,1)S(1)}, bf16[528,256]{1,0:T(8,128)(2,1)S(1)}, u32[]{:S(2)}, u32[]{:S(2)}) collective-permute-start(bf16[528,256]{1,0:T(8,128)(2,1)S(1)} %shard_map.46.refs_0_.refs_1_), channel_id=1, source_target_pairs={{0,1},{1,0},{2,3},{3,2},{4,5},{5,4},{6,7},{7,6},{8,9},{9,8},{10,11... | collective-permute-start | bytes 811016 | tf_op jit(solution)/shard_map/ppermute | solution.py:212
  4.0 16.6 %collective-permute-start.7 = (bf16[528,256]{1,0:T(8,128)(2,1)S(1)}, bf16[528,256]{1,0:T(8,128)(2,1)S(1)}, u32[]{:S(2)}, u32[]{:S(2)}) collective-permute-start(bf16[528,256]{1,0:T(8,128)(2,1)S(1)} %shard_map.46.refs_0_.refs_1_), channel_id=1, source_target_pairs={{12,4},{4,8},{8,0},{0,12},{13,5},{5,9},{9,1},{1,13},{14,6},{6,10},... | collective-permute-start | bytes 811016 | tf_op jit(solution)/shard_map/ppermute | solution.py:219
  8.7 14.5 %collective-permute-start.3 = (bf16[528,256]{1,0:T(8,128)(2,1)S(1)}, bf16[528,256]{1,0:T(8,128)(2,1)S(1)}, u32[]{:S(2)}, u32[]{:S(2)}) collective-permute-start(bf16[528,256]{1,0:T(8,128)(2,1)S(1)} %shard_map.46.refs_0_.refs_1_), channel_id=1, source_target_pairs={{12,8},{4,0},{8,12},{0,4},{13,9},{5,1},{9,13},{1,5},{14,10},{6,2},... | collective-permute-start | bytes 811016 | tf_op jit(solution)/shard_map/ppermute | solution.py:220
  8.7 8.6 %collective-permute-start = (bf16[528,256]{1,0:T(8,128)(2,1)S(1)}, bf16[528,256]{1,0:T(8,128)(2,1)S(1)}, u32[]{:S(2)}, u32[]{:S(2)}) collective-permute-start(bf16[528,256]{1,0:T(8,128)(2,1)S(1)} %get-tuple-element.123), channel_id=1, source_target_pairs={{0,2},{1,3},{2,0},{3,1},{4,6},{5,7},{6,4},{7,5},{8,10},{9,11},{10,... | collective-permute-start | bytes 811016 | tf_op jit(solution)/shard_map/while/body/ppermute | solution.py:212
  17.4 1.6 %collective-permute-start.6 = (bf16[272,256]{1,0:T(8,128)(2,1)S(1)}, bf16[272,256]{1,0:T(8,128)(2,1)S(1)}, u32[]{:S(2)}, u32[]{:S(2)}) collective-permute-start(bf16[272,256]{1,0:T(8,128)(2,1)S(1)} %slice.17), channel_id=1, source_target_pairs={{0,1},{1,0},{2,3},{3,2},{4,5},{5,4},{6,7},{7,6},{8,9},{9,8},{10,11... | collective-permute-start | bytes 417800 | tf_op jit(solution)/shard_map/ppermute | solution.py:212
  17.5 1.5 %collective-permute-start.5 = (bf16[256,256]{1,0:T(8,128)(2,1)S(1)}, bf16[256,256]{1,0:T(8,128)(2,1)S(1)}, u32[]{:S(2)}, u32[]{:S(2)}) collective-permute-start(bf16[256,256]{1,0:T(8,128)(2,1)S(1)} %slice.16), channel_id=1, source_target_pairs={{0,1},{1,0},{2,3},{3,2},{4,5},{5,4},{6,7},{7,6},{8,9},{9,8},{10,11... | collective-permute-start | bytes 393224 | tf_op jit(solution)/shard_map/ppermute | solution.py:212
  21.5 7.4 %collective-permute-start.8 = (f32[4,128]{1,0:T(4,128)S(1)}, f32[4,128]{1,0:T(4,128)S(1)}, u32[]{:S(2)}, u32[]{:S(2)}) collective-permute-start(f32[4,128]{1,0:T(4,128)S(1)} %get-tuple-element.57), channel_id=1, source_target_pairs={{4,12},{8,4},{0,8},{12,0},{5,13},{9,5},{1,9},{13,1},{6,14},{10,6},... | collective-permute-start | bytes 6152 | tf_op jit(solution)/shard_map/ppermute | solution.py:235
  24.1 1.2 %collective-permute-start.1 = (f32[8,128]{1,0:T(8,128)S(1)}, f32[8,128]{1,0:T(8,128)S(1)}, u32[]{:S(2)}, u32[]{:S(2)}) collective-permute-start(f32[8,128]{1,0:T(8,128)S(1)} %get-tuple-element.137), channel_id=1, source_target_pairs={{0,1},{1,0},{2,3},{3,2},{4,5},{5,4},{6,7},{7,6},{8,9},{9,8},{10,11... | collective-permute-start | bytes 12296 | tf_op jit(solution)/shard_map/while/body/ppermute | solution.py:212
  25.3 3.6 %collective-permute-start.2 = (f32[4,128]{1,0:T(4,128)S(1)}, f32[4,128]{1,0:T(4,128)S(1)}, u32[]{:S(2)}, u32[]{:S(2)}) collective-permute-start(f32[4,128]{1,0:T(4,128)S(1)} %slice.24), channel_id=1, source_target_pairs={{0,2},{1,3},{2,0},{3,1},{4,6},{5,7},{6,4},{7,5},{8,10},{9,11},{10,... | collective-permute-start | bytes 6152 | tf_op jit(solution)/shard_map/while/body/ppermute | solution.py:212

commit v23 on v21

--- a/solution.py
+++ b/solution.py
@@ -11,39 +11,57 @@
 LANES = 128
 TAG_ROWS = 16
 ABSENT = -2.0
-STEPS = 8
+STEPS = 2
 ROW_PARTS = 4
+DEPTH_PARTS = 4
 VMEM_LIMIT = 48 * 1024 * 1024
 
 
 def project_kernel(source_hbm, basis_hbm, owner_hbm, sub_hbm, packed_ref, *scratch):
-    source, basis, owner, sub, sems, tag_sems = scratch
+    source, basis, owner, sub, basis_sems, source_sems, tag_sems = scratch
     row_count, depth = source.shape
     width = basis.shape[1]
-    spans = cut(depth, STEPS)
-    copies = [
-        (
-            pltpu.make_async_copy(basis_hbm.at[span, :], basis.at[span, :], sems.at[0, step]),
-            pltpu.make_async_copy(source_hbm.at[:, span], source.at[:, span], sems.at[1, step]),
-        )
+    spans, groups = cut(depth, STEPS), cut(row_count, ROW_PARTS)
+    basis_copies = [
+        pltpu.make_async_copy(basis_hbm.at[span, :], basis.at[span, :], basis_sems.at[step])
+        for step, span in enumerate(spans)
+    ]
+    source_copies = [
+        [
+            pltpu.make_async_copy(
+                source_hbm.at[rows, span], source.at[rows, span], source_sems.at[step, at]
+            )
+            for at, rows in enumerate(groups)
+        ]
         for step, span in enumerate(spans)
     ]
     tag_copies = [
         pltpu.make_async_copy(owner_hbm, owner, tag_sems.at[0]),
         pltpu.make_async_copy(sub_hbm, sub, tag_sems.at[1]),
     ]
-    for copy in [copy for pair in copies for copy in pair] + tag_copies:
+    for basis_copy, row_copies in zip(basis_copies, source_copies):
+        basis_copy.start()
+        for copy in row_copies:
+            copy.start()
+    for copy in tag_copies:
         copy.start()
     totals = [None] * ROW_PARTS
-    for span, pair in zip(spans, copies):
-        for copy in pair:
-            copy.wait()
-        for at, rows in enumerate(cut(row_count, ROW_PARTS)):
-            part = jnp.dot(source[rows, span], basis[span, :], preferred_element_type=jnp.float32)
-            totals[at] = part if totals[at] is None else totals[at] + part
-    for projected, rows in zip(totals, cut(row_count, ROW_PARTS)):
-        norms = jnp.sum(projected * projected, axis=1, keepdims=True)
-        packed_ref[rows, :] = (projected * lax.rsqrt(norms + 1e-06)).astype(jnp.bfloat16)
+    for step, span in enumerate(spans):
+        basis_copies[step].wait()
+        for at, rows in enumerate(groups):
+            source_copies[step][at].wait()
+            chunk = depth // STEPS // DEPTH_PARTS
+            for part in range(DEPTH_PARTS):
+                here = pl.ds(span.start + part * chunk, chunk)
+                found = jnp.dot(
+                    source[rows, here], basis[here, :], preferred_element_type=jnp.float32
+                )
+                totals[at] = found if totals[at] is None else totals[at] + found
+            if step == STEPS - 1:
+                projected = totals[at]
+                norms = jnp.sum(projected * projected, axis=1, keepdims=True)
+                units = projected * lax.rsqrt(norms + 1e-06)
+                packed_ref[rows, :] = units.astype(jnp.bfloat16)
     for copy in tag_copies:
         copy.wait()
     tags = (owner[...] * CPO + sub[...] + 1).astype(jnp.float32)
@@ -72,7 +90,8 @@
             pltpu.VMEM((depth, width), jnp.bfloat16),
             pltpu.VMEM(tag_shape, jnp.int32),
             pltpu.VMEM(tag_shape, jnp.int32),
-            pltpu.SemaphoreType.DMA((2, STEPS)),
+            pltpu.SemaphoreType.DMA((STEPS,)),
+            pltpu.SemaphoreType.DMA((STEPS, ROW_PARTS)),
             pltpu.SemaphoreType.DMA((2,)),
         ],
         compiler_params=pltpu.CompilerParams(vmem_limit_bytes=VMEM_LIMIT),

time: 28.8 us -> 31 us (1.076)
  Pallas kernels: 5.82 us -> 7.97 us
    pallas_call x1, Pallas kernels: 3.38 us -> 5.53 us  [project(): pl.pallas_call(project_kernel, in_specs=[pl.BlockSpec(memory_space=pltpu....]
  transfers between devices with their start and end apart: 9 -> 9, of which waited for: 5 -> 5; matrix products, arithmetic and copies ran while one was open for 0% -> 0% of each run, Pallas kernels for 6% -> 5%
where the time goes in v23:
time: 31 us; the launch traced here: 30.8 us
  waiting for transfers between devices  11.8 us (38%)
  starting transfers between devices  10.3 us (33%)
  Pallas kernels  7.97 us (26%)
  other arithmetic  0.59 us (2%)
    ppermute x6, waiting for transfers between devices, swap(): lax.ppermute(block, 'split', [(s, s ^ offset) for s in range(split_count)])  8.06 us
    pallas_call x1, Pallas kernels, project(): pl.pallas_call(project_kernel, in_specs=[pl.BlockSpec(memory_space=pltpu....  5.53 us
    ppermute x1, starting transfers between devices, per_device(): keys = [lax.ppermute(own, 'owners', step) for step in steps]  4.66 us
    ppermute x6, starting transfers between devices, swap(): lax.ppermute(block, 'split', [(s, s ^ offset) for s in range(split_count)])  4.32 us
    pallas_call x3, Pallas kernels, score(): pl.pallas_call(functools.partial(score_kernel, len(keys), cols, [len(row)...  2.44 us
    ppermute x1, waiting for transfers between devices, per_device(): backs.append(lax.ppermute(found, 'owners', [(b, a) for a, b in step]))  1.76 us
    ppermute x1, waiting for transfers between devices, per_device(): keys = [lax.ppermute(own, 'owners', step) for step in steps]  1.62 us
    ppermute x1, starting transfers between devices, per_device(): backs.append(lax.ppermute(found, 'owners', [(b, a) for a, b in step]))  1.35 us
  transfers between devices with their start and end apart: 9, of which 5 were waited for; matrix products, arithmetic and copies ran while one was open for 0% of the time, Pallas kernels for 5%

profile of v23, /device:TPU:0, one launch (start us, length us, event | category | flops | bytes accessed | tf_op | source)
XLA Modules:
  0.0 30.8 jit_solution(234538489705815565)
XLA Ops:
  0.0 5.5 %shard_map.46.refs_1_.refs_0_ = bf16[528,256]{1,0:T(8,128)(2,1)S(1)} custom-call(bf16[512,4096]{1,0:T(8,128)(2,1)} %source_hbm.1, bf16[4096,256]{1,0:T(8,128)(2,1)} %basis_hbm.1, s32[4,128]{1,0:T(4,128)} %bitcast.4, s32[4,128]{1,0:T(4,128)} %bitcast.5), custom_call_target="tpu_custom_call" | custom-call | flops 1073741824 | bytes 6291456 | tf_op jit(solution)/shard_map/pallas_call | solution.py:83
  5.5 0.5 %collective-permute-start.2 = (bf16[528,256]{1,0:T(8,128)(2,1)S(1)}, bf16[528,256]{1,0:T(8,128)(2,1)S(1)}, u32[]{:S(2)}, u32[]{:S(2)}) collective-permute-start(bf16[528,256]{1,0:T(8,128)(2,1)S(1)} %shard_map.46.refs_1_.refs_0_), channel_id=1, source_target_pairs={{0,1},{1,0},{2,3},{3,2},{4,5},{5,4},{6,7},{7,6},{8,9},{9,8},{10,11... | collective-permute-start | bytes 811016 | tf_op jit(solution)/shard_map/ppermute | solution.py:231
  6.1 4.7 %collective-permute-start.5 = (bf16[528,256]{1,0:T(8,128)(2,1)S(1)}, bf16[528,256]{1,0:T(8,128)(2,1)S(1)}, u32[]{:S(2)}, u32[]{:S(2)}) collective-permute-start(bf16[528,256]{1,0:T(8,128)(2,1)S(1)} %shard_map.46.refs_1_.refs_0_), channel_id=1, source_target_pairs={{12,4},{4,8},{8,0},{0,12},{13,5},{5,9},{9,1},{1,13},{14,6},{6,10},... | collective-permute-start | bytes 811016 | tf_op jit(solution)/shard_map/ppermute | solution.py:238
  10.7 0.0 collective-permute-start.1
  10.8 8.7 %while.10 = (s32[]{:T(128)}, bf16[528,256]{1,0:T(8,128)(2,1)S(1)}, s32[]{:T(128)}, s32[]{:T(128)}) while((s32[]{:T(128)}, bf16[528,256]{1,0:T(8,128)(2,1)S(1)}, s32[]{:T(128)}, s32[]{:T(128)}) %tuple.18), condition=%wide.region_1.0_spmd, body=%wide.region_0.0_spmd.sunk | while | flops 2 | bytes 1622109 | solution.py:242
  10.8 1.6 %collective-permute-start = (bf16[528,256]{1,0:T(8,128)(2,1)S(1)}, bf16[528,256]{1,0:T(8,128)(2,1)S(1)}, u32[]{:S(2)}, u32[]{:S(2)}) collective-permute-start(bf16[528,256]{1,0:T(8,128)(2,1)S(1)} %get-tuple-element.65), channel_id=1, source_target_pairs={{0,2},{1,3},{2,0},{3,1},{4,6},{5,7},{6,4},{7,5},{8,10},{9,11},{10,... | collective-permute-start | bytes 811016 | tf_op jit(solution)/shard_map/while/body/ppermute | solution.py:231
  12.3 7.1 %collective-permute-done = bf16[528,256]{1,0:T(8,128)(2,1)S(1)} collective-permute-done((bf16[528,256]{1,0:T(8,128)(2,1)S(1)}, bf16[528,256]{1,0:T(8,128)(2,1)S(1)}, u32[]{:S(2)}, u32[]{:S(2)}) %collective-permute-start) | collective-permute-done | bytes 270368 | tf_op jit(solution)/shard_map/while/body/ppermute | solution.py:231
  19.4 0.1 collective-permute-start.4
  19.5 0.6 %collective-permute-start.3 = (bf16[256,256]{1,0:T(8,128)(2,1)S(1)}, bf16[256,256]{1,0:T(8,128)(2,1)S(1)}, u32[]{:S(2)}, u32[]{:S(2)}) collective-permute-start(bf16[256,256]{1,0:T(8,128)(2,1)S(1)} %slice.15), channel_id=1, source_target_pairs={{0,1},{1,0},{2,3},{3,2},{4,5},{5,4},{6,7},{7,6},{8,9},{9,8},{10,11... | collective-permute-start | bytes 393224 | tf_op jit(solution)/shard_map/ppermute | solution.py:231
  20.1 1.0 %collective-permute-done.3.refs_4_ = bf16[256,256]{1,0:T(8,128)(2,1)S(1)} collective-permute-done((bf16[256,256]{1,0:T(8,128)(2,1)S(1)}, bf16[256,256]{1,0:T(8,128)(2,1)S(1)}, u32[]{:S(2)}, u32[]{:S(2)}) %collective-permute-start.3) | collective-permute-done | bytes 131104 | tf_op jit(solution)/shard_map/ppermute | solution.py:231
  21.1 0.0 collective-permute-done.4.refs_5_
  21.1 0.0 collective-permute-done.2.refs_3_
  21.1 1.6 %collective-permute-done.5.refs_0_ = bf16[528,256]{1,0:T(8,128)(2,1)S(1)} collective-permute-done((bf16[528,256]{1,0:T(8,128)(2,1)S(1)}, bf16[528,256]{1,0:T(8,128)(2,1)S(1)}, u32[]{:S(2)}, u32[]{:S(2)}) %collective-permute-start.5) | collective-permute-done | bytes 270368 | tf_op jit(solution)/shard_map/ppermute | solution.py:238
  22.7 0.8 %shard_map.47 = (f32[4,128]{1,0:T(4,128)S(1)}, f32[8,128]{1,0:T(8,128)S(1)}, f32[8,128]{1,0:T(8,128)S(1)}) custom-call(bf16[528,256]{1,0:T(8,128)(2,1)S(1)} %collective-permute-done.5.refs_0_, bf16[528,256]{1,0:T(8,128)(2,1)S(1)} %shard_map.46.refs_1_.refs_0_, bf16[528,256]{1,0:T(8,128)(2,1)S(1)} %get-tuple-element.28.refs_2_, ...), custom_call_target="tpu_custom_call" | custom-call | tf_op jit(solution)/shard_map/pallas_call | solution.py:198
  23.5 0.4 %collective-permute-done.1.refs_0_ = bf16[528,256]{1,0:T(8,128)(2,1)S(1)} collective-permute-done((bf16[528,256]{1,0:T(8,128)(2,1)S(1)}, bf16[528,256]{1,0:T(8,128)(2,1)S(1)}, u32[]{:S(2)}, u32[]{:S(2)}) %collective-permute-start.1) | collective-permute-done | bytes 270368 | tf_op jit(solution)/shard_map/ppermute | solution.py:239
  23.9 0.8 %shard_map.48 = (f32[8,128]{1,0:T(8,128)S(1)}, f32[8,128]{1,0:T(8,128)S(1)}) custom-call(bf16[528,256]{1,0:T(8,128)(2,1)S(1)} %collective-permute-done.1.refs_0_, bf16[528,256]{1,0:T(8,128)(2,1)S(1)} %shard_map.46.refs_1_.refs_0_, bf16[528,256]{1,0:T(8,128)(2,1)S(1)} %get-tuple-element.28.refs_2_, bf16[528,256]{1,0:T(8,128)(2,1)S(1)} %collective-permute-done.2.refs_3_, ...), custom_call_target="tpu_custom_call" | custom-call | tf_op jit(solution)/shard_map/pallas_call | solution.py:198
  24.7 0.1 collective-permute-start.6
  24.8 1.3 %collective-permute-start.8 = (f32[4,128]{1,0:T(4,128)S(1)}, f32[4,128]{1,0:T(4,128)S(1)}, u32[]{:S(2)}, u32[]{:S(2)}) collective-permute-start(f32[4,128]{1,0:T(4,128)S(1)} %get-tuple-element.33), channel_id=1, source_target_pairs={{4,12},{8,4},{0,8},{12,0},{5,13},{9,5},{1,9},{13,1},{6,14},{10,6},... | collective-permute-start | bytes 6152 | tf_op jit(solution)/shard_map/ppermute | solution.py:253
  26.2 0.0 collective-permute-done.6
  26.2 1.6 %collective-permute-start.7 = (f32[4,128]{1,0:T(4,128)S(1)}, f32[4,128]{1,0:T(4,128)S(1)}, u32[]{:S(2)}, u32[]{:S(2)}) collective-permute-start(f32[4,128]{1,0:T(4,128)S(1)} %slice.19), channel_id=1, source_target_pairs={{0,2},{1,3},{2,0},{3,1},{4,6},{5,7},{6,4},{7,5},{8,10},{9,11},{10,... | collective-permute-start | bytes 6152 | tf_op jit(solution)/shard_map/ppermute | solution.py:231
  27.7 0.8 %shard_map.49 = f32[8,128]{1,0:T(8,128)S(1)} custom-call(bf16[528,256]{1,0:T(8,128)(2,1)S(1)} %shard_map.46.refs_1_.refs_0_, bf16[528,256]{1,0:T(8,128)(2,1)S(1)} %shard_map.46.refs_1_.refs_0_, bf16[528,256]{1,0:T(8,128)(2,1)S(1)} %get-tuple-element.28.refs_2_, bf16[528,256]{1,0:T(8,128)(2,1)S(1)} %collective-permute-done.2.refs_3_, ...), custom_call_target="tpu_custom_call" | custom-call | tf_op jit(solution)/shard_map/pallas_call | solution.py:198
  28.5 1.8 %collective-permute-done.8 = f32[4,128]{1,0:T(4,128)S(1)} collective-permute-done((f32[4,128]{1,0:T(4,128)S(1)}, f32[4,128]{1,0:T(4,128)S(1)}, u32[]{:S(2)}, u32[]{:S(2)}) %collective-permute-start.8) | collective-permute-done | bytes 2080 | tf_op jit(solution)/shard_map/ppermute | solution.py:253
  30.2 0.0 collective-permute-done.7
  30.3 0.6 %maximum_bitcast_fusion = f32[512]{0:T(512)} fusion(f32[4,128]{1,0:T(4,128)S(1)} %collective-permute-done.8, f32[4,128]{1,0:T(4,128)S(1)} %collective-permute-done.7, f32[8,128]{1,0:T(8,128)S(1)} %shard_map.49, f32[8,128]{1,0:T(8,128)S(1)} %max.18), kind=kLoop, calls=%fused_computation | loop fusion | flops 2048 | bytes 10240 | tf_op jit(solution)/shard_map/reshape | solution.py:262
  (6 shorter events, 0.1 us)
Async XLA Ops:
  5.5 15.5 %collective-permute-start.2 = (bf16[528,256]{1,0:T(8,128)(2,1)S(1)}, bf16[528,256]{1,0:T(8,128)(2,1)S(1)}, u32[]{:S(2)}, u32[]{:S(2)}) collective-permute-start(bf16[528,256]{1,0:T(8,128)(2,1)S(1)} %shard_map.46.refs_1_.refs_0_), channel_id=1, source_target_pairs={{0,1},{1,0},{2,3},{3,2},{4,5},{5,4},{6,7},{7,6},{8,9},{9,8},{10,11... | collective-permute-start | bytes 811016 | tf_op jit(solution)/shard_map/ppermute | solution.py:231
  6.1 16.6 %collective-permute-start.5 = (bf16[528,256]{1,0:T(8,128)(2,1)S(1)}, bf16[528,256]{1,0:T(8,128)(2,1)S(1)}, u32[]{:S(2)}, u32[]{:S(2)}) collective-permute-start(bf16[528,256]{1,0:T(8,128)(2,1)S(1)} %shard_map.46.refs_1_.refs_0_), channel_id=1, source_target_pairs={{12,4},{4,8},{8,0},{0,12},{13,5},{5,9},{9,1},{1,13},{14,6},{6,10},... | collective-permute-start | bytes 811016 | tf_op jit(solution)/shard_map/ppermute | solution.py:238
  10.7 13.2 %collective-permute-start.1 = (bf16[528,256]{1,0:T(8,128)(2,1)S(1)}, bf16[528,256]{1,0:T(8,128)(2,1)S(1)}, u32[]{:S(2)}, u32[]{:S(2)}) collective-permute-start(bf16[528,256]{1,0:T(8,128)(2,1)S(1)} %shard_map.46.refs_1_.refs_0_), channel_id=1, source_target_pairs={{12,8},{4,0},{8,12},{0,4},{13,9},{5,1},{9,13},{1,5},{14,10},{6,2},... | collective-permute-start | bytes 811016 | tf_op jit(solution)/shard_map/ppermute | solution.py:239
  10.8 8.6 %collective-permute-start = (bf16[528,256]{1,0:T(8,128)(2,1)S(1)}, bf16[528,256]{1,0:T(8,128)(2,1)S(1)}, u32[]{:S(2)}, u32[]{:S(2)}) collective-permute-start(bf16[528,256]{1,0:T(8,128)(2,1)S(1)} %get-tuple-element.65), channel_id=1, source_target_pairs={{0,2},{1,3},{2,0},{3,1},{4,6},{5,7},{6,4},{7,5},{8,10},{9,11},{10,... | collective-permute-start | bytes 811016 | tf_op jit(solution)/shard_map/while/body/ppermute | solution.py:231
  19.4 1.6 %collective-permute-start.4 = (bf16[272,256]{1,0:T(8,128)(2,1)S(1)}, bf16[272,256]{1,0:T(8,128)(2,1)S(1)}, u32[]{:S(2)}, u32[]{:S(2)}) collective-permute-start(bf16[272,256]{1,0:T(8,128)(2,1)S(1)} %slice.16), channel_id=1, source_target_pairs={{0,1},{1,0},{2,3},{3,2},{4,5},{5,4},{6,7},{7,6},{8,9},{9,8},{10,11... | collective-permute-start | bytes 417800 | tf_op jit(solution)/shard_map/ppermute | solution.py:231
  19.5 1.5 %collective-permute-start.3 = (bf16[256,256]{1,0:T(8,128)(2,1)S(1)}, bf16[256,256]{1,0:T(8,128)(2,1)S(1)}, u32[]{:S(2)}, u32[]{:S(2)}) collective-permute-start(bf16[256,256]{1,0:T(8,128)(2,1)S(1)} %slice.15), channel_id=1, source_target_pairs={{0,1},{1,0},{2,3},{3,2},{4,5},{5,4},{6,7},{7,6},{8,9},{9,8},{10,11... | collective-permute-start | bytes 393224 | tf_op jit(solution)/shard_map/ppermute | solution.py:231
  24.7 1.4 %collective-permute-start.6 = (f32[8,128]{1,0:T(8,128)S(1)}, f32[8,128]{1,0:T(8,128)S(1)}, u32[]{:S(2)}, u32[]{:S(2)}) collective-permute-start(f32[8,128]{1,0:T(8,128)S(1)} %get-tuple-element.32), channel_id=1, source_target_pairs={{0,1},{1,0},{2,3},{3,2},{4,5},{5,4},{6,7},{7,6},{8,9},{9,8},{10,11... | collective-permute-start | bytes 12296 | tf_op jit(solution)/shard_map/ppermute | solution.py:231
  24.8 5.4 %collective-permute-start.8 = (f32[4,128]{1,0:T(4,128)S(1)}, f32[4,128]{1,0:T(4,128)S(1)}, u32[]{:S(2)}, u32[]{:S(2)}) collective-permute-start(f32[4,128]{1,0:T(4,128)S(1)} %get-tuple-element.33), channel_id=1, source_target_pairs={{4,12},{8,4},{0,8},{12,0},{5,13},{9,5},{1,9},{13,1},{6,14},{10,6},... | collective-permute-start | bytes 6152 | tf_op jit(solution)/shard_map/ppermute | solution.py:253
  26.2 4.1 %collective-permute-start.7 = (f32[4,128]{1,0:T(4,128)S(1)}, f32[4,128]{1,0:T(4,128)S(1)}, u32[]{:S(2)}, u32[]{:S(2)}) collective-permute-start(f32[4,128]{1,0:T(4,128)S(1)} %slice.19), channel_id=1, source_target_pairs={{0,2},{1,3},{2,0},{3,1},{4,6},{5,7},{6,4},{7,5},{8,10},{9,11},{10,... | collective-permute-start | bytes 6152 | tf_op jit(solution)/shard_map/ppermute | solution.py:231

commit v24 on v21

--- a/solution.py
+++ b/solution.py
@@ -216,7 +216,12 @@
 
     own = project(embeddings, basis, owner_ids, sub_cluster)
     *steps, last = owner_steps(owner_count)
-    keys = [lax.ppermute(own, "owners", step) for step in steps]
+    steps = [
+        [(a * split_count + s, b * split_count + (s ^ 1)) for a, b in step for s in range(split_count)]
+        for step in steps
+    ]
+    both = ("owners", "split")
+    keys = [lax.ppermute(own, both, step) for step in steps]
     nearby = lax.ppermute(own, "owners", last)
     offsets = range(2, split_count, 2)
     one_turn = 1 + (lax.axis_index("groups") >> 16)
@@ -231,7 +236,7 @@
     row_best, backs = [], []
     for key, step in zip(keys, steps):
         (found,), row_best = score([key], rows, cols=1, known=row_best)
-        backs.append(lax.ppermute(found, "owners", [(b, a) for a, b in step]))
+        backs.append(lax.ppermute(found, both, [(b, a) for a, b in step]))
     _, row_best = score([nearby], rows, known=row_best)
     _, (own_best,) = score([own], rows, own_first=True)
     local = jnp.maximum(row_best[0], swap(row_best[1], 1))

time: 28.8 us -> 28.2 us (0.979)
  starting transfers between devices: 10.3 us -> 9.94 us
    ppermute x2, waiting for transfers between devices: 3.37 us -> 2.84 us  [the longest x1 1.43 us: per_device(): backs.append(lax.ppermute(found, both, [(b, a) for a, b in step]))]
    ppermute x2, starting transfers between devices: 6.01 us -> 5.66 us  [the longest x1 4.71 us: per_device(): keys = [lax.ppermute(own, both, step) for step in steps]]
  transfers between devices with their start and end apart: 9 -> 9, of which waited for: 5 -> 6; matrix products, arithmetic and copies ran while one was open for 0% -> 0% of each run, Pallas kernels for 6% -> 6%
where the time goes in v24:
time: 28.2 us; the launch traced here: 28.1 us
  waiting for transfers between devices  11.6 us (41%)
  starting transfers between devices  9.94 us (35%)
  Pallas kernels  5.81 us (21%)
  other arithmetic  0.59 us (2%)
    ppermute x6, waiting for transfers between devices, swap(): lax.ppermute(block, 'split', [(s, s ^ offset) for s in range(split_count)])  8.16 us
    ppermute x1, starting transfers between devices, per_device(): keys = [lax.ppermute(own, both, step) for step in steps]  4.71 us
    ppermute x6, starting transfers between devices, swap(): lax.ppermute(block, 'split', [(s, s ^ offset) for s in range(split_count)])  4.28 us
    pallas_call x1, Pallas kernels, project(): pl.pallas_call(project_kernel, in_specs=[pl.BlockSpec(memory_space=pltpu....  3.38 us
    pallas_call x3, Pallas kernels, score(): pl.pallas_call(functools.partial(score_kernel, len(keys), cols, [len(row)...  2.43 us
    ppermute x1, waiting for transfers between devices, per_device(): backs.append(lax.ppermute(found, both, [(b, a) for a, b in step]))  1.43 us
    ppermute x1, waiting for transfers between devices, per_device(): keys = [lax.ppermute(own, both, step) for step in steps]  1.41 us
    ppermute x1, starting transfers between devices, per_device(): backs.append(lax.ppermute(found, both, [(b, a) for a, b in step]))  0.95 us
  transfers between devices with their start and end apart: 9, of which 6 were waited for; matrix products, arithmetic and copies ran while one was open for 0% of the time, Pallas kernels for 6%

profile of v24, /device:TPU:0, one launch (start us, length us, event | category | flops | bytes accessed | tf_op | source)
XLA Modules:
  0.0 28.1 jit_solution(3603955354867282070)
XLA Ops:
  0.0 3.4 %shard_map.46.refs_1_.refs_0_ = bf16[528,256]{1,0:T(8,128)(2,1)S(1)} custom-call(bf16[512,4096]{1,0:T(8,128)(2,1)} %source_hbm.1, bf16[4096,256]{1,0:T(8,128)(2,1)} %basis_hbm.1, s32[4,128]{1,0:T(4,128)} %bitcast.4, s32[4,128]{1,0:T(4,128)} %bitcast.5), custom_call_target="tpu_custom_call" | custom-call | flops 1073741824 | bytes 6291456 | tf_op jit(solution)/shard_map/pallas_call | solution.py:65
  3.4 0.5 %collective-permute-start.2 = (bf16[528,256]{1,0:T(8,128)(2,1)S(1)}, bf16[528,256]{1,0:T(8,128)(2,1)S(1)}, u32[]{:S(2)}, u32[]{:S(2)}) collective-permute-start(bf16[528,256]{1,0:T(8,128)(2,1)S(1)} %shard_map.46.refs_1_.refs_0_), channel_id=1, source_target_pairs={{0,1},{1,0},{2,3},{3,2},{4,5},{5,4},{6,7},{7,6},{8,9},{9,8},{10,11... | collective-permute-start | bytes 811016 | tf_op jit(solution)/shard_map/ppermute | solution.py:212
  3.9 4.7 %collective-permute-start.5 = (bf16[528,256]{1,0:T(8,128)(2,1)S(1)}, bf16[528,256]{1,0:T(8,128)(2,1)S(1)}, u32[]{:S(2)}, u32[]{:S(2)}) collective-permute-start(bf16[528,256]{1,0:T(8,128)(2,1)S(1)} %shard_map.46.refs_1_.refs_0_), channel_id=1, source_target_pairs={{12,5},{13,4},{14,7},{15,6},{4,9},{5,8},{6,11},{7,10},{8,1},{9,0},... | collective-permute-start | bytes 811016 | tf_op jit(solution)/shard_map/ppermute | solution.py:224
  8.6 0.0 collective-permute-start.1
  8.6 8.6 %while.10 = (s32[]{:T(128)}, bf16[528,256]{1,0:T(8,128)(2,1)S(1)}, s32[]{:T(128)}, s32[]{:T(128)}) while((s32[]{:T(128)}, bf16[528,256]{1,0:T(8,128)(2,1)S(1)}, s32[]{:T(128)}, s32[]{:T(128)}) %tuple.18), condition=%wide.region_1.0_spmd, body=%wide.region_0.0_spmd.sunk | while | flops 2 | bytes 1622109 | solution.py:228
  8.7 1.6 %collective-permute-start = (bf16[528,256]{1,0:T(8,128)(2,1)S(1)}, bf16[528,256]{1,0:T(8,128)(2,1)S(1)}, u32[]{:S(2)}, u32[]{:S(2)}) collective-permute-start(bf16[528,256]{1,0:T(8,128)(2,1)S(1)} %get-tuple-element.65), channel_id=1, source_target_pairs={{0,2},{1,3},{2,0},{3,1},{4,6},{5,7},{6,4},{7,5},{8,10},{9,11},{10,... | collective-permute-start | bytes 811016 | tf_op jit(solution)/shard_map/while/body/ppermute | solution.py:212
  10.2 7.0 %collective-permute-done = bf16[528,256]{1,0:T(8,128)(2,1)S(1)} collective-permute-done((bf16[528,256]{1,0:T(8,128)(2,1)S(1)}, bf16[528,256]{1,0:T(8,128)(2,1)S(1)}, u32[]{:S(2)}, u32[]{:S(2)}) %collective-permute-start) | collective-permute-done | bytes 270368 | tf_op jit(solution)/shard_map/while/body/ppermute | solution.py:212
  17.2 0.1 collective-permute-start.4
  17.3 0.6 %collective-permute-start.3 = (bf16[256,256]{1,0:T(8,128)(2,1)S(1)}, bf16[256,256]{1,0:T(8,128)(2,1)S(1)}, u32[]{:S(2)}, u32[]{:S(2)}) collective-permute-start(bf16[256,256]{1,0:T(8,128)(2,1)S(1)} %slice.15), channel_id=1, source_target_pairs={{0,1},{1,0},{2,3},{3,2},{4,5},{5,4},{6,7},{7,6},{8,9},{9,8},{10,11... | collective-permute-start | bytes 393224 | tf_op jit(solution)/shard_map/ppermute | solution.py:212
  17.9 1.0 %collective-permute-done.3.refs_4_ = bf16[256,256]{1,0:T(8,128)(2,1)S(1)} collective-permute-done((bf16[256,256]{1,0:T(8,128)(2,1)S(1)}, bf16[256,256]{1,0:T(8,128)(2,1)S(1)}, u32[]{:S(2)}, u32[]{:S(2)}) %collective-permute-start.3) | collective-permute-done | bytes 131104 | tf_op jit(solution)/shard_map/ppermute | solution.py:212
  18.9 0.0 collective-permute-done.4.refs_5_
  18.9 0.0 collective-permute-done.2.refs_3_
  18.9 1.4 %collective-permute-done.5.refs_0_ = bf16[528,256]{1,0:T(8,128)(2,1)S(1)} collective-permute-done((bf16[528,256]{1,0:T(8,128)(2,1)S(1)}, bf16[528,256]{1,0:T(8,128)(2,1)S(1)}, u32[]{:S(2)}, u32[]{:S(2)}) %collective-permute-start.5) | collective-permute-done | bytes 270368 | tf_op jit(solution)/shard_map/ppermute | solution.py:224
  20.3 0.9 %shard_map.47 = (f32[4,128]{1,0:T(4,128)S(1)}, f32[8,128]{1,0:T(8,128)S(1)}, f32[8,128]{1,0:T(8,128)S(1)}) custom-call(bf16[528,256]{1,0:T(8,128)(2,1)S(1)} %collective-permute-done.5.refs_0_, bf16[528,256]{1,0:T(8,128)(2,1)S(1)} %shard_map.46.refs_1_.refs_0_, bf16[528,256]{1,0:T(8,128)(2,1)S(1)} %get-tuple-element.28.refs_2_, ...), custom_call_target="tpu_custom_call" | custom-call | tf_op jit(solution)/shard_map/pallas_call | solution.py:179
  21.1 0.6 %collective-permute-done.1.refs_0_ = bf16[528,256]{1,0:T(8,128)(2,1)S(1)} collective-permute-done((bf16[528,256]{1,0:T(8,128)(2,1)S(1)}, bf16[528,256]{1,0:T(8,128)(2,1)S(1)}, u32[]{:S(2)}, u32[]{:S(2)}) %collective-permute-start.1) | collective-permute-done | bytes 270368 | tf_op jit(solution)/shard_map/ppermute | solution.py:225
  21.7 0.8 %shard_map.48 = (f32[8,128]{1,0:T(8,128)S(1)}, f32[8,128]{1,0:T(8,128)S(1)}) custom-call(bf16[528,256]{1,0:T(8,128)(2,1)S(1)} %collective-permute-done.1.refs_0_, bf16[528,256]{1,0:T(8,128)(2,1)S(1)} %shard_map.46.refs_1_.refs_0_, bf16[528,256]{1,0:T(8,128)(2,1)S(1)} %get-tuple-element.28.refs_2_, bf16[528,256]{1,0:T(8,128)(2,1)S(1)} %collective-permute-done.2.refs_3_, ...), custom_call_target="tpu_custom_call" | custom-call | tf_op jit(solution)/shard_map/pallas_call | solution.py:179
  22.6 0.1 collective-permute-start.6
  22.7 1.0 %collective-permute-start.8 = (f32[4,128]{1,0:T(4,128)S(1)}, f32[4,128]{1,0:T(4,128)S(1)}, u32[]{:S(2)}, u32[]{:S(2)}) collective-permute-start(f32[4,128]{1,0:T(4,128)S(1)} %get-tuple-element.33), channel_id=1, source_target_pairs={{5,12},{4,13},{7,14},{6,15},{9,4},{8,5},{11,6},{10,7},{1,8},{0,9},... | collective-permute-start | bytes 6152 | tf_op jit(solution)/shard_map/ppermute | solution.py:239
  23.6 0.2 collective-permute-done.6
  23.8 1.5 %collective-permute-start.7 = (f32[4,128]{1,0:T(4,128)S(1)}, f32[4,128]{1,0:T(4,128)S(1)}, u32[]{:S(2)}, u32[]{:S(2)}) collective-permute-start(f32[4,128]{1,0:T(4,128)S(1)} %slice.19), channel_id=1, source_target_pairs={{0,2},{1,3},{2,0},{3,1},{4,6},{5,7},{6,4},{7,5},{8,10},{9,11},{10,... | collective-permute-start | bytes 6152 | tf_op jit(solution)/shard_map/ppermute | solution.py:212
  25.3 0.8 %shard_map.49 = f32[8,128]{1,0:T(8,128)S(1)} custom-call(bf16[528,256]{1,0:T(8,128)(2,1)S(1)} %shard_map.46.refs_1_.refs_0_, bf16[528,256]{1,0:T(8,128)(2,1)S(1)} %shard_map.46.refs_1_.refs_0_, bf16[528,256]{1,0:T(8,128)(2,1)S(1)} %get-tuple-element.28.refs_2_, bf16[528,256]{1,0:T(8,128)(2,1)S(1)} %collective-permute-done.2.refs_3_, ...), custom_call_target="tpu_custom_call" | custom-call | tf_op jit(solution)/shard_map/pallas_call | solution.py:179
  26.1 1.4 %collective-permute-done.8 = f32[4,128]{1,0:T(4,128)S(1)} collective-permute-done((f32[4,128]{1,0:T(4,128)S(1)}, f32[4,128]{1,0:T(4,128)S(1)}, u32[]{:S(2)}, u32[]{:S(2)}) %collective-permute-start.8) | collective-permute-done | bytes 2080 | tf_op jit(solution)/shard_map/ppermute | solution.py:239
  27.5 0.0 collective-permute-done.7
  27.5 0.6 %maximum_bitcast_fusion = f32[512]{0:T(512)} fusion(f32[4,128]{1,0:T(4,128)S(1)} %collective-permute-done.8, f32[4,128]{1,0:T(4,128)S(1)} %collective-permute-done.7, f32[8,128]{1,0:T(8,128)S(1)} %shard_map.49, f32[8,128]{1,0:T(8,128)S(1)} %max.18), kind=kLoop, calls=%fused_computation | loop fusion | flops 2048 | bytes 10240 | tf_op jit(solution)/shard_map/reshape | solution.py:248
  (6 shorter events, 0.1 us)
Async XLA Ops:
  3.4 15.5 %collective-permute-start.2 = (bf16[528,256]{1,0:T(8,128)(2,1)S(1)}, bf16[528,256]{1,0:T(8,128)(2,1)S(1)}, u32[]{:S(2)}, u32[]{:S(2)}) collective-permute-start(bf16[528,256]{1,0:T(8,128)(2,1)S(1)} %shard_map.46.refs_1_.refs_0_), channel_id=1, source_target_pairs={{0,1},{1,0},{2,3},{3,2},{4,5},{5,4},{6,7},{7,6},{8,9},{9,8},{10,11... | collective-permute-start | bytes 811016 | tf_op jit(solution)/shard_map/ppermute | solution.py:212
  3.9 16.4 %collective-permute-start.5 = (bf16[528,256]{1,0:T(8,128)(2,1)S(1)}, bf16[528,256]{1,0:T(8,128)(2,1)S(1)}, u32[]{:S(2)}, u32[]{:S(2)}) collective-permute-start(bf16[528,256]{1,0:T(8,128)(2,1)S(1)} %shard_map.46.refs_1_.refs_0_), channel_id=1, source_target_pairs={{12,5},{13,4},{14,7},{15,6},{4,9},{5,8},{6,11},{7,10},{8,1},{9,0},... | collective-permute-start | bytes 811016 | tf_op jit(solution)/shard_map/ppermute | solution.py:224
  8.6 13.1 %collective-permute-start.1 = (bf16[528,256]{1,0:T(8,128)(2,1)S(1)}, bf16[528,256]{1,0:T(8,128)(2,1)S(1)}, u32[]{:S(2)}, u32[]{:S(2)}) collective-permute-start(bf16[528,256]{1,0:T(8,128)(2,1)S(1)} %shard_map.46.refs_1_.refs_0_), channel_id=1, source_target_pairs={{12,8},{4,0},{8,12},{0,4},{13,9},{5,1},{9,13},{1,5},{14,10},{6,2},... | collective-permute-start | bytes 811016 | tf_op jit(solution)/shard_map/ppermute | solution.py:225
  8.7 8.5 %collective-permute-start = (bf16[528,256]{1,0:T(8,128)(2,1)S(1)}, bf16[528,256]{1,0:T(8,128)(2,1)S(1)}, u32[]{:S(2)}, u32[]{:S(2)}) collective-permute-start(bf16[528,256]{1,0:T(8,128)(2,1)S(1)} %get-tuple-element.65), channel_id=1, source_target_pairs={{0,2},{1,3},{2,0},{3,1},{4,6},{5,7},{6,4},{7,5},{8,10},{9,11},{10,... | collective-permute-start | bytes 811016 | tf_op jit(solution)/shard_map/while/body/ppermute | solution.py:212
  17.2 1.6 %collective-permute-start.4 = (bf16[272,256]{1,0:T(8,128)(2,1)S(1)}, bf16[272,256]{1,0:T(8,128)(2,1)S(1)}, u32[]{:S(2)}, u32[]{:S(2)}) collective-permute-start(bf16[272,256]{1,0:T(8,128)(2,1)S(1)} %slice.16), channel_id=1, source_target_pairs={{0,1},{1,0},{2,3},{3,2},{4,5},{5,4},{6,7},{7,6},{8,9},{9,8},{10,11... | collective-permute-start | bytes 417800 | tf_op jit(solution)/shard_map/ppermute | solution.py:212
  17.3 1.5 %collective-permute-start.3 = (bf16[256,256]{1,0:T(8,128)(2,1)S(1)}, bf16[256,256]{1,0:T(8,128)(2,1)S(1)}, u32[]{:S(2)}, u32[]{:S(2)}) collective-permute-start(bf16[256,256]{1,0:T(8,128)(2,1)S(1)} %slice.15), channel_id=1, source_target_pairs={{0,1},{1,0},{2,3},{3,2},{4,5},{5,4},{6,7},{7,6},{8,9},{9,8},{10,11... | collective-permute-start | bytes 393224 | tf_op jit(solution)/shard_map/ppermute | solution.py:212
  22.6 1.2 %collective-permute-start.6 = (f32[8,128]{1,0:T(8,128)S(1)}, f32[8,128]{1,0:T(8,128)S(1)}, u32[]{:S(2)}, u32[]{:S(2)}) collective-permute-start(f32[8,128]{1,0:T(8,128)S(1)} %get-tuple-element.32), channel_id=1, source_target_pairs={{0,1},{1,0},{2,3},{3,2},{4,5},{5,4},{6,7},{7,6},{8,9},{9,8},{10,11... | collective-permute-start | bytes 12296 | tf_op jit(solution)/shard_map/ppermute | solution.py:212
  22.7 4.9 %collective-permute-start.8 = (f32[4,128]{1,0:T(4,128)S(1)}, f32[4,128]{1,0:T(4,128)S(1)}, u32[]{:S(2)}, u32[]{:S(2)}) collective-permute-start(f32[4,128]{1,0:T(4,128)S(1)} %get-tuple-element.33), channel_id=1, source_target_pairs={{5,12},{4,13},{7,14},{6,15},{9,4},{8,5},{11,6},{10,7},{1,8},{0,9},... | collective-permute-start | bytes 6152 | tf_op jit(solution)/shard_map/ppermute | solution.py:239
  23.8 3.7 %collective-permute-start.7 = (f32[4,128]{1,0:T(4,128)S(1)}, f32[4,128]{1,0:T(4,128)S(1)}, u32[]{:S(2)}, u32[]{:S(2)}) collective-permute-start(f32[4,128]{1,0:T(4,128)S(1)} %slice.19), channel_id=1, source_target_pairs={{0,2},{1,3},{2,0},{3,1},{4,6},{5,7},{6,4},{7,5},{8,10},{9,11},{10,... | collective-permute-start | bytes 6152 | tf_op jit(solution)/shard_map/ppermute | solution.py:212

commit v25 on v24

--- a/solution.py
+++ b/solution.py
@@ -215,14 +215,13 @@
         return block[: row_count // 2], block[row_count // 2 :]
 
     own = project(embeddings, basis, owner_ids, sub_cluster)
-    *steps, last = owner_steps(owner_count)
-    steps = [
+    both = ("owners", "split")
+    *steps, last = [
         [(a * split_count + s, b * split_count + (s ^ 1)) for a, b in step for s in range(split_count)]
-        for step in steps
-    ]
-    both = ("owners", "split")
+        for step in owner_steps(owner_count)
+    ]
     keys = [lax.ppermute(own, both, step) for step in steps]
-    nearby = lax.ppermute(own, "owners", last)
+    nearby = lax.ppermute(own, both, last)
     offsets = range(2, split_count, 2)
     one_turn = 1 + (lax.axis_index("groups") >> 16)
     besides = lax.fori_loop(

time: 28.2 us -> 28.4 us (level)
  waiting for transfers between devices: 11.6 us -> 12 us
    ppermute x1, starting transfers between devices: 0.95 us -> 0.6 us  [per_device(): backs.append(lax.ppermute(found, both, [(b, a) for a, b in step]))]
where the time goes in v25:
time: 28.4 us; the launch traced here: 28.3 us
  waiting for transfers between devices  12 us (42%)
  starting transfers between devices  9.7 us (34%)
  Pallas kernels  5.82 us (20%)
  other arithmetic  0.59 us (2%)
    ppermute x6, waiting for transfers between devices, swap(): lax.ppermute(block, 'split', [(s, s ^ offset) for s in range(split_count)])  8.4 us
    ppermute x1, starting transfers between devices, per_device(): keys = [lax.ppermute(own, both, step) for step in steps]  4.71 us
    ppermute x6, starting transfers between devices, swap(): lax.ppermute(block, 'split', [(s, s ^ offset) for s in range(split_count)])  4.39 us
    pallas_call x1, Pallas kernels, project(): pl.pallas_call(project_kernel, in_specs=[pl.BlockSpec(memory_space=pltpu....  3.38 us
    pallas_call x3, Pallas kernels, score(): pl.pallas_call(functools.partial(score_kernel, len(keys), cols, [len(row)...  2.44 us
    ppermute x1, waiting for transfers between devices, per_device(): backs.append(lax.ppermute(found, both, [(b, a) for a, b in step]))  1.51 us
    ppermute x1, waiting for transfers between devices, per_device(): keys = [lax.ppermute(own, both, step) for step in steps]  1.41 us
    ppermute x1, waiting for transfers between devices, per_device(): nearby = lax.ppermute(own, both, last)  0.69 us
  transfers between devices with their start and end apart: 9, of which 6 were waited for; matrix products, arithmetic and copies ran while one was open for 0% of the time, Pallas kernels for 6%

profile of v25, /device:TPU:0, one launch (start us, length us, event | category | flops | bytes accessed | tf_op | source)
XLA Modules:
  0.0 28.3 jit_solution(6985011695428629896)
XLA Ops:
  0.0 3.4 %shard_map.46.refs_1_.refs_0_ = bf16[528,256]{1,0:T(8,128)(2,1)S(1)} custom-call(bf16[512,4096]{1,0:T(8,128)(2,1)} %source_hbm.1, bf16[4096,256]{1,0:T(8,128)(2,1)} %basis_hbm.1, s32[4,128]{1,0:T(4,128)} %bitcast.4, s32[4,128]{1,0:T(4,128)} %bitcast.5), custom_call_target="tpu_custom_call" | custom-call | flops 1073741824 | bytes 6291456 | tf_op jit(solution)/shard_map/pallas_call | solution.py:65
  3.4 0.5 %collective-permute-start.2 = (bf16[528,256]{1,0:T(8,128)(2,1)S(1)}, bf16[528,256]{1,0:T(8,128)(2,1)S(1)}, u32[]{:S(2)}, u32[]{:S(2)}) collective-permute-start(bf16[528,256]{1,0:T(8,128)(2,1)S(1)} %shard_map.46.refs_1_.refs_0_), channel_id=1, source_target_pairs={{0,1},{1,0},{2,3},{3,2},{4,5},{5,4},{6,7},{7,6},{8,9},{9,8},{10,11... | collective-permute-start | bytes 811016 | tf_op jit(solution)/shard_map/ppermute | solution.py:212
  3.9 4.7 %collective-permute-start.5 = (bf16[528,256]{1,0:T(8,128)(2,1)S(1)}, bf16[528,256]{1,0:T(8,128)(2,1)S(1)}, u32[]{:S(2)}, u32[]{:S(2)}) collective-permute-start(bf16[528,256]{1,0:T(8,128)(2,1)S(1)} %shard_map.46.refs_1_.refs_0_), channel_id=1, source_target_pairs={{12,5},{13,4},{14,7},{15,6},{4,9},{5,8},{6,11},{7,10},{8,1},{9,0},... | collective-permute-start | bytes 811016 | tf_op jit(solution)/shard_map/ppermute | solution.py:223
  8.6 0.0 collective-permute-start.1
  8.6 8.6 %while.10 = (s32[]{:T(128)}, bf16[528,256]{1,0:T(8,128)(2,1)S(1)}, s32[]{:T(128)}, s32[]{:T(128)}) while((s32[]{:T(128)}, bf16[528,256]{1,0:T(8,128)(2,1)S(1)}, s32[]{:T(128)}, s32[]{:T(128)}) %tuple.18), condition=%wide.region_1.0_spmd, body=%wide.region_0.0_spmd.sunk | while | flops 2 | bytes 1622109 | solution.py:227
  8.7 1.6 %collective-permute-start = (bf16[528,256]{1,0:T(8,128)(2,1)S(1)}, bf16[528,256]{1,0:T(8,128)(2,1)S(1)}, u32[]{:S(2)}, u32[]{:S(2)}) collective-permute-start(bf16[528,256]{1,0:T(8,128)(2,1)S(1)} %get-tuple-element.65), channel_id=1, source_target_pairs={{0,2},{1,3},{2,0},{3,1},{4,6},{5,7},{6,4},{7,5},{8,10},{9,11},{10,... | collective-permute-start | bytes 811016 | tf_op jit(solution)/shard_map/while/body/ppermute | solution.py:212
  10.2 7.0 %collective-permute-done = bf16[528,256]{1,0:T(8,128)(2,1)S(1)} collective-permute-done((bf16[528,256]{1,0:T(8,128)(2,1)S(1)}, bf16[528,256]{1,0:T(8,128)(2,1)S(1)}, u32[]{:S(2)}, u32[]{:S(2)}) %collective-permute-start) | collective-permute-done | bytes 270368 | tf_op jit(solution)/shard_map/while/body/ppermute | solution.py:212
  17.2 0.1 collective-permute-start.4
  17.3 0.6 %collective-permute-start.3 = (bf16[256,256]{1,0:T(8,128)(2,1)S(1)}, bf16[256,256]{1,0:T(8,128)(2,1)S(1)}, u32[]{:S(2)}, u32[]{:S(2)}) collective-permute-start(bf16[256,256]{1,0:T(8,128)(2,1)S(1)} %slice.15), channel_id=1, source_target_pairs={{0,1},{1,0},{2,3},{3,2},{4,5},{5,4},{6,7},{7,6},{8,9},{9,8},{10,11... | collective-permute-start | bytes 393224 | tf_op jit(solution)/shard_map/ppermute | solution.py:212
  17.9 1.0 %collective-permute-done.3.refs_4_ = bf16[256,256]{1,0:T(8,128)(2,1)S(1)} collective-permute-done((bf16[256,256]{1,0:T(8,128)(2,1)S(1)}, bf16[256,256]{1,0:T(8,128)(2,1)S(1)}, u32[]{:S(2)}, u32[]{:S(2)}) %collective-permute-start.3) | collective-permute-done | bytes 131104 | tf_op jit(solution)/shard_map/ppermute | solution.py:212
  18.9 0.0 collective-permute-done.4.refs_5_
  18.9 0.0 collective-permute-done.2.refs_3_
  18.9 1.4 %collective-permute-done.5.refs_0_ = bf16[528,256]{1,0:T(8,128)(2,1)S(1)} collective-permute-done((bf16[528,256]{1,0:T(8,128)(2,1)S(1)}, bf16[528,256]{1,0:T(8,128)(2,1)S(1)}, u32[]{:S(2)}, u32[]{:S(2)}) %collective-permute-start.5) | collective-permute-done | bytes 270368 | tf_op jit(solution)/shard_map/ppermute | solution.py:223
  20.3 0.9 %shard_map.47 = (f32[4,128]{1,0:T(4,128)S(1)}, f32[8,128]{1,0:T(8,128)S(1)}, f32[8,128]{1,0:T(8,128)S(1)}) custom-call(bf16[528,256]{1,0:T(8,128)(2,1)S(1)} %collective-permute-done.5.refs_0_, bf16[528,256]{1,0:T(8,128)(2,1)S(1)} %shard_map.46.refs_1_.refs_0_, bf16[528,256]{1,0:T(8,128)(2,1)S(1)} %get-tuple-element.28.refs_2_, ...), custom_call_target="tpu_custom_call" | custom-call | tf_op jit(solution)/shard_map/pallas_call | solution.py:179
  21.1 0.7 %collective-permute-done.1.refs_0_ = bf16[528,256]{1,0:T(8,128)(2,1)S(1)} collective-permute-done((bf16[528,256]{1,0:T(8,128)(2,1)S(1)}, bf16[528,256]{1,0:T(8,128)(2,1)S(1)}, u32[]{:S(2)}, u32[]{:S(2)}) %collective-permute-start.1) | collective-permute-done | bytes 270368 | tf_op jit(solution)/shard_map/ppermute | solution.py:224
  21.8 0.8 %shard_map.48 = (f32[8,128]{1,0:T(8,128)S(1)}, f32[8,128]{1,0:T(8,128)S(1)}) custom-call(bf16[528,256]{1,0:T(8,128)(2,1)S(1)} %collective-permute-done.1.refs_0_, bf16[528,256]{1,0:T(8,128)(2,1)S(1)} %shard_map.46.refs_1_.refs_0_, bf16[528,256]{1,0:T(8,128)(2,1)S(1)} %get-tuple-element.28.refs_2_, bf16[528,256]{1,0:T(8,128)(2,1)S(1)} %collective-permute-done.2.refs_3_, ...), custom_call_target="tpu_custom_call" | custom-call | tf_op jit(solution)/shard_map/pallas_call | solution.py:179
  22.7 0.2 collective-permute-start.6
  22.8 0.6 %collective-permute-start.8 = (f32[4,128]{1,0:T(4,128)S(1)}, f32[4,128]{1,0:T(4,128)S(1)}, u32[]{:S(2)}, u32[]{:S(2)}) collective-permute-start(f32[4,128]{1,0:T(4,128)S(1)} %get-tuple-element.33), channel_id=1, source_target_pairs={{5,12},{4,13},{7,14},{6,15},{9,4},{8,5},{11,6},{10,7},{1,8},{0,9},... | collective-permute-start | bytes 6152 | tf_op jit(solution)/shard_map/ppermute | solution.py:238
  23.4 0.4 %collective-permute-done.6 = f32[8,128]{1,0:T(8,128)S(1)} collective-permute-done((f32[8,128]{1,0:T(8,128)S(1)}, f32[8,128]{1,0:T(8,128)S(1)}, u32[]{:S(2)}, u32[]{:S(2)}) %collective-permute-start.6) | collective-permute-done | bytes 4128 | tf_op jit(solution)/shard_map/ppermute | solution.py:212
  23.9 1.5 %collective-permute-start.7 = (f32[4,128]{1,0:T(4,128)S(1)}, f32[4,128]{1,0:T(4,128)S(1)}, u32[]{:S(2)}, u32[]{:S(2)}) collective-permute-start(f32[4,128]{1,0:T(4,128)S(1)} %slice.19), channel_id=1, source_target_pairs={{0,2},{1,3},{2,0},{3,1},{4,6},{5,7},{6,4},{7,5},{8,10},{9,11},{10,... | collective-permute-start | bytes 6152 | tf_op jit(solution)/shard_map/ppermute | solution.py:212
  25.4 0.8 %shard_map.49 = f32[8,128]{1,0:T(8,128)S(1)} custom-call(bf16[528,256]{1,0:T(8,128)(2,1)S(1)} %shard_map.46.refs_1_.refs_0_, bf16[528,256]{1,0:T(8,128)(2,1)S(1)} %shard_map.46.refs_1_.refs_0_, bf16[528,256]{1,0:T(8,128)(2,1)S(1)} %get-tuple-element.28.refs_2_, bf16[528,256]{1,0:T(8,128)(2,1)S(1)} %collective-permute-done.2.refs_3_, ...), custom_call_target="tpu_custom_call" | custom-call | tf_op jit(solution)/shard_map/pallas_call | solution.py:179
  26.2 1.5 %collective-permute-done.8 = f32[4,128]{1,0:T(4,128)S(1)} collective-permute-done((f32[4,128]{1,0:T(4,128)S(1)}, f32[4,128]{1,0:T(4,128)S(1)}, u32[]{:S(2)}, u32[]{:S(2)}) %collective-permute-start.8) | collective-permute-done | bytes 2080 | tf_op jit(solution)/shard_map/ppermute | solution.py:238
  27.7 0.0 collective-permute-done.7
  27.7 0.6 %maximum_bitcast_fusion = f32[512]{0:T(512)} fusion(f32[4,128]{1,0:T(4,128)S(1)} %collective-permute-done.8, f32[4,128]{1,0:T(4,128)S(1)} %collective-permute-done.7, f32[8,128]{1,0:T(8,128)S(1)} %shard_map.49, f32[8,128]{1,0:T(8,128)S(1)} %max.18), kind=kLoop, calls=%fused_computation | loop fusion | flops 2048 | bytes 10240 | tf_op jit(solution)/shard_map/reshape | solution.py:247
  (6 shorter events, 0.1 us)
Async XLA Ops:
  3.4 15.5 %collective-permute-start.2 = (bf16[528,256]{1,0:T(8,128)(2,1)S(1)}, bf16[528,256]{1,0:T(8,128)(2,1)S(1)}, u32[]{:S(2)}, u32[]{:S(2)}) collective-permute-start(bf16[528,256]{1,0:T(8,128)(2,1)S(1)} %shard_map.46.refs_1_.refs_0_), channel_id=1, source_target_pairs={{0,1},{1,0},{2,3},{3,2},{4,5},{5,4},{6,7},{7,6},{8,9},{9,8},{10,11... | collective-permute-start | bytes 811016 | tf_op jit(solution)/shard_map/ppermute | solution.py:212
  3.9 16.4 %collective-permute-start.5 = (bf16[528,256]{1,0:T(8,128)(2,1)S(1)}, bf16[528,256]{1,0:T(8,128)(2,1)S(1)}, u32[]{:S(2)}, u32[]{:S(2)}) collective-permute-start(bf16[528,256]{1,0:T(8,128)(2,1)S(1)} %shard_map.46.refs_1_.refs_0_), channel_id=1, source_target_pairs={{12,5},{13,4},{14,7},{15,6},{4,9},{5,8},{6,11},{7,10},{8,1},{9,0},... | collective-permute-start | bytes 811016 | tf_op jit(solution)/shard_map/ppermute | solution.py:223
  8.6 13.2 %collective-permute-start.1 = (bf16[528,256]{1,0:T(8,128)(2,1)S(1)}, bf16[528,256]{1,0:T(8,128)(2,1)S(1)}, u32[]{:S(2)}, u32[]{:S(2)}) collective-permute-start(bf16[528,256]{1,0:T(8,128)(2,1)S(1)} %shard_map.46.refs_1_.refs_0_), channel_id=1, source_target_pairs={{12,9},{13,8},{14,11},{15,10},{4,1},{5,0},{6,3},{7,2},{8,13},{9,12... | collective-permute-start | bytes 811016 | tf_op jit(solution)/shard_map/ppermute | solution.py:224
  8.7 8.5 %collective-permute-start = (bf16[528,256]{1,0:T(8,128)(2,1)S(1)}, bf16[528,256]{1,0:T(8,128)(2,1)S(1)}, u32[]{:S(2)}, u32[]{:S(2)}) collective-permute-start(bf16[528,256]{1,0:T(8,128)(2,1)S(1)} %get-tuple-element.65), channel_id=1, source_target_pairs={{0,2},{1,3},{2,0},{3,1},{4,6},{5,7},{6,4},{7,5},{8,10},{9,11},{10,... | collective-permute-start | bytes 811016 | tf_op jit(solution)/shard_map/while/body/ppermute | solution.py:212
  17.2 1.6 %collective-permute-start.4 = (bf16[272,256]{1,0:T(8,128)(2,1)S(1)}, bf16[272,256]{1,0:T(8,128)(2,1)S(1)}, u32[]{:S(2)}, u32[]{:S(2)}) collective-permute-start(bf16[272,256]{1,0:T(8,128)(2,1)S(1)} %slice.16), channel_id=1, source_target_pairs={{0,1},{1,0},{2,3},{3,2},{4,5},{5,4},{6,7},{7,6},{8,9},{9,8},{10,11... | collective-permute-start | bytes 417800 | tf_op jit(solution)/shard_map/ppermute | solution.py:212
  17.3 1.5 %collective-permute-start.3 = (bf16[256,256]{1,0:T(8,128)(2,1)S(1)}, bf16[256,256]{1,0:T(8,128)(2,1)S(1)}, u32[]{:S(2)}, u32[]{:S(2)}) collective-permute-start(bf16[256,256]{1,0:T(8,128)(2,1)S(1)} %slice.15), channel_id=1, source_target_pairs={{0,1},{1,0},{2,3},{3,2},{4,5},{5,4},{6,7},{7,6},{8,9},{9,8},{10,11... | collective-permute-start | bytes 393224 | tf_op jit(solution)/shard_map/ppermute | solution.py:212
  22.7 1.2 %collective-permute-start.6 = (f32[8,128]{1,0:T(8,128)S(1)}, f32[8,128]{1,0:T(8,128)S(1)}, u32[]{:S(2)}, u32[]{:S(2)}) collective-permute-start(f32[8,128]{1,0:T(8,128)S(1)} %get-tuple-element.32), channel_id=1, source_target_pairs={{0,1},{1,0},{2,3},{3,2},{4,5},{5,4},{6,7},{7,6},{8,9},{9,8},{10,11... | collective-permute-start | bytes 12296 | tf_op jit(solution)/shard_map/ppermute | solution.py:212
  22.8 4.8 %collective-permute-start.8 = (f32[4,128]{1,0:T(4,128)S(1)}, f32[4,128]{1,0:T(4,128)S(1)}, u32[]{:S(2)}, u32[]{:S(2)}) collective-permute-start(f32[4,128]{1,0:T(4,128)S(1)} %get-tuple-element.33), channel_id=1, source_target_pairs={{5,12},{4,13},{7,14},{6,15},{9,4},{8,5},{11,6},{10,7},{1,8},{0,9},... | collective-permute-start | bytes 6152 | tf_op jit(solution)/shard_map/ppermute | solution.py:238
  23.9 3.8 %collective-permute-start.7 = (f32[4,128]{1,0:T(4,128)S(1)}, f32[4,128]{1,0:T(4,128)S(1)}, u32[]{:S(2)}, u32[]{:S(2)}) collective-permute-start(f32[4,128]{1,0:T(4,128)S(1)} %slice.19), channel_id=1, source_target_pairs={{0,2},{1,3},{2,0},{3,1},{4,6},{5,7},{6,4},{7,5},{8,10},{9,11},{10,... | collective-permute-start | bytes 6152 | tf_op jit(solution)/shard_map/ppermute | solution.py:212

commit v26 on v25

--- a/solution.py
+++ b/solution.py
@@ -232,11 +232,11 @@
     )
     rows = [own, *besides, swap(own, 1)]
     rows += [tuple(swap(part, 1) for part in halves(beside)) for beside in besides]
-    row_best, backs = [], []
+    _, row_best = score([nearby], rows)
+    backs = []
     for key, step in zip(keys, steps):
         (found,), row_best = score([key], rows, cols=1, known=row_best)
         backs.append(lax.ppermute(found, both, [(b, a) for a, b in step]))
-    _, row_best = score([nearby], rows, known=row_best)
     _, (own_best,) = score([own], rows, own_first=True)
     local = jnp.maximum(row_best[0], swap(row_best[1], 1))
     best = jnp.maximum(local[:tiles], own_best[:tiles])

time: 28.4 us -> 29 us (1.021)
  starting transfers between devices: 9.7 us -> 11 us
  waiting for transfers between devices: 12 us -> 11.3 us
    ppermute x1, starting transfers between devices: 0.01 us -> 2.7 us  [per_device(): nearby = lax.ppermute(own, both, last)]
    ppermute x1, starting transfers between devices: 4.71 us -> 2.14 us  [per_device(): keys = [lax.ppermute(own, both, step) for step in steps]]
    ppermute x1, starting transfers between devices: 0.6 us -> 1.67 us  [per_device(): backs.append(lax.ppermute(found, both, [(b, a) for a, b in step]))]
    ppermute x1, waiting for transfers between devices: 1.51 us -> 0.79 us  [per_device(): backs.append(lax.ppermute(found, both, [(b, a) for a, b in step]))]
    ppermute x1, waiting for transfers between devices: 0.69 us -> 0.01 us  [per_device(): nearby = lax.ppermute(own, both, last)]
    ppermute x6, waiting for transfers between devices: 8.4 us -> 8.86 us  [swap(): lax.ppermute(block, 'split', [(s, s ^ offset) for s in range(split_count)])]
  transfers between devices with their start and end apart: 9 -> 9, of which waited for: 6 -> 5; matrix products, arithmetic and copies ran while one was open for 0% -> 0% of each run, Pallas kernels for 6% -> 6%
where the time goes in v26:
time: 29 us; the launch traced here: 28.8 us
  waiting for transfers between devices  11.3 us (39%)
  starting transfers between devices  11 us (38%)
  Pallas kernels  5.82 us (20%)
  other arithmetic  0.59 us (2%)
    ppermute x6, waiting for transfers between devices, swap(): lax.ppermute(block, 'split', [(s, s ^ offset) for s in range(split_count)])  8.86 us
    ppermute x6, starting transfers between devices, swap(): lax.ppermute(block, 'split', [(s, s ^ offset) for s in range(split_count)])  4.44 us
    pallas_call x1, Pallas kernels, project(): pl.pallas_call(project_kernel, in_specs=[pl.BlockSpec(memory_space=pltpu....  3.38 us
    ppermute x1, starting transfers between devices, per_device(): nearby = lax.ppermute(own, both, last)  2.7 us
    pallas_call x3, Pallas kernels, score(): pl.pallas_call(functools.partial(score_kernel, len(keys), cols, [len(row)...  2.44 us
    ppermute x1, starting transfers between devices, per_device(): keys = [lax.ppermute(own, both, step) for step in steps]  2.14 us
    ppermute x1, starting transfers between devices, per_device(): backs.append(lax.ppermute(found, both, [(b, a) for a, b in step]))  1.67 us
    ppermute x1, waiting for transfers between devices, per_device(): keys = [lax.ppermute(own, both, step) for step in steps]  1.65 us
  transfers between devices with their start and end apart: 9, of which 5 were waited for; matrix products, arithmetic and copies ran while one was open for 0% of the time, Pallas kernels for 6%

profile of v26, /device:TPU:0, one launch (start us, length us, event | category | flops | bytes accessed | tf_op | source)
XLA Modules:
  0.0 28.8 jit_solution(15980529372472174899)
XLA Ops:
  0.0 3.4 %shard_map.46.refs_1_.refs_0_ = bf16[528,256]{1,0:T(8,128)(2,1)S(1)} custom-call(bf16[512,4096]{1,0:T(8,128)(2,1)} %source_hbm.1, bf16[4096,256]{1,0:T(8,128)(2,1)} %basis_hbm.1, s32[4,128]{1,0:T(4,128)} %bitcast.4, s32[4,128]{1,0:T(4,128)} %bitcast.5), custom_call_target="tpu_custom_call" | custom-call | flops 1073741824 | bytes 6291456 | tf_op jit(solution)/shard_map/pallas_call | solution.py:65
  3.4 0.5 %collective-permute-start.2 = (bf16[528,256]{1,0:T(8,128)(2,1)S(1)}, bf16[528,256]{1,0:T(8,128)(2,1)S(1)}, u32[]{:S(2)}, u32[]{:S(2)}) collective-permute-start(bf16[528,256]{1,0:T(8,128)(2,1)S(1)} %shard_map.46.refs_1_.refs_0_), channel_id=1, source_target_pairs={{0,1},{1,0},{2,3},{3,2},{4,5},{5,4},{6,7},{7,6},{8,9},{9,8},{10,11... | collective-permute-start | bytes 811016 | tf_op jit(solution)/shard_map/ppermute | solution.py:212
  3.9 2.7 %collective-permute-start.5 = (bf16[528,256]{1,0:T(8,128)(2,1)S(1)}, bf16[528,256]{1,0:T(8,128)(2,1)S(1)}, u32[]{:S(2)}, u32[]{:S(2)}) collective-permute-start(bf16[528,256]{1,0:T(8,128)(2,1)S(1)} %shard_map.46.refs_1_.refs_0_), channel_id=1, source_target_pairs={{12,9},{13,8},{14,11},{15,10},{4,1},{5,0},{6,3},{7,2},{8,13},{9,12... | collective-permute-start | bytes 811016 | tf_op jit(solution)/shard_map/ppermute | solution.py:224
  6.6 2.1 %collective-permute-start.1 = (bf16[528,256]{1,0:T(8,128)(2,1)S(1)}, bf16[528,256]{1,0:T(8,128)(2,1)S(1)}, u32[]{:S(2)}, u32[]{:S(2)}) collective-permute-start(bf16[528,256]{1,0:T(8,128)(2,1)S(1)} %shard_map.46.refs_1_.refs_0_), channel_id=1, source_target_pairs={{12,5},{13,4},{14,7},{15,6},{4,9},{5,8},{6,11},{7,10},{8,1},{9,0},... | collective-permute-start | bytes 811016 | tf_op jit(solution)/shard_map/ppermute | solution.py:223
  8.8 8.9 %while.10 = (s32[]{:T(128)}, bf16[528,256]{1,0:T(8,128)(2,1)S(1)}, s32[]{:T(128)}, s32[]{:T(128)}) while((s32[]{:T(128)}, bf16[528,256]{1,0:T(8,128)(2,1)S(1)}, s32[]{:T(128)}, s32[]{:T(128)}) %tuple.18), condition=%wide.region_1.0_spmd, body=%wide.region_0.0_spmd.sunk | while | flops 2 | bytes 1622109 | solution.py:227
  8.8 1.6 %collective-permute-start = (bf16[528,256]{1,0:T(8,128)(2,1)S(1)}, bf16[528,256]{1,0:T(8,128)(2,1)S(1)}, u32[]{:S(2)}, u32[]{:S(2)}) collective-permute-start(bf16[528,256]{1,0:T(8,128)(2,1)S(1)} %get-tuple-element.65), channel_id=1, source_target_pairs={{0,2},{1,3},{2,0},{3,1},{4,6},{5,7},{6,4},{7,5},{8,10},{9,11},{10,... | collective-permute-start | bytes 811016 | tf_op jit(solution)/shard_map/while/body/ppermute | solution.py:212
  10.3 7.3 %collective-permute-done = bf16[528,256]{1,0:T(8,128)(2,1)S(1)} collective-permute-done((bf16[528,256]{1,0:T(8,128)(2,1)S(1)}, bf16[528,256]{1,0:T(8,128)(2,1)S(1)}, u32[]{:S(2)}, u32[]{:S(2)}) %collective-permute-start) | collective-permute-done | bytes 270368 | tf_op jit(solution)/shard_map/while/body/ppermute | solution.py:212
  17.7 0.1 collective-permute-start.4
  17.8 0.6 %collective-permute-start.3 = (bf16[256,256]{1,0:T(8,128)(2,1)S(1)}, bf16[256,256]{1,0:T(8,128)(2,1)S(1)}, u32[]{:S(2)}, u32[]{:S(2)}) collective-permute-start(bf16[256,256]{1,0:T(8,128)(2,1)S(1)} %slice.15), channel_id=1, source_target_pairs={{0,1},{1,0},{2,3},{3,2},{4,5},{5,4},{6,7},{7,6},{8,9},{9,8},{10,11... | collective-permute-start | bytes 393224 | tf_op jit(solution)/shard_map/ppermute | solution.py:212
  18.4 1.0 %collective-permute-done.3.refs_4_ = bf16[256,256]{1,0:T(8,128)(2,1)S(1)} collective-permute-done((bf16[256,256]{1,0:T(8,128)(2,1)S(1)}, bf16[256,256]{1,0:T(8,128)(2,1)S(1)}, u32[]{:S(2)}, u32[]{:S(2)}) %collective-permute-start.3) | collective-permute-done | bytes 131104 | tf_op jit(solution)/shard_map/ppermute | solution.py:212
  19.4 0.0 collective-permute-done.4.refs_5_
  19.4 0.0 collective-permute-done.2.refs_3_
  19.4 0.0 collective-permute-done.5.refs_0_
  19.4 0.8 %shard_map.47 = (f32[8,128]{1,0:T(8,128)S(1)}, f32[8,128]{1,0:T(8,128)S(1)}) custom-call(bf16[528,256]{1,0:T(8,128)(2,1)S(1)} %collective-permute-done.5.refs_0_, bf16[528,256]{1,0:T(8,128)(2,1)S(1)} %shard_map.46.refs_1_.refs_0_, bf16[528,256]{1,0:T(8,128)(2,1)S(1)} %get-tuple-element.28.refs_2_, bf16[528,256]{1,0:T(8,128)(2,1)S(1)} %collective-permute-done.2.refs_3_, ...), custom_call_target="tpu_custom_call" | custom-call | tf_op jit(solution)/shard_map/pallas_call | solution.py:179
  20.2 1.7 %collective-permute-done.1.refs_0_ = bf16[528,256]{1,0:T(8,128)(2,1)S(1)} collective-permute-done((bf16[528,256]{1,0:T(8,128)(2,1)S(1)}, bf16[528,256]{1,0:T(8,128)(2,1)S(1)}, u32[]{:S(2)}, u32[]{:S(2)}) %collective-permute-start.1) | collective-permute-done | bytes 270368 | tf_op jit(solution)/shard_map/ppermute | solution.py:223
  21.9 0.8 %shard_map.48 = (f32[4,128]{1,0:T(4,128)S(1)}, f32[8,128]{1,0:T(8,128)S(1)}, f32[8,128]{1,0:T(8,128)S(1)}) custom-call(bf16[528,256]{1,0:T(8,128)(2,1)S(1)} %collective-permute-done.1.refs_0_, bf16[528,256]{1,0:T(8,128)(2,1)S(1)} %shard_map.46.refs_1_.refs_0_, bf16[528,256]{1,0:T(8,128)(2,1)S(1)} %get-tuple-element.28.refs_2_, ...), custom_call_target="tpu_custom_call" | custom-call | tf_op jit(solution)/shard_map/pallas_call | solution.py:179
  22.7 0.2 collective-permute-start.6
  22.9 1.7 %collective-permute-start.8 = (f32[4,128]{1,0:T(4,128)S(1)}, f32[4,128]{1,0:T(4,128)S(1)}, u32[]{:S(2)}, u32[]{:S(2)}) collective-permute-start(f32[4,128]{1,0:T(4,128)S(1)} %get-tuple-element.33), channel_id=1, source_target_pairs={{5,12},{4,13},{7,14},{6,15},{9,4},{8,5},{11,6},{10,7},{1,8},{0,9},... | collective-permute-start | bytes 6152 | tf_op jit(solution)/shard_map/ppermute | solution.py:239
  24.6 0.0 collective-permute-done.6
  24.6 1.6 %collective-permute-start.7 = (f32[4,128]{1,0:T(4,128)S(1)}, f32[4,128]{1,0:T(4,128)S(1)}, u32[]{:S(2)}, u32[]{:S(2)}) collective-permute-start(f32[4,128]{1,0:T(4,128)S(1)} %slice.19), channel_id=1, source_target_pairs={{0,2},{1,3},{2,0},{3,1},{4,6},{5,7},{6,4},{7,5},{8,10},{9,11},{10,... | collective-permute-start | bytes 6152 | tf_op jit(solution)/shard_map/ppermute | solution.py:212
  26.2 0.8 %shard_map.49 = f32[8,128]{1,0:T(8,128)S(1)} custom-call(bf16[528,256]{1,0:T(8,128)(2,1)S(1)} %shard_map.46.refs_1_.refs_0_, bf16[528,256]{1,0:T(8,128)(2,1)S(1)} %shard_map.46.refs_1_.refs_0_, bf16[528,256]{1,0:T(8,128)(2,1)S(1)} %get-tuple-element.28.refs_2_, bf16[528,256]{1,0:T(8,128)(2,1)S(1)} %collective-permute-done.2.refs_3_, ...), custom_call_target="tpu_custom_call" | custom-call | tf_op jit(solution)/shard_map/pallas_call | solution.py:179
  26.9 0.8 %collective-permute-done.8 = f32[4,128]{1,0:T(4,128)S(1)} collective-permute-done((f32[4,128]{1,0:T(4,128)S(1)}, f32[4,128]{1,0:T(4,128)S(1)}, u32[]{:S(2)}, u32[]{:S(2)}) %collective-permute-start.8) | collective-permute-done | bytes 2080 | tf_op jit(solution)/shard_map/ppermute | solution.py:239
  27.7 0.5 %collective-permute-done.7 = f32[4,128]{1,0:T(4,128)S(1)} collective-permute-done((f32[4,128]{1,0:T(4,128)S(1)}, f32[4,128]{1,0:T(4,128)S(1)}, u32[]{:S(2)}, u32[]{:S(2)}) %collective-permute-start.7) | collective-permute-done | bytes 2080 | tf_op jit(solution)/shard_map/ppermute | solution.py:212
  28.2 0.6 %maximum_bitcast_fusion = f32[512]{0:T(512)} fusion(f32[4,128]{1,0:T(4,128)S(1)} %collective-permute-done.8, f32[4,128]{1,0:T(4,128)S(1)} %collective-permute-done.7, f32[8,128]{1,0:T(8,128)S(1)} %shard_map.49, f32[8,128]{1,0:T(8,128)S(1)} %max.18), kind=kLoop, calls=%fused_computation | loop fusion | flops 2048 | bytes 10240 | tf_op jit(solution)/shard_map/reshape | solution.py:247
  (6 shorter events, 0.1 us)
Async XLA Ops:
  3.4 16.0 %collective-permute-start.2 = (bf16[528,256]{1,0:T(8,128)(2,1)S(1)}, bf16[528,256]{1,0:T(8,128)(2,1)S(1)}, u32[]{:S(2)}, u32[]{:S(2)}) collective-permute-start(bf16[528,256]{1,0:T(8,128)(2,1)S(1)} %shard_map.46.refs_1_.refs_0_), channel_id=1, source_target_pairs={{0,1},{1,0},{2,3},{3,2},{4,5},{5,4},{6,7},{7,6},{8,9},{9,8},{10,11... | collective-permute-start | bytes 811016 | tf_op jit(solution)/shard_map/ppermute | solution.py:212
  3.9 15.5 %collective-permute-start.5 = (bf16[528,256]{1,0:T(8,128)(2,1)S(1)}, bf16[528,256]{1,0:T(8,128)(2,1)S(1)}, u32[]{:S(2)}, u32[]{:S(2)}) collective-permute-start(bf16[528,256]{1,0:T(8,128)(2,1)S(1)} %shard_map.46.refs_1_.refs_0_), channel_id=1, source_target_pairs={{12,9},{13,8},{14,11},{15,10},{4,1},{5,0},{6,3},{7,2},{8,13},{9,12... | collective-permute-start | bytes 811016 | tf_op jit(solution)/shard_map/ppermute | solution.py:224
  6.6 15.3 %collective-permute-start.1 = (bf16[528,256]{1,0:T(8,128)(2,1)S(1)}, bf16[528,256]{1,0:T(8,128)(2,1)S(1)}, u32[]{:S(2)}, u32[]{:S(2)}) collective-permute-start(bf16[528,256]{1,0:T(8,128)(2,1)S(1)} %shard_map.46.refs_1_.refs_0_), channel_id=1, source_target_pairs={{12,5},{13,4},{14,7},{15,6},{4,9},{5,8},{6,11},{7,10},{8,1},{9,0},... | collective-permute-start | bytes 811016 | tf_op jit(solution)/shard_map/ppermute | solution.py:223
  8.8 8.9 %collective-permute-start = (bf16[528,256]{1,0:T(8,128)(2,1)S(1)}, bf16[528,256]{1,0:T(8,128)(2,1)S(1)}, u32[]{:S(2)}, u32[]{:S(2)}) collective-permute-start(bf16[528,256]{1,0:T(8,128)(2,1)S(1)} %get-tuple-element.65), channel_id=1, source_target_pairs={{0,2},{1,3},{2,0},{3,1},{4,6},{5,7},{6,4},{7,5},{8,10},{9,11},{10,... | collective-permute-start | bytes 811016 | tf_op jit(solution)/shard_map/while/body/ppermute | solution.py:212
  17.7 1.6 %collective-permute-start.4 = (bf16[272,256]{1,0:T(8,128)(2,1)S(1)}, bf16[272,256]{1,0:T(8,128)(2,1)S(1)}, u32[]{:S(2)}, u32[]{:S(2)}) collective-permute-start(bf16[272,256]{1,0:T(8,128)(2,1)S(1)} %slice.16), channel_id=1, source_target_pairs={{0,1},{1,0},{2,3},{3,2},{4,5},{5,4},{6,7},{7,6},{8,9},{9,8},{10,11... | collective-permute-start | bytes 417800 | tf_op jit(solution)/shard_map/ppermute | solution.py:212
  17.8 1.5 %collective-permute-start.3 = (bf16[256,256]{1,0:T(8,128)(2,1)S(1)}, bf16[256,256]{1,0:T(8,128)(2,1)S(1)}, u32[]{:S(2)}, u32[]{:S(2)}) collective-permute-start(bf16[256,256]{1,0:T(8,128)(2,1)S(1)} %slice.15), channel_id=1, source_target_pairs={{0,1},{1,0},{2,3},{3,2},{4,5},{5,4},{6,7},{7,6},{8,9},{9,8},{10,11... | collective-permute-start | bytes 393224 | tf_op jit(solution)/shard_map/ppermute | solution.py:212
  22.7 1.9 %collective-permute-start.6 = (f32[8,128]{1,0:T(8,128)S(1)}, f32[8,128]{1,0:T(8,128)S(1)}, u32[]{:S(2)}, u32[]{:S(2)}) collective-permute-start(f32[8,128]{1,0:T(8,128)S(1)} %get-tuple-element.32), channel_id=1, source_target_pairs={{0,1},{1,0},{2,3},{3,2},{4,5},{5,4},{6,7},{7,6},{8,9},{9,8},{10,11... | collective-permute-start | bytes 12296 | tf_op jit(solution)/shard_map/ppermute | solution.py:212
  22.9 4.8 %collective-permute-start.8 = (f32[4,128]{1,0:T(4,128)S(1)}, f32[4,128]{1,0:T(4,128)S(1)}, u32[]{:S(2)}, u32[]{:S(2)}) collective-permute-start(f32[4,128]{1,0:T(4,128)S(1)} %get-tuple-element.33), channel_id=1, source_target_pairs={{5,12},{4,13},{7,14},{6,15},{9,4},{8,5},{11,6},{10,7},{1,8},{0,9},... | collective-permute-start | bytes 6152 | tf_op jit(solution)/shard_map/ppermute | solution.py:239
  24.6 3.6 %collective-permute-start.7 = (f32[4,128]{1,0:T(4,128)S(1)}, f32[4,128]{1,0:T(4,128)S(1)}, u32[]{:S(2)}, u32[]{:S(2)}) collective-permute-start(f32[4,128]{1,0:T(4,128)S(1)} %slice.19), channel_id=1, source_target_pairs={{0,2},{1,3},{2,0},{3,1},{4,6},{5,7},{6,4},{7,5},{8,10},{9,11},{10,... | collective-permute-start | bytes 6152 | tf_op jit(solution)/shard_map/ppermute | solution.py:212

commit v27 on v25

--- a/solution.py
+++ b/solution.py
@@ -230,8 +230,8 @@
         lambda _, blocks: [swap(block, offset) for block, offset in zip(blocks, offsets)],
         [own] * len(offsets),
     )
-    rows = [own, *besides, swap(own, 1)]
-    rows += [tuple(swap(part, 1) for part in halves(beside)) for beside in besides]
+    across = [tuple(swap(part, 1) for part in halves(beside)) for beside in besides]
+    rows = [own, *across, swap(own, 1), *besides]
     row_best, backs = [], []
     for key, step in zip(keys, steps):
         (found,), row_best = score([key], rows, cols=1, known=row_best)
@@ -241,7 +241,7 @@
     local = jnp.maximum(row_best[0], swap(row_best[1], 1))
     best = jnp.maximum(local[:tiles], own_best[:tiles])
     for at, offset in enumerate(offsets, start=1):
-        best = jnp.maximum(best, swap(local[at * tiles : (at + 1) * tiles], offset))
+        best = jnp.maximum(best, swap(local[at * tiles : (at + 1) * tiles], offset + 1))
     for back in backs:
         best = jnp.maximum(best, back)
     return jnp.maximum(best, -1.0).reshape(row_count)

time: 28.4 us -> 28.4 us (level)
  no operation moved by 1% of the time
where the time goes in v27:
time: 28.4 us; the launch traced here: 28.3 us
  waiting for transfers between devices  12.2 us (43%)
  starting transfers between devices  9.47 us (33%)
  Pallas kernels  5.81 us (20%)
  other arithmetic  0.59 us (2%)
    ppermute x6, waiting for transfers between devices, swap(): lax.ppermute(block, 'split', [(s, s ^ offset) for s in range(split_count)])  8.4 us
    ppermute x1, starting transfers between devices, per_device(): keys = [lax.ppermute(own, both, step) for step in steps]  4.71 us
    ppermute x6, starting transfers between devices, swap(): lax.ppermute(block, 'split', [(s, s ^ offset) for s in range(split_count)])  4.16 us
    pallas_call x1, Pallas kernels, project(): pl.pallas_call(project_kernel, in_specs=[pl.BlockSpec(memory_space=pltpu....  3.38 us
    pallas_call x3, Pallas kernels, score(): pl.pallas_call(functools.partial(score_kernel, len(keys), cols, [len(row)...  2.43 us
    ppermute x1, waiting for transfers between devices, per_device(): backs.append(lax.ppermute(found, both, [(b, a) for a, b in step]))  1.75 us
    ppermute x1, waiting for transfers between devices, per_device(): keys = [lax.ppermute(own, both, step) for step in steps]  1.41 us
    ppermute x1, waiting for transfers between devices, per_device(): nearby = lax.ppermute(own, both, last)  0.68 us
  transfers between devices with their start and end apart: 9, of which 6 were waited for; matrix products, arithmetic and copies ran while one was open for 0% of the time, Pallas kernels for 6%

profile of v27, /device:TPU:0, one launch (start us, length us, event | category | flops | bytes accessed | tf_op | source)
XLA Modules:
  0.0 28.3 jit_solution(17984535432013447929)
XLA Ops:
  0.0 3.4 %shard_map.46.refs_1_.refs_0_ = bf16[528,256]{1,0:T(8,128)(2,1)S(1)} custom-call(bf16[512,4096]{1,0:T(8,128)(2,1)} %source_hbm.1, bf16[4096,256]{1,0:T(8,128)(2,1)} %basis_hbm.1, s32[4,128]{1,0:T(4,128)} %bitcast.4, s32[4,128]{1,0:T(4,128)} %bitcast.5), custom_call_target="tpu_custom_call" | custom-call | flops 1073741824 | bytes 6291456 | tf_op jit(solution)/shard_map/pallas_call | solution.py:65
  3.4 0.5 %collective-permute-start.4 = (bf16[528,256]{1,0:T(8,128)(2,1)S(1)}, bf16[528,256]{1,0:T(8,128)(2,1)S(1)}, u32[]{:S(2)}, u32[]{:S(2)}) collective-permute-start(bf16[528,256]{1,0:T(8,128)(2,1)S(1)} %shard_map.46.refs_1_.refs_0_), channel_id=1, source_target_pairs={{0,1},{1,0},{2,3},{3,2},{4,5},{5,4},{6,7},{7,6},{8,9},{9,8},{10,11... | collective-permute-start | bytes 811016 | tf_op jit(solution)/shard_map/ppermute | solution.py:212
  3.9 4.7 %collective-permute-start.5 = (bf16[528,256]{1,0:T(8,128)(2,1)S(1)}, bf16[528,256]{1,0:T(8,128)(2,1)S(1)}, u32[]{:S(2)}, u32[]{:S(2)}) collective-permute-start(bf16[528,256]{1,0:T(8,128)(2,1)S(1)} %shard_map.46.refs_1_.refs_0_), channel_id=1, source_target_pairs={{12,5},{13,4},{14,7},{15,6},{4,9},{5,8},{6,11},{7,10},{8,1},{9,0},... | collective-permute-start | bytes 811016 | tf_op jit(solution)/shard_map/ppermute | solution.py:223
  8.6 0.0 collective-permute-start.1
  8.6 8.6 %while.10 = (s32[]{:T(128)}, bf16[528,256]{1,0:T(8,128)(2,1)S(1)}, s32[]{:T(128)}, s32[]{:T(128)}) while((s32[]{:T(128)}, bf16[528,256]{1,0:T(8,128)(2,1)S(1)}, s32[]{:T(128)}, s32[]{:T(128)}) %tuple.18), condition=%wide.region_1.0_spmd, body=%wide.region_0.0_spmd.sunk | while | flops 2 | bytes 1622109 | solution.py:227
  8.7 1.6 %collective-permute-start = (bf16[528,256]{1,0:T(8,128)(2,1)S(1)}, bf16[528,256]{1,0:T(8,128)(2,1)S(1)}, u32[]{:S(2)}, u32[]{:S(2)}) collective-permute-start(bf16[528,256]{1,0:T(8,128)(2,1)S(1)} %get-tuple-element.65), channel_id=1, source_target_pairs={{0,2},{1,3},{2,0},{3,1},{4,6},{5,7},{6,4},{7,5},{8,10},{9,11},{10,... | collective-permute-start | bytes 811016 | tf_op jit(solution)/shard_map/while/body/ppermute | solution.py:212
  10.2 7.0 %collective-permute-done = bf16[528,256]{1,0:T(8,128)(2,1)S(1)} collective-permute-done((bf16[528,256]{1,0:T(8,128)(2,1)S(1)}, bf16[528,256]{1,0:T(8,128)(2,1)S(1)}, u32[]{:S(2)}, u32[]{:S(2)}) %collective-permute-start) | collective-permute-done | bytes 270368 | tf_op jit(solution)/shard_map/while/body/ppermute | solution.py:212
  17.2 0.1 collective-permute-start.3
  17.3 0.6 %collective-permute-start.2 = (bf16[256,256]{1,0:T(8,128)(2,1)S(1)}, bf16[256,256]{1,0:T(8,128)(2,1)S(1)}, u32[]{:S(2)}, u32[]{:S(2)}) collective-permute-start(bf16[256,256]{1,0:T(8,128)(2,1)S(1)} %slice.15), channel_id=1, source_target_pairs={{0,1},{1,0},{2,3},{3,2},{4,5},{5,4},{6,7},{7,6},{8,9},{9,8},{10,11... | collective-permute-start | bytes 393224 | tf_op jit(solution)/shard_map/ppermute | solution.py:212
  17.9 1.0 %collective-permute-done.2.refs_2_ = bf16[256,256]{1,0:T(8,128)(2,1)S(1)} collective-permute-done((bf16[256,256]{1,0:T(8,128)(2,1)S(1)}, bf16[256,256]{1,0:T(8,128)(2,1)S(1)}, u32[]{:S(2)}, u32[]{:S(2)}) %collective-permute-start.2) | collective-permute-done | bytes 131104 | tf_op jit(solution)/shard_map/ppermute | solution.py:212
  18.9 0.0 collective-permute-done.3.refs_3_
  18.9 0.0 collective-permute-done.4.refs_4_
  18.9 1.4 %collective-permute-done.5.refs_0_ = bf16[528,256]{1,0:T(8,128)(2,1)S(1)} collective-permute-done((bf16[528,256]{1,0:T(8,128)(2,1)S(1)}, bf16[528,256]{1,0:T(8,128)(2,1)S(1)}, u32[]{:S(2)}, u32[]{:S(2)}) %collective-permute-start.5) | collective-permute-done | bytes 270368 | tf_op jit(solution)/shard_map/ppermute | solution.py:223
  20.3 0.9 %shard_map.47 = (f32[4,128]{1,0:T(4,128)S(1)}, f32[8,128]{1,0:T(8,128)S(1)}, f32[8,128]{1,0:T(8,128)S(1)}) custom-call(bf16[528,256]{1,0:T(8,128)(2,1)S(1)} %collective-permute-done.5.refs_0_, bf16[528,256]{1,0:T(8,128)(2,1)S(1)} %shard_map.46.refs_1_.refs_0_, bf16[256,256]{1,0:T(8,128)(2,1)S(1)} %collective-permute-done.2.refs_2_, ...), custom_call_target="tpu_custom_call" | custom-call | tf_op jit(solution)/shard_map/pallas_call | solution.py:179
  21.1 0.7 %collective-permute-done.1.refs_0_ = bf16[528,256]{1,0:T(8,128)(2,1)S(1)} collective-permute-done((bf16[528,256]{1,0:T(8,128)(2,1)S(1)}, bf16[528,256]{1,0:T(8,128)(2,1)S(1)}, u32[]{:S(2)}, u32[]{:S(2)}) %collective-permute-start.1) | collective-permute-done | bytes 270368 | tf_op jit(solution)/shard_map/ppermute | solution.py:224
  21.8 0.8 %shard_map.48 = (f32[8,128]{1,0:T(8,128)S(1)}, f32[8,128]{1,0:T(8,128)S(1)}) custom-call(bf16[528,256]{1,0:T(8,128)(2,1)S(1)} %collective-permute-done.1.refs_0_, bf16[528,256]{1,0:T(8,128)(2,1)S(1)} %shard_map.46.refs_1_.refs_0_, bf16[256,256]{1,0:T(8,128)(2,1)S(1)} %collective-permute-done.2.refs_2_, bf16[272,256]{1,0:T(8,128)(2,1)S(1)} %collective-permute-done.3.refs_3_, ...), custom_call_target="tpu_custom_call" | custom-call | tf_op jit(solution)/shard_map/pallas_call | solution.py:179
  22.7 0.2 collective-permute-start.6
  22.8 0.6 %collective-permute-start.8 = (f32[4,128]{1,0:T(4,128)S(1)}, f32[4,128]{1,0:T(4,128)S(1)}, u32[]{:S(2)}, u32[]{:S(2)}) collective-permute-start(f32[4,128]{1,0:T(4,128)S(1)} %get-tuple-element.33), channel_id=1, source_target_pairs={{5,12},{4,13},{7,14},{6,15},{9,4},{8,5},{11,6},{10,7},{1,8},{0,9},... | collective-permute-start | bytes 6152 | tf_op jit(solution)/shard_map/ppermute | solution.py:238
  23.4 0.4 %collective-permute-done.6 = f32[8,128]{1,0:T(8,128)S(1)} collective-permute-done((f32[8,128]{1,0:T(8,128)S(1)}, f32[8,128]{1,0:T(8,128)S(1)}, u32[]{:S(2)}, u32[]{:S(2)}) %collective-permute-start.6) | collective-permute-done | bytes 4128 | tf_op jit(solution)/shard_map/ppermute | solution.py:212
  23.9 1.3 %collective-permute-start.7 = (f32[4,128]{1,0:T(4,128)S(1)}, f32[4,128]{1,0:T(4,128)S(1)}, u32[]{:S(2)}, u32[]{:S(2)}) collective-permute-start(f32[4,128]{1,0:T(4,128)S(1)} %slice.19), channel_id=1, source_target_pairs={{0,3},{1,2},{2,1},{3,0},{4,7},{5,6},{6,5},{7,4},{8,11},{9,10},{10,... | collective-permute-start | bytes 6152 | tf_op jit(solution)/shard_map/ppermute | solution.py:212
  25.2 0.8 %shard_map.49 = f32[8,128]{1,0:T(8,128)S(1)} custom-call(bf16[528,256]{1,0:T(8,128)(2,1)S(1)} %shard_map.46.refs_1_.refs_0_, bf16[528,256]{1,0:T(8,128)(2,1)S(1)} %shard_map.46.refs_1_.refs_0_, bf16[256,256]{1,0:T(8,128)(2,1)S(1)} %collective-permute-done.2.refs_2_, bf16[272,256]{1,0:T(8,128)(2,1)S(1)} %collective-permute-done.3.refs_3_, ...), custom_call_target="tpu_custom_call" | custom-call | tf_op jit(solution)/shard_map/pallas_call | solution.py:179
  25.9 1.7 %collective-permute-done.8 = f32[4,128]{1,0:T(4,128)S(1)} collective-permute-done((f32[4,128]{1,0:T(4,128)S(1)}, f32[4,128]{1,0:T(4,128)S(1)}, u32[]{:S(2)}, u32[]{:S(2)}) %collective-permute-start.8) | collective-permute-done | bytes 2080 | tf_op jit(solution)/shard_map/ppermute | solution.py:238
  27.7 0.0 collective-permute-done.7
  27.7 0.6 %maximum_bitcast_fusion = f32[512]{0:T(512)} fusion(f32[4,128]{1,0:T(4,128)S(1)} %collective-permute-done.8, f32[4,128]{1,0:T(4,128)S(1)} %collective-permute-done.7, f32[8,128]{1,0:T(8,128)S(1)} %shard_map.49, f32[8,128]{1,0:T(8,128)S(1)} %max.18), kind=kLoop, calls=%fused_computation | loop fusion | flops 2048 | bytes 10240 | tf_op jit(solution)/shard_map/reshape | solution.py:247
  (6 shorter events, 0.1 us)
Async XLA Ops:
  3.4 15.5 %collective-permute-start.4 = (bf16[528,256]{1,0:T(8,128)(2,1)S(1)}, bf16[528,256]{1,0:T(8,128)(2,1)S(1)}, u32[]{:S(2)}, u32[]{:S(2)}) collective-permute-start(bf16[528,256]{1,0:T(8,128)(2,1)S(1)} %shard_map.46.refs_1_.refs_0_), channel_id=1, source_target_pairs={{0,1},{1,0},{2,3},{3,2},{4,5},{5,4},{6,7},{7,6},{8,9},{9,8},{10,11... | collective-permute-start | bytes 811016 | tf_op jit(solution)/shard_map/ppermute | solution.py:212
  3.9 16.4 %collective-permute-start.5 = (bf16[528,256]{1,0:T(8,128)(2,1)S(1)}, bf16[528,256]{1,0:T(8,128)(2,1)S(1)}, u32[]{:S(2)}, u32[]{:S(2)}) collective-permute-start(bf16[528,256]{1,0:T(8,128)(2,1)S(1)} %shard_map.46.refs_1_.refs_0_), channel_id=1, source_target_pairs={{12,5},{13,4},{14,7},{15,6},{4,9},{5,8},{6,11},{7,10},{8,1},{9,0},... | collective-permute-start | bytes 811016 | tf_op jit(solution)/shard_map/ppermute | solution.py:223
  8.6 13.2 %collective-permute-start.1 = (bf16[528,256]{1,0:T(8,128)(2,1)S(1)}, bf16[528,256]{1,0:T(8,128)(2,1)S(1)}, u32[]{:S(2)}, u32[]{:S(2)}) collective-permute-start(bf16[528,256]{1,0:T(8,128)(2,1)S(1)} %shard_map.46.refs_1_.refs_0_), channel_id=1, source_target_pairs={{12,9},{13,8},{14,11},{15,10},{4,1},{5,0},{6,3},{7,2},{8,13},{9,12... | collective-permute-start | bytes 811016 | tf_op jit(solution)/shard_map/ppermute | solution.py:224
  8.7 8.5 %collective-permute-start = (bf16[528,256]{1,0:T(8,128)(2,1)S(1)}, bf16[528,256]{1,0:T(8,128)(2,1)S(1)}, u32[]{:S(2)}, u32[]{:S(2)}) collective-permute-start(bf16[528,256]{1,0:T(8,128)(2,1)S(1)} %get-tuple-element.65), channel_id=1, source_target_pairs={{0,2},{1,3},{2,0},{3,1},{4,6},{5,7},{6,4},{7,5},{8,10},{9,11},{10,... | collective-permute-start | bytes 811016 | tf_op jit(solution)/shard_map/while/body/ppermute | solution.py:212
  17.2 1.6 %collective-permute-start.3 = (bf16[272,256]{1,0:T(8,128)(2,1)S(1)}, bf16[272,256]{1,0:T(8,128)(2,1)S(1)}, u32[]{:S(2)}, u32[]{:S(2)}) collective-permute-start(bf16[272,256]{1,0:T(8,128)(2,1)S(1)} %slice.16), channel_id=1, source_target_pairs={{0,1},{1,0},{2,3},{3,2},{4,5},{5,4},{6,7},{7,6},{8,9},{9,8},{10,11... | collective-permute-start | bytes 417800 | tf_op jit(solution)/shard_map/ppermute | solution.py:212
  17.3 1.5 %collective-permute-start.2 = (bf16[256,256]{1,0:T(8,128)(2,1)S(1)}, bf16[256,256]{1,0:T(8,128)(2,1)S(1)}, u32[]{:S(2)}, u32[]{:S(2)}) collective-permute-start(bf16[256,256]{1,0:T(8,128)(2,1)S(1)} %slice.15), channel_id=1, source_target_pairs={{0,1},{1,0},{2,3},{3,2},{4,5},{5,4},{6,7},{7,6},{8,9},{9,8},{10,11... | collective-permute-start | bytes 393224 | tf_op jit(solution)/shard_map/ppermute | solution.py:212
  22.7 1.2 %collective-permute-start.6 = (f32[8,128]{1,0:T(8,128)S(1)}, f32[8,128]{1,0:T(8,128)S(1)}, u32[]{:S(2)}, u32[]{:S(2)}) collective-permute-start(f32[8,128]{1,0:T(8,128)S(1)} %get-tuple-element.32), channel_id=1, source_target_pairs={{0,1},{1,0},{2,3},{3,2},{4,5},{5,4},{6,7},{7,6},{8,9},{9,8},{10,11... | collective-permute-start | bytes 12296 | tf_op jit(solution)/shard_map/ppermute | solution.py:212
  22.8 4.8 %collective-permute-start.8 = (f32[4,128]{1,0:T(4,128)S(1)}, f32[4,128]{1,0:T(4,128)S(1)}, u32[]{:S(2)}, u32[]{:S(2)}) collective-permute-start(f32[4,128]{1,0:T(4,128)S(1)} %get-tuple-element.33), channel_id=1, source_target_pairs={{5,12},{4,13},{7,14},{6,15},{9,4},{8,5},{11,6},{10,7},{1,8},{0,9},... | collective-permute-start | bytes 6152 | tf_op jit(solution)/shard_map/ppermute | solution.py:238
  23.9 3.8 %collective-permute-start.7 = (f32[4,128]{1,0:T(4,128)S(1)}, f32[4,128]{1,0:T(4,128)S(1)}, u32[]{:S(2)}, u32[]{:S(2)}) collective-permute-start(f32[4,128]{1,0:T(4,128)S(1)} %slice.19), channel_id=1, source_target_pairs={{0,3},{1,2},{2,1},{3,0},{4,7},{5,6},{6,5},{7,4},{8,11},{9,10},{10,... | collective-permute-start | bytes 6152 | tf_op jit(solution)/shard_map/ppermute | solution.py:212

commit v28 on v27

--- a/solution.py
+++ b/solution.py
@@ -230,8 +230,8 @@
         lambda _, blocks: [swap(block, offset) for block, offset in zip(blocks, offsets)],
         [own] * len(offsets),
     )
-    across = [tuple(swap(part, 1) for part in halves(beside)) for beside in besides]
-    rows = [own, *across, swap(own, 1), *besides]
+    core, *across = [tuple(swap(part, 1) for part in halves(block)) for block in [own, *besides]]
+    rows = [own, *across, core, *besides]
     row_best, backs = [], []
     for key, step in zip(keys, steps):
         (found,), row_best = score([key], rows, cols=1, known=row_best)

time: 28.4 us -> 27.8 us (0.979)
  waiting for transfers between devices: 12.2 us -> 9.72 us
  starting transfers between devices: 9.47 us -> 11.3 us
    ppermute x1, starting transfers between devices: 0.6 us -> 2.32 us  [per_device(): backs.append(lax.ppermute(found, both, [(b, a) for a, b in step]))]
    ppermute x1, waiting for transfers between devices: 1.41 us -> 0.01 us  [per_device(): keys = [lax.ppermute(own, both, step) for step in steps]]
    ppermute x1, waiting for transfers between devices: 1.75 us -> 0.43 us  [per_device(): backs.append(lax.ppermute(found, both, [(b, a) for a, b in step]))]
    ppermute x6 -> x7, waiting for transfers between devices: 8.4 us -> 8.98 us  [swap(): lax.ppermute(block, 'split', [(s, s ^ offset) for s in range(split_count)])]
    ppermute x1, waiting for transfers between devices: 0.68 us -> 0.3 us  [per_device(): nearby = lax.ppermute(own, both, last)]
    ppermute x6 -> x7, starting transfers between devices: 4.16 us -> 4.43 us  [swap(): lax.ppermute(block, 'split', [(s, s ^ offset) for s in range(split_count)])]
  transfers between devices with their start and end apart: 9 -> 10, of which waited for: 6 -> 5; matrix products, arithmetic and copies ran while one was open for 0% -> 0% of each run, Pallas kernels for 6% -> 6%
where the time goes in v28:
time: 27.8 us; the launch traced here: 27.6 us
  starting transfers between devices  11.3 us (41%)
  waiting for transfers between devices  9.72 us (35%)
  Pallas kernels  5.82 us (21%)
  other arithmetic  0.59 us (2%)
    ppermute x7, waiting for transfers between devices, swap(): lax.ppermute(block, 'split', [(s, s ^ offset) for s in range(split_count)])  8.98 us
    ppermute x1, starting transfers between devices, per_device(): keys = [lax.ppermute(own, both, step) for step in steps]  4.54 us
    ppermute x7, starting transfers between devices, swap(): lax.ppermute(block, 'split', [(s, s ^ offset) for s in range(split_count)])  4.43 us
    pallas_call x1, Pallas kernels, project(): pl.pallas_call(project_kernel, in_specs=[pl.BlockSpec(memory_space=pltpu....  3.38 us
    pallas_call x3, Pallas kernels, score(): pl.pallas_call(functools.partial(score_kernel, len(keys), cols, [len(row)...  2.44 us
    ppermute x1, starting transfers between devices, per_device(): backs.append(lax.ppermute(found, both, [(b, a) for a, b in step]))  2.32 us
    reshape x1, other arithmetic, per_device(): return jnp.maximum(best, -1.0).reshape(row_count)  0.58 us
  transfers between devices with their start and end apart: 10, of which 5 were waited for; matrix products, arithmetic and copies ran while one was open for 0% of the time, Pallas kernels for 6%

profile of v28, /device:TPU:0, one launch (start us, length us, event | category | flops | bytes accessed | tf_op | source)
XLA Modules:
  0.0 27.6 jit_solution(4509913661031570112)
XLA Ops:
  0.0 3.4 %shard_map.46.refs_1_.refs_0_ = bf16[528,256]{1,0:T(8,128)(2,1)S(1)} custom-call(bf16[512,4096]{1,0:T(8,128)(2,1)} %source_hbm.1, bf16[4096,256]{1,0:T(8,128)(2,1)} %basis_hbm.1, s32[4,128]{1,0:T(4,128)} %bitcast.4, s32[4,128]{1,0:T(4,128)} %bitcast.5), custom_call_target="tpu_custom_call" | custom-call | flops 1073741824 | bytes 6291456 | tf_op jit(solution)/shard_map/pallas_call | solution.py:65
  3.4 4.5 %collective-permute-start.6 = (bf16[528,256]{1,0:T(8,128)(2,1)S(1)}, bf16[528,256]{1,0:T(8,128)(2,1)S(1)}, u32[]{:S(2)}, u32[]{:S(2)}) collective-permute-start(bf16[528,256]{1,0:T(8,128)(2,1)S(1)} %shard_map.46.refs_1_.refs_0_), channel_id=1, source_target_pairs={{12,5},{13,4},{14,7},{15,6},{4,9},{5,8},{6,11},{7,10},{8,1},{9,0},... | collective-permute-start | bytes 811016 | tf_op jit(solution)/shard_map/ppermute | solution.py:223
  7.9 0.0 collective-permute-start.1
  7.9 0.7 %collective-permute-start.4 = (bf16[256,256]{1,0:T(8,128)(2,1)S(1)}, bf16[256,256]{1,0:T(8,128)(2,1)S(1)}, u32[]{:S(2)}, u32[]{:S(2)}) collective-permute-start(bf16[256,256]{1,0:T(8,128)(2,1)S(1)} %slice.28), channel_id=1, source_target_pairs={{0,1},{1,0},{2,3},{3,2},{4,5},{5,4},{6,7},{7,6},{8,9},{9,8},{10,11... | collective-permute-start | bytes 393224 | tf_op jit(solution)/shard_map/ppermute | solution.py:212
  8.7 0.1 collective-permute-start.5
  8.8 9.0 %while.10 = (s32[]{:T(128)}, bf16[528,256]{1,0:T(8,128)(2,1)S(1)}, s32[]{:T(128)}, s32[]{:T(128)}) while((s32[]{:T(128)}, bf16[528,256]{1,0:T(8,128)(2,1)S(1)}, s32[]{:T(128)}, s32[]{:T(128)}) %tuple.18), condition=%wide.region_1.0_spmd, body=%wide.region_0.0_spmd.sunk | while | flops 2 | bytes 1622109 | solution.py:227
  8.8 1.6 %collective-permute-start = (bf16[528,256]{1,0:T(8,128)(2,1)S(1)}, bf16[528,256]{1,0:T(8,128)(2,1)S(1)}, u32[]{:S(2)}, u32[]{:S(2)}) collective-permute-start(bf16[528,256]{1,0:T(8,128)(2,1)S(1)} %get-tuple-element.65), channel_id=1, source_target_pairs={{0,2},{1,3},{2,0},{3,1},{4,6},{5,7},{6,4},{7,5},{8,10},{9,11},{10,... | collective-permute-start | bytes 811016 | tf_op jit(solution)/shard_map/while/body/ppermute | solution.py:212
  10.4 7.4 %collective-permute-done = bf16[528,256]{1,0:T(8,128)(2,1)S(1)} collective-permute-done((bf16[528,256]{1,0:T(8,128)(2,1)S(1)}, bf16[528,256]{1,0:T(8,128)(2,1)S(1)}, u32[]{:S(2)}, u32[]{:S(2)}) %collective-permute-start) | collective-permute-done | bytes 270368 | tf_op jit(solution)/shard_map/while/body/ppermute | solution.py:212
  17.8 0.1 collective-permute-start.3
  17.9 0.0 collective-permute-done.4.refs_4_
  17.9 0.6 %collective-permute-start.2 = (bf16[256,256]{1,0:T(8,128)(2,1)S(1)}, bf16[256,256]{1,0:T(8,128)(2,1)S(1)}, u32[]{:S(2)}, u32[]{:S(2)}) collective-permute-start(bf16[256,256]{1,0:T(8,128)(2,1)S(1)} %slice.21), channel_id=1, source_target_pairs={{0,1},{1,0},{2,3},{3,2},{4,5},{5,4},{6,7},{7,6},{8,9},{9,8},{10,11... | collective-permute-start | bytes 393224 | tf_op jit(solution)/shard_map/ppermute | solution.py:212
  18.5 1.0 %collective-permute-done.2.refs_2_ = bf16[256,256]{1,0:T(8,128)(2,1)S(1)} collective-permute-done((bf16[256,256]{1,0:T(8,128)(2,1)S(1)}, bf16[256,256]{1,0:T(8,128)(2,1)S(1)}, u32[]{:S(2)}, u32[]{:S(2)}) %collective-permute-start.2) | collective-permute-done | bytes 131104 | tf_op jit(solution)/shard_map/ppermute | solution.py:212
  19.5 0.0 collective-permute-done.5.refs_5_
  19.5 0.0 collective-permute-done.3.refs_3_
  19.5 0.9 %shard_map.47 = (f32[4,128]{1,0:T(4,128)S(1)}, f32[8,128]{1,0:T(8,128)S(1)}, f32[8,128]{1,0:T(8,128)S(1)}) custom-call(bf16[528,256]{1,0:T(8,128)(2,1)S(1)} %collective-permute-done.6.refs_0_, bf16[528,256]{1,0:T(8,128)(2,1)S(1)} %shard_map.46.refs_1_.refs_0_, bf16[256,256]{1,0:T(8,128)(2,1)S(1)} %collective-permute-done.2.refs_2_, ...), custom_call_target="tpu_custom_call" | custom-call | tf_op jit(solution)/shard_map/pallas_call | solution.py:179
  20.3 0.3 %collective-permute-done.1.refs_0_ = bf16[528,256]{1,0:T(8,128)(2,1)S(1)} collective-permute-done((bf16[528,256]{1,0:T(8,128)(2,1)S(1)}, bf16[528,256]{1,0:T(8,128)(2,1)S(1)}, u32[]{:S(2)}, u32[]{:S(2)}) %collective-permute-start.1) | collective-permute-done | bytes 270368 | tf_op jit(solution)/shard_map/ppermute | solution.py:224
  20.6 0.8 %shard_map.48 = (f32[8,128]{1,0:T(8,128)S(1)}, f32[8,128]{1,0:T(8,128)S(1)}) custom-call(bf16[528,256]{1,0:T(8,128)(2,1)S(1)} %collective-permute-done.1.refs_0_, bf16[528,256]{1,0:T(8,128)(2,1)S(1)} %shard_map.46.refs_1_.refs_0_, bf16[256,256]{1,0:T(8,128)(2,1)S(1)} %collective-permute-done.2.refs_2_, bf16[272,256]{1,0:T(8,128)(2,1)S(1)} %collective-permute-done.3.refs_3_, ...), custom_call_target="tpu_custom_call" | custom-call | tf_op jit(solution)/shard_map/pallas_call | solution.py:179
  21.5 0.1 collective-permute-start.7
  21.6 2.3 %collective-permute-start.9 = (f32[4,128]{1,0:T(4,128)S(1)}, f32[4,128]{1,0:T(4,128)S(1)}, u32[]{:S(2)}, u32[]{:S(2)}) collective-permute-start(f32[4,128]{1,0:T(4,128)S(1)} %get-tuple-element.33), channel_id=1, source_target_pairs={{5,12},{4,13},{7,14},{6,15},{9,4},{8,5},{11,6},{10,7},{1,8},{0,9},... | collective-permute-start | bytes 6152 | tf_op jit(solution)/shard_map/ppermute | solution.py:238
  24.0 1.3 %collective-permute-start.8 = (f32[4,128]{1,0:T(4,128)S(1)}, f32[4,128]{1,0:T(4,128)S(1)}, u32[]{:S(2)}, u32[]{:S(2)}) collective-permute-start(f32[4,128]{1,0:T(4,128)S(1)} %slice.27), channel_id=1, source_target_pairs={{0,3},{1,2},{2,1},{3,0},{4,7},{5,6},{6,5},{7,4},{8,11},{9,10},{10,... | collective-permute-start | bytes 6152 | tf_op jit(solution)/shard_map/ppermute | solution.py:212
  25.2 0.8 %shard_map.49 = f32[8,128]{1,0:T(8,128)S(1)} custom-call(bf16[528,256]{1,0:T(8,128)(2,1)S(1)} %shard_map.46.refs_1_.refs_0_, bf16[528,256]{1,0:T(8,128)(2,1)S(1)} %shard_map.46.refs_1_.refs_0_, bf16[256,256]{1,0:T(8,128)(2,1)S(1)} %collective-permute-done.2.refs_2_, bf16[272,256]{1,0:T(8,128)(2,1)S(1)} %collective-permute-done.3.refs_3_, ...), custom_call_target="tpu_custom_call" | custom-call | tf_op jit(solution)/shard_map/pallas_call | solution.py:179
  26.0 0.4 %collective-permute-done.9 = f32[4,128]{1,0:T(4,128)S(1)} collective-permute-done((f32[4,128]{1,0:T(4,128)S(1)}, f32[4,128]{1,0:T(4,128)S(1)}, u32[]{:S(2)}, u32[]{:S(2)}) %collective-permute-start.9) | collective-permute-done | bytes 2080 | tf_op jit(solution)/shard_map/ppermute | solution.py:238
  26.4 0.6 %collective-permute-done.8 = f32[4,128]{1,0:T(4,128)S(1)} collective-permute-done((f32[4,128]{1,0:T(4,128)S(1)}, f32[4,128]{1,0:T(4,128)S(1)}, u32[]{:S(2)}, u32[]{:S(2)}) %collective-permute-start.8) | collective-permute-done | bytes 2080 | tf_op jit(solution)/shard_map/ppermute | solution.py:212
  27.0 0.6 %maximum_bitcast_fusion = f32[512]{0:T(512)} fusion(f32[4,128]{1,0:T(4,128)S(1)} %collective-permute-done.9, f32[4,128]{1,0:T(4,128)S(1)} %collective-permute-done.8, f32[8,128]{1,0:T(8,128)S(1)} %shard_map.49, f32[8,128]{1,0:T(8,128)S(1)} %max.18), kind=kLoop, calls=%fused_computation | loop fusion | flops 2048 | bytes 10240 | tf_op jit(solution)/shard_map/reshape | solution.py:247
  (10 shorter events, 0.1 us)
Async XLA Ops:
  3.4 16.1 %collective-permute-start.6 = (bf16[528,256]{1,0:T(8,128)(2,1)S(1)}, bf16[528,256]{1,0:T(8,128)(2,1)S(1)}, u32[]{:S(2)}, u32[]{:S(2)}) collective-permute-start(bf16[528,256]{1,0:T(8,128)(2,1)S(1)} %shard_map.46.refs_1_.refs_0_), channel_id=1, source_target_pairs={{12,5},{13,4},{14,7},{15,6},{4,9},{5,8},{6,11},{7,10},{8,1},{9,0},... | collective-permute-start | bytes 811016 | tf_op jit(solution)/shard_map/ppermute | solution.py:223
  7.9 12.7 %collective-permute-start.1 = (bf16[528,256]{1,0:T(8,128)(2,1)S(1)}, bf16[528,256]{1,0:T(8,128)(2,1)S(1)}, u32[]{:S(2)}, u32[]{:S(2)}) collective-permute-start(bf16[528,256]{1,0:T(8,128)(2,1)S(1)} %shard_map.46.refs_1_.refs_0_), channel_id=1, source_target_pairs={{12,9},{13,8},{14,11},{15,10},{4,1},{5,0},{6,3},{7,2},{8,13},{9,12... | collective-permute-start | bytes 811016 | tf_op jit(solution)/shard_map/ppermute | solution.py:224
  7.9 10.0 %collective-permute-start.4 = (bf16[256,256]{1,0:T(8,128)(2,1)S(1)}, bf16[256,256]{1,0:T(8,128)(2,1)S(1)}, u32[]{:S(2)}, u32[]{:S(2)}) collective-permute-start(bf16[256,256]{1,0:T(8,128)(2,1)S(1)} %slice.28), channel_id=1, source_target_pairs={{0,1},{1,0},{2,3},{3,2},{4,5},{5,4},{6,7},{7,6},{8,9},{9,8},{10,11... | collective-permute-start | bytes 393224 | tf_op jit(solution)/shard_map/ppermute | solution.py:212
  8.7 10.8 %collective-permute-start.5 = (bf16[272,256]{1,0:T(8,128)(2,1)S(1)}, bf16[272,256]{1,0:T(8,128)(2,1)S(1)}, u32[]{:S(2)}, u32[]{:S(2)}) collective-permute-start(bf16[272,256]{1,0:T(8,128)(2,1)S(1)} %slice.29), channel_id=1, source_target_pairs={{0,1},{1,0},{2,3},{3,2},{4,5},{5,4},{6,7},{7,6},{8,9},{9,8},{10,11... | collective-permute-start | bytes 417800 | tf_op jit(solution)/shard_map/ppermute | solution.py:212
  8.8 8.9 %collective-permute-start = (bf16[528,256]{1,0:T(8,128)(2,1)S(1)}, bf16[528,256]{1,0:T(8,128)(2,1)S(1)}, u32[]{:S(2)}, u32[]{:S(2)}) collective-permute-start(bf16[528,256]{1,0:T(8,128)(2,1)S(1)} %get-tuple-element.65), channel_id=1, source_target_pairs={{0,2},{1,3},{2,0},{3,1},{4,6},{5,7},{6,4},{7,5},{8,10},{9,11},{10,... | collective-permute-start | bytes 811016 | tf_op jit(solution)/shard_map/while/body/ppermute | solution.py:212
  17.8 1.7 %collective-permute-start.3 = (bf16[272,256]{1,0:T(8,128)(2,1)S(1)}, bf16[272,256]{1,0:T(8,128)(2,1)S(1)}, u32[]{:S(2)}, u32[]{:S(2)}) collective-permute-start(bf16[272,256]{1,0:T(8,128)(2,1)S(1)} %slice.22), channel_id=1, source_target_pairs={{0,1},{1,0},{2,3},{3,2},{4,5},{5,4},{6,7},{7,6},{8,9},{9,8},{10,11... | collective-permute-start | bytes 417800 | tf_op jit(solution)/shard_map/ppermute | solution.py:212
  17.9 1.5 %collective-permute-start.2 = (bf16[256,256]{1,0:T(8,128)(2,1)S(1)}, bf16[256,256]{1,0:T(8,128)(2,1)S(1)}, u32[]{:S(2)}, u32[]{:S(2)}) collective-permute-start(bf16[256,256]{1,0:T(8,128)(2,1)S(1)} %slice.21), channel_id=1, source_target_pairs={{0,1},{1,0},{2,3},{3,2},{4,5},{5,4},{6,7},{7,6},{8,9},{9,8},{10,11... | collective-permute-start | bytes 393224 | tf_op jit(solution)/shard_map/ppermute | solution.py:212
  21.5 2.5 %collective-permute-start.7 = (f32[8,128]{1,0:T(8,128)S(1)}, f32[8,128]{1,0:T(8,128)S(1)}, u32[]{:S(2)}, u32[]{:S(2)}) collective-permute-start(f32[8,128]{1,0:T(8,128)S(1)} %get-tuple-element.32), channel_id=1, source_target_pairs={{0,1},{1,0},{2,3},{3,2},{4,5},{5,4},{6,7},{7,6},{8,9},{9,8},{10,11... | collective-permute-start | bytes 12296 | tf_op jit(solution)/shard_map/ppermute | solution.py:212
  21.6 4.8 %collective-permute-start.9 = (f32[4,128]{1,0:T(4,128)S(1)}, f32[4,128]{1,0:T(4,128)S(1)}, u32[]{:S(2)}, u32[]{:S(2)}) collective-permute-start(f32[4,128]{1,0:T(4,128)S(1)} %get-tuple-element.33), channel_id=1, source_target_pairs={{5,12},{4,13},{7,14},{6,15},{9,4},{8,5},{11,6},{10,7},{1,8},{0,9},... | collective-permute-start | bytes 6152 | tf_op jit(solution)/shard_map/ppermute | solution.py:238
  24.0 3.1 %collective-permute-start.8 = (f32[4,128]{1,0:T(4,128)S(1)}, f32[4,128]{1,0:T(4,128)S(1)}, u32[]{:S(2)}, u32[]{:S(2)}) collective-permute-start(f32[4,128]{1,0:T(4,128)S(1)} %slice.27), channel_id=1, source_target_pairs={{0,3},{1,2},{2,1},{3,0},{4,7},{5,6},{6,5},{7,4},{8,11},{9,10},{10,... | collective-permute-start | bytes 6152 | tf_op jit(solution)/shard_map/ppermute | solution.py:212

commit v29 on v28

--- a/solution.py
+++ b/solution.py
@@ -232,11 +232,11 @@
     )
     core, *across = [tuple(swap(part, 1) for part in halves(block)) for block in [own, *besides]]
     rows = [own, *across, core, *besides]
-    row_best, backs = [], []
-    for key, step in zip(keys, steps):
-        (found,), row_best = score([key], rows, cols=1, known=row_best)
-        backs.append(lax.ppermute(found, both, [(b, a) for a, b in step]))
-    _, row_best = score([nearby], rows, known=row_best)
+    col_best, row_best = score([*keys, nearby], rows, cols=len(keys))
+    backs = [
+        lax.ppermute(found, both, [(b, a) for a, b in step])
+        for found, step in zip(col_best, steps)
+    ]
     _, (own_best,) = score([own], rows, own_first=True)
     local = jnp.maximum(row_best[0], swap(row_best[1], 1))
     best = jnp.maximum(local[:tiles], own_best[:tiles])

time: 27.8 us -> 27.8 us (level)
  waiting for transfers between devices: 9.72 us -> 11.4 us
  starting transfers between devices: 11.3 us -> 9.87 us
    ppermute x1, starting transfers between devices: 2.32 us -> 1.43 us  [per_device(): lax.ppermute(found, both, [(b, a) for a, b in step])]
    ppermute x1, waiting for transfers between devices: 0.43 us -> 1.24 us  [per_device(): lax.ppermute(found, both, [(b, a) for a, b in step])]
    ppermute x7, starting transfers between devices: 4.43 us -> 3.9 us  [swap(): lax.ppermute(block, 'split', [(s, s ^ offset) for s in range(split_count)])]
    ppermute x7, waiting for transfers between devices: 8.98 us -> 9.43 us  [swap(): lax.ppermute(block, 'split', [(s, s ^ offset) for s in range(split_count)])]
    ppermute x1, waiting for transfers between devices: 0.3 us -> 0.72 us  [per_device(): nearby = lax.ppermute(own, both, last)]
    pallas_call x3 -> x2, Pallas kernels: 2.44 us -> 2.2 us  [score(): pl.pallas_call(functools.partial(score_kernel, len(keys), cols, [len(row)...]
  transfers between devices with their start and end apart: 10 -> 10, of which waited for: 5 -> 5; matrix products, arithmetic and copies ran while one was open for 0% -> 0% of each run, Pallas kernels for 6% -> 3%
where the time goes in v29:
time: 27.8 us; the launch traced here: 27.6 us
  waiting for transfers between devices  11.4 us (41%)
  starting transfers between devices  9.87 us (36%)
  Pallas kernels  5.58 us (20%)
  other arithmetic  0.59 us (2%)
    ppermute x7, waiting for transfers between devices, swap(): lax.ppermute(block, 'split', [(s, s ^ offset) for s in range(split_count)])  9.43 us
    ppermute x1, starting transfers between devices, per_device(): keys = [lax.ppermute(own, both, step) for step in steps]  4.54 us
    ppermute x7, starting transfers between devices, swap(): lax.ppermute(block, 'split', [(s, s ^ offset) for s in range(split_count)])  3.9 us
    pallas_call x1, Pallas kernels, project(): pl.pallas_call(project_kernel, in_specs=[pl.BlockSpec(memory_space=pltpu....  3.38 us
    pallas_call x2, Pallas kernels, score(): pl.pallas_call(functools.partial(score_kernel, len(keys), cols, [len(row)...  2.2 us
    ppermute x1, starting transfers between devices, per_device(): lax.ppermute(found, both, [(b, a) for a, b in step])  1.43 us
    ppermute x1, waiting for transfers between devices, per_device(): lax.ppermute(found, both, [(b, a) for a, b in step])  1.24 us
    ppermute x1, waiting for transfers between devices, per_device(): nearby = lax.ppermute(own, both, last)  0.72 us
  transfers between devices with their start and end apart: 10, of which 5 were waited for; matrix products, arithmetic and copies ran while one was open for 0% of the time, Pallas kernels for 3%

profile of v29, /device:TPU:0, one launch (start us, length us, event | category | flops | bytes accessed | tf_op | source)
XLA Modules:
  0.0 27.6 jit_solution(17365906808531200418)
XLA Ops:
  0.0 3.4 %shard_map.46.refs_2_.refs_0_.refs_1_ = bf16[528,256]{1,0:T(8,128)(2,1)S(1)} custom-call(bf16[512,4096]{1,0:T(8,128)(2,1)} %source_hbm.1, bf16[4096,256]{1,0:T(8,128)(2,1)} %basis_hbm.1, s32[4,128]{1,0:T(4,128)} %bitcast.4, s32[4,128]{1,0:T(4,128)} %bitcast.5), custom_call_target="tpu_custom_call" | custom-call | flops 1073741824 | bytes 6291456 | tf_op jit(solution)/shard_map/pallas_call | solution.py:65
  3.4 4.5 %collective-permute-start.1 = (bf16[528,256]{1,0:T(8,128)(2,1)S(1)}, bf16[528,256]{1,0:T(8,128)(2,1)S(1)}, u32[]{:S(2)}, u32[]{:S(2)}) collective-permute-start(bf16[528,256]{1,0:T(8,128)(2,1)S(1)} %shard_map.46.refs_2_.refs_0_.refs_1_), channel_id=1, source_target_pairs={{12,5},{13,4},{14,7},{15,6},{4,9},{5,8},{6,11},{7,10},{8,1},{9,0},... | collective-permute-start | bytes 811016 | tf_op jit(solution)/shard_map/ppermute | solution.py:223
  8.0 9.2 %while.10 = (s32[]{:T(128)}, bf16[528,256]{1,0:T(8,128)(2,1)S(1)}, s32[]{:T(128)}, s32[]{:T(128)}) while((s32[]{:T(128)}, bf16[528,256]{1,0:T(8,128)(2,1)S(1)}, s32[]{:T(128)}, s32[]{:T(128)}) %tuple.18), condition=%wide.region_1.0_spmd, body=%wide.region_0.0_spmd.sunk | while | flops 2 | bytes 1622109 | solution.py:227
  8.0 1.6 %collective-permute-start = (bf16[528,256]{1,0:T(8,128)(2,1)S(1)}, bf16[528,256]{1,0:T(8,128)(2,1)S(1)}, u32[]{:S(2)}, u32[]{:S(2)}) collective-permute-start(bf16[528,256]{1,0:T(8,128)(2,1)S(1)} %get-tuple-element.61), channel_id=1, source_target_pairs={{0,2},{1,3},{2,0},{3,1},{4,6},{5,7},{6,4},{7,5},{8,10},{9,11},{10,... | collective-permute-start | bytes 811016 | tf_op jit(solution)/shard_map/while/body/ppermute | solution.py:212
  9.5 7.6 %collective-permute-done = bf16[528,256]{1,0:T(8,128)(2,1)S(1)} collective-permute-done((bf16[528,256]{1,0:T(8,128)(2,1)S(1)}, bf16[528,256]{1,0:T(8,128)(2,1)S(1)}, u32[]{:S(2)}, u32[]{:S(2)}) %collective-permute-start) | collective-permute-done | bytes 270368 | tf_op jit(solution)/shard_map/while/body/ppermute | solution.py:212
  17.1 0.1 collective-permute-start.3
  17.2 0.6 %collective-permute-start.4 = (bf16[272,256]{1,0:T(8,128)(2,1)S(1)}, bf16[272,256]{1,0:T(8,128)(2,1)S(1)}, u32[]{:S(2)}, u32[]{:S(2)}) collective-permute-start(bf16[272,256]{1,0:T(8,128)(2,1)S(1)} %slice.22), channel_id=1, source_target_pairs={{0,1},{1,0},{2,3},{3,2},{4,5},{5,4},{6,7},{7,6},{8,9},{9,8},{10,11... | collective-permute-start | bytes 417800 | tf_op jit(solution)/shard_map/ppermute | solution.py:212
  17.8 0.1 collective-permute-start.6
  17.9 0.6 %collective-permute-done.3.refs_3_.refs_2_ = bf16[256,256]{1,0:T(8,128)(2,1)S(1)} collective-permute-done((bf16[256,256]{1,0:T(8,128)(2,1)S(1)}, bf16[256,256]{1,0:T(8,128)(2,1)S(1)}, u32[]{:S(2)}, u32[]{:S(2)}) %collective-permute-start.3) | collective-permute-done | bytes 131104 | tf_op jit(solution)/shard_map/ppermute | solution.py:212
  18.6 0.1 collective-permute-start.5
  18.7 1.2 %collective-permute-done.5.refs_5_.refs_4_ = bf16[256,256]{1,0:T(8,128)(2,1)S(1)} collective-permute-done((bf16[256,256]{1,0:T(8,128)(2,1)S(1)}, bf16[256,256]{1,0:T(8,128)(2,1)S(1)}, u32[]{:S(2)}, u32[]{:S(2)}) %collective-permute-start.5) | collective-permute-done | bytes 131104 | tf_op jit(solution)/shard_map/ppermute | solution.py:212
  19.9 0.0 collective-permute-done.4.refs_4_.refs_3_
  19.9 0.0 collective-permute-done.6.refs_6_.refs_5_
  19.9 0.0 collective-permute-done.1.refs_0_
  19.9 0.7 %collective-permute-done.2.refs_1_ = bf16[528,256]{1,0:T(8,128)(2,1)S(1)} collective-permute-done((bf16[528,256]{1,0:T(8,128)(2,1)S(1)}, bf16[528,256]{1,0:T(8,128)(2,1)S(1)}, u32[]{:S(2)}, u32[]{:S(2)}) %collective-permute-start.2) | collective-permute-done | bytes 270368 | tf_op jit(solution)/shard_map/ppermute | solution.py:224
  20.6 1.4 %shard_map.47 = (f32[4,128]{1,0:T(4,128)S(1)}, f32[8,128]{1,0:T(8,128)S(1)}, f32[8,128]{1,0:T(8,128)S(1)}) custom-call(bf16[528,256]{1,0:T(8,128)(2,1)S(1)} %collective-permute-done.1.refs_0_, bf16[528,256]{1,0:T(8,128)(2,1)S(1)} %collective-permute-done.2.refs_1_, bf16[528,256]{1,0:T(8,128)(2,1)S(1)} %shard_map.46.refs_2_.refs_0_.refs_1_, ...), custom_call_target="tpu_custom_call" | custom-call | tf_op jit(solution)/shard_map/pallas_call | solution.py:179
  22.1 0.1 collective-permute-start.7
  22.2 1.4 %collective-permute-start.9 = (f32[4,128]{1,0:T(4,128)S(1)}, f32[4,128]{1,0:T(4,128)S(1)}, u32[]{:S(2)}, u32[]{:S(2)}) collective-permute-start(f32[4,128]{1,0:T(4,128)S(1)} %get-tuple-element.29), channel_id=1, source_target_pairs={{5,12},{4,13},{7,14},{6,15},{9,4},{8,5},{11,6},{10,7},{1,8},{0,9},... | collective-permute-start | bytes 6152 | tf_op jit(solution)/shard_map/ppermute | solution.py:237
  23.6 0.0 collective-permute-done.7
  23.7 1.4 %collective-permute-start.8 = (f32[4,128]{1,0:T(4,128)S(1)}, f32[4,128]{1,0:T(4,128)S(1)}, u32[]{:S(2)}, u32[]{:S(2)}) collective-permute-start(f32[4,128]{1,0:T(4,128)S(1)} %slice.27), channel_id=1, source_target_pairs={{0,3},{1,2},{2,1},{3,0},{4,7},{5,6},{6,5},{7,4},{8,11},{9,10},{10,... | collective-permute-start | bytes 6152 | tf_op jit(solution)/shard_map/ppermute | solution.py:212
  25.0 0.8 %shard_map.48 = f32[8,128]{1,0:T(8,128)S(1)} custom-call(bf16[528,256]{1,0:T(8,128)(2,1)S(1)} %shard_map.46.refs_2_.refs_0_.refs_1_, bf16[528,256]{1,0:T(8,128)(2,1)S(1)} %shard_map.46.refs_2_.refs_0_.refs_1_, bf16[256,256]{1,0:T(8,128)(2,1)S(1)} %collective-permute-done.3.refs_3_.refs_2_, bf16[272,256]{1,0:T(8,128)(2,1)S(1)} %collective-permute-done.4.refs_4_.refs_3_, ...), custom_call_target="tpu_custom_call" | custom-call | tf_op jit(solution)/shard_map/pallas_call | solution.py:179
  25.8 1.2 %collective-permute-done.9 = f32[4,128]{1,0:T(4,128)S(1)} collective-permute-done((f32[4,128]{1,0:T(4,128)S(1)}, f32[4,128]{1,0:T(4,128)S(1)}, u32[]{:S(2)}, u32[]{:S(2)}) %collective-permute-start.9) | collective-permute-done | bytes 2080 | tf_op jit(solution)/shard_map/ppermute | solution.py:237
  27.0 0.0 collective-permute-done.8
  27.0 0.6 %maximum_bitcast_fusion = f32[512]{0:T(512)} fusion(f32[4,128]{1,0:T(4,128)S(1)} %collective-permute-done.9, f32[4,128]{1,0:T(4,128)S(1)} %collective-permute-done.8, f32[8,128]{1,0:T(8,128)S(1)} %shard_map.48, f32[8,128]{1,0:T(8,128)S(1)} %max.18), kind=kLoop, calls=%fused_computation | loop fusion | flops 2048 | bytes 10240 | tf_op jit(solution)/shard_map/reshape | solution.py:247
  (9 shorter events, 0.1 us)
Async XLA Ops:
  3.4 16.5 %collective-permute-start.1 = (bf16[528,256]{1,0:T(8,128)(2,1)S(1)}, bf16[528,256]{1,0:T(8,128)(2,1)S(1)}, u32[]{:S(2)}, u32[]{:S(2)}) collective-permute-start(bf16[528,256]{1,0:T(8,128)(2,1)S(1)} %shard_map.46.refs_2_.refs_0_.refs_1_), channel_id=1, source_target_pairs={{12,5},{13,4},{14,7},{15,6},{4,9},{5,8},{6,11},{7,10},{8,1},{9,0},... | collective-permute-start | bytes 811016 | tf_op jit(solution)/shard_map/ppermute | solution.py:223
  7.9 12.7 %collective-permute-start.2 = (bf16[528,256]{1,0:T(8,128)(2,1)S(1)}, bf16[528,256]{1,0:T(8,128)(2,1)S(1)}, u32[]{:S(2)}, u32[]{:S(2)}) collective-permute-start(bf16[528,256]{1,0:T(8,128)(2,1)S(1)} %shard_map.46.refs_2_.refs_0_.refs_1_), channel_id=1, source_target_pairs={{12,9},{13,8},{14,11},{15,10},{4,1},{5,0},{6,3},{7,2},{8,13},{9,12... | collective-permute-start | bytes 811016 | tf_op jit(solution)/shard_map/ppermute | solution.py:224
  8.0 9.1 %collective-permute-start = (bf16[528,256]{1,0:T(8,128)(2,1)S(1)}, bf16[528,256]{1,0:T(8,128)(2,1)S(1)}, u32[]{:S(2)}, u32[]{:S(2)}) collective-permute-start(bf16[528,256]{1,0:T(8,128)(2,1)S(1)} %get-tuple-element.61), channel_id=1, source_target_pairs={{0,2},{1,3},{2,0},{3,1},{4,6},{5,7},{6,4},{7,5},{8,10},{9,11},{10,... | collective-permute-start | bytes 811016 | tf_op jit(solution)/shard_map/while/body/ppermute | solution.py:212
  17.1 1.4 %collective-permute-start.3 = (bf16[256,256]{1,0:T(8,128)(2,1)S(1)}, bf16[256,256]{1,0:T(8,128)(2,1)S(1)}, u32[]{:S(2)}, u32[]{:S(2)}) collective-permute-start(bf16[256,256]{1,0:T(8,128)(2,1)S(1)} %slice.21), channel_id=1, source_target_pairs={{0,1},{1,0},{2,3},{3,2},{4,5},{5,4},{6,7},{7,6},{8,9},{9,8},{10,11... | collective-permute-start | bytes 393224 | tf_op jit(solution)/shard_map/ppermute | solution.py:212
  17.2 2.7 %collective-permute-start.4 = (bf16[272,256]{1,0:T(8,128)(2,1)S(1)}, bf16[272,256]{1,0:T(8,128)(2,1)S(1)}, u32[]{:S(2)}, u32[]{:S(2)}) collective-permute-start(bf16[272,256]{1,0:T(8,128)(2,1)S(1)} %slice.22), channel_id=1, source_target_pairs={{0,1},{1,0},{2,3},{3,2},{4,5},{5,4},{6,7},{7,6},{8,9},{9,8},{10,11... | collective-permute-start | bytes 417800 | tf_op jit(solution)/shard_map/ppermute | solution.py:212
  17.8 2.1 %collective-permute-start.6 = (bf16[272,256]{1,0:T(8,128)(2,1)S(1)}, bf16[272,256]{1,0:T(8,128)(2,1)S(1)}, u32[]{:S(2)}, u32[]{:S(2)}) collective-permute-start(bf16[272,256]{1,0:T(8,128)(2,1)S(1)} %slice.29), channel_id=1, source_target_pairs={{0,1},{1,0},{2,3},{3,2},{4,5},{5,4},{6,7},{7,6},{8,9},{9,8},{10,11... | collective-permute-start | bytes 417800 | tf_op jit(solution)/shard_map/ppermute | solution.py:212
  18.6 1.3 %collective-permute-start.5 = (bf16[256,256]{1,0:T(8,128)(2,1)S(1)}, bf16[256,256]{1,0:T(8,128)(2,1)S(1)}, u32[]{:S(2)}, u32[]{:S(2)}) collective-permute-start(bf16[256,256]{1,0:T(8,128)(2,1)S(1)} %slice.28), channel_id=1, source_target_pairs={{0,1},{1,0},{2,3},{3,2},{4,5},{5,4},{6,7},{7,6},{8,9},{9,8},{10,11... | collective-permute-start | bytes 393224 | tf_op jit(solution)/shard_map/ppermute | solution.py:212
  22.1 1.6 %collective-permute-start.7 = (f32[8,128]{1,0:T(8,128)S(1)}, f32[8,128]{1,0:T(8,128)S(1)}, u32[]{:S(2)}, u32[]{:S(2)}) collective-permute-start(f32[8,128]{1,0:T(8,128)S(1)} %get-tuple-element.28), channel_id=1, source_target_pairs={{0,1},{1,0},{2,3},{3,2},{4,5},{5,4},{6,7},{7,6},{8,9},{9,8},{10,11... | collective-permute-start | bytes 12296 | tf_op jit(solution)/shard_map/ppermute | solution.py:212
  22.2 4.8 %collective-permute-start.9 = (f32[4,128]{1,0:T(4,128)S(1)}, f32[4,128]{1,0:T(4,128)S(1)}, u32[]{:S(2)}, u32[]{:S(2)}) collective-permute-start(f32[4,128]{1,0:T(4,128)S(1)} %get-tuple-element.29), channel_id=1, source_target_pairs={{5,12},{4,13},{7,14},{6,15},{9,4},{8,5},{11,6},{10,7},{1,8},{0,9},... | collective-permute-start | bytes 6152 | tf_op jit(solution)/shard_map/ppermute | solution.py:237
  23.7 3.4 %collective-permute-start.8 = (f32[4,128]{1,0:T(4,128)S(1)}, f32[4,128]{1,0:T(4,128)S(1)}, u32[]{:S(2)}, u32[]{:S(2)}) collective-permute-start(f32[4,128]{1,0:T(4,128)S(1)} %slice.27), channel_id=1, source_target_pairs={{0,3},{1,2},{2,1},{3,0},{4,7},{5,6},{6,5},{7,4},{8,11},{9,10},{10,... | collective-permute-start | bytes 6152 | tf_op jit(solution)/shard_map/ppermute | solution.py:212

commit v30 on v28

--- a/solution.py
+++ b/solution.py
@@ -198,7 +198,7 @@
     half = count // 2
     circle = [count - 1 - 2 * i for i in range(half)] + [count - 2 - 2 * i for i in range(half)]
     return [
-        [(circle[i], circle[(i + step) % count]) for i in range(count)]
+        [(circle[(i + step) % count], circle[i]) for i in range(count)]
         for step in range(1, half + 1)
     ]
 

time: 27.8 us -> 29.6 us (1.065)
  starting transfers between devices: 11.3 us -> 13.6 us
  waiting for transfers between devices: 9.72 us -> 9.24 us
    ppermute x1, starting transfers between devices: 0.01 us -> 1.85 us  [per_device(): nearby = lax.ppermute(own, both, last)]
    ppermute x1, starting transfers between devices: 2.32 us -> 3.94 us  [per_device(): backs.append(lax.ppermute(found, both, [(b, a) for a, b in step]))]
    ppermute x1, starting transfers between devices: 4.54 us -> 3.53 us  [per_device(): keys = [lax.ppermute(own, both, step) for step in steps]]
    ppermute x1, waiting for transfers between devices: 0.43 us -> 0.01 us  [per_device(): backs.append(lax.ppermute(found, both, [(b, a) for a, b in step]))]
  transfers between devices with their start and end apart: 10 -> 10, of which waited for: 5 -> 4; matrix products, arithmetic and copies ran while one was open for 0% -> 0% of each run, Pallas kernels for 6% -> 5%
where the time goes in v30:
time: 29.6 us; the launch traced here: 29.4 us
  starting transfers between devices  13.6 us (46%)
  waiting for transfers between devices  9.24 us (31%)
  Pallas kernels  5.82 us (20%)
  other arithmetic  0.59 us (2%)
    ppermute x7, waiting for transfers between devices, swap(): lax.ppermute(block, 'split', [(s, s ^ offset) for s in range(split_count)])  8.97 us
    ppermute x7, starting transfers between devices, swap(): lax.ppermute(block, 'split', [(s, s ^ offset) for s in range(split_count)])  4.24 us
    ppermute x1, starting transfers between devices, per_device(): backs.append(lax.ppermute(found, both, [(b, a) for a, b in step]))  3.94 us
    ppermute x1, starting transfers between devices, per_device(): keys = [lax.ppermute(own, both, step) for step in steps]  3.53 us
    pallas_call x1, Pallas kernels, project(): pl.pallas_call(project_kernel, in_specs=[pl.BlockSpec(memory_space=pltpu....  3.38 us
    pallas_call x3, Pallas kernels, score(): pl.pallas_call(functools.partial(score_kernel, len(keys), cols, [len(row)...  2.44 us
    ppermute x1, starting transfers between devices, per_device(): nearby = lax.ppermute(own, both, last)  1.85 us
  transfers between devices with their start and end apart: 10, of which 4 were waited for; matrix products, arithmetic and copies ran while one was open for 0% of the time, Pallas kernels for 5%

profile of v30, /device:TPU:0, one launch (start us, length us, event | category | flops | bytes accessed | tf_op | source)
XLA Modules:
  0.0 29.4 jit_solution(16941428820489545855)
XLA Ops:
  0.0 3.4 %shard_map.46.refs_1_.refs_0_ = bf16[528,256]{1,0:T(8,128)(2,1)S(1)} custom-call(bf16[512,4096]{1,0:T(8,128)(2,1)} %source_hbm.1, bf16[4096,256]{1,0:T(8,128)(2,1)} %basis_hbm.1, s32[4,128]{1,0:T(4,128)} %bitcast.4, s32[4,128]{1,0:T(4,128)} %bitcast.5), custom_call_target="tpu_custom_call" | custom-call | flops 1073741824 | bytes 6291456 | tf_op jit(solution)/shard_map/pallas_call | solution.py:65
  3.4 3.5 %collective-permute-start.6 = (bf16[528,256]{1,0:T(8,128)(2,1)S(1)}, bf16[528,256]{1,0:T(8,128)(2,1)S(1)}, u32[]{:S(2)}, u32[]{:S(2)}) collective-permute-start(bf16[528,256]{1,0:T(8,128)(2,1)S(1)} %shard_map.46.refs_1_.refs_0_), channel_id=1, source_target_pairs={{4,13},{5,12},{6,15},{7,14},{8,5},{9,4},{10,7},{11,6},{0,9},{1,8},... | collective-permute-start | bytes 811016 | tf_op jit(solution)/shard_map/ppermute | solution.py:223
  6.9 1.9 %collective-permute-start.1 = (bf16[528,256]{1,0:T(8,128)(2,1)S(1)}, bf16[528,256]{1,0:T(8,128)(2,1)S(1)}, u32[]{:S(2)}, u32[]{:S(2)}) collective-permute-start(bf16[528,256]{1,0:T(8,128)(2,1)S(1)} %shard_map.46.refs_1_.refs_0_), channel_id=1, source_target_pairs={{8,13},{9,12},{10,15},{11,14},{0,5},{1,4},{2,7},{3,6},{12,9},{13,8... | collective-permute-start | bytes 811016 | tf_op jit(solution)/shard_map/ppermute | solution.py:224
  8.8 0.1 collective-permute-start.4
  8.9 0.6 %collective-permute-start.5 = (bf16[272,256]{1,0:T(8,128)(2,1)S(1)}, bf16[272,256]{1,0:T(8,128)(2,1)S(1)}, u32[]{:S(2)}, u32[]{:S(2)}) collective-permute-start(bf16[272,256]{1,0:T(8,128)(2,1)S(1)} %slice.29), channel_id=1, source_target_pairs={{0,1},{1,0},{2,3},{3,2},{4,5},{5,4},{6,7},{7,6},{8,9},{9,8},{10,11... | collective-permute-start | bytes 417800 | tf_op jit(solution)/shard_map/ppermute | solution.py:212
  9.5 8.5 %while.10 = (s32[]{:T(128)}, bf16[528,256]{1,0:T(8,128)(2,1)S(1)}, s32[]{:T(128)}, s32[]{:T(128)}) while((s32[]{:T(128)}, bf16[528,256]{1,0:T(8,128)(2,1)S(1)}, s32[]{:T(128)}, s32[]{:T(128)}) %tuple.18), condition=%wide.region_1.0_spmd, body=%wide.region_0.0_spmd.sunk | while | flops 2 | bytes 1622109 | solution.py:227
  9.5 1.6 %collective-permute-start = (bf16[528,256]{1,0:T(8,128)(2,1)S(1)}, bf16[528,256]{1,0:T(8,128)(2,1)S(1)}, u32[]{:S(2)}, u32[]{:S(2)}) collective-permute-start(bf16[528,256]{1,0:T(8,128)(2,1)S(1)} %get-tuple-element.65), channel_id=1, source_target_pairs={{0,2},{1,3},{2,0},{3,1},{4,6},{5,7},{6,4},{7,5},{8,10},{9,11},{10,... | collective-permute-start | bytes 811016 | tf_op jit(solution)/shard_map/while/body/ppermute | solution.py:212
  11.0 6.9 %collective-permute-done = bf16[528,256]{1,0:T(8,128)(2,1)S(1)} collective-permute-done((bf16[528,256]{1,0:T(8,128)(2,1)S(1)}, bf16[528,256]{1,0:T(8,128)(2,1)S(1)}, u32[]{:S(2)}, u32[]{:S(2)}) %collective-permute-start) | collective-permute-done | bytes 270368 | tf_op jit(solution)/shard_map/while/body/ppermute | solution.py:212
  18.0 0.1 collective-permute-start.3
  18.1 0.0 collective-permute-done.4.refs_4_
  18.1 0.6 %collective-permute-start.2 = (bf16[256,256]{1,0:T(8,128)(2,1)S(1)}, bf16[256,256]{1,0:T(8,128)(2,1)S(1)}, u32[]{:S(2)}, u32[]{:S(2)}) collective-permute-start(bf16[256,256]{1,0:T(8,128)(2,1)S(1)} %slice.21), channel_id=1, source_target_pairs={{0,1},{1,0},{2,3},{3,2},{4,5},{5,4},{6,7},{7,6},{8,9},{9,8},{10,11... | collective-permute-start | bytes 393224 | tf_op jit(solution)/shard_map/ppermute | solution.py:212
  18.7 1.0 %collective-permute-done.2.refs_2_ = bf16[256,256]{1,0:T(8,128)(2,1)S(1)} collective-permute-done((bf16[256,256]{1,0:T(8,128)(2,1)S(1)}, bf16[256,256]{1,0:T(8,128)(2,1)S(1)}, u32[]{:S(2)}, u32[]{:S(2)}) %collective-permute-start.2) | collective-permute-done | bytes 131104 | tf_op jit(solution)/shard_map/ppermute | solution.py:212
  19.7 0.0 collective-permute-done.5.refs_5_
  19.7 0.0 collective-permute-done.3.refs_3_
  19.7 0.0 collective-permute-done.6.refs_0_
  19.7 0.9 %shard_map.47 = (f32[4,128]{1,0:T(4,128)S(1)}, f32[8,128]{1,0:T(8,128)S(1)}, f32[8,128]{1,0:T(8,128)S(1)}) custom-call(bf16[528,256]{1,0:T(8,128)(2,1)S(1)} %collective-permute-done.6.refs_0_, bf16[528,256]{1,0:T(8,128)(2,1)S(1)} %shard_map.46.refs_1_.refs_0_, bf16[256,256]{1,0:T(8,128)(2,1)S(1)} %collective-permute-done.2.refs_2_, ...), custom_call_target="tpu_custom_call" | custom-call | tf_op jit(solution)/shard_map/pallas_call | solution.py:179
  20.5 0.3 collective-permute-done.1.refs_0_
  20.8 0.8 %shard_map.48 = (f32[8,128]{1,0:T(8,128)S(1)}, f32[8,128]{1,0:T(8,128)S(1)}) custom-call(bf16[528,256]{1,0:T(8,128)(2,1)S(1)} %collective-permute-done.1.refs_0_, bf16[528,256]{1,0:T(8,128)(2,1)S(1)} %shard_map.46.refs_1_.refs_0_, bf16[256,256]{1,0:T(8,128)(2,1)S(1)} %collective-permute-done.2.refs_2_, bf16[272,256]{1,0:T(8,128)(2,1)S(1)} %collective-permute-done.3.refs_3_, ...), custom_call_target="tpu_custom_call" | custom-call | tf_op jit(solution)/shard_map/pallas_call | solution.py:179
  21.6 0.2 collective-permute-start.7
  21.8 3.9 %collective-permute-start.9 = (f32[4,128]{1,0:T(4,128)S(1)}, f32[4,128]{1,0:T(4,128)S(1)}, u32[]{:S(2)}, u32[]{:S(2)}) collective-permute-start(f32[4,128]{1,0:T(4,128)S(1)} %get-tuple-element.33), channel_id=1, source_target_pairs={{13,4},{12,5},{15,6},{14,7},{5,8},{4,9},{7,10},{6,11},{9,0},{8,1},... | collective-permute-start | bytes 6152 | tf_op jit(solution)/shard_map/ppermute | solution.py:238
  25.8 1.2 %collective-permute-start.8 = (f32[4,128]{1,0:T(4,128)S(1)}, f32[4,128]{1,0:T(4,128)S(1)}, u32[]{:S(2)}, u32[]{:S(2)}) collective-permute-start(f32[4,128]{1,0:T(4,128)S(1)} %slice.27), channel_id=1, source_target_pairs={{0,3},{1,2},{2,1},{3,0},{4,7},{5,6},{6,5},{7,4},{8,11},{9,10},{10,... | collective-permute-start | bytes 6152 | tf_op jit(solution)/shard_map/ppermute | solution.py:212
  27.0 0.8 %shard_map.49 = f32[8,128]{1,0:T(8,128)S(1)} custom-call(bf16[528,256]{1,0:T(8,128)(2,1)S(1)} %shard_map.46.refs_1_.refs_0_, bf16[528,256]{1,0:T(8,128)(2,1)S(1)} %shard_map.46.refs_1_.refs_0_, bf16[256,256]{1,0:T(8,128)(2,1)S(1)} %collective-permute-done.2.refs_2_, bf16[272,256]{1,0:T(8,128)(2,1)S(1)} %collective-permute-done.3.refs_3_, ...), custom_call_target="tpu_custom_call" | custom-call | tf_op jit(solution)/shard_map/pallas_call | solution.py:179
  27.8 1.1 %collective-permute-done.8 = f32[4,128]{1,0:T(4,128)S(1)} collective-permute-done((f32[4,128]{1,0:T(4,128)S(1)}, f32[4,128]{1,0:T(4,128)S(1)}, u32[]{:S(2)}, u32[]{:S(2)}) %collective-permute-start.8) | collective-permute-done | bytes 2080 | tf_op jit(solution)/shard_map/ppermute | solution.py:212
  28.8 0.6 %maximum_bitcast_fusion = f32[512]{0:T(512)} fusion(f32[4,128]{1,0:T(4,128)S(1)} %collective-permute-done.9, f32[4,128]{1,0:T(4,128)S(1)} %collective-permute-done.8, f32[8,128]{1,0:T(8,128)S(1)} %shard_map.49, f32[8,128]{1,0:T(8,128)S(1)} %max.18), kind=kLoop, calls=%fused_computation | loop fusion | flops 2048 | bytes 10240 | tf_op jit(solution)/shard_map/reshape | solution.py:247
  (10 shorter events, 0.1 us)
Async XLA Ops:
  3.4 16.3 %collective-permute-start.6 = (bf16[528,256]{1,0:T(8,128)(2,1)S(1)}, bf16[528,256]{1,0:T(8,128)(2,1)S(1)}, u32[]{:S(2)}, u32[]{:S(2)}) collective-permute-start(bf16[528,256]{1,0:T(8,128)(2,1)S(1)} %shard_map.46.refs_1_.refs_0_), channel_id=1, source_target_pairs={{4,13},{5,12},{6,15},{7,14},{8,5},{9,4},{10,7},{11,6},{0,9},{1,8},... | collective-permute-start | bytes 811016 | tf_op jit(solution)/shard_map/ppermute | solution.py:223
  6.9 13.9 %collective-permute-start.1 = (bf16[528,256]{1,0:T(8,128)(2,1)S(1)}, bf16[528,256]{1,0:T(8,128)(2,1)S(1)}, u32[]{:S(2)}, u32[]{:S(2)}) collective-permute-start(bf16[528,256]{1,0:T(8,128)(2,1)S(1)} %shard_map.46.refs_1_.refs_0_), channel_id=1, source_target_pairs={{8,13},{9,12},{10,15},{11,14},{0,5},{1,4},{2,7},{3,6},{12,9},{13,8... | collective-permute-start | bytes 811016 | tf_op jit(solution)/shard_map/ppermute | solution.py:224
  8.8 9.3 %collective-permute-start.4 = (bf16[256,256]{1,0:T(8,128)(2,1)S(1)}, bf16[256,256]{1,0:T(8,128)(2,1)S(1)}, u32[]{:S(2)}, u32[]{:S(2)}) collective-permute-start(bf16[256,256]{1,0:T(8,128)(2,1)S(1)} %slice.28), channel_id=1, source_target_pairs={{0,1},{1,0},{2,3},{3,2},{4,5},{5,4},{6,7},{7,6},{8,9},{9,8},{10,11... | collective-permute-start | bytes 393224 | tf_op jit(solution)/shard_map/ppermute | solution.py:212
  8.9 10.8 %collective-permute-start.5 = (bf16[272,256]{1,0:T(8,128)(2,1)S(1)}, bf16[272,256]{1,0:T(8,128)(2,1)S(1)}, u32[]{:S(2)}, u32[]{:S(2)}) collective-permute-start(bf16[272,256]{1,0:T(8,128)(2,1)S(1)} %slice.29), channel_id=1, source_target_pairs={{0,1},{1,0},{2,3},{3,2},{4,5},{5,4},{6,7},{7,6},{8,9},{9,8},{10,11... | collective-permute-start | bytes 417800 | tf_op jit(solution)/shard_map/ppermute | solution.py:212
  9.5 8.5 %collective-permute-start = (bf16[528,256]{1,0:T(8,128)(2,1)S(1)}, bf16[528,256]{1,0:T(8,128)(2,1)S(1)}, u32[]{:S(2)}, u32[]{:S(2)}) collective-permute-start(bf16[528,256]{1,0:T(8,128)(2,1)S(1)} %get-tuple-element.65), channel_id=1, source_target_pairs={{0,2},{1,3},{2,0},{3,1},{4,6},{5,7},{6,4},{7,5},{8,10},{9,11},{10,... | collective-permute-start | bytes 811016 | tf_op jit(solution)/shard_map/while/body/ppermute | solution.py:212
  18.0 1.7 %collective-permute-start.3 = (bf16[272,256]{1,0:T(8,128)(2,1)S(1)}, bf16[272,256]{1,0:T(8,128)(2,1)S(1)}, u32[]{:S(2)}, u32[]{:S(2)}) collective-permute-start(bf16[272,256]{1,0:T(8,128)(2,1)S(1)} %slice.22), channel_id=1, source_target_pairs={{0,1},{1,0},{2,3},{3,2},{4,5},{5,4},{6,7},{7,6},{8,9},{9,8},{10,11... | collective-permute-start | bytes 417800 | tf_op jit(solution)/shard_map/ppermute | solution.py:212
  18.1 1.5 %collective-permute-start.2 = (bf16[256,256]{1,0:T(8,128)(2,1)S(1)}, bf16[256,256]{1,0:T(8,128)(2,1)S(1)}, u32[]{:S(2)}, u32[]{:S(2)}) collective-permute-start(bf16[256,256]{1,0:T(8,128)(2,1)S(1)} %slice.21), channel_id=1, source_target_pairs={{0,1},{1,0},{2,3},{3,2},{4,5},{5,4},{6,7},{7,6},{8,9},{9,8},{10,11... | collective-permute-start | bytes 393224 | tf_op jit(solution)/shard_map/ppermute | solution.py:212
  21.6 4.1 %collective-permute-start.7 = (f32[8,128]{1,0:T(8,128)S(1)}, f32[8,128]{1,0:T(8,128)S(1)}, u32[]{:S(2)}, u32[]{:S(2)}) collective-permute-start(f32[8,128]{1,0:T(8,128)S(1)} %get-tuple-element.32), channel_id=1, source_target_pairs={{0,1},{1,0},{2,3},{3,2},{4,5},{5,4},{6,7},{7,6},{8,9},{9,8},{10,11... | collective-permute-start | bytes 12296 | tf_op jit(solution)/shard_map/ppermute | solution.py:212
  21.8 6.0 %collective-permute-start.9 = (f32[4,128]{1,0:T(4,128)S(1)}, f32[4,128]{1,0:T(4,128)S(1)}, u32[]{:S(2)}, u32[]{:S(2)}) collective-permute-start(f32[4,128]{1,0:T(4,128)S(1)} %get-tuple-element.33), channel_id=1, source_target_pairs={{13,4},{12,5},{15,6},{14,7},{5,8},{4,9},{7,10},{6,11},{9,0},{8,1},... | collective-permute-start | bytes 6152 | tf_op jit(solution)/shard_map/ppermute | solution.py:238
  25.8 3.1 %collective-permute-start.8 = (f32[4,128]{1,0:T(4,128)S(1)}, f32[4,128]{1,0:T(4,128)S(1)}, u32[]{:S(2)}, u32[]{:S(2)}) collective-permute-start(f32[4,128]{1,0:T(4,128)S(1)} %slice.27), channel_id=1, source_target_pairs={{0,3},{1,2},{2,1},{3,0},{4,7},{5,6},{6,5},{7,4},{8,11},{9,10},{10,... | collective-permute-start | bytes 6152 | tf_op jit(solution)/shard_map/ppermute | solution.py:212

commit v31 on v28

--- a/solution.py
+++ b/solution.py
@@ -13,6 +13,7 @@
 ABSENT = -2.0
 STEPS = 8
 ROW_PARTS = 4
+RUN = 2 * LANES
 VMEM_LIMIT = 48 * 1024 * 1024
 
 
@@ -112,8 +113,13 @@
         tag_ref = part_refs[-1]
         row_tags = tag_ref[tag_ref.shape[0] - TAG_ROWS :, :LANES].astype(jnp.float32)
         place = 0
-        for part_ref in part_refs:
-            count = part_ref.shape[0] // LANES * LANES
+        runs = [
+            (part_ref, first)
+            for part_ref in part_refs
+            for first in range(0, part_ref.shape[0] // LANES * LANES, RUN)
+        ]
+        for part_ref, first in runs:
+            count = RUN
             tags = [
                 jnp.broadcast_to(row_tags[at : at + 1, :], (LANES, LANES)).T
                 for at in range(place, place + count // LANES)
@@ -122,7 +128,7 @@
             for key, key_ref in enumerate(key_refs):
                 key_tags = key_ref[row_count:, :LANES].astype(jnp.float32)
                 scores = lax.dot_general(
-                    part_ref[:count, :],
+                    part_ref[first : first + count, :],
                     key_ref[:row_count, :],
                     (((1,), (1,)), ((), ())),
                     preferred_element_type=jnp.float32,

time: 27.8 us -> 27.8 us (level)
  no operation moved by 1% of the time
where the time goes in v31:
time: 27.8 us; the launch traced here: 27.6 us
  starting transfers between devices  11.3 us (41%)
  waiting for transfers between devices  9.75 us (35%)
  Pallas kernels  5.82 us (21%)
  other arithmetic  0.59 us (2%)
    ppermute x7, waiting for transfers between devices, swap(): lax.ppermute(block, 'split', [(s, s ^ offset) for s in range(split_count)])  8.99 us
    ppermute x1, starting transfers between devices, per_device(): keys = [lax.ppermute(own, both, step) for step in steps]  4.54 us
    ppermute x7, starting transfers between devices, swap(): lax.ppermute(block, 'split', [(s, s ^ offset) for s in range(split_count)])  4.4 us
    pallas_call x1, Pallas kernels, project(): pl.pallas_call(project_kernel, in_specs=[pl.BlockSpec(memory_space=pltpu....  3.38 us
    pallas_call x3, Pallas kernels, score(): pl.pallas_call(functools.partial(score_kernel, len(keys), cols, [len(row)...  2.44 us
    ppermute x1, starting transfers between devices, per_device(): backs.append(lax.ppermute(found, both, [(b, a) for a, b in step]))  2.33 us
    reshape x1, other arithmetic, per_device(): return jnp.maximum(best, -1.0).reshape(row_count)  0.58 us
  transfers between devices with their start and end apart: 10, of which 5 were waited for; matrix products, arithmetic and copies ran while one was open for 0% of the time, Pallas kernels for 6%

profile of v31, /device:TPU:0, one launch (start us, length us, event | category | flops | bytes accessed | tf_op | source)
XLA Modules:
  0.0 27.6 jit_solution(661727476526174562)
XLA Ops:
  0.0 3.4 %shard_map.46.refs_1_.refs_0_ = bf16[528,256]{1,0:T(8,128)(2,1)S(1)} custom-call(bf16[512,4096]{1,0:T(8,128)(2,1)} %source_hbm.1, bf16[4096,256]{1,0:T(8,128)(2,1)} %basis_hbm.1, s32[4,128]{1,0:T(4,128)} %bitcast.4, s32[4,128]{1,0:T(4,128)} %bitcast.5), custom_call_target="tpu_custom_call" | custom-call | flops 1073741824 | bytes 6291456 | tf_op jit(solution)/shard_map/pallas_call | solution.py:66
  3.4 4.5 %collective-permute-start.6 = (bf16[528,256]{1,0:T(8,128)(2,1)S(1)}, bf16[528,256]{1,0:T(8,128)(2,1)S(1)}, u32[]{:S(2)}, u32[]{:S(2)}) collective-permute-start(bf16[528,256]{1,0:T(8,128)(2,1)S(1)} %shard_map.46.refs_1_.refs_0_), channel_id=1, source_target_pairs={{12,5},{13,4},{14,7},{15,6},{4,9},{5,8},{6,11},{7,10},{8,1},{9,0},... | collective-permute-start | bytes 811016 | tf_op jit(solution)/shard_map/ppermute | solution.py:229
  7.9 0.0 collective-permute-start.1
  7.9 0.7 %collective-permute-start.4 = (bf16[256,256]{1,0:T(8,128)(2,1)S(1)}, bf16[256,256]{1,0:T(8,128)(2,1)S(1)}, u32[]{:S(2)}, u32[]{:S(2)}) collective-permute-start(bf16[256,256]{1,0:T(8,128)(2,1)S(1)} %slice.28), channel_id=1, source_target_pairs={{0,1},{1,0},{2,3},{3,2},{4,5},{5,4},{6,7},{7,6},{8,9},{9,8},{10,11... | collective-permute-start | bytes 393224 | tf_op jit(solution)/shard_map/ppermute | solution.py:218
  8.7 0.1 collective-permute-start.5
  8.8 9.0 %while.10 = (s32[]{:T(128)}, bf16[528,256]{1,0:T(8,128)(2,1)S(1)}, s32[]{:T(128)}, s32[]{:T(128)}) while((s32[]{:T(128)}, bf16[528,256]{1,0:T(8,128)(2,1)S(1)}, s32[]{:T(128)}, s32[]{:T(128)}) %tuple.18), condition=%wide.region_1.0_spmd, body=%wide.region_0.0_spmd.sunk | while | flops 2 | bytes 1622109 | solution.py:233
  8.8 1.6 %collective-permute-start = (bf16[528,256]{1,0:T(8,128)(2,1)S(1)}, bf16[528,256]{1,0:T(8,128)(2,1)S(1)}, u32[]{:S(2)}, u32[]{:S(2)}) collective-permute-start(bf16[528,256]{1,0:T(8,128)(2,1)S(1)} %get-tuple-element.65), channel_id=1, source_target_pairs={{0,2},{1,3},{2,0},{3,1},{4,6},{5,7},{6,4},{7,5},{8,10},{9,11},{10,... | collective-permute-start | bytes 811016 | tf_op jit(solution)/shard_map/while/body/ppermute | solution.py:218
  10.4 7.4 %collective-permute-done = bf16[528,256]{1,0:T(8,128)(2,1)S(1)} collective-permute-done((bf16[528,256]{1,0:T(8,128)(2,1)S(1)}, bf16[528,256]{1,0:T(8,128)(2,1)S(1)}, u32[]{:S(2)}, u32[]{:S(2)}) %collective-permute-start) | collective-permute-done | bytes 270368 | tf_op jit(solution)/shard_map/while/body/ppermute | solution.py:218
  17.8 0.1 collective-permute-start.3
  17.9 0.6 %collective-permute-start.2 = (bf16[256,256]{1,0:T(8,128)(2,1)S(1)}, bf16[256,256]{1,0:T(8,128)(2,1)S(1)}, u32[]{:S(2)}, u32[]{:S(2)}) collective-permute-start(bf16[256,256]{1,0:T(8,128)(2,1)S(1)} %slice.21), channel_id=1, source_target_pairs={{0,1},{1,0},{2,3},{3,2},{4,5},{5,4},{6,7},{7,6},{8,9},{9,8},{10,11... | collective-permute-start | bytes 393224 | tf_op jit(solution)/shard_map/ppermute | solution.py:218
  18.5 1.0 %collective-permute-done.2.refs_2_ = bf16[256,256]{1,0:T(8,128)(2,1)S(1)} collective-permute-done((bf16[256,256]{1,0:T(8,128)(2,1)S(1)}, bf16[256,256]{1,0:T(8,128)(2,1)S(1)}, u32[]{:S(2)}, u32[]{:S(2)}) %collective-permute-start.2) | collective-permute-done | bytes 131104 | tf_op jit(solution)/shard_map/ppermute | solution.py:218
  19.5 0.0 collective-permute-done.5.refs_5_
  19.5 0.0 collective-permute-done.3.refs_3_
  19.5 0.0 collective-permute-done.6.refs_0_
  19.5 0.9 %shard_map.47 = (f32[4,128]{1,0:T(4,128)S(1)}, f32[8,128]{1,0:T(8,128)S(1)}, f32[8,128]{1,0:T(8,128)S(1)}) custom-call(bf16[528,256]{1,0:T(8,128)(2,1)S(1)} %collective-permute-done.6.refs_0_, bf16[528,256]{1,0:T(8,128)(2,1)S(1)} %shard_map.46.refs_1_.refs_0_, bf16[256,256]{1,0:T(8,128)(2,1)S(1)} %collective-permute-done.2.refs_2_, ...), custom_call_target="tpu_custom_call" | custom-call | tf_op jit(solution)/shard_map/pallas_call | solution.py:185
  20.3 0.3 %collective-permute-done.1.refs_0_ = bf16[528,256]{1,0:T(8,128)(2,1)S(1)} collective-permute-done((bf16[528,256]{1,0:T(8,128)(2,1)S(1)}, bf16[528,256]{1,0:T(8,128)(2,1)S(1)}, u32[]{:S(2)}, u32[]{:S(2)}) %collective-permute-start.1) | collective-permute-done | bytes 270368 | tf_op jit(solution)/shard_map/ppermute | solution.py:230
  20.6 0.8 %shard_map.48 = (f32[8,128]{1,0:T(8,128)S(1)}, f32[8,128]{1,0:T(8,128)S(1)}) custom-call(bf16[528,256]{1,0:T(8,128)(2,1)S(1)} %collective-permute-done.1.refs_0_, bf16[528,256]{1,0:T(8,128)(2,1)S(1)} %shard_map.46.refs_1_.refs_0_, bf16[256,256]{1,0:T(8,128)(2,1)S(1)} %collective-permute-done.2.refs_2_, bf16[272,256]{1,0:T(8,128)(2,1)S(1)} %collective-permute-done.3.refs_3_, ...), custom_call_target="tpu_custom_call" | custom-call | tf_op jit(solution)/shard_map/pallas_call | solution.py:185
  21.5 0.1 collective-permute-start.7
  21.6 2.3 %collective-permute-start.9 = (f32[4,128]{1,0:T(4,128)S(1)}, f32[4,128]{1,0:T(4,128)S(1)}, u32[]{:S(2)}, u32[]{:S(2)}) collective-permute-start(f32[4,128]{1,0:T(4,128)S(1)} %get-tuple-element.33), channel_id=1, source_target_pairs={{5,12},{4,13},{7,14},{6,15},{9,4},{8,5},{11,6},{10,7},{1,8},{0,9},... | collective-permute-start | bytes 6152 | tf_op jit(solution)/shard_map/ppermute | solution.py:244
  24.0 1.2 %collective-permute-start.8 = (f32[4,128]{1,0:T(4,128)S(1)}, f32[4,128]{1,0:T(4,128)S(1)}, u32[]{:S(2)}, u32[]{:S(2)}) collective-permute-start(f32[4,128]{1,0:T(4,128)S(1)} %slice.27), channel_id=1, source_target_pairs={{0,3},{1,2},{2,1},{3,0},{4,7},{5,6},{6,5},{7,4},{8,11},{9,10},{10,... | collective-permute-start | bytes 6152 | tf_op jit(solution)/shard_map/ppermute | solution.py:218
  25.2 0.8 %shard_map.49 = f32[8,128]{1,0:T(8,128)S(1)} custom-call(bf16[528,256]{1,0:T(8,128)(2,1)S(1)} %shard_map.46.refs_1_.refs_0_, bf16[528,256]{1,0:T(8,128)(2,1)S(1)} %shard_map.46.refs_1_.refs_0_, bf16[256,256]{1,0:T(8,128)(2,1)S(1)} %collective-permute-done.2.refs_2_, bf16[272,256]{1,0:T(8,128)(2,1)S(1)} %collective-permute-done.3.refs_3_, ...), custom_call_target="tpu_custom_call" | custom-call | tf_op jit(solution)/shard_map/pallas_call | solution.py:185
  26.0 0.5 %collective-permute-done.9 = f32[4,128]{1,0:T(4,128)S(1)} collective-permute-done((f32[4,128]{1,0:T(4,128)S(1)}, f32[4,128]{1,0:T(4,128)S(1)}, u32[]{:S(2)}, u32[]{:S(2)}) %collective-permute-start.9) | collective-permute-done | bytes 2080 | tf_op jit(solution)/shard_map/ppermute | solution.py:244
  26.4 0.6 %collective-permute-done.8 = f32[4,128]{1,0:T(4,128)S(1)} collective-permute-done((f32[4,128]{1,0:T(4,128)S(1)}, f32[4,128]{1,0:T(4,128)S(1)}, u32[]{:S(2)}, u32[]{:S(2)}) %collective-permute-start.8) | collective-permute-done | bytes 2080 | tf_op jit(solution)/shard_map/ppermute | solution.py:218
  27.0 0.6 %maximum_bitcast_fusion = f32[512]{0:T(512)} fusion(f32[4,128]{1,0:T(4,128)S(1)} %collective-permute-done.9, f32[4,128]{1,0:T(4,128)S(1)} %collective-permute-done.8, f32[8,128]{1,0:T(8,128)S(1)} %shard_map.49, f32[8,128]{1,0:T(8,128)S(1)} %max.18), kind=kLoop, calls=%fused_computation | loop fusion | flops 2048 | bytes 10240 | tf_op jit(solution)/shard_map/reshape | solution.py:253
  (10 shorter events, 0.1 us)
Async XLA Ops:
  3.4 16.1 %collective-permute-start.6 = (bf16[528,256]{1,0:T(8,128)(2,1)S(1)}, bf16[528,256]{1,0:T(8,128)(2,1)S(1)}, u32[]{:S(2)}, u32[]{:S(2)}) collective-permute-start(bf16[528,256]{1,0:T(8,128)(2,1)S(1)} %shard_map.46.refs_1_.refs_0_), channel_id=1, source_target_pairs={{12,5},{13,4},{14,7},{15,6},{4,9},{5,8},{6,11},{7,10},{8,1},{9,0},... | collective-permute-start | bytes 811016 | tf_op jit(solution)/shard_map/ppermute | solution.py:229
  7.9 12.7 %collective-permute-start.1 = (bf16[528,256]{1,0:T(8,128)(2,1)S(1)}, bf16[528,256]{1,0:T(8,128)(2,1)S(1)}, u32[]{:S(2)}, u32[]{:S(2)}) collective-permute-start(bf16[528,256]{1,0:T(8,128)(2,1)S(1)} %shard_map.46.refs_1_.refs_0_), channel_id=1, source_target_pairs={{12,9},{13,8},{14,11},{15,10},{4,1},{5,0},{6,3},{7,2},{8,13},{9,12... | collective-permute-start | bytes 811016 | tf_op jit(solution)/shard_map/ppermute | solution.py:230
  7.9 10.0 %collective-permute-start.4 = (bf16[256,256]{1,0:T(8,128)(2,1)S(1)}, bf16[256,256]{1,0:T(8,128)(2,1)S(1)}, u32[]{:S(2)}, u32[]{:S(2)}) collective-permute-start(bf16[256,256]{1,0:T(8,128)(2,1)S(1)} %slice.28), channel_id=1, source_target_pairs={{0,1},{1,0},{2,3},{3,2},{4,5},{5,4},{6,7},{7,6},{8,9},{9,8},{10,11... | collective-permute-start | bytes 393224 | tf_op jit(solution)/shard_map/ppermute | solution.py:218
  8.7 10.8 %collective-permute-start.5 = (bf16[272,256]{1,0:T(8,128)(2,1)S(1)}, bf16[272,256]{1,0:T(8,128)(2,1)S(1)}, u32[]{:S(2)}, u32[]{:S(2)}) collective-permute-start(bf16[272,256]{1,0:T(8,128)(2,1)S(1)} %slice.29), channel_id=1, source_target_pairs={{0,1},{1,0},{2,3},{3,2},{4,5},{5,4},{6,7},{7,6},{8,9},{9,8},{10,11... | collective-permute-start | bytes 417800 | tf_op jit(solution)/shard_map/ppermute | solution.py:218
  8.8 8.9 %collective-permute-start = (bf16[528,256]{1,0:T(8,128)(2,1)S(1)}, bf16[528,256]{1,0:T(8,128)(2,1)S(1)}, u32[]{:S(2)}, u32[]{:S(2)}) collective-permute-start(bf16[528,256]{1,0:T(8,128)(2,1)S(1)} %get-tuple-element.65), channel_id=1, source_target_pairs={{0,2},{1,3},{2,0},{3,1},{4,6},{5,7},{6,4},{7,5},{8,10},{9,11},{10,... | collective-permute-start | bytes 811016 | tf_op jit(solution)/shard_map/while/body/ppermute | solution.py:218
  17.8 1.7 %collective-permute-start.3 = (bf16[272,256]{1,0:T(8,128)(2,1)S(1)}, bf16[272,256]{1,0:T(8,128)(2,1)S(1)}, u32[]{:S(2)}, u32[]{:S(2)}) collective-permute-start(bf16[272,256]{1,0:T(8,128)(2,1)S(1)} %slice.22), channel_id=1, source_target_pairs={{0,1},{1,0},{2,3},{3,2},{4,5},{5,4},{6,7},{7,6},{8,9},{9,8},{10,11... | collective-permute-start | bytes 417800 | tf_op jit(solution)/shard_map/ppermute | solution.py:218
  17.9 1.5 %collective-permute-start.2 = (bf16[256,256]{1,0:T(8,128)(2,1)S(1)}, bf16[256,256]{1,0:T(8,128)(2,1)S(1)}, u32[]{:S(2)}, u32[]{:S(2)}) collective-permute-start(bf16[256,256]{1,0:T(8,128)(2,1)S(1)} %slice.21), channel_id=1, source_target_pairs={{0,1},{1,0},{2,3},{3,2},{4,5},{5,4},{6,7},{7,6},{8,9},{9,8},{10,11... | collective-permute-start | bytes 393224 | tf_op jit(solution)/shard_map/ppermute | solution.py:218
  21.5 2.5 %collective-permute-start.7 = (f32[8,128]{1,0:T(8,128)S(1)}, f32[8,128]{1,0:T(8,128)S(1)}, u32[]{:S(2)}, u32[]{:S(2)}) collective-permute-start(f32[8,128]{1,0:T(8,128)S(1)} %get-tuple-element.32), channel_id=1, source_target_pairs={{0,1},{1,0},{2,3},{3,2},{4,5},{5,4},{6,7},{7,6},{8,9},{9,8},{10,11... | collective-permute-start | bytes 12296 | tf_op jit(solution)/shard_map/ppermute | solution.py:218
  21.6 4.8 %collective-permute-start.9 = (f32[4,128]{1,0:T(4,128)S(1)}, f32[4,128]{1,0:T(4,128)S(1)}, u32[]{:S(2)}, u32[]{:S(2)}) collective-permute-start(f32[4,128]{1,0:T(4,128)S(1)} %get-tuple-element.33), channel_id=1, source_target_pairs={{5,12},{4,13},{7,14},{6,15},{9,4},{8,5},{11,6},{10,7},{1,8},{0,9},... | collective-permute-start | bytes 6152 | tf_op jit(solution)/shard_map/ppermute | solution.py:244
  24.0 3.1 %collective-permute-start.8 = (f32[4,128]{1,0:T(4,128)S(1)}, f32[4,128]{1,0:T(4,128)S(1)}, u32[]{:S(2)}, u32[]{:S(2)}) collective-permute-start(f32[4,128]{1,0:T(4,128)S(1)} %slice.27), channel_id=1, source_target_pairs={{0,3},{1,2},{2,1},{3,0},{4,7},{5,6},{6,5},{7,4},{8,11},{9,10},{10,... | collective-permute-start | bytes 6152 | tf_op jit(solution)/shard_map/ppermute | solution.py:218

commit v32 on v28

--- a/solution.py
+++ b/solution.py
@@ -104,6 +104,7 @@
     row_outs = refs
     row_count = key_refs[0].shape[0] - TAG_ROWS
     tiles = row_count // LANES
+    columns = [key_ref[:row_count, :].T for key_ref in key_refs]
     best = [
         [jnp.full((8, LANES), ABSENT, jnp.float32) for _ in range(tiles)]
         for _ in range(key_count if own_first else cols)
@@ -121,11 +122,8 @@
             across = [None] * len(tags)
             for key, key_ref in enumerate(key_refs):
                 key_tags = key_ref[row_count:, :LANES].astype(jnp.float32)
-                scores = lax.dot_general(
-                    part_ref[:count, :],
-                    key_ref[:row_count, :],
-                    (((1,), (1,)), ((), ())),
-                    preferred_element_type=jnp.float32,
+                scores = jnp.dot(
+                    part_ref[:count, :], columns[key], preferred_element_type=jnp.float32
                 )
                 for tile, tag in enumerate(tags):
                     for at in range(tiles):

time: 27.8 us -> 27.8 us (level)
  no operation moved by 1% of the time
where the time goes in v32:
time: 27.8 us; the launch traced here: 27.6 us
  starting transfers between devices  11.3 us (41%)
  waiting for transfers between devices  9.76 us (35%)
  Pallas kernels  5.82 us (21%)
  other arithmetic  0.59 us (2%)
    ppermute x7, waiting for transfers between devices, swap(): lax.ppermute(block, 'split', [(s, s ^ offset) for s in range(split_count)])  8.98 us
    ppermute x1, starting transfers between devices, per_device(): keys = [lax.ppermute(own, both, step) for step in steps]  4.54 us
    ppermute x7, starting transfers between devices, swap(): lax.ppermute(block, 'split', [(s, s ^ offset) for s in range(split_count)])  4.4 us
    pallas_call x1, Pallas kernels, project(): pl.pallas_call(project_kernel, in_specs=[pl.BlockSpec(memory_space=pltpu....  3.38 us
    pallas_call x3, Pallas kernels, score(): pl.pallas_call(functools.partial(score_kernel, len(keys), cols, [len(row)...  2.44 us
    ppermute x1, starting transfers between devices, per_device(): backs.append(lax.ppermute(found, both, [(b, a) for a, b in step]))  2.32 us
    reshape x1, other arithmetic, per_device(): return jnp.maximum(best, -1.0).reshape(row_count)  0.58 us
  transfers between devices with their start and end apart: 10, of which 5 were waited for; matrix products, arithmetic and copies ran while one was open for 0% of the time, Pallas kernels for 6%

profile of v32, /device:TPU:0, one launch (start us, length us, event | category | flops | bytes accessed | tf_op | source)
XLA Modules:
  0.0 27.6 jit_solution(2951974120124515339)
XLA Ops:
  0.0 3.4 %shard_map.46.refs_1_.refs_0_ = bf16[528,256]{1,0:T(8,128)(2,1)S(1)} custom-call(bf16[512,4096]{1,0:T(8,128)(2,1)} %source_hbm.1, bf16[4096,256]{1,0:T(8,128)(2,1)} %basis_hbm.1, s32[4,128]{1,0:T(4,128)} %bitcast.4, s32[4,128]{1,0:T(4,128)} %bitcast.5), custom_call_target="tpu_custom_call" | custom-call | flops 1073741824 | bytes 6291456 | tf_op jit(solution)/shard_map/pallas_call | solution.py:65
  3.4 4.5 %collective-permute-start.6 = (bf16[528,256]{1,0:T(8,128)(2,1)S(1)}, bf16[528,256]{1,0:T(8,128)(2,1)S(1)}, u32[]{:S(2)}, u32[]{:S(2)}) collective-permute-start(bf16[528,256]{1,0:T(8,128)(2,1)S(1)} %shard_map.46.refs_1_.refs_0_), channel_id=1, source_target_pairs={{12,5},{13,4},{14,7},{15,6},{4,9},{5,8},{6,11},{7,10},{8,1},{9,0},... | collective-permute-start | bytes 811016 | tf_op jit(solution)/shard_map/ppermute | solution.py:221
  7.9 0.0 collective-permute-start.1
  7.9 0.7 %collective-permute-start.4 = (bf16[256,256]{1,0:T(8,128)(2,1)S(1)}, bf16[256,256]{1,0:T(8,128)(2,1)S(1)}, u32[]{:S(2)}, u32[]{:S(2)}) collective-permute-start(bf16[256,256]{1,0:T(8,128)(2,1)S(1)} %slice.28), channel_id=1, source_target_pairs={{0,1},{1,0},{2,3},{3,2},{4,5},{5,4},{6,7},{7,6},{8,9},{9,8},{10,11... | collective-permute-start | bytes 393224 | tf_op jit(solution)/shard_map/ppermute | solution.py:210
  8.7 0.1 collective-permute-start.5
  8.8 9.0 %while.10 = (s32[]{:T(128)}, bf16[528,256]{1,0:T(8,128)(2,1)S(1)}, s32[]{:T(128)}, s32[]{:T(128)}) while((s32[]{:T(128)}, bf16[528,256]{1,0:T(8,128)(2,1)S(1)}, s32[]{:T(128)}, s32[]{:T(128)}) %tuple.18), condition=%wide.region_1.0_spmd, body=%wide.region_0.0_spmd.sunk | while | flops 2 | bytes 1622109 | solution.py:225
  8.8 1.6 %collective-permute-start = (bf16[528,256]{1,0:T(8,128)(2,1)S(1)}, bf16[528,256]{1,0:T(8,128)(2,1)S(1)}, u32[]{:S(2)}, u32[]{:S(2)}) collective-permute-start(bf16[528,256]{1,0:T(8,128)(2,1)S(1)} %get-tuple-element.65), channel_id=1, source_target_pairs={{0,2},{1,3},{2,0},{3,1},{4,6},{5,7},{6,4},{7,5},{8,10},{9,11},{10,... | collective-permute-start | bytes 811016 | tf_op jit(solution)/shard_map/while/body/ppermute | solution.py:210
  10.4 7.4 %collective-permute-done = bf16[528,256]{1,0:T(8,128)(2,1)S(1)} collective-permute-done((bf16[528,256]{1,0:T(8,128)(2,1)S(1)}, bf16[528,256]{1,0:T(8,128)(2,1)S(1)}, u32[]{:S(2)}, u32[]{:S(2)}) %collective-permute-start) | collective-permute-done | bytes 270368 | tf_op jit(solution)/shard_map/while/body/ppermute | solution.py:210
  17.8 0.1 collective-permute-start.3
  17.9 0.6 %collective-permute-start.2 = (bf16[256,256]{1,0:T(8,128)(2,1)S(1)}, bf16[256,256]{1,0:T(8,128)(2,1)S(1)}, u32[]{:S(2)}, u32[]{:S(2)}) collective-permute-start(bf16[256,256]{1,0:T(8,128)(2,1)S(1)} %slice.21), channel_id=1, source_target_pairs={{0,1},{1,0},{2,3},{3,2},{4,5},{5,4},{6,7},{7,6},{8,9},{9,8},{10,11... | collective-permute-start | bytes 393224 | tf_op jit(solution)/shard_map/ppermute | solution.py:210
  18.5 1.0 %collective-permute-done.2.refs_2_ = bf16[256,256]{1,0:T(8,128)(2,1)S(1)} collective-permute-done((bf16[256,256]{1,0:T(8,128)(2,1)S(1)}, bf16[256,256]{1,0:T(8,128)(2,1)S(1)}, u32[]{:S(2)}, u32[]{:S(2)}) %collective-permute-start.2) | collective-permute-done | bytes 131104 | tf_op jit(solution)/shard_map/ppermute | solution.py:210
  19.5 0.0 collective-permute-done.5.refs_5_
  19.5 0.0 collective-permute-done.3.refs_3_
  19.5 0.0 collective-permute-done.6.refs_0_
  19.5 0.9 %shard_map.47 = (f32[4,128]{1,0:T(4,128)S(1)}, f32[8,128]{1,0:T(8,128)S(1)}, f32[8,128]{1,0:T(8,128)S(1)}) custom-call(bf16[528,256]{1,0:T(8,128)(2,1)S(1)} %collective-permute-done.6.refs_0_, bf16[528,256]{1,0:T(8,128)(2,1)S(1)} %shard_map.46.refs_1_.refs_0_, bf16[256,256]{1,0:T(8,128)(2,1)S(1)} %collective-permute-done.2.refs_2_, ...), custom_call_target="tpu_custom_call" | custom-call | tf_op jit(solution)/shard_map/pallas_call | solution.py:177
  20.3 0.3 %collective-permute-done.1.refs_0_ = bf16[528,256]{1,0:T(8,128)(2,1)S(1)} collective-permute-done((bf16[528,256]{1,0:T(8,128)(2,1)S(1)}, bf16[528,256]{1,0:T(8,128)(2,1)S(1)}, u32[]{:S(2)}, u32[]{:S(2)}) %collective-permute-start.1) | collective-permute-done | bytes 270368 | tf_op jit(solution)/shard_map/ppermute | solution.py:222
  20.6 0.8 %shard_map.48 = (f32[8,128]{1,0:T(8,128)S(1)}, f32[8,128]{1,0:T(8,128)S(1)}) custom-call(bf16[528,256]{1,0:T(8,128)(2,1)S(1)} %collective-permute-done.1.refs_0_, bf16[528,256]{1,0:T(8,128)(2,1)S(1)} %shard_map.46.refs_1_.refs_0_, bf16[256,256]{1,0:T(8,128)(2,1)S(1)} %collective-permute-done.2.refs_2_, bf16[272,256]{1,0:T(8,128)(2,1)S(1)} %collective-permute-done.3.refs_3_, ...), custom_call_target="tpu_custom_call" | custom-call | tf_op jit(solution)/shard_map/pallas_call | solution.py:177
  21.5 0.1 collective-permute-start.7
  21.6 2.3 %collective-permute-start.9 = (f32[4,128]{1,0:T(4,128)S(1)}, f32[4,128]{1,0:T(4,128)S(1)}, u32[]{:S(2)}, u32[]{:S(2)}) collective-permute-start(f32[4,128]{1,0:T(4,128)S(1)} %get-tuple-element.33), channel_id=1, source_target_pairs={{5,12},{4,13},{7,14},{6,15},{9,4},{8,5},{11,6},{10,7},{1,8},{0,9},... | collective-permute-start | bytes 6152 | tf_op jit(solution)/shard_map/ppermute | solution.py:236
  24.0 1.2 %collective-permute-start.8 = (f32[4,128]{1,0:T(4,128)S(1)}, f32[4,128]{1,0:T(4,128)S(1)}, u32[]{:S(2)}, u32[]{:S(2)}) collective-permute-start(f32[4,128]{1,0:T(4,128)S(1)} %slice.27), channel_id=1, source_target_pairs={{0,3},{1,2},{2,1},{3,0},{4,7},{5,6},{6,5},{7,4},{8,11},{9,10},{10,... | collective-permute-start | bytes 6152 | tf_op jit(solution)/shard_map/ppermute | solution.py:210
  25.2 0.8 %shard_map.49 = f32[8,128]{1,0:T(8,128)S(1)} custom-call(bf16[528,256]{1,0:T(8,128)(2,1)S(1)} %shard_map.46.refs_1_.refs_0_, bf16[528,256]{1,0:T(8,128)(2,1)S(1)} %shard_map.46.refs_1_.refs_0_, bf16[256,256]{1,0:T(8,128)(2,1)S(1)} %collective-permute-done.2.refs_2_, bf16[272,256]{1,0:T(8,128)(2,1)S(1)} %collective-permute-done.3.refs_3_, ...), custom_call_target="tpu_custom_call" | custom-call | tf_op jit(solution)/shard_map/pallas_call | solution.py:177
  26.0 0.5 %collective-permute-done.9 = f32[4,128]{1,0:T(4,128)S(1)} collective-permute-done((f32[4,128]{1,0:T(4,128)S(1)}, f32[4,128]{1,0:T(4,128)S(1)}, u32[]{:S(2)}, u32[]{:S(2)}) %collective-permute-start.9) | collective-permute-done | bytes 2080 | tf_op jit(solution)/shard_map/ppermute | solution.py:236
  26.4 0.6 %collective-permute-done.8 = f32[4,128]{1,0:T(4,128)S(1)} collective-permute-done((f32[4,128]{1,0:T(4,128)S(1)}, f32[4,128]{1,0:T(4,128)S(1)}, u32[]{:S(2)}, u32[]{:S(2)}) %collective-permute-start.8) | collective-permute-done | bytes 2080 | tf_op jit(solution)/shard_map/ppermute | solution.py:210
  27.0 0.6 %maximum_bitcast_fusion = f32[512]{0:T(512)} fusion(f32[4,128]{1,0:T(4,128)S(1)} %collective-permute-done.9, f32[4,128]{1,0:T(4,128)S(1)} %collective-permute-done.8, f32[8,128]{1,0:T(8,128)S(1)} %shard_map.49, f32[8,128]{1,0:T(8,128)S(1)} %max.18), kind=kLoop, calls=%fused_computation | loop fusion | flops 2048 | bytes 10240 | tf_op jit(solution)/shard_map/reshape | solution.py:245
  (10 shorter events, 0.1 us)
Async XLA Ops:
  3.4 16.1 %collective-permute-start.6 = (bf16[528,256]{1,0:T(8,128)(2,1)S(1)}, bf16[528,256]{1,0:T(8,128)(2,1)S(1)}, u32[]{:S(2)}, u32[]{:S(2)}) collective-permute-start(bf16[528,256]{1,0:T(8,128)(2,1)S(1)} %shard_map.46.refs_1_.refs_0_), channel_id=1, source_target_pairs={{12,5},{13,4},{14,7},{15,6},{4,9},{5,8},{6,11},{7,10},{8,1},{9,0},... | collective-permute-start | bytes 811016 | tf_op jit(solution)/shard_map/ppermute | solution.py:221
  7.9 12.7 %collective-permute-start.1 = (bf16[528,256]{1,0:T(8,128)(2,1)S(1)}, bf16[528,256]{1,0:T(8,128)(2,1)S(1)}, u32[]{:S(2)}, u32[]{:S(2)}) collective-permute-start(bf16[528,256]{1,0:T(8,128)(2,1)S(1)} %shard_map.46.refs_1_.refs_0_), channel_id=1, source_target_pairs={{12,9},{13,8},{14,11},{15,10},{4,1},{5,0},{6,3},{7,2},{8,13},{9,12... | collective-permute-start | bytes 811016 | tf_op jit(solution)/shard_map/ppermute | solution.py:222
  7.9 10.0 %collective-permute-start.4 = (bf16[256,256]{1,0:T(8,128)(2,1)S(1)}, bf16[256,256]{1,0:T(8,128)(2,1)S(1)}, u32[]{:S(2)}, u32[]{:S(2)}) collective-permute-start(bf16[256,256]{1,0:T(8,128)(2,1)S(1)} %slice.28), channel_id=1, source_target_pairs={{0,1},{1,0},{2,3},{3,2},{4,5},{5,4},{6,7},{7,6},{8,9},{9,8},{10,11... | collective-permute-start | bytes 393224 | tf_op jit(solution)/shard_map/ppermute | solution.py:210
  8.7 10.8 %collective-permute-start.5 = (bf16[272,256]{1,0:T(8,128)(2,1)S(1)}, bf16[272,256]{1,0:T(8,128)(2,1)S(1)}, u32[]{:S(2)}, u32[]{:S(2)}) collective-permute-start(bf16[272,256]{1,0:T(8,128)(2,1)S(1)} %slice.29), channel_id=1, source_target_pairs={{0,1},{1,0},{2,3},{3,2},{4,5},{5,4},{6,7},{7,6},{8,9},{9,8},{10,11... | collective-permute-start | bytes 417800 | tf_op jit(solution)/shard_map/ppermute | solution.py:210
  8.8 8.9 %collective-permute-start = (bf16[528,256]{1,0:T(8,128)(2,1)S(1)}, bf16[528,256]{1,0:T(8,128)(2,1)S(1)}, u32[]{:S(2)}, u32[]{:S(2)}) collective-permute-start(bf16[528,256]{1,0:T(8,128)(2,1)S(1)} %get-tuple-element.65), channel_id=1, source_target_pairs={{0,2},{1,3},{2,0},{3,1},{4,6},{5,7},{6,4},{7,5},{8,10},{9,11},{10,... | collective-permute-start | bytes 811016 | tf_op jit(solution)/shard_map/while/body/ppermute | solution.py:210
  17.8 1.7 %collective-permute-start.3 = (bf16[272,256]{1,0:T(8,128)(2,1)S(1)}, bf16[272,256]{1,0:T(8,128)(2,1)S(1)}, u32[]{:S(2)}, u32[]{:S(2)}) collective-permute-start(bf16[272,256]{1,0:T(8,128)(2,1)S(1)} %slice.22), channel_id=1, source_target_pairs={{0,1},{1,0},{2,3},{3,2},{4,5},{5,4},{6,7},{7,6},{8,9},{9,8},{10,11... | collective-permute-start | bytes 417800 | tf_op jit(solution)/shard_map/ppermute | solution.py:210
  17.9 1.5 %collective-permute-start.2 = (bf16[256,256]{1,0:T(8,128)(2,1)S(1)}, bf16[256,256]{1,0:T(8,128)(2,1)S(1)}, u32[]{:S(2)}, u32[]{:S(2)}) collective-permute-start(bf16[256,256]{1,0:T(8,128)(2,1)S(1)} %slice.21), channel_id=1, source_target_pairs={{0,1},{1,0},{2,3},{3,2},{4,5},{5,4},{6,7},{7,6},{8,9},{9,8},{10,11... | collective-permute-start | bytes 393224 | tf_op jit(solution)/shard_map/ppermute | solution.py:210
  21.5 2.5 %collective-permute-start.7 = (f32[8,128]{1,0:T(8,128)S(1)}, f32[8,128]{1,0:T(8,128)S(1)}, u32[]{:S(2)}, u32[]{:S(2)}) collective-permute-start(f32[8,128]{1,0:T(8,128)S(1)} %get-tuple-element.32), channel_id=1, source_target_pairs={{0,1},{1,0},{2,3},{3,2},{4,5},{5,4},{6,7},{7,6},{8,9},{9,8},{10,11... | collective-permute-start | bytes 12296 | tf_op jit(solution)/shard_map/ppermute | solution.py:210
  21.6 4.8 %collective-permute-start.9 = (f32[4,128]{1,0:T(4,128)S(1)}, f32[4,128]{1,0:T(4,128)S(1)}, u32[]{:S(2)}, u32[]{:S(2)}) collective-permute-start(f32[4,128]{1,0:T(4,128)S(1)} %get-tuple-element.33), channel_id=1, source_target_pairs={{5,12},{4,13},{7,14},{6,15},{9,4},{8,5},{11,6},{10,7},{1,8},{0,9},... | collective-permute-start | bytes 6152 | tf_op jit(solution)/shard_map/ppermute | solution.py:236
  24.0 3.1 %collective-permute-start.8 = (f32[4,128]{1,0:T(4,128)S(1)}, f32[4,128]{1,0:T(4,128)S(1)}, u32[]{:S(2)}, u32[]{:S(2)}) collective-permute-start(f32[4,128]{1,0:T(4,128)S(1)} %slice.27), channel_id=1, source_target_pairs={{0,3},{1,2},{2,1},{3,0},{4,7},{5,6},{6,5},{7,4},{8,11},{9,10},{10,... | collective-permute-start | bytes 6152 | tf_op jit(solution)/shard_map/ppermute | solution.py:210

commit v33 on v28

--- a/solution.py
+++ b/solution.py
@@ -12,7 +12,7 @@
 TAG_ROWS = 16
 ABSENT = -2.0
 STEPS = 8
-ROW_PARTS = 4
+ROW_PARTS = 2
 VMEM_LIMIT = 48 * 1024 * 1024
 
 

time: 27.8 us -> 27.8 us (level)
  no operation moved by 1% of the time
where the time goes in v33:
time: 27.8 us; the launch traced here: 27.6 us
  starting transfers between devices  11.3 us (41%)
  waiting for transfers between devices  9.75 us (35%)
  Pallas kernels  5.82 us (21%)
  other arithmetic  0.59 us (2%)
    ppermute x7, waiting for transfers between devices, swap(): lax.ppermute(block, 'split', [(s, s ^ offset) for s in range(split_count)])  8.99 us
    ppermute x1, starting transfers between devices, per_device(): keys = [lax.ppermute(own, both, step) for step in steps]  4.54 us
    ppermute x7, starting transfers between devices, swap(): lax.ppermute(block, 'split', [(s, s ^ offset) for s in range(split_count)])  4.41 us
    pallas_call x1, Pallas kernels, project(): pl.pallas_call(project_kernel, in_specs=[pl.BlockSpec(memory_space=pltpu....  3.37 us
    pallas_call x3, Pallas kernels, score(): pl.pallas_call(functools.partial(score_kernel, len(keys), cols, [len(row)...  2.46 us
    ppermute x1, starting transfers between devices, per_device(): backs.append(lax.ppermute(found, both, [(b, a) for a, b in step]))  2.32 us
    reshape x1, other arithmetic, per_device(): return jnp.maximum(best, -1.0).reshape(row_count)  0.58 us
  transfers between devices with their start and end apart: 10, of which 5 were waited for; matrix products, arithmetic and copies ran while one was open for 0% of the time, Pallas kernels for 6%

profile of v33, /device:TPU:0, one launch (start us, length us, event | category | flops | bytes accessed | tf_op | source)
XLA Modules:
  0.0 27.6 jit_solution(10317237943524653335)
XLA Ops:
  0.0 3.4 %shard_map.46.refs_1_.refs_0_ = bf16[528,256]{1,0:T(8,128)(2,1)S(1)} custom-call(bf16[512,4096]{1,0:T(8,128)(2,1)} %source_hbm.1, bf16[4096,256]{1,0:T(8,128)(2,1)} %basis_hbm.1, s32[4,128]{1,0:T(4,128)} %bitcast.4, s32[4,128]{1,0:T(4,128)} %bitcast.5), custom_call_target="tpu_custom_call" | custom-call | flops 1073741824 | bytes 6291456 | tf_op jit(solution)/shard_map/pallas_call | solution.py:65
  3.4 4.5 %collective-permute-start.6 = (bf16[528,256]{1,0:T(8,128)(2,1)S(1)}, bf16[528,256]{1,0:T(8,128)(2,1)S(1)}, u32[]{:S(2)}, u32[]{:S(2)}) collective-permute-start(bf16[528,256]{1,0:T(8,128)(2,1)S(1)} %shard_map.46.refs_1_.refs_0_), channel_id=1, source_target_pairs={{12,5},{13,4},{14,7},{15,6},{4,9},{5,8},{6,11},{7,10},{8,1},{9,0},... | collective-permute-start | bytes 811016 | tf_op jit(solution)/shard_map/ppermute | solution.py:223
  7.9 0.0 collective-permute-start.1
  7.9 0.7 %collective-permute-start.4 = (bf16[256,256]{1,0:T(8,128)(2,1)S(1)}, bf16[256,256]{1,0:T(8,128)(2,1)S(1)}, u32[]{:S(2)}, u32[]{:S(2)}) collective-permute-start(bf16[256,256]{1,0:T(8,128)(2,1)S(1)} %slice.28), channel_id=1, source_target_pairs={{0,1},{1,0},{2,3},{3,2},{4,5},{5,4},{6,7},{7,6},{8,9},{9,8},{10,11... | collective-permute-start | bytes 393224 | tf_op jit(solution)/shard_map/ppermute | solution.py:212
  8.7 0.1 collective-permute-start.5
  8.8 9.0 %while.10 = (s32[]{:T(128)}, bf16[528,256]{1,0:T(8,128)(2,1)S(1)}, s32[]{:T(128)}, s32[]{:T(128)}) while((s32[]{:T(128)}, bf16[528,256]{1,0:T(8,128)(2,1)S(1)}, s32[]{:T(128)}, s32[]{:T(128)}) %tuple.18), condition=%wide.region_1.0_spmd, body=%wide.region_0.0_spmd.sunk | while | flops 2 | bytes 1622109 | solution.py:227
  8.8 1.6 %collective-permute-start = (bf16[528,256]{1,0:T(8,128)(2,1)S(1)}, bf16[528,256]{1,0:T(8,128)(2,1)S(1)}, u32[]{:S(2)}, u32[]{:S(2)}) collective-permute-start(bf16[528,256]{1,0:T(8,128)(2,1)S(1)} %get-tuple-element.65), channel_id=1, source_target_pairs={{0,2},{1,3},{2,0},{3,1},{4,6},{5,7},{6,4},{7,5},{8,10},{9,11},{10,... | collective-permute-start | bytes 811016 | tf_op jit(solution)/shard_map/while/body/ppermute | solution.py:212
  10.4 7.4 %collective-permute-done = bf16[528,256]{1,0:T(8,128)(2,1)S(1)} collective-permute-done((bf16[528,256]{1,0:T(8,128)(2,1)S(1)}, bf16[528,256]{1,0:T(8,128)(2,1)S(1)}, u32[]{:S(2)}, u32[]{:S(2)}) %collective-permute-start) | collective-permute-done | bytes 270368 | tf_op jit(solution)/shard_map/while/body/ppermute | solution.py:212
  17.8 0.1 collective-permute-start.3
  17.9 0.6 %collective-permute-start.2 = (bf16[256,256]{1,0:T(8,128)(2,1)S(1)}, bf16[256,256]{1,0:T(8,128)(2,1)S(1)}, u32[]{:S(2)}, u32[]{:S(2)}) collective-permute-start(bf16[256,256]{1,0:T(8,128)(2,1)S(1)} %slice.21), channel_id=1, source_target_pairs={{0,1},{1,0},{2,3},{3,2},{4,5},{5,4},{6,7},{7,6},{8,9},{9,8},{10,11... | collective-permute-start | bytes 393224 | tf_op jit(solution)/shard_map/ppermute | solution.py:212
  18.5 1.0 %collective-permute-done.2.refs_2_ = bf16[256,256]{1,0:T(8,128)(2,1)S(1)} collective-permute-done((bf16[256,256]{1,0:T(8,128)(2,1)S(1)}, bf16[256,256]{1,0:T(8,128)(2,1)S(1)}, u32[]{:S(2)}, u32[]{:S(2)}) %collective-permute-start.2) | collective-permute-done | bytes 131104 | tf_op jit(solution)/shard_map/ppermute | solution.py:212
  19.5 0.0 collective-permute-done.5.refs_5_
  19.5 0.0 collective-permute-done.3.refs_3_
  19.5 0.0 collective-permute-done.6.refs_0_
  19.5 0.9 %shard_map.47 = (f32[4,128]{1,0:T(4,128)S(1)}, f32[8,128]{1,0:T(8,128)S(1)}, f32[8,128]{1,0:T(8,128)S(1)}) custom-call(bf16[528,256]{1,0:T(8,128)(2,1)S(1)} %collective-permute-done.6.refs_0_, bf16[528,256]{1,0:T(8,128)(2,1)S(1)} %shard_map.46.refs_1_.refs_0_, bf16[256,256]{1,0:T(8,128)(2,1)S(1)} %collective-permute-done.2.refs_2_, ...), custom_call_target="tpu_custom_call" | custom-call | tf_op jit(solution)/shard_map/pallas_call | solution.py:179
  20.3 0.3 %collective-permute-done.1.refs_0_ = bf16[528,256]{1,0:T(8,128)(2,1)S(1)} collective-permute-done((bf16[528,256]{1,0:T(8,128)(2,1)S(1)}, bf16[528,256]{1,0:T(8,128)(2,1)S(1)}, u32[]{:S(2)}, u32[]{:S(2)}) %collective-permute-start.1) | collective-permute-done | bytes 270368 | tf_op jit(solution)/shard_map/ppermute | solution.py:224
  20.6 0.8 %shard_map.48 = (f32[8,128]{1,0:T(8,128)S(1)}, f32[8,128]{1,0:T(8,128)S(1)}) custom-call(bf16[528,256]{1,0:T(8,128)(2,1)S(1)} %collective-permute-done.1.refs_0_, bf16[528,256]{1,0:T(8,128)(2,1)S(1)} %shard_map.46.refs_1_.refs_0_, bf16[256,256]{1,0:T(8,128)(2,1)S(1)} %collective-permute-done.2.refs_2_, bf16[272,256]{1,0:T(8,128)(2,1)S(1)} %collective-permute-done.3.refs_3_, ...), custom_call_target="tpu_custom_call" | custom-call | tf_op jit(solution)/shard_map/pallas_call | solution.py:179
  21.5 0.2 collective-permute-start.7
  21.6 2.3 %collective-permute-start.9 = (f32[4,128]{1,0:T(4,128)S(1)}, f32[4,128]{1,0:T(4,128)S(1)}, u32[]{:S(2)}, u32[]{:S(2)}) collective-permute-start(f32[4,128]{1,0:T(4,128)S(1)} %get-tuple-element.33), channel_id=1, source_target_pairs={{5,12},{4,13},{7,14},{6,15},{9,4},{8,5},{11,6},{10,7},{1,8},{0,9},... | collective-permute-start | bytes 6152 | tf_op jit(solution)/shard_map/ppermute | solution.py:238
  24.0 1.2 %collective-permute-start.8 = (f32[4,128]{1,0:T(4,128)S(1)}, f32[4,128]{1,0:T(4,128)S(1)}, u32[]{:S(2)}, u32[]{:S(2)}) collective-permute-start(f32[4,128]{1,0:T(4,128)S(1)} %slice.27), channel_id=1, source_target_pairs={{0,3},{1,2},{2,1},{3,0},{4,7},{5,6},{6,5},{7,4},{8,11},{9,10},{10,... | collective-permute-start | bytes 6152 | tf_op jit(solution)/shard_map/ppermute | solution.py:212
  25.2 0.8 %shard_map.49 = f32[8,128]{1,0:T(8,128)S(1)} custom-call(bf16[528,256]{1,0:T(8,128)(2,1)S(1)} %shard_map.46.refs_1_.refs_0_, bf16[528,256]{1,0:T(8,128)(2,1)S(1)} %shard_map.46.refs_1_.refs_0_, bf16[256,256]{1,0:T(8,128)(2,1)S(1)} %collective-permute-done.2.refs_2_, bf16[272,256]{1,0:T(8,128)(2,1)S(1)} %collective-permute-done.3.refs_3_, ...), custom_call_target="tpu_custom_call" | custom-call | tf_op jit(solution)/shard_map/pallas_call | solution.py:179
  26.0 0.5 %collective-permute-done.9 = f32[4,128]{1,0:T(4,128)S(1)} collective-permute-done((f32[4,128]{1,0:T(4,128)S(1)}, f32[4,128]{1,0:T(4,128)S(1)}, u32[]{:S(2)}, u32[]{:S(2)}) %collective-permute-start.9) | collective-permute-done | bytes 2080 | tf_op jit(solution)/shard_map/ppermute | solution.py:238
  26.4 0.6 %collective-permute-done.8 = f32[4,128]{1,0:T(4,128)S(1)} collective-permute-done((f32[4,128]{1,0:T(4,128)S(1)}, f32[4,128]{1,0:T(4,128)S(1)}, u32[]{:S(2)}, u32[]{:S(2)}) %collective-permute-start.8) | collective-permute-done | bytes 2080 | tf_op jit(solution)/shard_map/ppermute | solution.py:212
  27.0 0.6 %maximum_bitcast_fusion = f32[512]{0:T(512)} fusion(f32[4,128]{1,0:T(4,128)S(1)} %collective-permute-done.9, f32[4,128]{1,0:T(4,128)S(1)} %collective-permute-done.8, f32[8,128]{1,0:T(8,128)S(1)} %shard_map.49, f32[8,128]{1,0:T(8,128)S(1)} %max.18), kind=kLoop, calls=%fused_computation | loop fusion | flops 2048 | bytes 10240 | tf_op jit(solution)/shard_map/reshape | solution.py:247
  (10 shorter events, 0.1 us)
Async XLA Ops:
  3.4 16.1 %collective-permute-start.6 = (bf16[528,256]{1,0:T(8,128)(2,1)S(1)}, bf16[528,256]{1,0:T(8,128)(2,1)S(1)}, u32[]{:S(2)}, u32[]{:S(2)}) collective-permute-start(bf16[528,256]{1,0:T(8,128)(2,1)S(1)} %shard_map.46.refs_1_.refs_0_), channel_id=1, source_target_pairs={{12,5},{13,4},{14,7},{15,6},{4,9},{5,8},{6,11},{7,10},{8,1},{9,0},... | collective-permute-start | bytes 811016 | tf_op jit(solution)/shard_map/ppermute | solution.py:223
  7.9 12.7 %collective-permute-start.1 = (bf16[528,256]{1,0:T(8,128)(2,1)S(1)}, bf16[528,256]{1,0:T(8,128)(2,1)S(1)}, u32[]{:S(2)}, u32[]{:S(2)}) collective-permute-start(bf16[528,256]{1,0:T(8,128)(2,1)S(1)} %shard_map.46.refs_1_.refs_0_), channel_id=1, source_target_pairs={{12,9},{13,8},{14,11},{15,10},{4,1},{5,0},{6,3},{7,2},{8,13},{9,12... | collective-permute-start | bytes 811016 | tf_op jit(solution)/shard_map/ppermute | solution.py:224
  7.9 10.0 %collective-permute-start.4 = (bf16[256,256]{1,0:T(8,128)(2,1)S(1)}, bf16[256,256]{1,0:T(8,128)(2,1)S(1)}, u32[]{:S(2)}, u32[]{:S(2)}) collective-permute-start(bf16[256,256]{1,0:T(8,128)(2,1)S(1)} %slice.28), channel_id=1, source_target_pairs={{0,1},{1,0},{2,3},{3,2},{4,5},{5,4},{6,7},{7,6},{8,9},{9,8},{10,11... | collective-permute-start | bytes 393224 | tf_op jit(solution)/shard_map/ppermute | solution.py:212
  8.7 10.8 %collective-permute-start.5 = (bf16[272,256]{1,0:T(8,128)(2,1)S(1)}, bf16[272,256]{1,0:T(8,128)(2,1)S(1)}, u32[]{:S(2)}, u32[]{:S(2)}) collective-permute-start(bf16[272,256]{1,0:T(8,128)(2,1)S(1)} %slice.29), channel_id=1, source_target_pairs={{0,1},{1,0},{2,3},{3,2},{4,5},{5,4},{6,7},{7,6},{8,9},{9,8},{10,11... | collective-permute-start | bytes 417800 | tf_op jit(solution)/shard_map/ppermute | solution.py:212
  8.8 8.9 %collective-permute-start = (bf16[528,256]{1,0:T(8,128)(2,1)S(1)}, bf16[528,256]{1,0:T(8,128)(2,1)S(1)}, u32[]{:S(2)}, u32[]{:S(2)}) collective-permute-start(bf16[528,256]{1,0:T(8,128)(2,1)S(1)} %get-tuple-element.65), channel_id=1, source_target_pairs={{0,2},{1,3},{2,0},{3,1},{4,6},{5,7},{6,4},{7,5},{8,10},{9,11},{10,... | collective-permute-start | bytes 811016 | tf_op jit(solution)/shard_map/while/body/ppermute | solution.py:212
  17.8 1.7 %collective-permute-start.3 = (bf16[272,256]{1,0:T(8,128)(2,1)S(1)}, bf16[272,256]{1,0:T(8,128)(2,1)S(1)}, u32[]{:S(2)}, u32[]{:S(2)}) collective-permute-start(bf16[272,256]{1,0:T(8,128)(2,1)S(1)} %slice.22), channel_id=1, source_target_pairs={{0,1},{1,0},{2,3},{3,2},{4,5},{5,4},{6,7},{7,6},{8,9},{9,8},{10,11... | collective-permute-start | bytes 417800 | tf_op jit(solution)/shard_map/ppermute | solution.py:212
  17.9 1.5 %collective-permute-start.2 = (bf16[256,256]{1,0:T(8,128)(2,1)S(1)}, bf16[256,256]{1,0:T(8,128)(2,1)S(1)}, u32[]{:S(2)}, u32[]{:S(2)}) collective-permute-start(bf16[256,256]{1,0:T(8,128)(2,1)S(1)} %slice.21), channel_id=1, source_target_pairs={{0,1},{1,0},{2,3},{3,2},{4,5},{5,4},{6,7},{7,6},{8,9},{9,8},{10,11... | collective-permute-start | bytes 393224 | tf_op jit(solution)/shard_map/ppermute | solution.py:212
  21.5 2.5 %collective-permute-start.7 = (f32[8,128]{1,0:T(8,128)S(1)}, f32[8,128]{1,0:T(8,128)S(1)}, u32[]{:S(2)}, u32[]{:S(2)}) collective-permute-start(f32[8,128]{1,0:T(8,128)S(1)} %get-tuple-element.32), channel_id=1, source_target_pairs={{0,1},{1,0},{2,3},{3,2},{4,5},{5,4},{6,7},{7,6},{8,9},{9,8},{10,11... | collective-permute-start | bytes 12296 | tf_op jit(solution)/shard_map/ppermute | solution.py:212
  21.6 4.8 %collective-permute-start.9 = (f32[4,128]{1,0:T(4,128)S(1)}, f32[4,128]{1,0:T(4,128)S(1)}, u32[]{:S(2)}, u32[]{:S(2)}) collective-permute-start(f32[4,128]{1,0:T(4,128)S(1)} %get-tuple-element.33), channel_id=1, source_target_pairs={{5,12},{4,13},{7,14},{6,15},{9,4},{8,5},{11,6},{10,7},{1,8},{0,9},... | collective-permute-start | bytes 6152 | tf_op jit(solution)/shard_map/ppermute | solution.py:238
  24.0 3.1 %collective-permute-start.8 = (f32[4,128]{1,0:T(4,128)S(1)}, f32[4,128]{1,0:T(4,128)S(1)}, u32[]{:S(2)}, u32[]{:S(2)}) collective-permute-start(f32[4,128]{1,0:T(4,128)S(1)} %slice.27), channel_id=1, source_target_pairs={{0,3},{1,2},{2,1},{3,0},{4,7},{5,6},{6,5},{7,4},{8,11},{9,10},{10,... | collective-permute-start | bytes 6152 | tf_op jit(solution)/shard_map/ppermute | solution.py:212
